TPU v7x, 128 devices: a whole 4x4x4 slice. The times are simulated.
128 devices in a mesh: blk: 64 (over y_lo, z, x, core), head: 2 (over y_hi).
Axes of the slice: x: 4, y: 4 (y_hi: 2, y_lo: 2; y = y_hi * 2 + y_lo), z: 4, core: 2. Of those that a mesh axis runs over, the one named last changes fastest.
Arguments:
- tokens: bfloat16 [16384, 1536], P(('blk', 'head')), may hold values from -6 to 6
- segments: int32 [16384], replicated, may hold values from 0 to 31, as said below
- attn_gain: bfloat16 [1536], P(('blk', 'head')), may hold values from 0.25 to 1.75
- w_query: bfloat16 [1536, 1536], P(('blk', 'head')), may hold values from -0.15625 to 0.15625
- key_projection_weight: bfloat16 [1536, 512], P(('blk', 'head')), may hold values from -0.15625 to 0.15625
- value_projection_weight: bfloat16 [1536, 512], P(('blk', 'head')), may hold values from -0.15625 to 0.15625
- q_gain: bfloat16 [64], replicated, may hold values from 0.25 to 1.75
- k_gain: bfloat16 [64], replicated, may hold values from 0.25 to 1.75
- w_out: bfloat16 [1536, 1536], P('head', 'blk'), may hold values from -0.4375 to 0.4375
- ffn_gain: bfloat16 [1536], P(('blk', 'head')), may hold values from 0.25 to 1.75
- w_gate: bfloat16 [1536, 6912], P('blk', 'head'), may hold values from -0.15625 to 0.15625
- w_up: bfloat16 [1536, 6912], P('blk', 'head'), may hold values from -0.15625 to 0.15625
- w_down: bfloat16 [6912, 1536], P('head', 'blk'), may hold values from -0.078125 to 0.078125
- cotangent: bfloat16 [16384, 1536], P(('blk', 'head')), may hold values from -6 to 6
Outputs:
- output: bfloat16 [16384, 1536], P(('blk', 'head'))
- input_grad: bfloat16 [16384, 1536], P(('blk', 'head'))
- attn_gain_grad: float32 [1536], P(('blk', 'head'))
- w_query_grad: float32 [1536, 1536], P(('blk', 'head'))
- w_key_grad: float32 [1536, 512], P(('blk', 'head'))
- w_value_grad: float32 [1536, 512], P(('blk', 'head'))
- q_gain_grad: float32 [64], replicated
- k_gain_grad: float32 [64], replicated
- w_out_grad: float32 [1536, 1536], P('head', 'blk')
- ffn_gain_grad: float32 [1536], P(('blk', 'head'))
- w_gate_grad: float32 [1536, 6912], P('blk', 'head')
- w_up_grad: float32 [1536, 6912], P('blk', 'head')
- w_down_grad: float32 [6912, 1536], P('head', 'blk')
Inputs may be any that keep to these rules, and one draw needn't show every extreme that they name: `segments`: segment numbers never fall along the tokens and every number from 0 to 31 occurs; each document holds 1 to 4096 tokens; the first document holds exactly 4096.
All inputs are finite; a program needn't handle non-finite values.
Results may differ from a plain program's by a relative error of at most 0.034.
Values may be sent and summed in bfloat16 or wider, within the bound.
No kernel may reach another device: no remote copies, remote signals or barrier semaphores. Data moves between devices by JAX's collectives and lax.ppermute only.
A program may use at most 256 MiB of HBM per device.

v0:
```python
import jax
import jax.numpy as jnp
from jax import lax
from jax.sharding import PartitionSpec as P

DOCMAX = 4096


EPS = 1e-05
THETA = 1000000.0
NEG_FILL = -1e30
CONTRACT_LAST = (((1,), (1,)), ((), ()))
CONTRACT_FIRST = (((0,), (0,)), ((), ()))


def passed_along(block, axis, distance):
    devices = range(lax.axis_size(axis))
    route = [(i - distance, i) for i in devices if i - distance in devices]
    return lax.ppermute(block, axis, route)


def rms_scale(array_in):
    return lax.rsqrt(jnp.mean(array_in * array_in, axis=-1, keepdims=True) + EPS)


def rms_back(grad_in, array_in, scale_in):
    inner = jnp.mean(grad_in * array_in, axis=-1, keepdims=True)
    return scale_in * (grad_in - array_in * scale_in * scale_in * inner)


def rotary(positions, head_dim):
    half_dim = head_dim // 2
    frequency = THETA ** (-jnp.arange(half_dim, dtype=jnp.float32) * 2.0 / head_dim)
    angles = positions.astype(jnp.float32)[:, None] * frequency[None, :]
    return (jnp.cos(angles)[:, None, :], jnp.sin(angles)[:, None, :])


def rotate(array_in, cosine_table, sine_table):
    half_dim = array_in.shape[-1] // 2
    first_half = array_in[..., :half_dim]
    second_half = array_in[..., half_dim:]
    return jnp.concatenate(
        [
            first_half * cosine_table - second_half * sine_table,
            second_half * cosine_table + first_half * sine_table,
        ],
        axis=-1,
    )


def product(left_side, right_side, numbers):
    return lax.dot_general(left_side, right_side, numbers, preferred_element_type=jnp.float32)


def per_device(
    tokens,
    segments,
    attn_gain,
    w_query,
    key_projection_weight,
    value_projection_weight,
    q_gain,
    k_gain,
    w_out,
    ffn_gain,
    w_gate,
    w_up,
    w_down,
    cotangent,
):
    head_count = lax.axis_size("head")
    block_count = lax.axis_size("blk")
    blk_index = lax.axis_index("blk")
    head_index = lax.axis_index("head")
    tok_rows = tokens.shape[0]
    block_rows = tok_rows * head_count
    head_dim = q_gain.shape[0]
    query_cols = w_query.shape[1]
    value_cols = key_projection_weight.shape[1]
    query_heads = query_cols // head_dim
    value_heads = value_cols // head_dim
    local_kv = value_heads // head_count
    heads_per_group = query_cols // value_cols
    local_query_cols = query_cols // head_count
    local_value_cols = value_cols // head_count
    total_tokens = segments.shape[0]
    longest = min(DOCMAX, tok_rows * block_count)
    cycle_len = min(block_count, (longest - 1) // block_rows + 2)
    qk_scale = head_dim ** (-0.5)

    def own_rows(array_in):
        return lax.dynamic_slice_in_dim(array_in, head_index * tok_rows, tok_rows, 0)

    token_index = jnp.arange(total_tokens, dtype=jnp.int32)
    begins = jnp.concatenate([jnp.ones((1,), jnp.bool_), segments[1:] != segments[:-1]])
    positions = token_index - lax.cummax(jnp.where(begins, token_index, 0), axis=0)
    own_start = (blk_index * head_count + head_index) * tok_rows
    cosine_table, sine_table = rotary(
        lax.dynamic_slice_in_dim(positions, own_start, tok_rows, 0), head_dim
    )
    block_start = blk_index * block_rows
    row_index = jnp.arange(block_rows, dtype=jnp.int32)
    query_segments = lax.dynamic_slice_in_dim(segments, block_start, block_rows, 0)
    query_index = block_start + row_index

    def allowed_pairs(source):
        key_start = jnp.maximum(source, 0) * block_rows
        key_segments = lax.dynamic_slice_in_dim(segments, key_start, block_rows, 0)
        key_index = key_start + row_index
        return (
            (query_segments[:, None] == key_segments[None, :])
            & (key_index[None, :] <= query_index[:, None])
            & (source >= 0)
        )

    gain_attn, gain_ffn, full_query, full_key, full_value = (
        lax.all_gather(attn_gain, ("blk", "head"), axis=0, tiled=True),
        lax.all_gather(ffn_gain, ("blk", "head"), axis=0, tiled=True),
        lax.all_gather(w_query, ("blk", "head"), axis=0, tiled=True),
        lax.all_gather(key_projection_weight, ("blk", "head"), axis=0, tiled=True),
        lax.all_gather(value_projection_weight, ("blk", "head"), axis=0, tiled=True),
    )
    out_rows, gate_part, up_part, down_part = (
        lax.all_gather(w_out, "blk", axis=1, tiled=True),
        lax.all_gather(w_gate, "blk", axis=0, tiled=True),
        lax.all_gather(w_up, "blk", axis=0, tiled=True),
        lax.all_gather(w_down, "blk", axis=1, tiled=True),
    )
    inputs = tokens.astype(jnp.float32)
    scale_attn = rms_scale(inputs)
    normalized_input = (inputs * scale_attn * gain_attn.astype(jnp.float32)).astype(jnp.bfloat16)
    raw_query = jnp.dot(normalized_input, full_query, preferred_element_type=jnp.float32).reshape(
        tok_rows, query_heads, head_dim
    )
    raw_key = jnp.dot(normalized_input, full_key, preferred_element_type=jnp.float32).reshape(
        tok_rows, value_heads, head_dim
    )
    raw_value = jnp.dot(normalized_input, full_value, preferred_element_type=jnp.float32)
    query_scale = rms_scale(raw_query)
    key_scale = rms_scale(raw_key)
    query_gain = q_gain.astype(jnp.float32)
    key_gain = k_gain.astype(jnp.float32)
    rot_query = rotate(raw_query * query_scale * query_gain, cosine_table, sine_table).astype(
        jnp.bfloat16
    )
    rot_key = rotate(raw_key * key_scale * key_gain, cosine_table, sine_table).astype(jnp.bfloat16)
    value_low = raw_value.astype(jnp.bfloat16)
    head_query, head_key, head_value = (
        lax.all_to_all(
            rot_query.reshape(tok_rows, head_count, local_query_cols),
            "head",
            split_axis=1,
            concat_axis=0,
            tiled=True,
        ),
        lax.all_to_all(
            rot_key.reshape(tok_rows, head_count, local_value_cols),
            "head",
            split_axis=1,
            concat_axis=0,
            tiled=True,
        ),
        lax.all_to_all(
            value_low.reshape(tok_rows, head_count, local_value_cols),
            "head",
            split_axis=1,
            concat_axis=0,
            tiled=True,
        ),
    )
    query_tile_block = head_query.reshape(block_rows, local_kv, heads_per_group, head_dim)
    head_key = head_key.reshape(block_rows, local_value_cols)
    head_value = head_value.reshape(block_rows, local_value_cols)

    def scores_of(key_block, allowed):
        key_heads = key_block.reshape(block_rows, local_kv, head_dim)
        raw_scores = (
            jnp.einsum(
                "qkgd,tkd->kgqt", query_tile_block, key_heads, preferred_element_type=jnp.float32
            )
            * qk_scale
        )
        return jnp.where(allowed[None, None], raw_scores, NEG_FILL)

    def visit(softmax_state, key_block, value_block, cycle_step):
        allowed = allowed_pairs(blk_index - cycle_step)

        def visit_accumulate():
            row_max, row_total, accum = softmax_state
            scores = scores_of(key_block, allowed)
            new_max = jnp.maximum(row_max, jnp.max(scores, axis=-1))
            weights = jnp.exp(scores - new_max[..., None])
            factor = jnp.exp(row_max - new_max)
            new_total = row_total * factor + jnp.sum(weights, axis=-1)
            value_heads_block = value_block.reshape(block_rows, local_kv, head_dim)
            new_accum = accum * factor[..., None] + jnp.einsum(
                "kgqt,tkd->kgqd",
                weights.astype(jnp.bfloat16),
                value_heads_block,
                preferred_element_type=jnp.float32,
            )
            return (new_max, new_total, new_accum)

        return lax.cond(jnp.any(allowed), visit_accumulate, lambda: softmax_state)

    start_state = (
        jnp.full((local_kv, heads_per_group, block_rows), NEG_FILL, jnp.float32),
        jnp.zeros((local_kv, heads_per_group, block_rows), jnp.float32),
        jnp.zeros((local_kv, heads_per_group, block_rows, head_dim), jnp.float32),
    )
    softmax_state = visit(start_state, head_key, head_value, 0)

    def cycle_forward(carry, cycle_step):
        current_state, key_block, value_block = carry
        key_block, value_block = passed_along((key_block, value_block), "blk", 1)
        current_state = visit(current_state, key_block, value_block, cycle_step)
        return ((current_state, key_block, value_block), (key_block, value_block))

    (softmax_state, last_key, last_value), visited = lax.scan(
        cycle_forward,
        (softmax_state, head_key, head_value),
        jnp.arange(1, cycle_len, dtype=jnp.int32),
    )
    keys_stack = jnp.concatenate([head_key[None], visited[0]], axis=0)
    values_stack = jnp.concatenate([head_value[None], visited[1]], axis=0)
    row_max, row_total, accum = softmax_state
    log_total = row_max + jnp.log(row_total)
    mixture_heads = jnp.transpose(accum / row_total[..., None], (2, 0, 1, 3))
    mixture_low = mixture_heads.reshape(block_rows, local_query_cols).astype(jnp.bfloat16)
    partial_out = jnp.dot(mixture_low, out_rows, preferred_element_type=jnp.float32)
    attention_sum = lax.psum(partial_out.astype(jnp.bfloat16), "head").astype(jnp.float32)
    gate_weights, up_weights, down_weights = (gate_part, up_part, down_part)
    pair_tokens, pair_cot = (
        lax.all_gather(tokens, "head", axis=0, tiled=True),
        lax.all_gather(cotangent, "head", axis=0, tiled=True),
    )
    residual = pair_tokens.astype(jnp.float32) + attention_sum
    gain_ffn_float = gain_ffn.astype(jnp.float32)
    scale_ffn = rms_scale(residual)
    scaled_ffn = residual * scale_ffn
    normed_ffn = (scaled_ffn * gain_ffn_float).astype(jnp.bfloat16)
    gate_value = jnp.dot(normed_ffn, gate_weights, preferred_element_type=jnp.float32)
    up_value = jnp.dot(normed_ffn, up_weights, preferred_element_type=jnp.float32)
    sigmoid_gate = jax.nn.sigmoid(gate_value)
    silu_gate = gate_value * sigmoid_gate
    activation = (silu_gate * up_value).astype(jnp.bfloat16)
    ffn_term = jnp.dot(activation, down_weights, preferred_element_type=jnp.float32)
    output = (
        own_rows(residual)
        + lax.psum_scatter(
            ffn_term.astype(jnp.bfloat16), "head", scatter_dimension=0, tiled=True
        ).astype(jnp.float32)
    ).astype(jnp.bfloat16)
    grad_act = product(pair_cot, down_weights, CONTRACT_LAST)
    grad_gate = (
        grad_act * up_value * sigmoid_gate * (1.0 + gate_value * (1.0 - sigmoid_gate))
    ).astype(jnp.bfloat16)
    grad_up = (grad_act * silu_gate).astype(jnp.bfloat16)
    grad_normed_ffn = product(grad_gate, gate_weights, CONTRACT_LAST) + product(
        grad_up, up_weights, CONTRACT_LAST
    )
    grad_gate_w = product(normed_ffn, grad_gate, CONTRACT_FIRST)
    grad_up_w = product(normed_ffn, grad_up, CONTRACT_FIRST)
    grad_down_w = product(activation, pair_cot, CONTRACT_FIRST)
    pair_total = lax.psum(grad_normed_ffn.astype(jnp.bfloat16), "head").astype(jnp.float32)
    ffn_gain_part = jnp.sum(own_rows(pair_total * scaled_ffn), axis=0)
    grad_hidden = pair_cot.astype(jnp.float32) + rms_back(
        pair_total * gain_ffn_float, residual, scale_ffn
    )
    grad_branch = grad_hidden.astype(jnp.bfloat16)
    grad_out_rows = product(mixture_low, grad_branch, CONTRACT_FIRST)
    grad_mixture = product(grad_branch, out_rows, CONTRACT_LAST).astype(jnp.bfloat16)
    grad_heads = grad_mixture.reshape(block_rows, local_kv, heads_per_group, head_dim)
    row_delta = jnp.einsum("qkgd,qkgd->kgq", grad_heads.astype(jnp.float32), mixture_heads)

    def back_visit(gradients, key_block, value_block, cycle_step):
        allowed = allowed_pairs(blk_index - cycle_step)

        def back_accumulate():
            grad_query, grad_key, grad_value = gradients
            key_heads = key_block.reshape(block_rows, local_kv, head_dim)
            value_heads_block = value_block.reshape(block_rows, local_kv, head_dim)
            weights = jnp.exp(scores_of(key_block, allowed) - log_total[..., None])
            grad_weights = jnp.einsum(
                "qkgd,tkd->kgqt", grad_heads, value_heads_block, preferred_element_type=jnp.float32
            )
            grad_scores = (weights * (grad_weights - row_delta[..., None])).astype(jnp.bfloat16)
            new_value = jnp.einsum(
                "kgqt,qkgd->tkd",
                weights.astype(jnp.bfloat16),
                grad_heads,
                preferred_element_type=jnp.float32,
            )
            new_key = (
                jnp.einsum(
                    "kgqt,qkgd->tkd",
                    grad_scores,
                    query_tile_block,
                    preferred_element_type=jnp.float32,
                )
                * qk_scale
            )
            new_query = (
                jnp.einsum(
                    "kgqt,tkd->kgqd", grad_scores, key_heads, preferred_element_type=jnp.float32
                )
                * qk_scale
            )
            return (
                grad_query + new_query,
                grad_key + new_key.reshape(block_rows, local_value_cols),
                grad_value + new_value.reshape(block_rows, local_value_cols),
            )

        return lax.cond(jnp.any(allowed), back_accumulate, lambda: gradients)

    empty_grads = (
        jnp.zeros((local_kv, heads_per_group, block_rows, head_dim), jnp.float32),
        jnp.zeros((block_rows, local_value_cols), jnp.float32),
        jnp.zeros((block_rows, local_value_cols), jnp.float32),
    )
    gradients = back_visit(
        empty_grads, keys_stack[cycle_len - 1], values_stack[cycle_len - 1], cycle_len - 1
    )

    def cycle_backward(carry, scanned):
        cycle_step, key_block, value_block = scanned
        grad_query, grad_key, grad_value = carry
        grad_key, grad_value = (
            passed_along(grad_key.astype(jnp.bfloat16), "blk", -1).astype(grad_key.dtype),
            passed_along(grad_value.astype(jnp.bfloat16), "blk", -1).astype(grad_value.dtype),
        )
        return (
            back_visit((grad_query, grad_key, grad_value), key_block, value_block, cycle_step),
            None,
        )

    gradients, unused = lax.scan(
        cycle_backward,
        gradients,
        (
            jnp.arange(cycle_len - 1, dtype=jnp.int32),
            keys_stack[: cycle_len - 1],
            values_stack[: cycle_len - 1],
        ),
        reverse=True,
    )
    grad_query, grad_key, grad_value = gradients
    grad_query_rows = jnp.transpose(grad_query, (2, 0, 1, 3)).reshape(
        block_rows, 1, local_query_cols
    )
    token_query, token_key, token_value = (
        lax.all_to_all(
            grad_query_rows.astype(jnp.bfloat16), "head", split_axis=0, concat_axis=1, tiled=True
        ),
        lax.all_to_all(
            grad_key.astype(jnp.bfloat16).reshape(block_rows, 1, local_value_cols),
            "head",
            split_axis=0,
            concat_axis=1,
            tiled=True,
        ),
        lax.all_to_all(
            grad_value.astype(jnp.bfloat16).reshape(block_rows, 1, local_value_cols),
            "head",
            split_axis=0,
            concat_axis=1,
            tiled=True,
        ),
    )
    grad_query_norm = rotate(
        token_query.astype(jnp.float32).reshape(tok_rows, query_heads, head_dim),
        cosine_table,
        -sine_table,
    )
    grad_key_norm = rotate(
        token_key.astype(jnp.float32).reshape(tok_rows, value_heads, head_dim),
        cosine_table,
        -sine_table,
    )
    q_gain_part = jnp.sum(grad_query_norm * raw_query * query_scale, axis=(0, 1))
    k_gain_part = jnp.sum(grad_key_norm * raw_key * key_scale, axis=(0, 1))
    grad_raw_query = (
        rms_back(grad_query_norm * query_gain, raw_query, query_scale)
        .astype(jnp.bfloat16)
        .reshape(tok_rows, query_cols)
    )
    grad_raw_key = (
        rms_back(grad_key_norm * key_gain, raw_key, key_scale)
        .astype(jnp.bfloat16)
        .reshape(tok_rows, value_cols)
    )
    grad_raw_value = token_value.reshape(tok_rows, value_cols)
    grad_normed = (
        product(grad_raw_query, full_query, CONTRACT_LAST)
        + product(grad_raw_key, full_key, CONTRACT_LAST)
        + product(grad_raw_value, full_value, CONTRACT_LAST)
    )
    grad_wq = product(normalized_input, grad_raw_query, CONTRACT_FIRST)
    grad_wk = product(normalized_input, grad_raw_key, CONTRACT_FIRST)
    grad_wv = product(normalized_input, grad_raw_value, CONTRACT_FIRST)
    attn_gain_part = jnp.sum(grad_normed * inputs * scale_attn, axis=0)
    input_grad = (
        own_rows(grad_hidden)
        + rms_back(grad_normed * gain_attn.astype(jnp.float32), inputs, scale_attn)
    ).astype(jnp.bfloat16)
    device_count = block_count * head_count
    gain_rows = jnp.broadcast_to(
        jnp.concatenate([q_gain_part, k_gain_part])[None, :], (device_count, 2 * head_dim)
    )
    attn_gain_grad, ffn_gain_grad, w_query_grad, w_key_grad, w_value_grad, gain_total = (
        lax.psum_scatter(attn_gain_part, ("blk", "head"), scatter_dimension=0, tiled=True),
        lax.psum_scatter(ffn_gain_part, ("blk", "head"), scatter_dimension=0, tiled=True),
        lax.psum_scatter(grad_wq, ("blk", "head"), scatter_dimension=0, tiled=True),
        lax.psum_scatter(grad_wk, ("blk", "head"), scatter_dimension=0, tiled=True),
        lax.psum_scatter(grad_wv, ("blk", "head"), scatter_dimension=0, tiled=True),
        lax.psum_scatter(gain_rows, ("blk", "head"), scatter_dimension=0, tiled=True),
    )
    w_out_grad, w_gate_grad, w_up_grad, w_down_grad = (
        lax.psum_scatter(grad_out_rows, "blk", scatter_dimension=1, tiled=True),
        lax.psum_scatter(grad_gate_w, "blk", scatter_dimension=0, tiled=True),
        lax.psum_scatter(grad_up_w, "blk", scatter_dimension=0, tiled=True),
        lax.psum_scatter(grad_down_w, "blk", scatter_dimension=1, tiled=True),
    )
    return (
        output,
        input_grad,
        attn_gain_grad,
        w_query_grad,
        w_key_grad,
        w_value_grad,
        gain_total[0, :head_dim],
        gain_total[0, head_dim:],
        w_out_grad,
        ffn_gain_grad,
        w_gate_grad,
        w_up_grad,
        w_down_grad,
    )


def solution(mesh):
    placed = (
        P(("blk", "head"), None),
        P(),
        P(("blk", "head")),
        P(("blk", "head"), None),
        P(("blk", "head"), None),
        P(("blk", "head"), None),
        P(),
        P(),
        P("head", "blk"),
        P(("blk", "head")),
        P("blk", "head"),
        P("blk", "head"),
        P("head", "blk"),
        P(("blk", "head"), None),
    )
    return jax.shard_map(
        per_device,
        mesh=mesh,
        in_specs=placed,
        out_specs=(
            P(("blk", "head"), None),
            P(("blk", "head"), None),
            P(("blk", "head")),
            P(("blk", "head"), None),
            P(("blk", "head"), None),
            P(("blk", "head"), None),
            P(),
            P(),
            P("head", "blk"),
            P(("blk", "head")),
            P("blk", "head"),
            P("blk", "head"),
            P("head", "blk"),
        ),
        check_vma=False,
    )
```

profile of v0, /device:TPU:8, one launch (start us, length us, event | category | flops | bytes accessed | tf_op | source)
XLA Modules:
  0.0 4099.3 jit_solution(4659438815626731084)
XLA Ops:
  12.9 66.8 %all-reduce.15 = (bf16[1536]{0:T(1024)(128)(2,1)S(1)}, bf16[1536]{0:T(1024)(128)(2,1)}) all-reduce(bf16[1536]{0:T(1024)(128)(2,1)S(1)} %dynamic-update-slice, bf16[1536]{0:T(1024)(128)(2,1)S(1)} %dynamic-update-slice.1), channel_id=1, replica_groups=mesh['blk'=64,'head'=2] {'blk','head'}, use_global_device_ids=true, to_apply=%add | all-reduce | flops 3072 | bytes 12288
  86.9 224.6 %all-gather.19.cloned.1.call-done = bf16[128,12,512]{2,1,0:T(8,128)(2,1)} async-done(((bf16[1,12,512]{2,1,0:T(8,128)(2,1)}), bf16[128,12,512]{2,1,0:T(8,128)(2,1)}) %all-gather.19.cloned.1.call-update) | async-done | bytes 1572880 | tf_op jit(solution)/shard_map/all_gather | solution.py:120
  320.1 294.6 %all-gather.23.cloned.1.call-done = bf16[128,12,512]{2,1,0:T(8,128)(2,1)} async-done(((bf16[1,12,512]{2,1,0:T(8,128)(2,1)}), bf16[128,12,512]{2,1,0:T(8,128)(2,1)}) %all-gather.23.cloned.1.call-update) | async-done | bytes 1572880 | tf_op jit(solution)/shard_map/all_gather | solution.py:121
  620.0 307.6 %all-gather.21.cloned.1.call-done = bf16[128,12,1536]{2,1,0:T(8,128)(2,1)} async-done(((bf16[1,12,1536]{2,1,0:T(8,128)(2,1)}), bf16[128,12,1536]{2,1,0:T(8,128)(2,1)}) %all-gather.21.cloned.1.call-update) | async-done | bytes 4718608 | tf_op jit(solution)/shard_map/all_gather | solution.py:119
  927.7 8.2 reshape.364
  963.5 8.8 conditional.4
  972.3 255.6 %while.42 = (s32[]{:T(128)}, f32[4,3,256]{2,1,0:T(4,128)}, f32[4,3,256]{2,1,0:T(4,128)S(1)}, f32[4,3,256,64]{2,3,1,0:T(8,128)S(1)}, bf16[256,256]{0,1:T(8,128)(2...) while((s32[]{:T(128)}, f32[4,3,256]{2,1,0:T(4,128)}, ...), condition=%wide.region_16.17_spmd.clone, body=%wide.region_10.16_spmd.clone.sunk | while | flops 210704896 | bytes 14229987 | solution.py:219
  1233.9 20.7 all_gather.33
  1254.5 10.2 all_gather.43
  1264.7 8.4 all-reduce.21.cloned.1.call-done
  1278.0 111.6 %all-gather.13.cloned.1.call-done = bf16[1536,3456]{1,0:T(8,128)(2,1)} async-done(((bf16[24,3456]{1,0:T(8,128)(2,1)}), bf16[1536,3456]{1,0:T(8,128)(2,1)}) %all-gather.13.cloned.1.call-update) | async-done | bytes 10616848 | tf_op jit(solution)/shard_map/all_gather | solution.py:125
  1389.6 9.1 fusion.114
  1398.7 107.1 %all-gather.15.cloned.1.call-done = bf16[1536,3456]{1,0:T(8,128)(2,1)} async-done(((bf16[24,3456]{1,0:T(8,128)(2,1)}), bf16[1536,3456]{1,0:T(8,128)(2,1)}) %all-gather.15.cloned.1.call-update) | async-done | bytes 10616848 | tf_op jit(solution)/shard_map/all_gather | solution.py:126
  1505.8 9.0 fusion.115
  1514.9 107.2 %all-gather.17.cloned.1.call-done = bf16[3456,1536]{0,1:T(8,128)(2,1)} async-done(((bf16[3456,24]{0,1:T(8,128)(2,1)}), bf16[3456,1536]{0,1:T(8,128)(2,1)}) %all-gather.17.cloned.1.call-update) | async-done | bytes 10616848 | tf_op jit(solution)/shard_map/all_gather | solution.py:127
  1622.1 11.5 multiply_convert_fusion
  1633.6 7.7 fusion.116
  1651.5 35.1 all-reduce.23.cloned.1.call-done
  1695.9 500.0 %while.43 = (s32[]{:T(128)}, f32[4,3,256,64]{2,3,1,0:T(8,128)S(1)}, f32[256,256]{0,1:T(8,128)S(1)}, f32[256,256]{0,1:T(8,128)S(1)}, s32[256]{0:T(256)S(1)}, /*in...) while((s32[]{:T(128)}, f32[4,3,256,64]{2,3,1,0:T(8,128)S(1)}, ...), condition=%wide.region_29.30_spmd.clone, body=%wide.region_25.29_spmd.clone.sunk | while | flops 512360960 | bytes 23180368 | solution.py:338
  1696.0 8.9 collective-permute-start.2
  1704.9 10.2 collective-permute-start.3
  1719.3 16.3 collective-permute-start.2
  1735.6 10.2 collective-permute-start.3
  1750.1 16.5 collective-permute-start.2
  1766.6 10.2 collective-permute-start.3
  1781.1 16.8 collective-permute-start.2
  1797.9 10.2 collective-permute-start.3
  1812.3 16.8 collective-permute-start.2
  1829.2 10.2 collective-permute-start.3
  1843.6 16.8 collective-permute-start.2
  1860.5 10.2 collective-permute-start.3
  1874.9 16.8 collective-permute-start.2
  1891.8 10.2 collective-permute-start.3
  1906.2 16.8 collective-permute-start.2
  1923.1 10.2 collective-permute-start.3
  1944.4 10.0 collective-permute-start.2
  1954.4 10.2 collective-permute-start.3
  1975.7 10.0 collective-permute-start.2
  1985.7 10.2 collective-permute-start.3
  2007.0 10.0 collective-permute-start.2
  2017.0 10.2 collective-permute-start.3
  2038.3 10.2 collective-permute-start.2
  2048.5 10.2 collective-permute-start.3
  2069.8 10.2 collective-permute-start.2
  2080.1 10.2 collective-permute-start.3
  2101.4 10.2 collective-permute-start.2
  2111.6 10.2 collective-permute-start.3
  2132.9 10.2 collective-permute-start.2
  2143.1 10.2 collective-permute-start.3
  2164.4 10.2 collective-permute-start.2
  2174.7 10.2 collective-permute-start.3
  2235.4 8.6 convolution_convert_fusion
  2248.4 10.2 fusion.118
  2258.7 10.2 fusion.119
  2270.0 10.2 fusion.120
  2281.1 8.6 all_to_all.80
  2299.7 462.6 %fusion.106 = (f32[16,1536]{1,0:T(8,128)}, f32[16,512]{1,0:T(8,128)S(1)}, f32[16,512]{1,0:T(8,128)S(1)}) fusion(f32[1536,1536]{1,0:T(8,128)} %fusion.99, f32[1536,512]{1,0:T(8,128)} %fusion.97, f32[1536,512]{1,0:T(8,128)} %fusion.95), kind=kCustom, calls=%all-reduce-scatter.3 | all-reduce-scatter fusion | flops 5242881 | bytes 15892480
  2976.9 72.8 %all-reduce.14 = (f32[1536]{0:T(1024)S(1)}, f32[1536]{0:T(1024)S(1)}) all-reduce(f32[1536]{0:T(1024)S(1)} %get-tuple-element.795, f32[1536]{0:T(1024)S(1)} %fusion.84), channel_id=3, replica_groups=mesh['blk'=64,'head'=2] {'blk','head'}, use_global_device_ids=true, to_apply=%region_34.35.clone | all-reduce | flops 3072 | bytes 24576
  3082.0 25.2 concatenate.45
  3107.2 26.6 concatenate.44
  3173.5 51.0 %concatenate.43 = f32[524,1536]{1,0:T(8,128)} concatenate(f32[12,1536]{1,0:T(8,128)S(1)} %collective-permute-done.35, f32[16,1536]{1,0:T(8,128)} %copy-done.46, f32[16,1536]{1,0:T(8,128)} %copy-done.45, f32[16,1536]{1,0:T(8,128)} %copy-done.44, f32[16,1536]{1,0:T(8,128)S(1)} %collective-permute-done.31, f32[16,1536]{1,0:T(8,128)} %collective-permute-done.30, ...), dimensions={0} | concatenate | bytes 6438912
  3227.9 224.2 %reduce-scatter.25.cloned.1.call-done = f32[24,3456]{1,0:T(8,128)} async-done(((f32[1536,3456]{1,0:T(8,128)}), f32[24,3456]{1,0:T(8,128)}) %reduce-scatter.25.cloned.1.call-update) | async-done | bytes 331792
  3452.1 320.6 %reduce-scatter.27.cloned.1.call-done = f32[24,3456]{1,0:T(8,128)} async-done(((f32[1536,3456]{1,0:T(8,128)}), f32[24,3456]{1,0:T(8,128)}) %reduce-scatter.27.cloned.1.call-update) | async-done | bytes 331792
  3772.7 319.6 %reduce-scatter.29.cloned.1.call-done = f32[3456,24]{0,1:T(8,128)} async-done(((f32[3456,1536]{0,1:T(8,128)}), f32[3456,24]{0,1:T(8,128)}) %reduce-scatter.29.cloned.1.call-update) | async-done | bytes 331792
  (1224 shorter events, 877.3 us)
Async XLA Ops:
  7.2 304.4 %all-gather.19.cloned.1.call-start = ((), (), s32[]{:S(2)}) async-start(), calls=%async_computation.19 | async-start | bytes 2113536 | tf_op jit(solution)/shard_map/all_gather | solution.py:120
  7.9 606.8 %all-gather.23.cloned.1.call-start = ((), (), s32[]{:S(2)}) async-start(), calls=%async_computation.21 | async-start | bytes 2113536 | tf_op jit(solution)/shard_map/all_gather | solution.py:121
  8.7 919.0 %all-gather.21.cloned.1.call-start = ((), (), s32[]{:S(2)}) async-start(), calls=%async_computation.20 | async-start | bytes 6340608 | tf_op jit(solution)/shard_map/all_gather | solution.py:119
  9.4 1218.6 %all-gather.11.cloned.1.call-start = ((), (), s32[]{:S(2)}) async-start(), calls=%async_computation.11 | async-start | bytes 2396160 | tf_op jit(solution)/shard_map/all_gather | solution.py:124
  316.1 624.4 %all-to-all-start = ((bf16[128,2,256]{0,2,1:T(8,128)(2,1)}), bf16[128,2,256]{0,2,1:T(8,128)(2,1)}, u32[]{:S(2)}, u32[]{:S(2)}) async-start(bf16[128,2,256]{0,2,1:T(8,128)(2,1)} %bitcast.48), calls=%async_computation | async-start | bytes 262144 | tf_op jit(solution)/shard_map/all_to_all | solution.py:156
  953.9 319.2 %all-reduce.21.cloned.1.call-start = ((), (), s32[]{:S(2)}) async-start(), calls=%async_computation.12 | async-start | bytes 1572864 | tf_op jit(solution)/shard_map/psum | solution.py:231
  1231.7 157.9 %all-gather.13.cloned.1.call-start = ((), (), s32[]{:S(2)}) async-start(), calls=%async_computation.13 | async-start | bytes 10782720 | tf_op jit(solution)/shard_map/all_gather | solution.py:125
  1232.3 273.6 %all-gather.15.cloned.1.call-start = ((), (), s32[]{:S(2)}) async-start(), calls=%async_computation.14 | async-start | bytes 10782720 | tf_op jit(solution)/shard_map/all_gather | solution.py:126
  1233.0 389.0 %all-gather.17.cloned.1.call-start = ((), (), s32[]{:S(2)}) async-start(), calls=%async_computation.15 | async-start | bytes 10782720 | tf_op jit(solution)/shard_map/all_gather | solution.py:127
  1233.8 452.8 %all-reduce.23.cloned.1.call-start = ((), (), s32[]{:S(2)}) async-start(), calls=%async_computation.17 | async-start | bytes 1572864 | tf_op jit(solution)/shard_map/psum | solution.py:265
  1696.0 22.6 collective-permute-start.2
  1719.3 30.0 collective-permute-start.2
  1750.1 30.2 collective-permute-start.2
  1781.1 30.5 collective-permute-start.2
  1812.3 30.5 collective-permute-start.2
  1843.6 30.5 collective-permute-start.2
  1874.9 30.5 collective-permute-start.2
  1906.2 30.5 collective-permute-start.2
  1944.4 23.7 collective-permute-start.2
  1975.7 23.7 collective-permute-start.2
  2007.0 23.7 collective-permute-start.2
  2038.3 23.9 collective-permute-start.2
  2069.8 23.9 collective-permute-start.2
  2101.4 23.9 collective-permute-start.2
  2132.9 23.9 collective-permute-start.2
  2164.4 23.9 collective-permute-start.2
  2215.1 851.3 %all-reduce.25.cloned.1.call-start = ((), (), s32[]{:S(2)}) async-start(), calls=%async_computation.22 | async-start | bytes 131072
  2235.3 990.8 %reduce-scatter.21.cloned.1.call-start = ((), (), s32[]{:S(2)}) async-start(), calls=%async_computation.16 | async-start | bytes 1179648 | tf_op jit(solution)/shard_map/reduce_scatter | solution.py:250
  2244.0 983.9 %reduce-scatter.23.cloned.1.call-start = ((), (), s32[]{:S(2)}) async-start(), calls=%async_computation.18 | async-start | bytes 4792320 | tf_op jit(solution)/shard_map/reduce_scatter | solution.py:420
  2247.2 1204.9 %reduce-scatter.25.cloned.1.call-start = ((), (), s32[]{:S(2)}) async-start(), calls=%async_computation.23 | async-start | bytes 21565440
  2258.6 1514.1 %reduce-scatter.27.cloned.1.call-start = ((), (), s32[]{:S(2)}) async-start(), calls=%async_computation.24 | async-start | bytes 21565440
  2268.9 1823.4 %reduce-scatter.29.cloned.1.call-start = ((), (), s32[]{:S(2)}) async-start(), calls=%async_computation.25 | async-start | bytes 21565440
  2765.0 26.5 collective-permute-start.68
  2768.4 25.2 collective-permute-start.69
  2770.4 27.7 collective-permute-start.70
  2774.4 27.5 collective-permute-start.71
  2786.1 20.5 collective-permute-start.72
  2791.4 18.3 collective-permute-start.73
  2793.7 19.7 collective-permute-start.74
  2798.0 17.3 collective-permute-start.75
  2801.9 16.3 collective-permute-start.76
  2857.2 17.5 collective-permute-start.36
  2866.8 16.3 collective-permute-start.39
  2869.1 18.5 collective-permute-start.40
  2876.7 16.1 collective-permute-start.42
  2940.5 21.8 collective-permute-start.10
  2944.4 16.0 collective-permute-start.35
  2947.2 17.1 collective-permute-start.11
  2949.6 16.6 collective-permute-start.12
  2964.3 86.6 %collective-permute-start.16 = (f32[16,1536]{1,0:T(8,128)}, f32[16,1536]{1,0:T(8,128)S(1)}, u32[]{:S(2)}, u32[]{:S(2)}) collective-permute-start(f32[16,1536]{1,0:T(8,128)} %get-tuple-element.862), channel_id=1, source_target_pairs={{0,13},{1,14},{2,15},{3,16},{4,17},{5,18},{6,19},{7,20},{8,21},{9,... | collective-permute-start | bytes 294920
  2966.2 86.9 %collective-permute-start.17 = (f32[16,1536]{1,0:T(8,128)}, f32[16,1536]{1,0:T(8,128)S(1)}, u32[]{:S(2)}, u32[]{:S(2)}) collective-permute-start(f32[16,1536]{1,0:T(8,128)} %get-tuple-element.862), channel_id=1, source_target_pairs={{0,14},{1,15},{2,16},{3,17},{4,18},{5,19},{6,20},{7,21},{8,22},{9,... | collective-permute-start | bytes 294920
  2968.1 90.2 %collective-permute-start.18 = (f32[16,1536]{1,0:T(8,128)}, f32[16,1536]{1,0:T(8,128)S(1)}, u32[]{:S(2)}, u32[]{:S(2)}) collective-permute-start(f32[16,1536]{1,0:T(8,128)} %get-tuple-element.862), channel_id=1, source_target_pairs={{0,15},{1,16},{2,17},{3,18},{4,19},{5,20},{6,21},{7,22},{8,23},{9,... | collective-permute-start | bytes 294920
  2970.8 90.4 %collective-permute-start.19 = (f32[16,1536]{1,0:T(8,128)}, f32[16,1536]{1,0:T(8,128)S(1)}, u32[]{:S(2)}, u32[]{:S(2)}) collective-permute-start(f32[16,1536]{1,0:T(8,128)} %get-tuple-element.862), channel_id=1, source_target_pairs={{0,16},{1,17},{2,18},{3,19},{4,20},{5,21},{6,22},{7,23},{8,24},{9,... | collective-permute-start | bytes 294920
  2973.7 90.8 %collective-permute-start.20 = (f32[16,1536]{1,0:T(8,128)}, f32[16,1536]{1,0:T(8,128)S(1)}, u32[]{:S(2)}, u32[]{:S(2)}) collective-permute-start(f32[16,1536]{1,0:T(8,128)} %get-tuple-element.862), channel_id=1, source_target_pairs={{0,17},{1,18},{2,19},{3,20},{4,21},{5,22},{6,23},{7,24},{8,25},{9,... | collective-permute-start | bytes 294920
  3050.8 16.3 collective-permute-start.21
  3053.1 16.0 collective-permute-start.22
  3067.1 66.7 %collective-permute-start.26 = (f32[16,1536]{1,0:T(8,128)}, f32[16,1536]{1,0:T(8,128)}, u32[]{:S(2)}, u32[]{:S(2)}) collective-permute-start(f32[16,1536]{1,0:T(8,128)} %get-tuple-element.862), channel_id=1, source_target_pairs={{0,23},{1,24},{2,25},{3,26},{4,27},{5,28},{6,29},{7,30},{8,31},{9,... | collective-permute-start | bytes 294920
  3069.1 66.7 %collective-permute-start.27 = (f32[16,1536]{1,0:T(8,128)}, f32[16,1536]{1,0:T(8,128)}, u32[]{:S(2)}, u32[]{:S(2)}) collective-permute-start(f32[16,1536]{1,0:T(8,128)} %get-tuple-element.862), channel_id=1, source_target_pairs={{0,24},{1,25},{2,26},{3,27},{4,28},{5,29},{6,30},{7,31},{8,32},{9,... | collective-permute-start | bytes 294920
  3071.0 66.7 %collective-permute-start.28 = (f32[16,1536]{1,0:T(8,128)}, f32[16,1536]{1,0:T(8,128)}, u32[]{:S(2)}, u32[]{:S(2)}) collective-permute-start(f32[16,1536]{1,0:T(8,128)} %get-tuple-element.862), channel_id=1, source_target_pairs={{0,25},{1,26},{2,27},{3,28},{4,29},{5,30},{6,31},{7,32},{8,33},{9,... | collective-permute-start | bytes 294920
  3075.3 64.3 %collective-permute-start.29 = (f32[16,1536]{1,0:T(8,128)}, f32[16,1536]{1,0:T(8,128)}, u32[]{:S(2)}, u32[]{:S(2)}) collective-permute-start(f32[16,1536]{1,0:T(8,128)} %get-tuple-element.862), channel_id=1, source_target_pairs={{0,26},{1,27},{2,28},{3,29},{4,30},{5,31},{6,32},{7,33},{8,34},{9,... | collective-permute-start | bytes 294920
  3079.5 62.1 %collective-permute-start.30 = (f32[16,1536]{1,0:T(8,128)}, f32[16,1536]{1,0:T(8,128)}, u32[]{:S(2)}, u32[]{:S(2)}) collective-permute-start(f32[16,1536]{1,0:T(8,128)} %get-tuple-element.862), channel_id=1, source_target_pairs={{0,27},{1,28},{2,29},{3,30},{4,31},{5,32},{6,33},{7,34},{8,35},{9,... | collective-permute-start | bytes 294920
  3137.7 18.3 collective-permute-start.33
  3139.7 18.5 collective-permute-start.34
  3141.6 18.5 collective-permute-start.4
  (263 other events, 10054.5 us)
Sparse Core Ops, SparseCore 0:
  9.7 301.8 all-gather.18
  313.3 301.3 all-gather.22
  616.4 311.2 all-gather.20
  929.2 106.9 all-gather.10
  1231.8 41.2 all-reduce.20
  1274.8 114.7 all-gather.12
  1391.4 114.3 all-gather.14
  1507.7 114.3 all-gather.16
  1645.4 41.1 all-reduce.22
  2235.4 568.2 all-reduce.24
  2806.2 20.7 reduce-scatter.20
  2829.9 301.1 reduce-scatter.22
  3134.0 318.0 reduce-scatter.24
  3454.9 317.7 reduce-scatter.26
  3775.6 316.6 reduce-scatter.28
where the time goes:
time: 4120 us; the launch traced here: 4100 us
  waiting for transfers between devices  2200 us (53%)
  starting transfers between devices  683 us (17%)
  blocking collectives  642 us (16%)
  local copies, waits for them, and re-layouts  246 us (6%)
  matrix products  174 us (4%)
  other arithmetic  86.5 us (2%)
  loops' own time  46 us (1%)
    unnamed x115, waiting for transfers between devices  910 us
    unnamed x3, blocking collectives  602 us
    ppermute x64, starting transfers between devices, passed_along(): return lax.ppermute(block, axis, route)  433 us
    all_gather x1, waiting for transfers between devices, per_device(): lax.all_gather(w_query, ('blk', 'head'), axis=0, tiled=True)  308 us
    all_gather x1, waiting for transfers between devices, per_device(): lax.all_gather(value_projection_weight, ('blk', 'head'), axis=0, tiled=True)  295 us
    unnamed x100, starting transfers between devices  231 us
    all_gather x1, waiting for transfers between devices, per_device(): lax.all_gather(key_projection_weight, ('blk', 'head'), axis=0, tiled=True)  225 us
    unnamed x257, local copies, waits for them, and re-layouts  130 us
  transfers between devices with their start and end apart: 180, of which 67 were waited for; matrix products, arithmetic and copies ran while one was open for 21% of the time, Pallas kernels for 0%

commit v1 on v0

v1 whole, which is shorter than its diff:
```python
import functools

import jax
import jax.numpy as jnp
import numpy as np
from jax import lax
from jax.experimental import pallas as pl
from jax.experimental.pallas import tpu as pltpu
from jax.sharding import Mesh
from jax.sharding import PartitionSpec as P

EPS = 1e-05
THETA = 1000000.0
HEAD = 64
ROWS = 128
PAIR = 2 * ROWS
GROUP = 3
QUERY = GROUP * HEAD
LANES = ROWS * GROUP
KEY_TILE = 512
SUPER = 2048
EARLIER = 2 * SUPER
PART = 432
PADDED = 512
WIDTH = 1536
ALL = ("ylo", "z", "x", "core", "yhi")
BLK = ("ylo", "z", "x", "core")
WIDE = ("yhi", "ylo", "z")
NEAR = ("x", "core")
NN = (((1,), (0,)), ((), ()))
NT = (((1,), (1,)), ((), ()))
TN = (((0,), (0,)), ((), ()))
F32 = jnp.float32
BF16 = jnp.bfloat16
SCORE = HEAD**-0.5 * 1.4426950408889634


def dot(a, b, numbers=NN):
    return lax.dot_general(a, b, numbers, preferred_element_type=F32)


def rms_scale(v):
    return lax.rsqrt(jnp.mean(v * v, axis=-1, keepdims=True) + EPS)


def rms_back(grad, v, scale):
    inner = jnp.mean(grad * v, axis=-1, keepdims=True)
    return scale * (grad - v * scale * scale * inner)


def shift_x(v, distance):
    return lax.ppermute(v, "x", [((i + distance) % 4, i) for i in range(4)])


def swap(v, axis):
    return lax.ppermute(v, axis, [(0, 1), (1, 0)])


def shift_super(v, distance):
    pairs = [(i, i + distance) for i in range(8) if 0 <= i + distance < 8]
    return lax.ppermute(v, ("ylo", "z"), pairs)


def exchange(v, axes):
    return lax.all_to_all(v, axes, split_axis=0, concat_axis=0, tiled=True)


def near_gather(v):
    blocks = [v] + [shift_x(v, d) for d in (1, 2, 3)]
    return [[b, swap(b, "core")] for b in blocks]


def near_keep(parts):
    return [
        (own.astype(F32) + swap(other, "core").astype(F32)).astype(BF16) for own, other in parts
    ]


def near_sum(kept):
    total = kept[0].astype(F32)
    for d in (1, 2, 3):
        total = total + shift_x(kept[d], -d).astype(F32)
    return total


def rel_to_abs(v, x, core):
    v = jnp.where(core == 0, v, v[:, ::-1])
    return lax.dynamic_slice_in_dim(jnp.concatenate([v, v], axis=0), (4 - x) % 4, 4, 0)


def abs_to_rel(v, x, core):
    v = jnp.where(core == 0, v, v[:, ::-1])
    return lax.dynamic_slice_in_dim(jnp.concatenate([v, v], axis=0), x, 4, 0)


def params(steps, mib):
    return pltpu.CompilerParams(
        dimension_semantics=("arbitrary",) * steps, vmem_limit_bytes=mib * 2**20
    )


def cost(flops, moved, exps=0):
    return pl.CostEstimate(flops=int(flops), bytes_accessed=int(moved), transcendentals=int(exps))


def stacked(a_ref, b_ref):
    return jnp.concatenate([a_ref[...], b_ref[...]], axis=0)


def head_sums(v):
    lane = lax.shift_right_logical(lax.broadcasted_iota(jnp.int32, (4 * HEAD, 4 * HEAD), 1), 6)
    row = lax.shift_right_logical(lax.broadcasted_iota(jnp.int32, (4 * HEAD, 4 * HEAD), 0), 6)
    ones = jnp.where(lane == row, 1.0, 0.0).astype(BF16)
    high = v.astype(BF16)
    low = (v - high.astype(F32)).astype(BF16)
    return dot(high, ones) + dot(low, ones)


def half_turn(v):
    lane = lax.broadcasted_iota(jnp.int32, v.shape, 1)
    return jnp.where(
        (lane & (HEAD - 1)) < HEAD // 2,
        pltpu.roll(v, v.shape[1] - HEAD // 2, 1),
        pltpu.roll(v, HEAD // 2, 1),
    )


def twice(v):
    return jnp.concatenate([v, v], axis=1)


def project_kernel(*refs):
    xs, (w_ref, gain_ref, cos_ref, sin_ref, head_gain_ref) = refs[:8], refs[8:13]
    normed_ref, q_ref, kv_ref, raw_ref = refs[13:]
    lane = lax.broadcasted_iota(jnp.int32, (PAIR, 2 * HEAD), 1)
    for d in range(4):
        rows = slice(d * PAIR, (d + 1) * PAIR)
        tiles = slice(2 * d, 2 * d + 2)
        x = stacked(*xs[tiles]).astype(F32)
        normed = (x * rms_scale(x) * gain_ref[...]).astype(BF16)
        normed_ref[rows, :] = normed
        raw = dot(normed, w_ref[...])
        heads = raw[:, : 4 * HEAD]
        raw_ref[d] = heads
        scale = lax.rsqrt(head_sums(heads * heads) * (1.0 / HEAD) + EPS)
        v = heads * scale * head_gain_ref[...]
        turned = v * twice(cos_ref[d]) + half_turn(v) * twice(sin_ref[d])
        q_ref[tiles] = turned[:, :QUERY].astype(BF16).reshape(2, ROWS, QUERY)
        kv = jnp.where(lane < HEAD, raw[:, 4 * HEAD :], turned[:, 2 * HEAD :])
        kv_ref[tiles] = kv.astype(BF16).reshape(2, ROWS, 2 * HEAD)


def project(xs, w, gain, cos, sin, head_gain):
    return pl.pallas_call(
        project_kernel,
        out_shape=(
            jax.ShapeDtypeStruct((4 * PAIR, WIDTH), BF16),
            jax.ShapeDtypeStruct((8, ROWS, QUERY), BF16),
            jax.ShapeDtypeStruct((8, ROWS, 2 * HEAD), BF16),
            jax.ShapeDtypeStruct((4, PAIR, 4 * HEAD), F32),
        ),
        compiler_params=params(0, 32),
        cost_estimate=cost(8 * PAIR * WIDTH * 384, 1e7),
    )(*xs, w, gain, cos, sin, head_gain)


def unproject_kernel(
    gq_ref, g0_ref, g1_ref, g2_ref, g3_ref, raw_ref, x0_ref, x1_ref, w_ref, cos_ref, sin_ref,
    head_gain_ref, part0_ref, part1_ref, graw_ref, attn_ref, heads_ref,
):
    gq = gq_ref[...].reshape(PAIR, 4 * HEAD).astype(F32)
    gkv = g0_ref[...] + g1_ref[...].astype(F32) + g2_ref[...].astype(F32) + g3_ref[...].astype(F32)
    gkv = gkv.reshape(PAIR, 2 * HEAD)
    lane = lax.broadcasted_iota(jnp.int32, (PAIR, 2 * HEAD), 1)
    gk = (gkv * HEAD**-0.5).astype(BF16).astype(F32)
    g = jnp.concatenate([gq[:, : 2 * HEAD], jnp.where(lane < HEAD, gq[:, 2 * HEAD :], gk)], axis=1)
    g = g * twice(cos_ref[0]) - half_turn(g) * twice(sin_ref[0])
    raw = raw_ref[0]
    scale = lax.rsqrt(head_sums(raw * raw) * (1.0 / HEAD) + EPS)
    heads_ref[...] = jnp.sum(g * raw * scale, axis=0, keepdims=True)
    e = g * head_gain_ref[...]
    inner = head_sums(e * raw) * (1.0 / HEAD)
    graw = scale * (e - raw * scale * scale * inner)
    graw = jnp.concatenate([graw, jnp.where(lane < HEAD, gkv, 0.0)], axis=1).astype(BF16)
    graw_ref[...] = graw
    grad = dot(graw, w_ref[...], NT)
    x = stacked(x0_ref, x1_ref).astype(F32)
    attn_ref[...] = jnp.sum(grad * x * rms_scale(x), axis=0, keepdims=True)
    grad = grad.astype(BF16)
    part0_ref[...] = grad[:ROWS]
    part1_ref[...] = grad[ROWS:]


def unproject(d, gq, gkvs, raw, x0, x1, w, cos, sin, head_gain):
    def whole_of(*shape):
        return pl.BlockSpec(shape, lambda i: (0,) * len(shape))

    def at_d(*shape):
        return pl.BlockSpec(shape, lambda i: (d,) + (0,) * (len(shape) - 1))

    rows = whole_of(ROWS, WIDTH)
    kv = at_d(2, ROWS, 2 * HEAD)
    table = at_d(1, PAIR, 2 * HEAD)
    outs = (
        jax.ShapeDtypeStruct((ROWS, WIDTH), BF16),
        jax.ShapeDtypeStruct((ROWS, WIDTH), BF16),
        jax.ShapeDtypeStruct((PAIR, 6 * HEAD), BF16),
        jax.ShapeDtypeStruct((1, WIDTH), F32),
        jax.ShapeDtypeStruct((1, 4 * HEAD), F32),
    )
    return pl.pallas_call(
        unproject_kernel,
        out_shape=outs,
        grid=(1,),
        in_specs=[at_d(2, ROWS, 4 * HEAD), kv, kv, kv, kv, at_d(1, PAIR, 4 * HEAD), rows, rows]
        + [whole_of(WIDTH, 6 * HEAD), table, table, whole_of(1, 4 * HEAD)],
        out_specs=tuple(whole_of(*o.shape) for o in outs),
        compiler_params=params(1, 24),
        cost_estimate=cost(2 * PAIR * WIDTH * 384, 4e6),
    )(gq, *gkvs, raw, x0, x1, w, cos, sin, head_gain)


def ffn_kernel(x0_ref, x1_ref, c0_ref, c1_ref, w_ref, part0_ref, part1_ref, act_ref, gu_ref, total):
    y = pl.program_id(0)
    x = stacked(x0_ref, x1_ref)
    gate_up = dot(x, w_ref[0, :, : 2 * PADDED])
    gate, up = gate_up[:, :PADDED], gate_up[:, PADDED:]
    grad_act = dot(stacked(c0_ref, c1_ref), w_ref[0, :, 2 * PADDED :])
    sig = 1.0 / (1.0 + jnp.exp(-gate))
    silu = gate * sig
    act_ref[0] = (silu * up).astype(BF16)
    grad_gate = grad_act * up * sig * (1.0 + gate * (1.0 - sig))
    grads = jnp.concatenate([grad_gate, grad_act * silu], axis=1).astype(BF16)
    gu_ref[0] = grads
    part = dot(grads, w_ref[0, :, : 2 * PADDED], NT)

    @pl.when(y == 0)
    def _():
        total[...] = part

    @pl.when(y == 1)
    def _():
        whole_part = (total[...] + part).astype(BF16)
        part0_ref[...] = whole_part[:ROWS]
        part1_ref[...] = whole_part[ROWS:]


def ffn(x0, x1, c0, c1, w):
    rows = pl.BlockSpec((ROWS, WIDTH), lambda y: (0, 0))
    return pl.pallas_call(
        ffn_kernel,
        out_shape=(
            jax.ShapeDtypeStruct((ROWS, WIDTH), BF16),
            jax.ShapeDtypeStruct((ROWS, WIDTH), BF16),
            jax.ShapeDtypeStruct((2, PAIR, PADDED), BF16),
            jax.ShapeDtypeStruct((2, PAIR, 2 * PADDED), BF16),
        ),
        grid=(2,),
        in_specs=[rows] * 4 + [pl.BlockSpec((1, WIDTH, 3 * PADDED), lambda y: (y, 0, 0))],
        out_specs=(
            rows,
            rows,
            pl.BlockSpec((1, PAIR, PADDED), lambda y: (y, 0, 0)),
            pl.BlockSpec((1, PAIR, 2 * PADDED), lambda y: (y, 0, 0)),
        ),
        scratch_shapes=[pltpu.VMEM((PAIR, WIDTH), F32)],
        compiler_params=params(1, 40),
        cost_estimate=cost(2 * 2 * PAIR * WIDTH * 5 * PADDED, 14e6),
    )(x0, x1, c0, c1, w)


def down_kernel(act_ref, w_ref, part0_ref, part1_ref, total):
    y = pl.program_id(0)
    part = dot(act_ref[0], w_ref[0], NT)

    @pl.when(y == 0)
    def _():
        total[...] = part

    @pl.when(y == 1)
    def _():
        whole_part = (total[...] + part).astype(BF16)
        part0_ref[...] = whole_part[:ROWS]
        part1_ref[...] = whole_part[ROWS:]


def down(act, w):
    rows = pl.BlockSpec((ROWS, WIDTH), lambda y: (0, 0))
    return pl.pallas_call(
        down_kernel,
        out_shape=(jax.ShapeDtypeStruct((ROWS, WIDTH), BF16),) * 2,
        grid=(2,),
        in_specs=[
            pl.BlockSpec((1, PAIR, PADDED), lambda y: (y, 0, 0)),
            pl.BlockSpec((1, WIDTH, PADDED), lambda y: (y, 0, 2)),
        ],
        out_specs=(rows, rows),
        scratch_shapes=[pltpu.VMEM((PAIR, WIDTH), F32)],
        compiler_params=params(1, 24),
        cost_estimate=cost(2 * 2 * PAIR * WIDTH * PADDED, 5e6),
    )(act, w)


def ffn_weights_kernel(*refs):
    xs, cs, gus, acts, out_ref = refs[:8], refs[8:16], refs[16:20], refs[20:24], refs[24]
    grad_gu, grad_d = 0.0, 0.0
    for d in range(4):
        grad_gu = grad_gu + dot(stacked(*xs[2 * d : 2 * d + 2]), gus[d][0], TN)
        grad_d = grad_d + dot(stacked(*cs[2 * d : 2 * d + 2]), acts[d][0], TN)
    out_ref[0, :, : 2 * PADDED] = grad_gu.astype(BF16)
    out_ref[0, :, 2 * PADDED :] = grad_d.astype(BF16)


def ffn_weights(xs, cs, gus, acts):
    tall = 256
    rows = pl.BlockSpec((ROWS, tall), lambda y, m: (0, m))
    return pl.pallas_call(
        ffn_weights_kernel,
        out_shape=jax.ShapeDtypeStruct((2, WIDTH, 3 * PADDED), BF16),
        grid=(2, WIDTH // tall),
        in_specs=[rows] * 16
        + [pl.BlockSpec((1, PAIR, 2 * PADDED), lambda y, m: (y, 0, 0))] * 4
        + [pl.BlockSpec((1, PAIR, PADDED), lambda y, m: (y, 0, 0))] * 4,
        out_specs=pl.BlockSpec((1, tall, 3 * PADDED), lambda y, m: (y, m, 0)),
        compiler_params=params(2, 40),
        cost_estimate=cost(2 * 2 * 1024 * WIDTH * 3 * PADDED, 24e6),
    )(*xs, *cs, *gus, *acts)


def side_by_side(t):
    return jnp.concatenate([t[g * HEAD : (g + 1) * HEAD] for g in range(GROUP)], axis=1)


def on_top(t):
    return jnp.concatenate([t[:, g * ROWS : (g + 1) * ROWS] for g in range(GROUP)], axis=0)


def key_loops(plan, at, base, start, visit, state):
    f = pl.program_id(0)
    lo, m1, m2, hi = (plan[f, at + i] for i in range(4))
    place = lax.rem(lax.broadcasted_iota(jnp.int32, (1, LANES), 1), ROWS) + plan[f, 0]

    def masked(j, state):
        key = lax.broadcasted_iota(jnp.int32, (KEY_TILE, LANES), 0) + (j * KEY_TILE + base)
        return visit(j, state, (key >= start) & (key <= place))

    state = lax.fori_loop(lo, m1, masked, state)
    state = lax.fori_loop(m1, m2, lambda j, s: visit(j, s, None), state)
    return lax.fori_loop(m2, hi, masked, state)


def rows_of(j):
    return pl.ds(pl.multiple_of(j * KEY_TILE, KEY_TILE), KEY_TILE)


def chunks(plan, supers):
    for b in range(supers):
        for half in (0, 1):
            for f in range(8):
                side = plan[0, 10] if half == 0 else 1 - plan[0, 10]
                yield b, half, pl.multiple_of(b * SUPER + f * PAIR + side * ROWS, ROWS), plan[f, 1]


def line_up(plan, kv_refs, kv, kvt):
    @pl.when(pl.program_id(0) == 0)
    def _():
        for b, half, place, sent in chunks(plan, len(kv_refs) // 2):
            block = kv_refs[2 * b + half][sent]
            kv[pl.ds(place, ROWS), :] = block
            kvt[:, pl.ds(place, ROWS)] = block.astype(F32).T.astype(BF16)


def attend_body(at, base, plan, q_ref, start_ref, kv, kvt, state):
    qt = side_by_side(q_ref[0].astype(F32).T)
    qt = jnp.concatenate([jnp.zeros_like(qt), qt], axis=0).astype(BF16)

    def visit(j, state, mask):
        total, accum = state
        weights = jnp.exp2(dot(kv[rows_of(j), :], qt) * SCORE)
        if mask is not None:
            weights = jnp.where(mask, weights, 0.0)
        total = total + jnp.sum(weights, axis=0, keepdims=True)
        return total, accum + dot(kvt[:HEAD, rows_of(j)], weights.astype(BF16))

    return key_loops(plan, at, base, start_ref[0], visit, state)


def attend_own_kernel(plan, q_ref, start_ref, *refs):
    kv_refs, (accum_ref, total_ref, kv, kvt) = refs[:2], refs[2:]
    line_up(plan, kv_refs, kv, kvt)
    state = (jnp.zeros((1, LANES), F32), jnp.zeros((HEAD, LANES), F32))
    total, accum = attend_body(6, EARLIER, plan, q_ref, start_ref, kv, kvt, state)
    accum_ref[0] = accum
    total_ref[0] = total


def attend_earlier_kernel(plan, q_ref, start_ref, *refs):
    kv_refs, (accum_ref, total_ref, mix_ref, out_ref, lse_ref, kv, kvt) = refs[:4], refs[4:]
    line_up(plan, kv_refs, kv, kvt)
    state = (total_ref[0], accum_ref[0])
    total, accum = attend_body(2, 0, plan, q_ref, start_ref, kv, kvt, state)
    out = accum / total
    out_ref[0] = out
    mix_ref[0] = on_top(out).astype(BF16)
    lse_ref[0] = jnp.log2(total)


def back_body(at, base, plan, q_ref, start_ref, g_ref, out_ref, lse_ref, kv, kvt, dkv, dqt):
    @pl.when(pl.program_id(0) == 0)
    def _():
        dkv[...] = jnp.zeros_like(dkv)

    qt = side_by_side(q_ref[0].astype(F32).T)
    gt = side_by_side(g_ref[0].astype(F32))
    delta = jnp.sum(gt * out_ref[0], axis=0, keepdims=True)
    zero = jnp.zeros_like(qt)
    gt = jnp.concatenate([gt, zero], axis=0)
    qt = jnp.concatenate([zero, qt], axis=0)
    both_t = jnp.concatenate([gt, qt], axis=1).astype(BF16)
    both = jnp.concatenate([gt.T, qt.T], axis=0).astype(BF16)
    lse = lse_ref[0]

    def visit(j, dqt, mask):
        pair = dot(kv[rows_of(j), :], both_t)
        weights = jnp.exp2(pair[:, LANES:] * SCORE - lse)
        if mask is not None:
            weights = jnp.where(mask, weights, 0.0)
        grads = (weights * (pair[:, :LANES] - delta)).astype(BF16)
        sides = jnp.concatenate([weights.astype(BF16), grads], axis=1)
        dkv[rows_of(j), :] += dot(sides, both)
        return dqt + dot(kvt[HEAD:, rows_of(j)], grads)

    return key_loops(plan, at, base, start_ref[0], visit, dqt)


def hand_out(plan, supers, dkv, mine_ref, theirs_ref):
    @pl.when(pl.program_id(0) == 7)
    def _():
        for b, half, place, sent in chunks(plan, supers):
            ref = (mine_ref, theirs_ref)[half]
            ref[b, sent] = dkv[pl.ds(place, ROWS), :].astype(ref.dtype)


def back_earlier_kernel(plan, q_ref, start_ref, *refs):
    kv_refs, (g_ref, out_ref, lse_ref, dqt_ref, mine_ref, theirs_ref, kv, kvt, dkv) = refs[:4], refs[4:]
    line_up(plan, kv_refs, kv, kvt)
    dqt = jnp.zeros((HEAD, LANES), F32)
    dqt_ref[0] = back_body(
        2, 0, plan, q_ref, start_ref, g_ref, out_ref, lse_ref, kv, kvt, dkv, dqt
    )
    hand_out(plan, 2, dkv, mine_ref, theirs_ref)


def back_own_kernel(plan, q_ref, start_ref, *refs):
    kv_refs, (g_ref, out_ref, lse_ref, dqt_ref) = refs[:2], refs[2:6]
    dq_ref, mine_ref, theirs_ref, kv, kvt, dkv = refs[6:]
    line_up(plan, kv_refs, kv, kvt)
    dqt = back_body(
        6, EARLIER, plan, q_ref, start_ref, g_ref, out_ref, lse_ref, kv, kvt, dkv, dqt_ref[0]
    )
    dq = on_top(dqt * HEAD**-0.5).T
    dq_ref[0] = jnp.concatenate([dq, jnp.zeros((ROWS, HEAD), F32)], axis=1).astype(BF16)
    hand_out(plan, 1, dkv, mine_ref, theirs_ref)


def whole(*shape):
    return pl.BlockSpec(shape, lambda f, plan: (0,) * len(shape))


def tile(*shape):
    return pl.BlockSpec((1,) + shape, lambda f, plan: (f,) + (0,) * len(shape))


def placed(*shape):
    return pl.BlockSpec((1,) + shape, lambda f, plan: (plan[f, 1],) + (0,) * len(shape))


def tiles_call(kernel, supers, outs, more_ins, out_specs, flops, back):
    keys = supers * SUPER
    scratch = [pltpu.VMEM((keys, 2 * HEAD), BF16), pltpu.VMEM((2 * HEAD, keys), BF16)]
    if back:
        scratch.append(pltpu.VMEM((keys, 2 * HEAD), F32))
    ins = [placed(ROWS, QUERY), tile(1, LANES)] + [whole(8, ROWS, 2 * HEAD)] * (2 * supers)
    return pl.pallas_call(
        kernel,
        out_shape=outs,
        grid_spec=pltpu.PrefetchScalarGridSpec(
            num_scalar_prefetch=1,
            grid=(8,),
            in_specs=ins + more_ins,
            out_specs=out_specs,
            scratch_shapes=scratch,
        ),
        compiler_params=params(1, 32),
        cost_estimate=cost(flops, 8e6, 1e7),
    )


TILE_T = jax.ShapeDtypeStruct((8, HEAD, LANES), F32)
TILE_ROW = jax.ShapeDtypeStruct((8, 1, LANES), F32)
STATE = [tile(HEAD, LANES), tile(1, LANES)]


def attend_own(plan, q, start, kvs):
    call = tiles_call(attend_own_kernel, 1, (TILE_T, TILE_ROW), [], tuple(STATE), 4e9, False)
    return call(plan, q, start, *kvs)


def attend_earlier(plan, q, start, kvs, state):
    outs = (jax.ShapeDtypeStruct((8, QUERY, ROWS), BF16), TILE_T, TILE_ROW)
    specs = (tile(QUERY, ROWS),) + tuple(STATE)
    call = tiles_call(attend_earlier_kernel, 2, outs, STATE, specs, 8e9, False)
    return call(plan, q, start, *kvs, *state)


def sent_back(supers):
    shape = (supers, 8, ROWS, 2 * HEAD)
    return [jax.ShapeDtypeStruct(shape, F32), jax.ShapeDtypeStruct(shape, BF16)], [whole(*shape)] * 2


def back_earlier(plan, q, start, kvs, grad, out, lse):
    shapes, specs = sent_back(2)
    call = tiles_call(
        back_earlier_kernel, 2, [TILE_T] + shapes, [tile(QUERY, ROWS)] + STATE,
        [tile(HEAD, LANES)] + specs, 20e9, True,
    )
    return call(plan, q, start, *kvs, grad, out, lse)


def back_own(plan, q, start, kvs, grad, out, lse, dqt):
    shapes, specs = sent_back(1)
    dq = jax.ShapeDtypeStruct((8, ROWS, 4 * HEAD), BF16)
    call = tiles_call(
        back_own_kernel, 1, [dq] + shapes, [tile(QUERY, ROWS)] + STATE + [tile(HEAD, LANES)],
        [placed(ROWS, 4 * HEAD)] + specs, 10e9, True,
    )
    return call(plan, q, start, *kvs, grad, out, lse, dqt)


def out_weights_kernel(plan, mix_ref, *refs):
    branches, (out_ref, total) = refs[:8], refs[8:]
    grad = 0.0
    for t in range(8):
        grad = grad + dot(mix_ref[plan[t, 11]], branches[t][...])
    total[...] = grad
    for half in (0, 1):
        for s in range(8):
            out_ref[half * 8 + s] = total[half * 96 : half * 96 + 96, s * 192 : s * 192 + 192].astype(BF16)


def out_weights(plan, mix, branches):
    return pl.pallas_call(
        out_weights_kernel,
        out_shape=jax.ShapeDtypeStruct((16, 96, 192), BF16),
        grid_spec=pltpu.PrefetchScalarGridSpec(
            num_scalar_prefetch=1,
            grid=(1,),
            in_specs=[whole(8, QUERY, ROWS)] + [whole(ROWS, WIDTH)] * 8,
            out_specs=whole(16, 96, 192),
            scratch_shapes=[pltpu.VMEM((QUERY, WIDTH), F32)],
        ),
        compiler_params=params(1, 24),
        cost_estimate=cost(2 * 1024 * WIDTH * QUERY, 4e6),
    )(plan, mix, *branches)


def after(v, *others):
    return lax.optimization_barrier((v,) + others)[0]


def per_device(
    tokens,
    segments,
    attn_gain,
    w_query,
    w_key,
    w_value,
    q_gain,
    k_gain,
    w_out,
    ffn_gain,
    w_gate,
    w_up,
    w_down,
    cotangent,
):
    ylo, z, x, core, yhi = (lax.axis_index(a) for a in ALL)
    sup = ylo * 4 + z

    qkv_own = jnp.concatenate(
        [
            w_query.reshape(12, 8, QUERY),
            w_key.reshape(12, 8, HEAD),
            w_value.reshape(12, 8, HEAD),
            jnp.broadcast_to(attn_gain[:, None, None], (12, 8, 1)),
            jnp.broadcast_to(ffn_gain[:, None, None], (12, 8, 1)),
            jnp.zeros((12, 8, HEAD - 2), BF16),
        ],
        axis=-1,
    )
    qkv_own = jnp.transpose(qkv_own, (1, 0, 2))
    qkv_sent = jnp.broadcast_to(qkv_own[None, :, None], (8, 8, 2, 12, 6 * HEAD))
    qkv = exchange(qkv_sent.reshape(128, 12, 6 * HEAD), ALL).reshape(WIDTH, 6 * HEAD)
    gain_attn = qkv[:, 5 * HEAD].astype(F32)
    gain_ffn = qkv[:, 5 * HEAD + 1].astype(F32)
    token_blocks = near_gather(tokens)

    out_own = near_gather(w_out.T)
    out_own = rel_to_abs(jnp.stack([jnp.stack(p) for p in out_own]), x, core).reshape(192, 768)
    out_full = lax.all_gather(out_own, WIDE, axis=0, tiled=True).reshape(2, WIDTH, 768)

    token_index = jnp.arange(segments.shape[0], dtype=jnp.int32)
    begins = jnp.concatenate([jnp.ones((1,), jnp.bool_), segments[1:] != segments[:-1]])
    starts = lax.cummax(jnp.where(begins, token_index, 0), axis=0)
    own_starts = lax.dynamic_slice(
        starts.reshape(8, 8, 2, ROWS), (sup, 0, yhi, 0), (1, 8, 1, ROWS)
    ).reshape(8, ROWS)
    first = sup * SUPER + jnp.arange(8, dtype=jnp.int32) * PAIR + yhi * ROWS
    own_places = first[:, None] + jnp.arange(ROWS, dtype=jnp.int32)[None]
    positions = abs_to_rel((own_places - own_starts).reshape(4, 2, ROWS), x, core)
    frequency = THETA ** (-jnp.arange(HEAD // 2, dtype=F32) * 2.0 / HEAD)
    angles = positions.reshape(4, PAIR, 1).astype(F32) * frequency
    cosine, sine = jnp.cos(angles), jnp.sin(angles)
    cos = jnp.concatenate([cosine] * 4, axis=-1)
    sin = jnp.concatenate([-sine, sine] * 2, axis=-1)
    head_gain = jnp.concatenate([q_gain, q_gain, q_gain, k_gain]).astype(F32)[None]

    window = (sup - 2) * SUPER
    lo = (own_starts[:, 0] - window) // KEY_TILE
    hi = (first + ROWS - 1 - window) // KEY_TILE + 1
    m1 = jnp.clip((own_starts[:, -1] - window + KEY_TILE - 1) // KEY_TILE, lo, hi)
    m2 = jnp.clip((first + 1 - window) // KEY_TILE, m1, hi)
    order = jnp.arange(8, dtype=jnp.int32)
    relative = ((order // 2 - x) % 4) * 2 + (order % 2 + core) % 2
    edge = EARLIER // KEY_TILE
    plan = jnp.stack(
        [first - window, relative]
        + [jnp.minimum(v, edge) for v in (lo, m1, m2, hi)]
        + [jnp.maximum(v - edge, 0) for v in (lo, m1, m2, hi)]
        + [jnp.broadcast_to(yhi, (8,)), ((order // 2 + x) % 4) * 2 + (order % 2 + core) % 2],
        axis=1,
    ).astype(jnp.int32)
    start_lanes = jnp.tile(own_starts - window, (1, GROUP)).reshape(8, 1, LANES)

    normed, rot_q, kv, raw = project(
        [b for p in token_blocks for b in p], qkv, gain_attn[None], cos, sin, head_gain
    )

    ffn_own = jnp.concatenate(
        [
            jnp.pad(w.reshape(24, 8, PART), ((0, 0), (0, 0), (0, PADDED - PART)))
            for w in after((w_gate, w_up, w_down.T), qkv)
        ],
        axis=-1,
    )
    ffn_rows = exchange(jnp.transpose(ffn_own, (1, 0, 2)), NEAR).reshape(192, 3 * PADDED)
    ffn_full = lax.all_gather(ffn_rows, WIDE, axis=0, tiled=True).reshape(2, WIDTH, 3 * PADDED)

    kv_one, kv_two = shift_super(kv, 1), shift_super(kv, 2)
    kv_own = [kv, swap(kv, "yhi")]
    kv_earlier = [kv_two, swap(kv_two, "yhi"), kv_one, swap(kv_one, "yhi")]
    state = attend_own(plan, rot_q, start_lanes, kv_own)
    cot_blocks = near_gather(after(cotangent, kv))
    state, cot_blocks = lax.optimization_barrier((state, cot_blocks))
    mix_tiles, out_tiles, lse = attend_earlier(plan, rot_q, start_lanes, kv_earlier, state)

    mixture_t = exchange(mix_tiles, NEAR).reshape(2, 768, ROWS)
    inputs = tokens.astype(F32)
    hidden = inputs
    for y in range(2):
        hidden = hidden + lax.dot_general(
            mixture_t[y], out_full[y], (((0,), (1,)), ((), ())), preferred_element_type=F32
        )
    scale_ffn = rms_scale(hidden)
    scaled_ffn = hidden * scale_ffn
    normed_ffn = (scaled_ffn * gain_ffn).astype(BF16)

    ffn_blocks = near_gather(normed_ffn)
    ffn_outs = [None] * 4
    for d in (0, 1, 3, 2):
        ffn_outs[d] = ffn(*ffn_blocks[d], *cot_blocks[d], ffn_full)
    acts, gus = [o[2] for o in ffn_outs], [o[3] for o in ffn_outs]
    kept, gus = lax.optimization_barrier((near_keep([o[:2] for o in ffn_outs]), gus))
    pair_total = near_sum(kept)
    weight_grads = ffn_weights(
        [b for p in ffn_blocks for b in p], [b for p in cot_blocks for b in p], gus, acts
    )
    pair_total, weight_grads = lax.optimization_barrier((pair_total, weight_grads))
    ffn_got = exchange(weight_grads.reshape(16, 192, 3 * PADDED), WIDE)

    ffn_gain_part = jnp.sum(pair_total * scaled_ffn, axis=0)
    grad_hidden = cotangent.astype(F32) + rms_back(pair_total * gain_ffn, hidden, scale_ffn)
    grad_branch = grad_hidden.astype(BF16)
    grad_mixture = jnp.concatenate(
        [
            lax.dot_general(
                out_full[y], grad_branch, (((0,), (1,)), ((), ())), preferred_element_type=F32
            )
            for y in range(2)
        ],
        axis=0,
    ).astype(BF16)
    grad_tiles = exchange(grad_mixture.reshape(8, QUERY, ROWS), NEAR)

    dqt, mine, theirs = back_earlier(
        plan, rot_q, start_lanes, kv_earlier, grad_tiles, out_tiles, lse
    )
    earlier = (mine + swap(theirs, "yhi").astype(F32)).astype(BF16)
    back_one, back_two = shift_super(earlier[1], -1), shift_super(earlier[0], -2)
    grad_q, mine, theirs = back_own(
        plan, rot_q, start_lanes, kv_own, grad_tiles, out_tiles, lse, dqt
    )
    grad_kvs = (mine[0], swap(theirs[0], "yhi"), back_one, back_two)

    acts, grad_tiles = lax.optimization_barrier((acts, grad_tiles))
    output = (hidden + near_sum(near_keep([down(a, ffn_full) for a in acts]))).astype(BF16)
    branches = near_gather(after(grad_branch, grad_tiles))
    grad_out = exchange(out_weights(plan, mix_tiles, [b for p in branches for b in p]), WIDE)
    grad_out = jnp.sum(grad_out.astype(F32), axis=0).astype(BF16)
    grad_out = jnp.transpose(grad_out.reshape(96, 8, 24), (1, 2, 0))
    grad_out = exchange(grad_out, NEAR).reshape(2, 4, 24, 96)
    kept = jnp.where(yhi == 0, grad_out[0], grad_out[1])
    got = swap(jnp.where(yhi == 0, grad_out[1], grad_out[0]), "yhi")
    w_out_grad = jnp.stack(
        [jnp.where(yhi == 0, kept, got), jnp.where(yhi == 0, got, kept)], axis=1
    )
    w_out_grad = jnp.transpose(w_out_grad, (0, 1, 3, 2)).reshape(768, 24).astype(F32)

    unprojected = [None] * 4
    for d in (2, 1, 3, 0):
        unprojected[d] = unproject(
            d, grad_q, grad_kvs, raw, *token_blocks[d], qkv, cos, sin, head_gain
        )
    grad_normed = near_sum(near_keep([u[:2] for u in unprojected]))
    qkv_grad = dot(normed, jnp.concatenate([u[2] for u in unprojected], axis=0), TN)

    attn_gain_part = sum(u[3] for u in unprojected).reshape(128, 12, 1)
    head_part = sum(u[4] for u in unprojected)[0]
    q_gain_part = head_part[:HEAD] + head_part[HEAD : 2 * HEAD] + head_part[2 * HEAD : QUERY]
    head_part = jnp.concatenate([q_gain_part, head_part[QUERY:], jnp.zeros((4,), F32)])
    gain_parts = jnp.concatenate(
        [
            attn_gain_part,
            ffn_gain_part.reshape(128, 12, 1),
            jnp.broadcast_to(head_part.reshape(1, 12, 11), (128, 12, 11)),
        ],
        axis=2,
    )
    gain_high = gain_parts.astype(BF16)
    gain_low = (gain_parts - gain_high.astype(F32)).astype(BF16)
    qkv_grad = jnp.concatenate(
        [
            qkv_grad[:, : 5 * HEAD].astype(BF16).reshape(128, 12, 5 * HEAD),
            gain_high,
            gain_low,
            jnp.zeros((128, 12, HEAD - 26), BF16),
        ],
        axis=2,
    )
    qkv_grad = exchange(qkv_grad, ALL).reshape(8, 8, 2, 12, 6 * HEAD).astype(F32)
    qkv_grad = jnp.sum(qkv_grad, axis=(0, 2))
    gains = jnp.sum(qkv_grad[:, :, 5 * HEAD :], axis=0)
    gains = gains[:, :13] + gains[:, 13:26]
    head_gains = gains[:, 2:].reshape(-1)
    qkv_grad = jnp.transpose(qkv_grad, (1, 0, 2))
    w_query_grad = qkv_grad[:, :, :QUERY].reshape(12, -1)
    w_key_grad = qkv_grad[:, :, QUERY : QUERY + HEAD].reshape(12, -1)
    w_value_grad = qkv_grad[:, :, QUERY + HEAD : QUERY + 2 * HEAD].reshape(12, -1)

    scale_attn = rms_scale(inputs)
    input_grad = (grad_hidden + rms_back(grad_normed * gain_attn, inputs, scale_attn)).astype(BF16)

    ffn_sum = jnp.sum(ffn_got.astype(F32), axis=0).astype(BF16)
    ffn_grad = exchange(ffn_sum.reshape(8, 24, 3 * PADDED), NEAR)
    ffn_grad = jnp.transpose(ffn_grad, (1, 0, 2)).astype(F32)
    w_gate_grad, w_up_grad, w_down_grad = (
        ffn_grad[:, :, i * PADDED : i * PADDED + PART].reshape(24, -1) for i in range(3)
    )
    return (
        output,
        input_grad,
        gains[:, 0],
        w_query_grad,
        w_key_grad,
        w_value_grad,
        head_gains[:HEAD],
        head_gains[HEAD : 2 * HEAD],
        w_out_grad,
        gains[:, 1],
        w_gate_grad,
        w_up_grad,
        w_down_grad.T,
    )


def solution(mesh):
    mesh = Mesh(np.asarray(mesh.devices).reshape(2, 4, 4, 2, 2), ALL)
    rows = P(ALL, None)
    weights = (P("yhi", BLK), P(ALL), P(BLK, "yhi"), P(BLK, "yhi"), P("yhi", BLK))
    placed_in = (rows, P(), P(ALL), rows, rows, rows, P(), P()) + weights + (rows,)
    placed_out = (rows, rows, P(ALL), rows, rows, rows, P(), P()) + weights
    return jax.shard_map(
        per_device, mesh=mesh, in_specs=placed_in, out_specs=placed_out, check_vma=False
    )
```

time: 4120 us -> 683 us (0.17)
  waiting for transfers between devices: 2200 us -> 219 us
  starting transfers between devices: 683 us -> 90 us
  blocking collectives: 642 us -> 92.2 us
  local copies, waits for them, and re-layouts: 246 us -> 66.9 us
  matrix products: 174 us -> 13.6 us
  Pallas kernels: 0 us -> 144 us
  other arithmetic: 86.5 us -> 29.7 us
  loops' own time: 46 us -> 0 us
    all_gather x7 -> x2, waiting for transfers between devices: 1150 us -> 0.01 us  [the longest x1 0.01 us: per_device(): lax.all_gather(out_own, WIDE, axis=0, tiled=True).reshape(2, WIDTH, 768)]
    unnamed x115 -> x2, waiting for transfers between devices: 910 us -> 0.03 us
    unnamed x3 -> x0, blocking collectives: 602 us -> none
    ppermute x64 -> x66, starting transfers between devices: 433 us -> 59 us  [the longest x24 29.4 us: shift_x(): return lax.ppermute(v, 'x', [((i + distance) % 4, i) for i in range(4)])]
    unnamed x100 -> x0, starting transfers between devices: 231 us -> none
    dot_general x84 -> x5, matrix products: 174 us -> 13.6 us  [the longest x2 5.37 us: per_device(): lax.dot_general(mixture_t[y], out_full[y], (((0,), (1,)), ((), ())), pref...]
    pallas_call x0 -> x19, Pallas kernels: none -> 144 us  [the longest x4 27.3 us: ffn(): pl.pallas_call(ffn_kernel, out_shape=(jax.ShapeDtypeStruct((ROWS, WIDTH),...]
    ppermute x64 -> x66, waiting for transfers between devices: 80.2 us -> 201 us  [the longest x38 139 us: swap(): return lax.ppermute(v, axis, [(0, 1), (1, 0)])]
  transfers between devices with their start and end apart: 180 -> 73, of which waited for: 67 -> 25; matrix products, arithmetic and copies ran while one was open for 21% -> 7% of each run, Pallas kernels for 0% -> 21%
where the time goes in v1:
time: 683 us; the launch traced here: 672 us
  waiting for transfers between devices  219 us (32%)
  Pallas kernels  144 us (21%)
  blocking collectives  92.2 us (13%)
  starting transfers between devices  90 us (13%)
  local copies, waits for them, and re-layouts  66.9 us (10%)
  other arithmetic  29.7 us (4%)
  between operations  16.1 us (2%)
  matrix products  13.6 us (2%)
    ppermute x38, waiting for transfers between devices, swap(): return lax.ppermute(v, axis, [(0, 1), (1, 0)])  139 us
    all_to_all x4, blocking collectives, exchange(): return lax.all_to_all(v, axes, split_axis=0, concat_axis=0, tiled=True)  92.2 us
    ppermute x24, waiting for transfers between devices, shift_x(): return lax.ppermute(v, 'x', [((i + distance) % 4, i) for i in range(4)])  48 us
    unnamed x253, local copies, waits for them, and re-layouts  45.4 us
    all_to_all x5, starting transfers between devices, exchange(): return lax.all_to_all(v, axes, split_axis=0, concat_axis=0, tiled=True)  30.9 us
    ppermute x24, starting transfers between devices, shift_x(): return lax.ppermute(v, 'x', [((i + distance) % 4, i) for i in range(4)])  29.4 us
    pallas_call x4, Pallas kernels, ffn(): pl.pallas_call(ffn_kernel, out_shape=(jax.ShapeDtypeStruct((ROWS, WIDTH),...  27.3 us
    pallas_call x1, Pallas kernels, back_earlier(): return call(plan, q, start, *kvs, grad, out, lse)  27.1 us
  transfers between devices with their start and end apart: 73, of which 25 were waited for; matrix products, arithmetic and copies ran while one was open for 7% of the time, Pallas kernels for 21%

profile of v1, /device:TPU:8, one launch (start us, length us, event | category | flops | bytes accessed | tf_op | source)
XLA Modules:
  0.0 671.7 jit_solution(10823292114174825813)
XLA Ops:
  8.8 2.7 collective-permute-start.22
  18.8 34.9 %all_to_all.45 = bf16[128,12,384]{2,1,0:T(8,128)(2,1)} all-to-all(bf16[128,12,384]{2,1,0:T(8,128)(2,1)S(1)} %bitcast.96), channel_id=1, replica_groups=mesh['ylo'=2,'z'=4,'x'=4,'core'=2,'yhi'=2] {'ylo','z','x','core','yhi'}, dimensions={0} | all-to-all | bytes 2359296 | tf_op jit(solution)/shard_map/all_to_all | solution.py:65
  53.7 2.3 reshape.610.refs_8_.w_ref
  57.6 15.7 %all_to_all.46 = bf16[8,24,1536]{2,1,0:T(8,128)(2,1)} all-to-all(bf16[8,24,1536]{2,1,0:T(8,128)(2,1)S(1)} %copy.132), channel_id=1, replica_groups=mesh['ylo'=2,'z'=4,'x'=4,'core'=2,'yhi'=2] {'x','core'}, dimensions={0} | all-to-all | bytes 1179648 | tf_op jit(solution)/shard_map/all_to_all | solution.py:65
  77.6 1.9 fusion.36
  80.4 5.0 collective-permute-done.1.refs_2_.x0_ref
  85.4 2.9 collective-permute-done.3.refs_4_.x0_ref
  88.2 7.6 %collective-permute-done.5.refs_6_.x0_ref = bf16[128,1536]{1,0:T(8,128)(2,1)} collective-permute-done((bf16[128,1536]{1,0:T(8,128)(2,1)S(1)}, bf16[128,1536]{1,0:T(8,128)(2,1)}, u32[]{:S(2)}, u32[]{:S(2)}) %collective-permute-start.5) | collective-permute-done | bytes 393248 | tf_op jit(solution)/shard_map/ppermute | solution.py:52
  98.2 4.6 shard_map.237
  104.7 1.9 collective-permute-start.7
  106.6 3.1 collective-permute-start.9
  112.6 9.9 %collective-permute-done.7.refs_0_ = bf16[8,128,128]{2,1,0:T(8,128)(2,1)} collective-permute-done((bf16[8,128,128]{2,1,0:T(8,128)(2,1)}, bf16[8,128,128]{2,1,0:T(8,128)(2,1)}, u32[]{:S(2)}, u32[]{:S(2)}) %collective-permute-start.7) | collective-permute-done | bytes 262176 | tf_op jit(solution)/shard_map/ppermute | solution.py:61
  123.0 4.2 collective-permute-done.9.refs_2_
  128.0 3.0 collective-permute-done.17.c0_ref.refs_14_
  132.6 2.8 collective-permute-start.10
  136.5 12.5 %shard_map.238 = (f32[8,64,384]{2,1,0:T(8,128)S(1)}, f32[8,1,384]{2,1,0:T(1,128)S(1)}) custom-call(s32[8,12]{1,0:T(8,128)S(1)} %stack.74.plan, bf16[8,128,192]{2,1,0:T(8,128)(2,1)S(1)} %copy-done.58, s32[8,1,384]{2,1,0:T(1,128)S(1)} %copy.131.start_ref, bf16[8,128,128]{2,1,0:T(8,128)(2,1)} %get-tuple-element.101.refs_0_, ...), custom_call_target="tpu_custom_call" | custom-call | flops 4000000000 | bytes 8000000 | tf_op jit(solution)/shard_map/pallas_call | solution.py:506
  149.0 9.5 %collective-permute-done.10.refs_3_ = bf16[8,128,128]{2,1,0:T(8,128)(2,1)S(1)} collective-permute-done((bf16[8,128,128]{2,1,0:T(8,128)(2,1)}, bf16[8,128,128]{2,1,0:T(8,128)(2,1)S(1)}, u32[]{:S(2)}, u32[]{:S(2)}) %collective-permute-start.10) | collective-permute-done | bytes 262176 | tf_op jit(solution)/shard_map/ppermute | solution.py:56
  158.6 18.0 %shard_map.239 = (bf16[8,192,128]{2,1,0:T(8,128)(2,1)S(1)}, f32[8,64,384]{2,1,0:T(8,128)S(1)}, f32[8,1,384]{2,1,0:T(1,128)S(1)}) custom-call(s32[8,12]{1,0:T(8,128)S(1)} %stack.74.plan, bf16[8,128,192]{2,1,0:T(8,128)(2,1)S(1)} %copy-done.58, s32[8,1,384]{2,1,0:T(1,128)S(1)} %copy.131.start_ref, bf16[8,128,128]{2,1,0:T(8,128)(2,1)} %collective-permute-done.7.refs_0_, ...), custom_call_target="tpu_custom_call" | custom-call | flops 8000000000 | bytes 8000000 | tf_op jit(solution)/shard_map/pallas_call | solution.py:513
  176.6 11.4 %all_to_all.47 = bf16[8,192,128]{2,1,0:T(8,128)(2,1)S(1)} all-to-all(bf16[8,192,128]{2,1,0:T(8,128)(2,1)S(1)} %get-tuple-element.107.mix_ref), channel_id=1, replica_groups=mesh['ylo'=2,'z'=4,'x'=4,'core'=2,'yhi'=2] {'x','core'}, dimensions={0} | all-to-all | bytes 786432 | tf_op jit(solution)/shard_map/all_to_all | solution.py:65
  189.5 2.7 convolution_add_fusion.1
  192.2 2.6 multiply_reduce_fusion.2
  198.0 9.1 %collective-permute-done.27.x0_ref.refs_2_ = bf16[128,1536]{1,0:T(8,128)(2,1)S(1)} collective-permute-done((bf16[128,1536]{1,0:T(8,128)(2,1)S(1)}, bf16[128,1536]{1,0:T(8,128)(2,1)S(1)}, u32[]{:S(2)}, u32[]{:S(2)}) %collective-permute-start.27) | collective-permute-done | bytes 393248 | tf_op jit(solution)/shard_map/ppermute | solution.py:52
  207.2 2.8 collective-permute-done.29.x0_ref.refs_4_
  210.0 6.7 collective-permute-done.31.x0_ref.refs_6_
  217.5 3.7 copy-done
  222.2 6.8 %shard_map.240 = (bf16[128,1536]{1,0:T(8,128)(2,1)S(1)}, bf16[128,1536]{1,0:T(8,128)(2,1)}, bf16[2,256,512]{2,1,0:T(8,128)(2,1)S(1)}, bf16[2,256,1024]{2,1,0:T(8,128)(2,1)S(1)}) custom-call(bf16[128,1536]{1,0:T(8,128)(2,1)S(1)} %multiply_convert_fusion.x0_ref.refs_0_, bf16[128,1536]{1,0:T(8,128)(2,1)S(1)} %copy-done.76, bf16[128,1536]{1,0:T(8,128)(2,1)} %refs_8_, ...), custom_call_target="tpu_custom_call" | custom-call | flops 4026531840 | bytes 14000000 | tf_op jit(solution)/shard_map/pallas_call | solution.py:250
  232.1 7.0 %shard_map.241 = (bf16[128,1536]{1,0:T(8,128)(2,1)S(1)}, bf16[128,1536]{1,0:T(8,128)(2,1)}, bf16[2,256,512]{2,1,0:T(8,128)(2,1)S(1)}, bf16[2,256,1024]{2,1,0:T(8,128)(2,1)S(1)}) custom-call(bf16[128,1536]{1,0:T(8,128)(2,1)S(1)} %collective-permute-done.27.x0_ref.refs_2_, bf16[128,1536]{1,0:T(8,128)(2,1)} %collective-permute-done.28.x1_ref.refs_3_, ...), custom_call_target="tpu_custom_call" | custom-call | flops 4026531840 | bytes 14000000 | tf_op jit(solution)/shard_map/pallas_call | solution.py:250
  241.6 7.0 %shard_map.242 = (bf16[128,1536]{1,0:T(8,128)(2,1)S(1)}, bf16[128,1536]{1,0:T(8,128)(2,1)}, bf16[2,256,512]{2,1,0:T(8,128)(2,1)S(1)}, bf16[2,256,1024]{2,1,0:T(8,128)(2,1)S(1)}) custom-call(bf16[128,1536]{1,0:T(8,128)(2,1)} %collective-permute-done.29.x0_ref.refs_4_, bf16[128,1536]{1,0:T(8,128)(2,1)} %collective-permute-done.30.x1_ref.refs_5_, ...), custom_call_target="tpu_custom_call" | custom-call | flops 4026531840 | bytes 14000000 | tf_op jit(solution)/shard_map/pallas_call | solution.py:250
  251.7 6.4 shard_map.243
  266.8 16.3 %shard_map.244 = bf16[2,1536,1536]{2,1,0:T(8,128)(2,1)} custom-call(bf16[128,1536]{1,0:T(8,128)(2,1)S(1)} %copy-done.49, bf16[128,1536]{1,0:T(8,128)(2,1)S(1)} %copy-done.77, bf16[128,1536]{1,0:T(8,128)(2,1)S(1)} %copy-done.74, bf16[128,1536]{1,0:T(8,128)(2,1)} %collective-permute-done.28.x1_ref.refs_3_, ...), custom_call_target="tpu_custom_call" | custom-call | flops 9663676416 | bytes 24000000 | tf_op jit(solution)/shard_map/pallas_call | solution.py:317
  286.4 2.5 fusion.13
  288.9 2.5 fusion.10
  292.1 4.6 all-to-all-start.3
  297.2 2.9 collective-permute-start.59
  301.8 4.4 all-to-all-done.3.refs_4_.refs_2_
  310.3 27.1 %shard_map.249 = (f32[8,64,384]{2,1,0:T(8,128)S(1)}, f32[2,8,128,128]{3,2,1,0:T(8,128)S(1)}, bf16[2,8,128,128]{3,2,1,0:T(8,128)(2,1)S(1)}) custom-call(s32[8,12]{1,0:T(8,128)S(1)} %stack.74.plan, bf16[8,128,192]{2,1,0:T(8,128)(2,1)S(1)} %copy-done.59, s32[8,1,384]{2,1,0:T(1,128)S(1)} %copy.131.start_ref, ...), custom_call_target="tpu_custom_call" | custom-call | flops 20000000000 | bytes 8000000 | tf_op jit(solution)/shard_map/pallas_call | solution.py:527
  338.5 20.1 %shard_map.250 = (bf16[8,128,256]{2,1,0:T(8,128)(2,1)S(1)}, f32[1,8,128,128]{3,2,1,0:T(8,128)S(1)}, bf16[1,8,128,128]{3,2,1,0:T(8,128)(2,1)}) custom-call(s32[8,12]{1,0:T(8,128)S(1)} %stack.74.plan, bf16[8,128,192]{2,1,0:T(8,128)(2,1)S(1)} %copy-done.59, s32[8,1,384]{2,1,0:T(1,128)S(1)} %copy.131.start_ref, bf16[8,128,128]{2,1,0:T(8,128)(2,1)} %get-tuple-element.101.refs_0_, ...), custom_call_target="tpu_custom_call" | custom-call | flops 10000000000 | bytes 8000000 | tf_op jit(solution)/shard_map/pallas_call | solution.py:537
  358.6 2.6 collective-permute-start.47
  362.8 2.4 collective-permute-start.49
  366.0 6.9 %collective-permute-start.50 = (bf16[8,128,128]{2,1,0:T(8,128)(2,1)}, bf16[8,128,128]{2,1,0:T(8,128)(2,1)}, u32[]{:S(2)}, u32[]{:S(2)}) collective-permute-start(bf16[8,128,128]{2,1,0:T(8,128)(2,1)} %get-tuple-element.203), channel_id=1, source_target_pairs={{32,0},{48,16},{64,32},{80,48},{96,64},{112,80},{33,1},{49,17},{65... | collective-permute-start | bytes 786440 | tf_op jit(solution)/shard_map/ppermute | solution.py:61
  374.2 3.5 shard_map.255
  378.6 4.3 all-to-all-start.5
  386.0 2.1 shard_map.254
  389.6 2.2 shard_map.253
  393.3 2.0 shard_map.252
  397.6 1.9 shard_map.251
  404.8 3.3 fusion.24
  411.3 3.3 all-to-all-start.6
  414.7 2.0 maximum_maximum_fusion
  416.7 3.5 all-to-all-done.6
  420.1 30.3 %all_to_all.48 = bf16[128,12,384]{2,1,0:T(8,128)(2,1)} all-to-all(bf16[128,12,384]{2,1,0:T(8,128)(2,1)S(1)} %maximum_maximum_fusion), channel_id=1, replica_groups=mesh['ylo'=2,'z'=4,'x'=4,'core'=2,'yhi'=2] {'ylo','z','x','core','yhi'}, dimensions={0} | all-to-all | bytes 2359296 | tf_op jit(solution)/shard_map/all_to_all | solution.py:65
  450.4 6.1 all-to-all-start.7
  456.5 3.7 copy-done.1
  462.0 3.7 copy-done.2
  469.8 1.7 shard_map.245
  480.6 2.1 collective-permute-start.65
  484.2 2.3 collective-permute-start.57
  488.0 7.2 %collective-permute-done.42 = bf16[128,1536]{1,0:T(8,128)(2,1)S(1)} collective-permute-done((bf16[128,1536]{1,0:T(8,128)(2,1)S(1)}, bf16[128,1536]{1,0:T(8,128)(2,1)S(1)}, u32[]{:S(2)}, u32[]{:S(2)}) %collective-permute-start.42) | collective-permute-done | bytes 393248 | tf_op jit(solution)/shard_map/ppermute | solution.py:52
  497.3 124.3 %collective-permute-done.65 = bf16[4,24,96]{2,1,0:T(8,128)(2,1)S(1)} collective-permute-done((bf16[4,24,96]{2,1,0:T(8,128)(2,1)S(1)}, bf16[4,24,96]{2,1,0:T(8,128)(2,1)S(1)}, u32[]{:S(2)}, u32[]{:S(2)}) %collective-permute-start.65) | collective-permute-done | bytes 18464 | tf_op jit(solution)/shard_map/ppermute | solution.py:56
  622.4 1.7 reshape.635
  625.7 2.8 fusion.22
  631.2 6.0 reduce_sum.95
  637.2 12.6 %all-to-all-start.8 = ((bf16[8,24,1536]{2,1,0:T(8,128)(2,1)}), bf16[8,24,1536]{2,1,0:T(8,128)(2,1)S(1)}, u32[]{:S(2)}, u32[]{:S(2)}) async-start(bf16[8,24,1536]{2,1,0:T(8,128)(2,1)} %bitcast.45), calls=%async_computation.8 | async-start | bytes 1179648 | tf_op jit(solution)/shard_map/all_to_all | solution.py:65
  651.3 9.5 %all-to-all-done.8 = bf16[8,24,1536]{2,1,0:T(8,128)(2,1)S(1)} async-done(((bf16[8,24,1536]{2,1,0:T(8,128)(2,1)}), bf16[8,24,1536]{2,1,0:T(8,128)(2,1)S(1)}, u32[]{:S(2)}, u32[]{:S(2)}) %all-to-all-start.8) | async-done | bytes 589856 | tf_op jit(solution)/shard_map/all_to_all | solution.py:65
  (497 shorter events, 112.6 us)
Async XLA Ops:
  7.2 182.2 %all-gather.3.cloned.1.call-start = ((), (), s32[]{:S(2)}) async-start(), calls=%async_computation.9 | async-start | bytes 5013504 | tf_op jit(solution)/shard_map/all_gather | solution.py:610
  7.3 5.7 collective-permute-start.24
  8.8 4.2 collective-permute-start.19
  8.8 5.7 collective-permute-start.22
  11.6 4.2 collective-permute-start.20
  17.9 199.5 %all-gather.5.cloned.1.call-start = ((), (), s32[]{:S(2)}) async-start(), calls=%async_computation.10 | async-start | bytes 10027008 | tf_op jit(solution)/shard_map/all_gather | solution.py:657
  73.3 23.7 %collective-permute-start = (bf16[128,1536]{1,0:T(8,128)(2,1)S(1)}, bf16[128,1536]{1,0:T(8,128)(2,1)S(1)}, u32[]{:S(2)}, u32[]{:S(2)}) collective-permute-start(bf16[128,1536]{1,0:T(8,128)(2,1)S(1)} %copy-done.5), channel_id=1, source_target_pairs={{0,2},{2,0},{1,3},{3,1},{4,6},{6,4},{5,7},{7,5},{8,10},{10,8},{9,1... | collective-permute-start | bytes 1179656 | tf_op jit(solution)/shard_map/ppermute | solution.py:56
  73.4 12.0 %collective-permute-start.1 = (bf16[128,1536]{1,0:T(8,128)(2,1)S(1)}, bf16[128,1536]{1,0:T(8,128)(2,1)S(1)}, u32[]{:S(2)}, u32[]{:S(2)}) collective-permute-start(bf16[128,1536]{1,0:T(8,128)(2,1)S(1)} %copy-done.5), channel_id=1, source_target_pairs={{4,0},{8,4},{12,8},{0,12},{5,1},{9,5},{13,9},{1,13},{6,2},{10,6},{... | collective-permute-start | bytes 1179656 | tf_op jit(solution)/shard_map/ppermute | solution.py:52
  74.6 13.6 %collective-permute-start.3 = (bf16[128,1536]{1,0:T(8,128)(2,1)S(1)}, bf16[128,1536]{1,0:T(8,128)(2,1)}, u32[]{:S(2)}, u32[]{:S(2)}) collective-permute-start(bf16[128,1536]{1,0:T(8,128)(2,1)S(1)} %copy-done.5), channel_id=1, source_target_pairs={{8,0},{12,4},{0,8},{4,12},{9,1},{13,5},{1,9},{5,13},{10,2},{14,6},... | collective-permute-start | bytes 1179656 | tf_op jit(solution)/shard_map/ppermute | solution.py:52
  76.1 19.8 %collective-permute-start.5 = (bf16[128,1536]{1,0:T(8,128)(2,1)S(1)}, bf16[128,1536]{1,0:T(8,128)(2,1)}, u32[]{:S(2)}, u32[]{:S(2)}) collective-permute-start(bf16[128,1536]{1,0:T(8,128)(2,1)S(1)} %copy-done.5), channel_id=1, source_target_pairs={{12,0},{0,4},{4,8},{8,12},{13,1},{1,5},{5,9},{9,13},{14,2},{2,6},{... | collective-permute-start | bytes 1179656 | tf_op jit(solution)/shard_map/ppermute | solution.py:52
  85.4 11.7 %collective-permute-start.2 = (bf16[128,1536]{1,0:T(8,128)(2,1)S(1)}, bf16[128,1536]{1,0:T(8,128)(2,1)S(1)}, u32[]{:S(2)}, u32[]{:S(2)}) collective-permute-start(bf16[128,1536]{1,0:T(8,128)(2,1)S(1)} %collective-permute-done.1.refs_2_.x0_ref), channel_id=1, source_target_pairs={{0,2},{2,0},{1,3},{3,1},{4,6},{6,4},{5,7},{7,5},{8,10},{10,8},{9,1... | collective-permute-start | bytes 1179656 | tf_op jit(solution)/shard_map/ppermute | solution.py:56
  88.2 8.8 %collective-permute-start.4 = (bf16[128,1536]{1,0:T(8,128)(2,1)}, bf16[128,1536]{1,0:T(8,128)(2,1)S(1)}, u32[]{:S(2)}, u32[]{:S(2)}) collective-permute-start(bf16[128,1536]{1,0:T(8,128)(2,1)} %collective-permute-done.3.refs_4_.x0_ref), channel_id=1, source_target_pairs={{0,2},{2,0},{1,3},{3,1},{4,6},{6,4},{5,7},{7,5},{8,10},{10,8},{9,1... | collective-permute-start | bytes 1179656 | tf_op jit(solution)/shard_map/ppermute | solution.py:56
  104.7 17.9 %collective-permute-start.7 = (bf16[8,128,128]{2,1,0:T(8,128)(2,1)}, bf16[8,128,128]{2,1,0:T(8,128)(2,1)}, u32[]{:S(2)}, u32[]{:S(2)}) collective-permute-start(bf16[8,128,128]{2,1,0:T(8,128)(2,1)} %get-tuple-element.101.refs_0_), channel_id=1, source_target_pairs={{0,32},{16,48},{32,64},{48,80},{64,96},{80,112},{1,33},{17,49},{33... | collective-permute-start | bytes 786440 | tf_op jit(solution)/shard_map/ppermute | solution.py:61
  106.6 20.6 %collective-permute-start.9 = (bf16[8,128,128]{2,1,0:T(8,128)(2,1)}, bf16[8,128,128]{2,1,0:T(8,128)(2,1)}, u32[]{:S(2)}, u32[]{:S(2)}) collective-permute-start(bf16[8,128,128]{2,1,0:T(8,128)(2,1)} %get-tuple-element.101.refs_0_), channel_id=1, source_target_pairs={{0,16},{16,32},{32,48},{48,64},{64,80},{80,96},{96,112},{1,17},{17... | collective-permute-start | bytes 786440 | tf_op jit(solution)/shard_map/ppermute | solution.py:61
  109.7 17.6 %collective-permute-start.13 = (bf16[128,1536]{1,0:T(8,128)(2,1)}, bf16[128,1536]{1,0:T(8,128)(2,1)S(1)}, u32[]{:S(2)}, u32[]{:S(2)}) collective-permute-start(bf16[128,1536]{1,0:T(8,128)(2,1)} %refs_8_), channel_id=1, source_target_pairs={{4,0},{8,4},{12,8},{0,12},{5,1},{9,5},{13,9},{1,13},{6,2},{10,6},{... | collective-permute-start | bytes 1179656 | tf_op jit(solution)/shard_map/ppermute | solution.py:52
  110.4 17.5 %collective-permute-start.15 = (bf16[128,1536]{1,0:T(8,128)(2,1)}, bf16[128,1536]{1,0:T(8,128)(2,1)S(1)}, u32[]{:S(2)}, u32[]{:S(2)}) collective-permute-start(bf16[128,1536]{1,0:T(8,128)(2,1)} %refs_8_), channel_id=1, source_target_pairs={{8,0},{12,4},{0,8},{4,12},{9,1},{13,5},{1,9},{5,13},{10,2},{14,6},... | collective-permute-start | bytes 1179656 | tf_op jit(solution)/shard_map/ppermute | solution.py:52
  111.8 19.1 %collective-permute-start.17 = (bf16[128,1536]{1,0:T(8,128)(2,1)}, bf16[128,1536]{1,0:T(8,128)(2,1)}, u32[]{:S(2)}, u32[]{:S(2)}) collective-permute-start(bf16[128,1536]{1,0:T(8,128)(2,1)} %refs_8_), channel_id=1, source_target_pairs={{12,0},{0,4},{4,8},{8,12},{13,1},{1,5},{5,9},{9,13},{14,2},{2,6},{... | collective-permute-start | bytes 1179656 | tf_op jit(solution)/shard_map/ppermute | solution.py:52
  122.5 9.4 %collective-permute-start.11 = (bf16[8,128,128]{2,1,0:T(8,128)(2,1)}, bf16[8,128,128]{2,1,0:T(8,128)(2,1)}, u32[]{:S(2)}, u32[]{:S(2)}) collective-permute-start(bf16[8,128,128]{2,1,0:T(8,128)(2,1)} %get-tuple-element.101.refs_0_), channel_id=1, source_target_pairs={{0,1},{1,0},{2,3},{3,2},{4,5},{5,4},{6,7},{7,6},{8,9},{9,8},{10,11... | collective-permute-start | bytes 786440 | tf_op jit(solution)/shard_map/ppermute | solution.py:56
  127.2 5.4 collective-permute-start.12
  127.3 21.7 %collective-permute-start.14 = (bf16[128,1536]{1,0:T(8,128)(2,1)S(1)}, bf16[128,1536]{1,0:T(8,128)(2,1)}, u32[]{:S(2)}, u32[]{:S(2)}) collective-permute-start(bf16[128,1536]{1,0:T(8,128)(2,1)S(1)} %collective-permute-done.13.c0_ref.refs_10_), channel_id=1, source_target_pairs={{0,2},{2,0},{1,3},{3,1},{4,6},{6,4},{5,7},{7,5},{8,10},{10,8},{9,1... | collective-permute-start | bytes 1179656 | tf_op jit(solution)/shard_map/ppermute | solution.py:56
  127.9 21.1 %collective-permute-start.16 = (bf16[128,1536]{1,0:T(8,128)(2,1)S(1)}, bf16[128,1536]{1,0:T(8,128)(2,1)}, u32[]{:S(2)}, u32[]{:S(2)}) collective-permute-start(bf16[128,1536]{1,0:T(8,128)(2,1)S(1)} %collective-permute-done.15.c0_ref.refs_12_), channel_id=1, source_target_pairs={{0,2},{2,0},{1,3},{3,1},{4,6},{6,4},{5,7},{7,5},{8,10},{10,8},{9,1... | collective-permute-start | bytes 1179656 | tf_op jit(solution)/shard_map/ppermute | solution.py:56
  131.0 18.0 %collective-permute-start.18 = (bf16[128,1536]{1,0:T(8,128)(2,1)}, bf16[128,1536]{1,0:T(8,128)(2,1)}, u32[]{:S(2)}, u32[]{:S(2)}) collective-permute-start(bf16[128,1536]{1,0:T(8,128)(2,1)} %collective-permute-done.17.c0_ref.refs_14_), channel_id=1, source_target_pairs={{0,2},{2,0},{1,3},{3,1},{4,6},{6,4},{5,7},{7,5},{8,10},{10,8},{9,1... | collective-permute-start | bytes 1179656 | tf_op jit(solution)/shard_map/ppermute | solution.py:56
  131.9 17.1 %collective-permute-start.8 = (bf16[8,128,128]{2,1,0:T(8,128)(2,1)}, bf16[8,128,128]{2,1,0:T(8,128)(2,1)S(1)}, u32[]{:S(2)}, u32[]{:S(2)}) collective-permute-start(bf16[8,128,128]{2,1,0:T(8,128)(2,1)} %collective-permute-done.7.refs_0_), channel_id=1, source_target_pairs={{0,1},{1,0},{2,3},{3,2},{4,5},{5,4},{6,7},{7,6},{8,9},{9,8},{10,11... | collective-permute-start | bytes 786440 | tf_op jit(solution)/shard_map/ppermute | solution.py:56
  132.6 25.9 %collective-permute-start.10 = (bf16[8,128,128]{2,1,0:T(8,128)(2,1)}, bf16[8,128,128]{2,1,0:T(8,128)(2,1)S(1)}, u32[]{:S(2)}, u32[]{:S(2)}) collective-permute-start(bf16[8,128,128]{2,1,0:T(8,128)(2,1)} %collective-permute-done.9.refs_2_), channel_id=1, source_target_pairs={{0,1},{1,0},{2,3},{3,2},{4,5},{5,4},{6,7},{7,6},{8,9},{9,8},{10,11... | collective-permute-start | bytes 786440 | tf_op jit(solution)/shard_map/ppermute | solution.py:56
  195.0 12.1 %collective-permute-start.27 = (bf16[128,1536]{1,0:T(8,128)(2,1)S(1)}, bf16[128,1536]{1,0:T(8,128)(2,1)S(1)}, u32[]{:S(2)}, u32[]{:S(2)}) collective-permute-start(bf16[128,1536]{1,0:T(8,128)(2,1)S(1)} %multiply_convert_fusion.x0_ref.refs_0_), channel_id=1, source_target_pairs={{4,0},{8,4},{12,8},{0,12},{5,1},{9,5},{13,9},{1,13},{6,2},{10,6},{... | collective-permute-start | bytes 1179656 | tf_op jit(solution)/shard_map/ppermute | solution.py:52
  196.3 13.7 %collective-permute-start.29 = (bf16[128,1536]{1,0:T(8,128)(2,1)S(1)}, bf16[128,1536]{1,0:T(8,128)(2,1)}, u32[]{:S(2)}, u32[]{:S(2)}) collective-permute-start(bf16[128,1536]{1,0:T(8,128)(2,1)S(1)} %multiply_convert_fusion.x0_ref.refs_0_), channel_id=1, source_target_pairs={{8,0},{12,4},{0,8},{4,12},{9,1},{13,5},{1,9},{5,13},{10,2},{14,6},... | collective-permute-start | bytes 1179656 | tf_op jit(solution)/shard_map/ppermute | solution.py:52
  197.7 19.0 %collective-permute-start.31 = (bf16[128,1536]{1,0:T(8,128)(2,1)S(1)}, bf16[128,1536]{1,0:T(8,128)(2,1)}, u32[]{:S(2)}, u32[]{:S(2)}) collective-permute-start(bf16[128,1536]{1,0:T(8,128)(2,1)S(1)} %multiply_convert_fusion.x0_ref.refs_0_), channel_id=1, source_target_pairs={{12,0},{0,4},{4,8},{8,12},{13,1},{1,5},{5,9},{9,13},{14,2},{2,6},{... | collective-permute-start | bytes 1179656 | tf_op jit(solution)/shard_map/ppermute | solution.py:52
  197.9 18.8 %collective-permute-start.26 = (bf16[128,1536]{1,0:T(8,128)(2,1)S(1)}, bf16[128,1536]{1,0:T(8,128)(2,1)S(1)}, u32[]{:S(2)}, u32[]{:S(2)}) collective-permute-start(bf16[128,1536]{1,0:T(8,128)(2,1)S(1)} %multiply_convert_fusion.x0_ref.refs_0_), channel_id=1, source_target_pairs={{0,2},{2,0},{1,3},{3,1},{4,6},{6,4},{5,7},{7,5},{8,10},{10,8},{9,1... | collective-permute-start | bytes 1179656 | tf_op jit(solution)/shard_map/ppermute | solution.py:56
  207.1 24.9 %collective-permute-start.28 = (bf16[128,1536]{1,0:T(8,128)(2,1)S(1)}, bf16[128,1536]{1,0:T(8,128)(2,1)}, u32[]{:S(2)}, u32[]{:S(2)}) collective-permute-start(bf16[128,1536]{1,0:T(8,128)(2,1)S(1)} %collective-permute-done.27.x0_ref.refs_2_), channel_id=1, source_target_pairs={{0,2},{2,0},{1,3},{3,1},{4,6},{6,4},{5,7},{7,5},{8,10},{10,8},{9,1... | collective-permute-start | bytes 1179656 | tf_op jit(solution)/shard_map/ppermute | solution.py:56
  210.0 31.6 %collective-permute-start.30 = (bf16[128,1536]{1,0:T(8,128)(2,1)}, bf16[128,1536]{1,0:T(8,128)(2,1)}, u32[]{:S(2)}, u32[]{:S(2)}) collective-permute-start(bf16[128,1536]{1,0:T(8,128)(2,1)} %collective-permute-done.29.x0_ref.refs_4_), channel_id=1, source_target_pairs={{0,2},{2,0},{1,3},{3,1},{4,6},{6,4},{5,7},{7,5},{8,10},{10,8},{9,1... | collective-permute-start | bytes 1179656 | tf_op jit(solution)/shard_map/ppermute | solution.py:56
  216.7 34.9 %collective-permute-start.32 = (bf16[128,1536]{1,0:T(8,128)(2,1)}, bf16[128,1536]{1,0:T(8,128)(2,1)}, u32[]{:S(2)}, u32[]{:S(2)}) collective-permute-start(bf16[128,1536]{1,0:T(8,128)(2,1)} %collective-permute-done.31.x0_ref.refs_6_), channel_id=1, source_target_pairs={{0,2},{2,0},{1,3},{3,1},{4,6},{6,4},{5,7},{7,5},{8,10},{10,8},{9,1... | collective-permute-start | bytes 1179656 | tf_op jit(solution)/shard_map/ppermute | solution.py:56
  231.6 26.8 %collective-permute-start.33 = (bf16[128,1536]{1,0:T(8,128)(2,1)}, bf16[128,1536]{1,0:T(8,128)(2,1)}, u32[]{:S(2)}, u32[]{:S(2)}) collective-permute-start(bf16[128,1536]{1,0:T(8,128)(2,1)} %get-tuple-element.124), channel_id=1, source_target_pairs={{0,2},{2,0},{1,3},{3,1},{4,6},{6,4},{5,7},{7,5},{8,10},{10,8},{9,1... | collective-permute-start | bytes 1179656 | tf_op jit(solution)/shard_map/ppermute | solution.py:56
  241.6 17.9 %collective-permute-start.34 = (bf16[128,1536]{1,0:T(8,128)(2,1)}, bf16[128,1536]{1,0:T(8,128)(2,1)}, u32[]{:S(2)}, u32[]{:S(2)}) collective-permute-start(bf16[128,1536]{1,0:T(8,128)(2,1)} %get-tuple-element.126), channel_id=1, source_target_pairs={{0,2},{2,0},{1,3},{3,1},{4,6},{6,4},{5,7},{7,5},{8,10},{10,8},{9,1... | collective-permute-start | bytes 1179656 | tf_op jit(solution)/shard_map/ppermute | solution.py:56
  251.2 9.6 %collective-permute-start.35 = (bf16[128,1536]{1,0:T(8,128)(2,1)}, bf16[128,1536]{1,0:T(8,128)(2,1)S(1)}, u32[]{:S(2)}, u32[]{:S(2)}) collective-permute-start(bf16[128,1536]{1,0:T(8,128)(2,1)} %get-tuple-element.128), channel_id=1, source_target_pairs={{0,2},{2,0},{1,3},{3,1},{4,6},{6,4},{5,7},{7,5},{8,10},{10,8},{9,1... | collective-permute-start | bytes 1179656 | tf_op jit(solution)/shard_map/ppermute | solution.py:56
  261.1 22.0 %collective-permute-start.39 = (bf16[128,1536]{1,0:T(8,128)(2,1)S(1)}, bf16[128,1536]{1,0:T(8,128)(2,1)S(1)}, u32[]{:S(2)}, u32[]{:S(2)}) collective-permute-start(bf16[128,1536]{1,0:T(8,128)(2,1)S(1)} %add_convert_fusion.10), channel_id=1, source_target_pairs={{4,0},{8,4},{12,8},{0,12},{5,1},{9,5},{13,9},{1,13},{6,2},{10,6},{... | collective-permute-start | bytes 1179656 | tf_op jit(solution)/shard_map/ppermute | solution.py:52
  261.9 21.2 %collective-permute-start.38 = (bf16[128,1536]{1,0:T(8,128)(2,1)S(1)}, bf16[128,1536]{1,0:T(8,128)(2,1)S(1)}, u32[]{:S(2)}, u32[]{:S(2)}) collective-permute-start(bf16[128,1536]{1,0:T(8,128)(2,1)S(1)} %add_convert_fusion.11), channel_id=1, source_target_pairs={{8,0},{12,4},{0,8},{4,12},{9,1},{13,5},{1,9},{5,13},{10,2},{14,6},... | collective-permute-start | bytes 1179656 | tf_op jit(solution)/shard_map/ppermute | solution.py:52
  263.2 19.9 %collective-permute-start.37 = (bf16[128,1536]{1,0:T(8,128)(2,1)S(1)}, bf16[128,1536]{1,0:T(8,128)(2,1)S(1)}, u32[]{:S(2)}, u32[]{:S(2)}) collective-permute-start(bf16[128,1536]{1,0:T(8,128)(2,1)S(1)} %add_convert_fusion.12), channel_id=1, source_target_pairs={{12,0},{0,4},{4,8},{8,12},{13,1},{1,5},{5,9},{9,13},{14,2},{2,6},{... | collective-permute-start | bytes 1179656 | tf_op jit(solution)/shard_map/ppermute | solution.py:52
  292.1 14.1 %all-to-all-start.3 = ((bf16[8,192,128]{2,1,0:T(8,128)(2,1)}), bf16[8,192,128]{2,1,0:T(8,128)(2,1)S(1)}, u32[]{:S(2)}, u32[]{:S(2)}) async-start(bf16[8,192,128]{2,1,0:T(8,128)(2,1)} %bitcast.30), calls=%async_computation.3 | async-start | bytes 786432 | tf_op jit(solution)/shard_map/all_to_all | solution.py:65
  296.7 66.1 %collective-permute-start.58 = (bf16[128,1536]{1,0:T(8,128)(2,1)S(1)}, bf16[128,1536]{1,0:T(8,128)(2,1)S(1)}, u32[]{:S(2)}, u32[]{:S(2)}) collective-permute-start(bf16[128,1536]{1,0:T(8,128)(2,1)S(1)} %fusion.77.refs_0_), channel_id=1, source_target_pairs={{0,2},{2,0},{1,3},{3,1},{4,6},{6,4},{5,7},{7,5},{8,10},{10,8},{9,1... | collective-permute-start | bytes 1179656 | tf_op jit(solution)/shard_map/ppermute | solution.py:56
  297.2 61.4 %collective-permute-start.59 = (bf16[128,1536]{1,0:T(8,128)(2,1)S(1)}, bf16[128,1536]{1,0:T(8,128)(2,1)}, u32[]{:S(2)}, u32[]{:S(2)}) collective-permute-start(bf16[128,1536]{1,0:T(8,128)(2,1)S(1)} %fusion.77.refs_0_), channel_id=1, source_target_pairs={{4,0},{8,4},{12,8},{0,12},{5,1},{9,5},{13,9},{1,13},{6,2},{10,6},{... | collective-permute-start | bytes 1179656 | tf_op jit(solution)/shard_map/ppermute | solution.py:52
  300.1 61.1 %collective-permute-start.61 = (bf16[128,1536]{1,0:T(8,128)(2,1)S(1)}, bf16[128,1536]{1,0:T(8,128)(2,1)}, u32[]{:S(2)}, u32[]{:S(2)}) collective-permute-start(bf16[128,1536]{1,0:T(8,128)(2,1)S(1)} %fusion.77.refs_0_), channel_id=1, source_target_pairs={{8,0},{12,4},{0,8},{4,12},{9,1},{13,5},{1,9},{5,13},{10,2},{14,6},... | collective-permute-start | bytes 1179656 | tf_op jit(solution)/shard_map/ppermute | solution.py:52
  300.9 60.3 %collective-permute-start.63 = (bf16[128,1536]{1,0:T(8,128)(2,1)S(1)}, bf16[128,1536]{1,0:T(8,128)(2,1)}, u32[]{:S(2)}, u32[]{:S(2)}) collective-permute-start(bf16[128,1536]{1,0:T(8,128)(2,1)S(1)} %fusion.77.refs_0_), channel_id=1, source_target_pairs={{12,0},{0,4},{4,8},{8,12},{13,1},{1,5},{5,9},{9,13},{14,2},{2,6},{... | collective-permute-start | bytes 1179656 | tf_op jit(solution)/shard_map/ppermute | solution.py:52
  337.4 24.3 %collective-permute-start.48 = (bf16[2,8,128,128]{3,2,1,0:T(8,128)(2,1)S(1)}, bf16[2,8,128,128]{3,2,1,0:T(8,128)(2,1)S(1)}, u32[]{:S(2)}, u32[]{:S(2)}) collective-permute-start(bf16[2,8,128,128]{3,2,1,0:T(8,128)(2,1)S(1)} %get-tuple-element.163), channel_id=1, source_target_pairs={{0,1},{1,0},{2,3},{3,2},{4,5},{5,4},{6,7},{7,6},{8,9},{9,8},{10,11... | collective-permute-start | bytes 1572872 | tf_op jit(solution)/shard_map/ppermute | solution.py:56
  358.6 24.3 %collective-permute-start.47 = (bf16[8,128,128]{2,1,0:T(8,128)(2,1)}, bf16[8,128,128]{2,1,0:T(8,128)(2,1)}, u32[]{:S(2)}, u32[]{:S(2)}) collective-permute-start(bf16[8,128,128]{2,1,0:T(8,128)(2,1)} %bitcast.32), channel_id=1, source_target_pairs={{0,1},{1,0},{2,3},{3,2},{4,5},{5,4},{6,7},{7,6},{8,9},{9,8},{10,11... | collective-permute-start | bytes 786440 | tf_op jit(solution)/shard_map/ppermute | solution.py:56
  361.2 11.9 %collective-permute-start.62 = (bf16[128,1536]{1,0:T(8,128)(2,1)}, bf16[128,1536]{1,0:T(8,128)(2,1)}, u32[]{:S(2)}, u32[]{:S(2)}) collective-permute-start(bf16[128,1536]{1,0:T(8,128)(2,1)} %collective-permute-done.61.refs_4_), channel_id=1, source_target_pairs={{0,2},{2,0},{1,3},{3,1},{4,6},{6,4},{5,7},{7,5},{8,10},{10,8},{9,1... | collective-permute-start | bytes 1179656 | tf_op jit(solution)/shard_map/ppermute | solution.py:56
  361.7 11.4 %collective-permute-start.64 = (bf16[128,1536]{1,0:T(8,128)(2,1)}, bf16[128,1536]{1,0:T(8,128)(2,1)}, u32[]{:S(2)}, u32[]{:S(2)}) collective-permute-start(bf16[128,1536]{1,0:T(8,128)(2,1)} %collective-permute-done.63.refs_6_), channel_id=1, source_target_pairs={{0,2},{2,0},{1,3},{3,1},{4,6},{6,4},{5,7},{7,5},{8,10},{10,8},{9,1... | collective-permute-start | bytes 1179656 | tf_op jit(solution)/shard_map/ppermute | solution.py:56
  362.8 20.1 %collective-permute-start.49 = (bf16[8,128,128]{2,1,0:T(8,128)(2,1)}, bf16[8,128,128]{2,1,0:T(8,128)(2,1)}, u32[]{:S(2)}, u32[]{:S(2)}) collective-permute-start(bf16[8,128,128]{2,1,0:T(8,128)(2,1)} %get-tuple-element.204), channel_id=1, source_target_pairs={{16,0},{32,16},{48,32},{64,48},{80,64},{96,80},{112,96},{17,1},{33... | collective-permute-start | bytes 786440 | tf_op jit(solution)/shard_map/ppermute | solution.py:61
  366.0 17.0 %collective-permute-start.50 = (bf16[8,128,128]{2,1,0:T(8,128)(2,1)}, bf16[8,128,128]{2,1,0:T(8,128)(2,1)}, u32[]{:S(2)}, u32[]{:S(2)}) collective-permute-start(bf16[8,128,128]{2,1,0:T(8,128)(2,1)} %get-tuple-element.203), channel_id=1, source_target_pairs={{32,0},{48,16},{64,32},{80,48},{96,64},{112,80},{33,1},{49,17},{65... | collective-permute-start | bytes 786440 | tf_op jit(solution)/shard_map/ppermute | solution.py:61
  378.6 30.7 %all-to-all-start.5 = ((bf16[16,96,192]{2,1,0:T(8,128)(2,1)}), bf16[16,96,192]{2,1,0:T(8,128)(2,1)}, u32[]{:S(2)}, u32[]{:S(2)}) async-start(bf16[16,96,192]{2,1,0:T(8,128)(2,1)} %copy-done.14), calls=%async_computation.5 | async-start | bytes 1572864 | tf_op jit(solution)/shard_map/all_to_all | solution.py:65
  411.3 8.8 %all-to-all-start.6 = ((bf16[8,24,96]{2,1,0:T(8,128)(2,1)}), bf16[8,24,96]{2,1,0:T(8,128)(2,1)S(1)}, u32[]{:S(2)}, u32[]{:S(2)}) async-start(bf16[8,24,96]{2,1,0:T(8,128)(2,1)} %bitcast.40), calls=%async_computation.6 | async-start | bytes 98304 | tf_op jit(solution)/shard_map/all_to_all | solution.py:65
  450.4 180.8 %all-to-all-start.7 = ((bf16[16,192,1536]{2,1,0:T(8,128)(2,1)}), bf16[16,192,1536]{2,1,0:T(8,128)(2,1)}, u32[]{:S(2)}, u32[]{:S(2)}) async-start(bf16[16,192,1536]{2,1,0:T(8,128)(2,1)} %bitcast.94), calls=%async_computation.7 | async-start | bytes 18874368 | tf_op jit(solution)/shard_map/all_to_all | solution.py:65
  461.8 10.2 %collective-permute-start.45 = (bf16[128,1536]{1,0:T(8,128)(2,1)S(1)}, bf16[128,1536]{1,0:T(8,128)(2,1)S(1)}, u32[]{:S(2)}, u32[]{:S(2)}) collective-permute-start(bf16[128,1536]{1,0:T(8,128)(2,1)S(1)} %get-tuple-element.155), channel_id=1, source_target_pairs={{0,2},{2,0},{1,3},{3,1},{4,6},{6,4},{5,7},{7,5},{8,10},{10,8},{9,1... | collective-permute-start | bytes 1179656 | tf_op jit(solution)/shard_map/ppermute | solution.py:56
  467.3 5.8 collective-permute-start.43
  469.7 4.7 collective-permute-start.41
  471.5 9.1 %collective-permute-start.40 = (bf16[128,1536]{1,0:T(8,128)(2,1)S(1)}, bf16[128,1536]{1,0:T(8,128)(2,1)S(1)}, u32[]{:S(2)}, u32[]{:S(2)}) collective-permute-start(bf16[128,1536]{1,0:T(8,128)(2,1)S(1)} %get-tuple-element.146), channel_id=1, source_target_pairs={{0,2},{2,0},{1,3},{3,1},{4,6},{6,4},{5,7},{7,5},{8,10},{10,8},{9,1... | collective-permute-start | bytes 1179656 | tf_op jit(solution)/shard_map/ppermute | solution.py:56
  472.2 12.0 %collective-permute-start.46 = (bf16[128,1536]{1,0:T(8,128)(2,1)S(1)}, bf16[128,1536]{1,0:T(8,128)(2,1)S(1)}, u32[]{:S(2)}, u32[]{:S(2)}) collective-permute-start(bf16[128,1536]{1,0:T(8,128)(2,1)S(1)} %add_convert_fusion.6), channel_id=1, source_target_pairs={{4,0},{8,4},{12,8},{0,12},{5,1},{9,5},{13,9},{1,13},{6,2},{10,6},{... | collective-permute-start | bytes 1179656 | tf_op jit(solution)/shard_map/ppermute | solution.py:52
  473.2 13.6 %collective-permute-start.44 = (bf16[128,1536]{1,0:T(8,128)(2,1)S(1)}, bf16[128,1536]{1,0:T(8,128)(2,1)S(1)}, u32[]{:S(2)}, u32[]{:S(2)}) collective-permute-start(bf16[128,1536]{1,0:T(8,128)(2,1)S(1)} %add_convert_fusion.7), channel_id=1, source_target_pairs={{8,0},{12,4},{0,8},{4,12},{9,1},{13,5},{1,9},{5,13},{10,2},{14,6},... | collective-permute-start | bytes 1179656 | tf_op jit(solution)/shard_map/ppermute | solution.py:52
  474.5 20.6 %collective-permute-start.42 = (bf16[128,1536]{1,0:T(8,128)(2,1)S(1)}, bf16[128,1536]{1,0:T(8,128)(2,1)S(1)}, u32[]{:S(2)}, u32[]{:S(2)}) collective-permute-start(bf16[128,1536]{1,0:T(8,128)(2,1)S(1)} %add_convert_fusion.8), channel_id=1, source_target_pairs={{12,0},{0,4},{4,8},{8,12},{13,1},{1,5},{5,9},{9,13},{14,2},{2,6},{... | collective-permute-start | bytes 1179656 | tf_op jit(solution)/shard_map/ppermute | solution.py:52
  479.6 144.5 %collective-permute-start.51 = (bf16[128,1536]{1,0:T(8,128)(2,1)S(1)}, bf16[128,1536]{1,0:T(8,128)(2,1)S(1)}, u32[]{:S(2)}, u32[]{:S(2)}) collective-permute-start(bf16[128,1536]{1,0:T(8,128)(2,1)S(1)} %copy-done.66), channel_id=1, source_target_pairs={{0,2},{2,0},{1,3},{3,1},{4,6},{6,4},{5,7},{7,5},{8,10},{10,8},{9,1... | collective-permute-start | bytes 1179656 | tf_op jit(solution)/shard_map/ppermute | solution.py:56
  480.6 141.0 %collective-permute-start.65 = (bf16[4,24,96]{2,1,0:T(8,128)(2,1)S(1)}, bf16[4,24,96]{2,1,0:T(8,128)(2,1)S(1)}, u32[]{:S(2)}, u32[]{:S(2)}) collective-permute-start(bf16[4,24,96]{2,1,0:T(8,128)(2,1)S(1)} %broadcast_select_fusion), channel_id=1, source_target_pairs={{0,1},{1,0},{2,3},{3,2},{4,5},{5,4},{6,7},{7,6},{8,9},{9,8},{10,11... | collective-permute-start | bytes 55304 | tf_op jit(solution)/shard_map/ppermute | solution.py:56
  484.2 139.8 %collective-permute-start.57 = (bf16[128,1536]{1,0:T(8,128)(2,1)}, bf16[128,1536]{1,0:T(8,128)(2,1)S(1)}, u32[]{:S(2)}, u32[]{:S(2)}) collective-permute-start(bf16[128,1536]{1,0:T(8,128)(2,1)} %add_convert_fusion.1), channel_id=1, source_target_pairs={{4,0},{8,4},{12,8},{0,12},{5,1},{9,5},{13,9},{1,13},{6,2},{10,6},{... | collective-permute-start | bytes 1179656 | tf_op jit(solution)/shard_map/ppermute | solution.py:52
  486.8 137.3 %collective-permute-start.55 = (bf16[128,1536]{1,0:T(8,128)(2,1)}, bf16[128,1536]{1,0:T(8,128)(2,1)}, u32[]{:S(2)}, u32[]{:S(2)}) collective-permute-start(bf16[128,1536]{1,0:T(8,128)(2,1)} %add_convert_fusion.2), channel_id=1, source_target_pairs={{8,0},{12,4},{0,8},{4,12},{9,1},{13,5},{1,9},{5,13},{10,2},{14,6},... | collective-permute-start | bytes 1179656 | tf_op jit(solution)/shard_map/ppermute | solution.py:52
  495.1 128.9 %collective-permute-start.53 = (bf16[128,1536]{1,0:T(8,128)(2,1)}, bf16[128,1536]{1,0:T(8,128)(2,1)}, u32[]{:S(2)}, u32[]{:S(2)}) collective-permute-start(bf16[128,1536]{1,0:T(8,128)(2,1)} %add_convert_fusion.3), channel_id=1, source_target_pairs={{12,0},{0,4},{4,8},{8,12},{13,1},{1,5},{5,9},{9,13},{14,2},{2,6},{... | collective-permute-start | bytes 1179656 | tf_op jit(solution)/shard_map/ppermute | solution.py:52
  637.2 23.6 %all-to-all-start.8 = ((bf16[8,24,1536]{2,1,0:T(8,128)(2,1)}), bf16[8,24,1536]{2,1,0:T(8,128)(2,1)S(1)}, u32[]{:S(2)}, u32[]{:S(2)}) async-start(bf16[8,24,1536]{2,1,0:T(8,128)(2,1)} %bitcast.45), calls=%async_computation.8 | async-start | bytes 1179648 | tf_op jit(solution)/shard_map/all_to_all | solution.py:65
  (135 other events, 1486.8 us)
Sparse Core Ops, SparseCore 0:
  18.1 70.6 all-gather.2
  90.9 94.5 all-gather.4

commit v2 on v1

--- a/solution.py
+++ b/solution.py
@@ -56,9 +56,14 @@
     return lax.ppermute(v, axis, [(0, 1), (1, 0)])
 
 
-def shift_super(v, distance):
-    pairs = [(i, i + distance) for i in range(8) if 0 <= i + distance < 8]
-    return lax.ppermute(v, ("ylo", "z"), pairs)
+def shift_super(v, distance, other):
+    pairs = [
+        (2 * i + h, 2 * (i + distance) + (h + other) % 2)
+        for i in range(8)
+        for h in (0, 1)
+        if 0 <= i + distance < 8
+    ]
+    return lax.ppermute(v, ("ylo", "z", "yhi"), pairs)
 
 
 def exchange(v, axes):
@@ -165,11 +170,13 @@
 
 
 def unproject_kernel(
-    gq_ref, g0_ref, g1_ref, g2_ref, g3_ref, raw_ref, x0_ref, x1_ref, w_ref, cos_ref, sin_ref,
-    head_gain_ref, part0_ref, part1_ref, graw_ref, attn_ref, heads_ref,
+    gq_ref, g0_ref, g1_ref, g2_ref, g3_ref, g4_ref, g5_ref, raw_ref, x0_ref, x1_ref, w_ref, cos_ref,
+    sin_ref, head_gain_ref, part0_ref, part1_ref, graw_ref, attn_ref, heads_ref,
 ):
     gq = gq_ref[...].reshape(PAIR, 4 * HEAD).astype(F32)
-    gkv = g0_ref[...] + g1_ref[...].astype(F32) + g2_ref[...].astype(F32) + g3_ref[...].astype(F32)
+    gkv = g0_ref[...]
+    for ref in (g1_ref, g2_ref, g3_ref, g4_ref, g5_ref):
+        gkv = gkv + ref[...].astype(F32)
     gkv = gkv.reshape(PAIR, 2 * HEAD)
     lane = lax.broadcasted_iota(jnp.int32, (PAIR, 2 * HEAD), 1)
     gk = (gkv * HEAD**-0.5).astype(BF16).astype(F32)
@@ -212,7 +219,7 @@
         unproject_kernel,
         out_shape=outs,
         grid=(1,),
-        in_specs=[at_d(2, ROWS, 4 * HEAD), kv, kv, kv, kv, at_d(1, PAIR, 4 * HEAD), rows, rows]
+        in_specs=[at_d(2, ROWS, 4 * HEAD)] + [kv] * 6 + [at_d(1, PAIR, 4 * HEAD), rows, rows]
         + [whole_of(WIDTH, 6 * HEAD), table, table, whole_of(1, 4 * HEAD)],
         out_specs=tuple(whole_of(*o.shape) for o in outs),
         compiler_params=params(1, 24),
@@ -307,8 +314,9 @@
     for d in range(4):
         grad_gu = grad_gu + dot(stacked(*xs[2 * d : 2 * d + 2]), gus[d][0], TN)
         grad_d = grad_d + dot(stacked(*cs[2 * d : 2 * d + 2]), acts[d][0], TN)
-    out_ref[0, :, : 2 * PADDED] = grad_gu.astype(BF16)
-    out_ref[0, :, 2 * PADDED :] = grad_d.astype(BF16)
+    out_ref[0, :, :PART] = grad_gu[:, :PART]
+    out_ref[0, :, PART : 2 * PART] = grad_gu[:, PADDED : PADDED + PART]
+    out_ref[0, :, 2 * PART :] = grad_d[:, :PART]
 
 
 def ffn_weights(xs, cs, gus, acts):
@@ -316,15 +324,74 @@
     rows = pl.BlockSpec((ROWS, tall), lambda y, m: (0, m))
     return pl.pallas_call(
         ffn_weights_kernel,
-        out_shape=jax.ShapeDtypeStruct((2, WIDTH, 3 * PADDED), BF16),
+        out_shape=jax.ShapeDtypeStruct((2, WIDTH, 3 * PART), F32),
         grid=(2, WIDTH // tall),
         in_specs=[rows] * 16
         + [pl.BlockSpec((1, PAIR, 2 * PADDED), lambda y, m: (y, 0, 0))] * 4
         + [pl.BlockSpec((1, PAIR, PADDED), lambda y, m: (y, 0, 0))] * 4,
-        out_specs=pl.BlockSpec((1, tall, 3 * PADDED), lambda y, m: (y, m, 0)),
+        out_specs=pl.BlockSpec((1, tall, 3 * PART), lambda y, m: (y, m, 0)),
         compiler_params=params(2, 40),
         cost_estimate=cost(2 * 2 * 1024 * WIDTH * 3 * PADDED, 24e6),
     )(*xs, *cs, *gus, *acts)
+
+
+def out_project_kernel(mix_ref, w_ref, part0_ref, part1_ref):
+    part = dot(mix_ref[...].reshape(PAIR, QUERY), w_ref[...], NT).astype(BF16)
+    part0_ref[...] = part[:ROWS]
+    part1_ref[...] = part[ROWS:]
+
+
+def out_project(d, mix, w):
+    rows = pl.BlockSpec((ROWS, WIDTH), lambda i: (0, 0))
+    return pl.pallas_call(
+        out_project_kernel,
+        out_shape=(jax.ShapeDtypeStruct((ROWS, WIDTH), BF16),) * 2,
+        grid=(1,),
+        in_specs=[
+            pl.BlockSpec((2, ROWS, QUERY), lambda i: (d, 0, 0)),
+            pl.BlockSpec((WIDTH, QUERY), lambda i: (0, 0)),
+        ],
+        out_specs=(rows, rows),
+        compiler_params=params(1, 16),
+        cost_estimate=cost(2 * PAIR * WIDTH * QUERY, 2e6),
+    )(mix, w)
+
+
+def out_back_kernel(w_ref, *refs):
+    for t in range(8):
+        refs[8][t] = dot(refs[t][...], w_ref[...]).astype(BF16)
+
+
+def out_back(branches, w):
+    return pl.pallas_call(
+        out_back_kernel,
+        out_shape=jax.ShapeDtypeStruct((8, ROWS, QUERY), BF16),
+        compiler_params=params(0, 16),
+        cost_estimate=cost(8 * PAIR * WIDTH * QUERY, 4e6),
+    )(w, *branches)
+
+
+def out_weights_kernel(mix_ref, *refs):
+    branches, (out_ref, total) = refs[:8], refs[8:]
+    grad = 0.0
+    for d in range(4):
+        mix = mix_ref[2 * d : 2 * d + 2].reshape(PAIR, QUERY)
+        grad = grad + dot(mix, stacked(*branches[2 * d : 2 * d + 2]), TN)
+    total[...] = grad
+    for half in (0, 1):
+        for s in range(8):
+            piece = total[half * 96 : half * 96 + 96, s * 192 : s * 192 + 192]
+            out_ref[half * 8 + s] = piece.astype(BF16)
+
+
+def out_weights(mix, branches):
+    return pl.pallas_call(
+        out_weights_kernel,
+        out_shape=jax.ShapeDtypeStruct((16, 96, 192), BF16),
+        scratch_shapes=[pltpu.VMEM((QUERY, WIDTH), F32)],
+        compiler_params=params(0, 24),
+        cost_estimate=cost(2 * 1024 * WIDTH * QUERY, 4e6),
+    )(mix, *branches)
 
 
 def side_by_side(t):
@@ -401,7 +468,7 @@
     total, accum = attend_body(2, 0, plan, q_ref, start_ref, kv, kvt, state)
     out = accum / total
     out_ref[0] = out
-    mix_ref[0] = on_top(out).astype(BF16)
+    mix_ref[0] = on_top(out).T.astype(BF16)
     lse_ref[0] = jnp.log2(total)
 
 
@@ -411,7 +478,7 @@
         dkv[...] = jnp.zeros_like(dkv)
 
     qt = side_by_side(q_ref[0].astype(F32).T)
-    gt = side_by_side(g_ref[0].astype(F32))
+    gt = side_by_side(g_ref[0].astype(F32).T)
     delta = jnp.sum(gt * out_ref[0], axis=0, keepdims=True)
     zero = jnp.zeros_like(qt)
     gt = jnp.concatenate([gt, zero], axis=0)
@@ -507,8 +574,8 @@
 
 
 def attend_earlier(plan, q, start, kvs, state):
-    outs = (jax.ShapeDtypeStruct((8, QUERY, ROWS), BF16), TILE_T, TILE_ROW)
-    specs = (tile(QUERY, ROWS),) + tuple(STATE)
+    outs = (jax.ShapeDtypeStruct((8, ROWS, QUERY), BF16), TILE_T, TILE_ROW)
+    specs = (placed(ROWS, QUERY),) + tuple(STATE)
     call = tiles_call(attend_earlier_kernel, 2, outs, STATE, specs, 8e9, False)
     return call(plan, q, start, *kvs, *state)
 
@@ -521,7 +588,7 @@
 def back_earlier(plan, q, start, kvs, grad, out, lse):
     shapes, specs = sent_back(2)
     call = tiles_call(
-        back_earlier_kernel, 2, [TILE_T] + shapes, [tile(QUERY, ROWS)] + STATE,
+        back_earlier_kernel, 2, [TILE_T] + shapes, [placed(ROWS, QUERY)] + STATE,
         [tile(HEAD, LANES)] + specs, 20e9, True,
     )
     return call(plan, q, start, *kvs, grad, out, lse)
@@ -531,37 +598,10 @@
     shapes, specs = sent_back(1)
     dq = jax.ShapeDtypeStruct((8, ROWS, 4 * HEAD), BF16)
     call = tiles_call(
-        back_own_kernel, 1, [dq] + shapes, [tile(QUERY, ROWS)] + STATE + [tile(HEAD, LANES)],
+        back_own_kernel, 1, [dq] + shapes, [placed(ROWS, QUERY)] + STATE + [tile(HEAD, LANES)],
         [placed(ROWS, 4 * HEAD)] + specs, 10e9, True,
     )
     return call(plan, q, start, *kvs, grad, out, lse, dqt)
-
-
-def out_weights_kernel(plan, mix_ref, *refs):
-    branches, (out_ref, total) = refs[:8], refs[8:]
-    grad = 0.0
-    for t in range(8):
-        grad = grad + dot(mix_ref[plan[t, 11]], branches[t][...])
-    total[...] = grad
-    for half in (0, 1):
-        for s in range(8):
-            out_ref[half * 8 + s] = total[half * 96 : half * 96 + 96, s * 192 : s * 192 + 192].astype(BF16)
-
-
-def out_weights(plan, mix, branches):
-    return pl.pallas_call(
-        out_weights_kernel,
-        out_shape=jax.ShapeDtypeStruct((16, 96, 192), BF16),
-        grid_spec=pltpu.PrefetchScalarGridSpec(
-            num_scalar_prefetch=1,
-            grid=(1,),
-            in_specs=[whole(8, QUERY, ROWS)] + [whole(ROWS, WIDTH)] * 8,
-            out_specs=whole(16, 96, 192),
-            scratch_shapes=[pltpu.VMEM((QUERY, WIDTH), F32)],
-        ),
-        compiler_params=params(1, 24),
-        cost_estimate=cost(2 * 1024 * WIDTH * QUERY, 4e6),
-    )(plan, mix, *branches)
 
 
 def after(v, *others):
@@ -598,16 +638,12 @@
         ],
         axis=-1,
     )
-    qkv_own = jnp.transpose(qkv_own, (1, 0, 2))
-    qkv_sent = jnp.broadcast_to(qkv_own[None, :, None], (8, 8, 2, 12, 6 * HEAD))
-    qkv = exchange(qkv_sent.reshape(128, 12, 6 * HEAD), ALL).reshape(WIDTH, 6 * HEAD)
+    token_blocks = near_gather(tokens)
+    qkv_rows = exchange(jnp.transpose(qkv_own, (1, 0, 2)), NEAR).reshape(1, 96, 6 * HEAD)
+    qkv = exchange(jnp.broadcast_to(qkv_rows, (16, 96, 6 * HEAD)), WIDE)
+    qkv = jnp.transpose(qkv.reshape(2, 8, 8, 12, 6 * HEAD), (1, 2, 0, 3, 4)).reshape(WIDTH, 6 * HEAD)
     gain_attn = qkv[:, 5 * HEAD].astype(F32)
     gain_ffn = qkv[:, 5 * HEAD + 1].astype(F32)
-    token_blocks = near_gather(tokens)
-
-    out_own = near_gather(w_out.T)
-    out_own = rel_to_abs(jnp.stack([jnp.stack(p) for p in out_own]), x, core).reshape(192, 768)
-    out_full = lax.all_gather(out_own, WIDE, axis=0, tiled=True).reshape(2, WIDTH, 768)
 
     token_index = jnp.arange(segments.shape[0], dtype=jnp.int32)
     begins = jnp.concatenate([jnp.ones((1,), jnp.bool_), segments[1:] != segments[:-1]])
@@ -637,7 +673,7 @@
         [first - window, relative]
         + [jnp.minimum(v, edge) for v in (lo, m1, m2, hi)]
         + [jnp.maximum(v - edge, 0) for v in (lo, m1, m2, hi)]
-        + [jnp.broadcast_to(yhi, (8,)), ((order // 2 + x) % 4) * 2 + (order % 2 + core) % 2],
+        + [jnp.broadcast_to(yhi, (8,))],
         axis=1,
     ).astype(jnp.int32)
     start_lanes = jnp.tile(own_starts - window, (1, GROUP)).reshape(8, 1, LANES)
@@ -646,39 +682,52 @@
         [b for p in token_blocks for b in p], qkv, gain_attn[None], cos, sin, head_gain
     )
 
-    ffn_own = jnp.concatenate(
+    out_own = jnp.transpose(w_out.reshape(4, QUERY, 24), (0, 2, 1))
+    rows_own = jnp.concatenate(
         [
-            jnp.pad(w.reshape(24, 8, PART), ((0, 0), (0, 0), (0, PADDED - PART)))
-            for w in after((w_gate, w_up, w_down.T), qkv)
-        ],
+            jnp.pad(w.reshape(24, 8, PART), ((0, 0), (0, 0), (0, PADDED - PART))).transpose(1, 0, 2)
+            for w in (w_gate, w_up, w_down.T)
+        ]
+        + [jnp.concatenate([out_own, out_own], axis=0)],
         axis=-1,
     )
-    ffn_rows = exchange(jnp.transpose(ffn_own, (1, 0, 2)), NEAR).reshape(192, 3 * PADDED)
-    ffn_full = lax.all_gather(ffn_rows, WIDE, axis=0, tiled=True).reshape(2, WIDTH, 3 * PADDED)
-
-    kv_one, kv_two = shift_super(kv, 1), shift_super(kv, 2)
+    rows_own = exchange(after(rows_own, kv), NEAR).reshape(192, 3 * PADDED + QUERY)
+    ffn_full = lax.all_gather(rows_own[:, : 3 * PADDED], WIDE, axis=0, tiled=True)
+    ffn_full = ffn_full.reshape(2, WIDTH, 3 * PADDED)
+
     kv_own = [kv, swap(kv, "yhi")]
-    kv_earlier = [kv_two, swap(kv_two, "yhi"), kv_one, swap(kv_one, "yhi")]
+    kv_earlier = [shift_super(kv, 2, 0), shift_super(kv, 2, 1), shift_super(kv, 1, 0), shift_super(kv, 1, 1)]
     state = attend_own(plan, rot_q, start_lanes, kv_own)
+    out_rows = jnp.broadcast_to(rows_own[None, :, 3 * PADDED :], (16, 192, QUERY))
+    out_both = exchange(out_rows, WIDE).reshape(2, WIDTH, QUERY)
+    w_out_t = jnp.where(x < 2, out_both[0], out_both[1])
     cot_blocks = near_gather(after(cotangent, kv))
-    state, cot_blocks = lax.optimization_barrier((state, cot_blocks))
-    mix_tiles, out_tiles, lse = attend_earlier(plan, rot_q, start_lanes, kv_earlier, state)
-
-    mixture_t = exchange(mix_tiles, NEAR).reshape(2, 768, ROWS)
+    mix, out_tiles, lse = attend_earlier(plan, rot_q, start_lanes, kv_earlier, state)
+    mix, cot_blocks, w_out_t = lax.optimization_barrier((mix, cot_blocks, w_out_t))
+
     inputs = tokens.astype(F32)
-    hidden = inputs
-    for y in range(2):
-        hidden = hidden + lax.dot_general(
-            mixture_t[y], out_full[y], (((0,), (1,)), ((), ())), preferred_element_type=F32
-        )
+    parts = [None] * 4
+    for d in (2, 1, 3, 0):
+        parts[d] = out_project(d, mix, w_out_t)
+    hidden = inputs + near_sum(near_keep(parts))
     scale_ffn = rms_scale(hidden)
     scaled_ffn = hidden * scale_ffn
     normed_ffn = (scaled_ffn * gain_ffn).astype(BF16)
 
-    ffn_blocks = near_gather(normed_ffn)
+    ffn_blocks = [[b] for b in [normed_ffn] + [shift_x(normed_ffn, d) for d in (1, 2, 3)]]
+    ffn_blocks[0].append(swap(normed_ffn, "core"))
     ffn_outs = [None] * 4
+    before = {1: 0, 3: 0, 2: 1}
     for d in (0, 1, 3, 2):
-        ffn_outs[d] = ffn(*ffn_blocks[d], *cot_blocks[d], ffn_full)
+        if d > 0:
+            block = after(ffn_blocks[d][0], ffn_outs[before[d]][0])
+            ffn_blocks[d] = [block, swap(block, "core")]
+        blocks = ffn_blocks[d]
+        if d == 3:
+            blocks = after(blocks, ffn_outs[1][0])
+        if d == 2:
+            blocks = after(blocks, ffn_outs[3][0])
+        ffn_outs[d] = ffn(*blocks, *cot_blocks[d], ffn_full)
     acts, gus = [o[2] for o in ffn_outs], [o[3] for o in ffn_outs]
     kept, gus = lax.optimization_barrier((near_keep([o[:2] for o in ffn_outs]), gus))
     pair_total = near_sum(kept)
@@ -686,36 +735,32 @@
         [b for p in ffn_blocks for b in p], [b for p in cot_blocks for b in p], gus, acts
     )
     pair_total, weight_grads = lax.optimization_barrier((pair_total, weight_grads))
-    ffn_got = exchange(weight_grads.reshape(16, 192, 3 * PADDED), WIDE)
+    ffn_sum = lax.psum_scatter(
+        weight_grads.reshape(2 * WIDTH, 3 * PART), WIDE, scatter_dimension=0, tiled=True
+    )
 
     ffn_gain_part = jnp.sum(pair_total * scaled_ffn, axis=0)
     grad_hidden = cotangent.astype(F32) + rms_back(pair_total * gain_ffn, hidden, scale_ffn)
     grad_branch = grad_hidden.astype(BF16)
-    grad_mixture = jnp.concatenate(
-        [
-            lax.dot_general(
-                out_full[y], grad_branch, (((0,), (1,)), ((), ())), preferred_element_type=F32
-            )
-            for y in range(2)
-        ],
-        axis=0,
-    ).astype(BF16)
-    grad_tiles = exchange(grad_mixture.reshape(8, QUERY, ROWS), NEAR)
-
-    dqt, mine, theirs = back_earlier(
-        plan, rot_q, start_lanes, kv_earlier, grad_tiles, out_tiles, lse
-    )
-    earlier = (mine + swap(theirs, "yhi").astype(F32)).astype(BF16)
-    back_one, back_two = shift_super(earlier[1], -1), shift_super(earlier[0], -2)
+    branches = [b for p in near_gather(grad_branch) for b in p]
+    grad_mix = out_back(branches, w_out_t)
+
+    dqt, mine, theirs = back_earlier(plan, rot_q, start_lanes, kv_earlier, grad_mix, out_tiles, lse)
+    mine = mine.astype(BF16)
+    sent = [
+        shift_super(mine[1], -1, 0),
+        shift_super(theirs[1], -1, 1),
+        shift_super(mine[0], -2, 0),
+        shift_super(theirs[0], -2, 1),
+    ]
     grad_q, mine, theirs = back_own(
-        plan, rot_q, start_lanes, kv_own, grad_tiles, out_tiles, lse, dqt
-    )
-    grad_kvs = (mine[0], swap(theirs[0], "yhi"), back_one, back_two)
-
-    acts, grad_tiles = lax.optimization_barrier((acts, grad_tiles))
+        plan, rot_q, start_lanes, kv_own, grad_mix, out_tiles, lse, dqt
+    )
+    grad_kvs = [mine[0], swap(theirs[0], "yhi")] + sent
+
+    acts, branches, dqt = lax.optimization_barrier((acts, branches, dqt))
     output = (hidden + near_sum(near_keep([down(a, ffn_full) for a in acts]))).astype(BF16)
-    branches = near_gather(after(grad_branch, grad_tiles))
-    grad_out = exchange(out_weights(plan, mix_tiles, [b for p in branches for b in p]), WIDE)
+    grad_out = exchange(out_weights(mix, branches), WIDE)
     grad_out = jnp.sum(grad_out.astype(F32), axis=0).astype(BF16)
     grad_out = jnp.transpose(grad_out.reshape(96, 8, 24), (1, 2, 0))
     grad_out = exchange(grad_out, NEAR).reshape(2, 4, 24, 96)
@@ -731,7 +776,9 @@
         unprojected[d] = unproject(
             d, grad_q, grad_kvs, raw, *token_blocks[d], qkv, cos, sin, head_gain
         )
-    grad_normed = near_sum(near_keep([u[:2] for u in unprojected]))
+    kept = near_keep([u[:2] for u in unprojected])
+    kept, normed = lax.optimization_barrier((kept, normed))
+    grad_normed = near_sum(kept)
     qkv_grad = dot(normed, jnp.concatenate([u[2] for u in unprojected], axis=0), TN)
 
     attn_gain_part = sum(u[3] for u in unprojected).reshape(128, 12, 1)
@@ -770,11 +817,10 @@
     scale_attn = rms_scale(inputs)
     input_grad = (grad_hidden + rms_back(grad_normed * gain_attn, inputs, scale_attn)).astype(BF16)
 
-    ffn_sum = jnp.sum(ffn_got.astype(F32), axis=0).astype(BF16)
-    ffn_grad = exchange(ffn_sum.reshape(8, 24, 3 * PADDED), NEAR)
+    ffn_grad = exchange(ffn_sum.astype(BF16).reshape(8, 24, 3 * PART), NEAR)
     ffn_grad = jnp.transpose(ffn_grad, (1, 0, 2)).astype(F32)
     w_gate_grad, w_up_grad, w_down_grad = (
-        ffn_grad[:, :, i * PADDED : i * PADDED + PART].reshape(24, -1) for i in range(3)
+        ffn_grad[:, :, i * PART : (i + 1) * PART].reshape(24, -1) for i in range(3)
     )
     return (
         output,

time: 683 us -> 537 us (0.79)
  waiting for transfers between devices: 219 us -> 110 us
  blocking collectives: 92.2 us -> 14.7 us
  starting transfers between devices: 90 us -> 121 us
  matrix products: 13.6 us -> 1.42 us
  other arithmetic: 29.7 us -> 40 us
  Pallas kernels: 144 us -> 154 us
    ppermute x38 -> x35, waiting for transfers between devices: 139 us -> 3.81 us  [swap(): return lax.ppermute(v, axis, [(0, 1), (1, 0)])]
    all_to_all x4 -> x1, blocking collectives: 92.2 us -> 14.7 us  [exchange(): return lax.all_to_all(v, axes, split_axis=0, concat_axis=0, tiled=True)]
    ppermute x24, waiting for transfers between devices: 48 us -> 68 us  [shift_x(): return lax.ppermute(v, 'x', [((i + distance) % 4, i) for i in range(4)])]
    all_to_all x5 -> x7, starting transfers between devices: 30.9 us -> 46.7 us  [exchange(): return lax.all_to_all(v, axes, split_axis=0, concat_axis=0, tiled=True)]
    ppermute x4 -> x8, starting transfers between devices: 14.3 us -> 26.2 us  [shift_super(): return lax.ppermute(v, ('ylo', 'z', 'yhi'), pairs)]
    all_to_all x5 -> x7, waiting for transfers between devices: 17.4 us -> 28 us  [exchange(): return lax.all_to_all(v, axes, split_axis=0, concat_axis=0, tiled=True)]
    dot_general x4 -> x0, matrix products: 10.3 us -> none  [the longest x2 5.37 us: per_device(): lax.dot_general(mixture_t[y], out_full[y], (((0,), (1,)), ((), ())), pref...]
    convert_element_type x10 -> x14, other arithmetic: 5.4 us -> 14.1 us  [near_keep(): (own.astype(F32) + swap(other, 'core').astype(F32)).astype(BF16)]
  transfers between devices with their start and end apart: 73 -> 76, of which waited for: 25 -> 14; matrix products, arithmetic and copies ran while one was open for 7% -> 12% of each run, Pallas kernels for 21% -> 28%
where the time goes in v2:
time: 537 us; the launch traced here: 527 us
  Pallas kernels  154 us (29%)
  starting transfers between devices  121 us (23%)
  waiting for transfers between devices  110 us (20%)
  local copies, waits for them, and re-layouts  69.1 us (13%)
  other arithmetic  40 us (7%)
  between operations  16.3 us (3%)
  blocking collectives  14.7 us (3%)
    ppermute x24, waiting for transfers between devices, shift_x(): return lax.ppermute(v, 'x', [((i + distance) % 4, i) for i in range(4)])  68 us
    all_to_all x7, starting transfers between devices, exchange(): return lax.all_to_all(v, axes, split_axis=0, concat_axis=0, tiled=True)  46.7 us
    unnamed x241, local copies, waits for them, and re-layouts  37.3 us
    ppermute x24, starting transfers between devices, shift_x(): return lax.ppermute(v, 'x', [((i + distance) % 4, i) for i in range(4)])  32.8 us
    all_to_all x7, waiting for transfers between devices, exchange(): return lax.all_to_all(v, axes, split_axis=0, concat_axis=0, tiled=True)  28 us
    pallas_call x4, Pallas kernels, ffn(): pl.pallas_call(ffn_kernel, out_shape=(jax.ShapeDtypeStruct((ROWS, WIDTH),...  26.7 us
    pallas_call x1, Pallas kernels, back_earlier(): return call(plan, q, start, *kvs, grad, out, lse)  26.5 us
    ppermute x8, starting transfers between devices, shift_super(): return lax.ppermute(v, ('ylo', 'z', 'yhi'), pairs)  26.2 us
  transfers between devices with their start and end apart: 76, of which 14 were waited for; matrix products, arithmetic and copies ran while one was open for 12% of the time, Pallas kernels for 28%

profile of v2, /device:TPU:8, one launch (start us, length us, event | category | flops | bytes accessed | tf_op | source)
XLA Modules:
  0.0 527.2 jit_solution(1280734014189564980)
XLA Ops:
  7.3 2.8 collective-permute-start.1
  16.6 3.6 all-to-all-start
  24.0 8.6 %all-to-all-done = bf16[8,12,384]{2,1,0:T(8,128)(2,1)S(1)} async-done(((bf16[8,12,384]{2,1,0:T(8,128)(2,1)}), bf16[8,12,384]{2,1,0:T(8,128)(2,1)S(1)}, u32[]{:S(2)}, u32[]{:S(2)}) %all-to-all-start) | async-done | bytes 73760 | tf_op jit(solution)/shard_map/all_to_all | solution.py:70
  33.7 8.4 %all-to-all-start.1 = ((bf16[16,96,384]{2,1,0:T(8,128)(2,1)}), bf16[16,96,384]{2,1,0:T(8,128)(2,1)S(1)}, u32[]{:S(2)}, u32[]{:S(2)}) async-start(bf16[16,96,384]{2,1,0:T(8,128)(2,1)} %broadcast_in_dim.27), calls=%async_computation.1 | async-start | bytes 2359296 | tf_op jit(solution)/shard_map/all_to_all | solution.py:70
  46.9 2.0 maximum_maximum_fusion.1
  48.9 9.6 %all-to-all-done.1 = bf16[16,96,384]{2,1,0:T(8,128)(2,1)S(1)} async-done(((bf16[16,96,384]{2,1,0:T(8,128)(2,1)}), bf16[16,96,384]{2,1,0:T(8,128)(2,1)S(1)}, u32[]{:S(2)}, u32[]{:S(2)}) %all-to-all-start.1) | async-done | bytes 1179680 | tf_op jit(solution)/shard_map/all_to_all | solution.py:70
  60.3 2.3 reshape.563.refs_8_.w_ref
  63.3 5.0 shard_map.237
  72.0 14.7 %all_to_all.40 = bf16[8,24,1728]{2,1,0:T(8,128)(2,1)S(1)} all-to-all(bf16[8,24,1728]{2,1,0:T(8,128)(2,1)S(1)} %copy.150), channel_id=1, replica_groups=mesh['ylo'=2,'z'=4,'x'=4,'core'=2,'yhi'=2] {'x','core'}, dimensions={0} | all-to-all | bytes 1327104 | tf_op jit(solution)/shard_map/all_to_all | solution.py:70
  87.7 2.3 collective-permute-start.11
  90.1 3.0 collective-permute-start.7
  93.1 2.9 collective-permute-start.8
  101.1 8.5 %all-to-all-start.3 = ((bf16[16,192,192]{2,1,0:T(8,128)(2,1)}), bf16[16,192,192]{2,1,0:T(8,128)(2,1)}, u32[]{:S(2)}, u32[]{:S(2)}) async-start(bf16[16,192,192]{2,1,0:T(8,128)(2,1)} %broadcast_in_dim.28), calls=%async_computation.3 | async-start | bytes 3145728 | tf_op jit(solution)/shard_map/all_to_all | solution.py:70
  109.7 3.4 collective-permute-start.9
  113.1 4.9 collective-permute-start.10
  118.1 12.4 %shard_map.238 = (f32[8,64,384]{2,1,0:T(8,128)S(1)}, f32[8,1,384]{2,1,0:T(1,128)S(1)}) custom-call(s32[8,11]{1,0:T(8,128)S(1)} %stack.8.plan, bf16[8,128,192]{2,1,0:T(8,128)(2,1)S(1)} %copy-done.56, s32[8,1,384]{2,1,0:T(1,128)S(1)} %copy.149.start_ref, bf16[8,128,128]{2,1,0:T(8,128)(2,1)} %get-tuple-element.127.refs_0_, ...), custom_call_target="tpu_custom_call" | custom-call | flops 4000000000 | bytes 8000000 | tf_op jit(solution)/shard_map/pallas_call | solution.py:573
  130.5 10.5 %collective-permute-done.9.refs_2_ = bf16[8,128,128]{2,1,0:T(8,128)(2,1)S(1)} collective-permute-done((bf16[8,128,128]{2,1,0:T(8,128)(2,1)}, bf16[8,128,128]{2,1,0:T(8,128)(2,1)S(1)}, u32[]{:S(2)}, u32[]{:S(2)}) %collective-permute-start.9) | collective-permute-done | bytes 262176 | tf_op jit(solution)/shard_map/ppermute | solution.py:66
  143.0 17.7 %shard_map.239 = (bf16[8,128,192]{2,1,0:T(8,128)(2,1)S(1)}, f32[8,64,384]{2,1,0:T(8,128)S(1)}, f32[8,1,384]{2,1,0:T(1,128)S(1)}) custom-call(s32[8,11]{1,0:T(8,128)S(1)} %stack.8.plan, bf16[8,128,192]{2,1,0:T(8,128)(2,1)S(1)} %copy-done.56, s32[8,1,384]{2,1,0:T(1,128)S(1)} %copy.149.start_ref, bf16[8,128,128]{2,1,0:T(8,128)(2,1)S(1)} %collective-permute-done.7.refs_0_, ...), custom_call_target="tpu_custom_call" | custom-call | flops 8000000000 | bytes 8000000 | tf_op jit(solution)/shard_map/pallas_call | solution.py:580
  168.1 3.8 collective-permute-start.25
  174.8 14.2 %collective-permute-done.25 = bf16[128,1536]{1,0:T(8,128)(2,1)S(1)} collective-permute-done((bf16[128,1536]{1,0:T(8,128)(2,1)S(1)}, bf16[128,1536]{1,0:T(8,128)(2,1)S(1)}, u32[]{:S(2)}, u32[]{:S(2)}) %collective-permute-start.25) | collective-permute-done | bytes 393248 | tf_op jit(solution)/shard_map/ppermute | solution.py:52
  189.0 3.9 collective-permute-done.21
  197.3 3.7 copy-done
  202.0 7.0 %shard_map.244 = (bf16[128,1536]{1,0:T(8,128)(2,1)S(1)}, bf16[128,1536]{1,0:T(8,128)(2,1)}, bf16[2,256,512]{2,1,0:T(8,128)(2,1)S(1)}, bf16[2,256,1024]{2,1,0:T(8,128)(2,1)S(1)}) custom-call(bf16[128,1536]{1,0:T(8,128)(2,1)} %multiply_convert_fusion.x0_ref.refs_0_, bf16[128,1536]{1,0:T(8,128)(2,1)S(1)} %copy-done.65, bf16[128,1536]{1,0:T(8,128)(2,1)S(1)} %copy-done.18, ...), custom_call_target="tpu_custom_call" | custom-call | flops 4026531840 | bytes 14000000 | tf_op jit(solution)/shard_map/pallas_call | solution.py:257
  215.2 7.0 %shard_map.245 = (bf16[128,1536]{1,0:T(8,128)(2,1)S(1)}, bf16[128,1536]{1,0:T(8,128)(2,1)}, bf16[2,256,512]{2,1,0:T(8,128)(2,1)S(1)}, bf16[2,256,1024]{2,1,0:T(8,128)(2,1)S(1)}) custom-call(bf16[128,1536]{1,0:T(8,128)(2,1)} %collective-permute-done.27.x0_ref.refs_2_, bf16[128,1536]{1,0:T(8,128)(2,1)S(1)} %copy-done.68, ...), custom_call_target="tpu_custom_call" | custom-call | flops 4026531840 | bytes 14000000 | tf_op jit(solution)/shard_map/pallas_call | solution.py:257
  225.7 6.3 %shard_map.246 = (bf16[128,1536]{1,0:T(8,128)(2,1)S(1)}, bf16[128,1536]{1,0:T(8,128)(2,1)S(1)}, bf16[2,256,512]{2,1,0:T(8,128)(2,1)S(1)}, bf16[2,256,1024]{2,1,0:T(8,128)(2,1)S(1)}) custom-call(bf16[128,1536]{1,0:T(8,128)(2,1)} %collective-permute-done.31.x0_ref.refs_6_, bf16[128,1536]{1,0:T(8,128)(2,1)} %collective-permute-done.32.x1_ref.refs_7_, ...), custom_call_target="tpu_custom_call" | custom-call | flops 4026531840 | bytes 14000000 | tf_op jit(solution)/shard_map/pallas_call | solution.py:257
  233.5 6.4 %shard_map.247 = (bf16[128,1536]{1,0:T(8,128)(2,1)S(1)}, bf16[128,1536]{1,0:T(8,128)(2,1)S(1)}, bf16[2,256,512]{2,1,0:T(8,128)(2,1)S(1)}, bf16[2,256,1024]{2,1,0:T(8,128)(2,1)S(1)}) custom-call(bf16[128,1536]{1,0:T(8,128)(2,1)} %collective-permute-done.29.x0_ref.refs_4_, bf16[128,1536]{1,0:T(8,128)(2,1)S(1)} %collective-permute-done.30.x1_ref.refs_5_, ...), custom_call_target="tpu_custom_call" | custom-call | flops 4026531840 | bytes 14000000 | tf_op jit(solution)/shard_map/pallas_call | solution.py:257
  248.0 19.3 %shard_map.248 = f32[2,1536,1296]{2,1,0:T(8,128)} custom-call(bf16[128,1536]{1,0:T(8,128)(2,1)} %multiply_convert_fusion.x0_ref.refs_0_, bf16[128,1536]{1,0:T(8,128)(2,1)S(1)} %copy-done.66, bf16[128,1536]{1,0:T(8,128)(2,1)} %collective-permute-done.27.x0_ref.refs_2_, bf16[128,1536]{1,0:T(8,128)(2,1)S(1)} %copy-done.69, ...), custom_call_target="tpu_custom_call" | custom-call | flops 9663676416 | bytes 24000000 | tf_op jit(solution)/shard_map/pallas_call | solution.py:325
  270.5 2.9 collective-permute-start.41
  274.6 15.3 %collective-permute-done.41.refs_2_ = bf16[128,1536]{1,0:T(8,128)(2,1)S(1)} collective-permute-done((bf16[128,1536]{1,0:T(8,128)(2,1)S(1)}, bf16[128,1536]{1,0:T(8,128)(2,1)S(1)}, u32[]{:S(2)}, u32[]{:S(2)}) %collective-permute-start.41) | collective-permute-done | bytes 393248 | tf_op jit(solution)/shard_map/ppermute | solution.py:52
  290.4 3.3 collective-permute-done.45.refs_6_
  295.9 2.7 shard_map.249.refs_4_.refs_2_
  298.7 26.5 %shard_map.250 = (f32[8,64,384]{2,1,0:T(8,128)S(1)}, f32[2,8,128,128]{3,2,1,0:T(8,128)S(1)}, bf16[2,8,128,128]{3,2,1,0:T(8,128)(2,1)S(1)}) custom-call(s32[8,11]{1,0:T(8,128)S(1)} %stack.8.plan, bf16[8,128,192]{2,1,0:T(8,128)(2,1)S(1)} %copy-done.57, s32[8,1,384]{2,1,0:T(1,128)S(1)} %copy.149.start_ref, bf16[8,128,128]{2,1,0:T(8,128)(2,1)S(1)} %copy-done.75, ...), custom_call_target="tpu_custom_call" | custom-call | flops 20000000000 | bytes 8000000 | tf_op jit(solution)/shard_map/pallas_call | solution.py:594
  325.3 20.8 %shard_map.255 = (bf16[8,128,256]{2,1,0:T(8,128)(2,1)S(1)}, f32[1,8,128,128]{3,2,1,0:T(8,128)S(1)}, bf16[1,8,128,128]{3,2,1,0:T(8,128)(2,1)}) custom-call(s32[8,11]{1,0:T(8,128)S(1)} %stack.8.plan, bf16[8,128,192]{2,1,0:T(8,128)(2,1)S(1)} %copy-done.57, s32[8,1,384]{2,1,0:T(1,128)S(1)} %copy.149.start_ref, bf16[8,128,128]{2,1,0:T(8,128)(2,1)} %get-tuple-element.127.refs_0_, ...), custom_call_target="tpu_custom_call" | custom-call | flops 10000000000 | bytes 8000000 | tf_op jit(solution)/shard_map/pallas_call | solution.py:604
  346.1 2.4 collective-permute-start.54
  349.5 1.9 collective-permute-start.55
  352.3 1.9 collective-permute-start.56
  354.2 6.1 %collective-permute-start.57 = (bf16[8,128,128]{2,1,0:T(8,128)(2,1)}, bf16[8,128,128]{2,1,0:T(8,128)(2,1)}, u32[]{:S(2)}, u32[]{:S(2)}) collective-permute-start(bf16[8,128,128]{2,1,0:T(8,128)(2,1)} %get-tuple-element.261), channel_id=1, source_target_pairs={{32,0},{33,1},{48,16},{49,17},{64,32},{65,33},{80,48},{81,49},{96,... | collective-permute-start | bytes 786440 | tf_op jit(solution)/shard_map/ppermute | solution.py:66
  360.3 2.1 collective-permute-start.58
  362.4 2.4 shard_map.254
  365.5 2.3 shard_map.260
  368.8 9.6 %all-to-all-start.5 = ((bf16[16,96,192]{2,1,0:T(8,128)(2,1)}), bf16[16,96,192]{2,1,0:T(8,128)(2,1)}, u32[]{:S(2)}, u32[]{:S(2)}) async-start(bf16[16,96,192]{2,1,0:T(8,128)(2,1)} %copy-done.13), calls=%async_computation.5 | async-start | bytes 1572864 | tf_op jit(solution)/shard_map/all_to_all | solution.py:70
  378.4 3.7 copy-done.1
  383.1 2.4 shard_map.253
  385.6 2.4 shard_map.252
  388.8 2.4 shard_map.251
  392.4 2.8 shard_map.256
  396.8 2.2 shard_map.257
  401.2 2.2 shard_map.258
  405.6 2.0 shard_map.259
  413.3 1.9 add_convert_fusion.5
  417.3 3.5 all-to-all-start.6
  423.1 3.1 all-to-all-done.6
  426.3 2.2 collective-permute-start.66
  435.0 2.0 add_convert_fusion.2
  441.1 2.5 collective-permute-start.64
  446.5 3.2 maximum_maximum_fusion
  449.8 9.5 %all-to-all-start.4 = ((bf16[128,12,384]{2,1,0:T(8,128)(2,1)}), bf16[128,12,384]{2,1,0:T(8,128)(2,1)S(1)}, u32[]{:S(2)}, u32[]{:S(2)}) async-start(bf16[128,12,384]{2,1,0:T(8,128)(2,1)} %maximum_maximum_fusion), calls=%async_computation.4 | async-start | bytes 3145728 | tf_op jit(solution)/shard_map/all_to_all | solution.py:70
  459.3 3.0 collective-permute-start.51
  464.6 23.7 %collective-permute-done.51 = bf16[128,1536]{1,0:T(8,128)(2,1)S(1)} collective-permute-done((bf16[128,1536]{1,0:T(8,128)(2,1)}, bf16[128,1536]{1,0:T(8,128)(2,1)S(1)}, u32[]{:S(2)}, u32[]{:S(2)}) %collective-permute-start.51) | collective-permute-done | bytes 393248 | tf_op jit(solution)/shard_map/ppermute | solution.py:52
  488.3 7.7 %collective-permute-done.49 = bf16[128,1536]{1,0:T(8,128)(2,1)S(1)} collective-permute-done((bf16[128,1536]{1,0:T(8,128)(2,1)}, bf16[128,1536]{1,0:T(8,128)(2,1)S(1)}, u32[]{:S(2)}, u32[]{:S(2)}) %collective-permute-start.49) | collective-permute-done | bytes 393248 | tf_op jit(solution)/shard_map/ppermute | solution.py:52
  496.0 3.3 fusion.6
  499.8 2.1 convert_element_type.391
  501.9 3.5 all-to-all-start.7
  509.2 6.7 %all-to-all-done.7 = bf16[8,24,1296]{2,1,0:T(8,128)(2,1)S(1)} async-done(((bf16[8,24,1296]{2,1,0:T(8,128)(2,1)}), bf16[8,24,1296]{2,1,0:T(8,128)(2,1)S(1)}, u32[]{:S(2)}, u32[]{:S(2)}) %all-to-all-start.7) | async-done | bytes 497696 | tf_op jit(solution)/shard_map/all_to_all | solution.py:70
  (498 shorter events, 118.1 us)
Async XLA Ops:
  7.2 56.0 %collective-permute-start = (bf16[128,1536]{1,0:T(8,128)(2,1)}, bf16[128,1536]{1,0:T(8,128)(2,1)}, u32[]{:S(2)}, u32[]{:S(2)}) collective-permute-start(bf16[128,1536]{1,0:T(8,128)(2,1)} %x0_ref.1), channel_id=1, source_target_pairs={{0,2},{2,0},{1,3},{3,1},{4,6},{6,4},{5,7},{7,5},{8,10},{10,8},{9,1... | collective-permute-start | bytes 1179656 | tf_op jit(solution)/shard_map/ppermute | solution.py:56
  7.3 38.5 %collective-permute-start.1 = (bf16[128,1536]{1,0:T(8,128)(2,1)}, bf16[128,1536]{1,0:T(8,128)(2,1)}, u32[]{:S(2)}, u32[]{:S(2)}) collective-permute-start(bf16[128,1536]{1,0:T(8,128)(2,1)} %x0_ref.1), channel_id=1, source_target_pairs={{4,0},{8,4},{12,8},{0,12},{5,1},{9,5},{13,9},{1,13},{6,2},{10,6},{... | collective-permute-start | bytes 1179656 | tf_op jit(solution)/shard_map/ppermute | solution.py:52
  10.1 35.8 %collective-permute-start.3 = (bf16[128,1536]{1,0:T(8,128)(2,1)}, bf16[128,1536]{1,0:T(8,128)(2,1)}, u32[]{:S(2)}, u32[]{:S(2)}) collective-permute-start(bf16[128,1536]{1,0:T(8,128)(2,1)} %x0_ref.1), channel_id=1, source_target_pairs={{8,0},{12,4},{0,8},{4,12},{9,1},{13,5},{1,9},{5,13},{10,2},{14,6},... | collective-permute-start | bytes 1179656 | tf_op jit(solution)/shard_map/ppermute | solution.py:52
  10.9 35.5 %collective-permute-start.5 = (bf16[128,1536]{1,0:T(8,128)(2,1)}, bf16[128,1536]{1,0:T(8,128)(2,1)S(1)}, u32[]{:S(2)}, u32[]{:S(2)}) collective-permute-start(bf16[128,1536]{1,0:T(8,128)(2,1)} %x0_ref.1), channel_id=1, source_target_pairs={{12,0},{0,4},{4,8},{8,12},{13,1},{1,5},{5,9},{9,13},{14,2},{2,6},{... | collective-permute-start | bytes 1179656 | tf_op jit(solution)/shard_map/ppermute | solution.py:52
  16.6 15.9 %all-to-all-start = ((bf16[8,12,384]{2,1,0:T(8,128)(2,1)}), bf16[8,12,384]{2,1,0:T(8,128)(2,1)S(1)}, u32[]{:S(2)}, u32[]{:S(2)}) async-start(bf16[8,12,384]{2,1,0:T(8,128)(2,1)} %bitcast.3), calls=%async_computation | async-start | bytes 196608 | tf_op jit(solution)/shard_map/all_to_all | solution.py:70
  33.7 24.8 %all-to-all-start.1 = ((bf16[16,96,384]{2,1,0:T(8,128)(2,1)}), bf16[16,96,384]{2,1,0:T(8,128)(2,1)S(1)}, u32[]{:S(2)}, u32[]{:S(2)}) async-start(bf16[16,96,384]{2,1,0:T(8,128)(2,1)} %broadcast_in_dim.27), calls=%async_computation.1 | async-start | bytes 2359296 | tf_op jit(solution)/shard_map/all_to_all | solution.py:70
  42.1 155.2 %all-gather.2.cloned.1.call-start = ((), (), s32[]{:S(2)}) async-start(), calls=%async_computation.9 | async-start | bytes 10027008 | tf_op jit(solution)/shard_map/all_gather | solution.py:695
  45.8 17.4 %collective-permute-start.2 = (bf16[128,1536]{1,0:T(8,128)(2,1)}, bf16[128,1536]{1,0:T(8,128)(2,1)}, u32[]{:S(2)}, u32[]{:S(2)}) collective-permute-start(bf16[128,1536]{1,0:T(8,128)(2,1)} %collective-permute-done.1.refs_2_.x0_ref), channel_id=1, source_target_pairs={{0,2},{2,0},{1,3},{3,1},{4,6},{6,4},{5,7},{7,5},{8,10},{10,8},{9,1... | collective-permute-start | bytes 1179656 | tf_op jit(solution)/shard_map/ppermute | solution.py:56
  45.9 17.3 %collective-permute-start.4 = (bf16[128,1536]{1,0:T(8,128)(2,1)}, bf16[128,1536]{1,0:T(8,128)(2,1)}, u32[]{:S(2)}, u32[]{:S(2)}) collective-permute-start(bf16[128,1536]{1,0:T(8,128)(2,1)} %collective-permute-done.3.refs_4_.x0_ref), channel_id=1, source_target_pairs={{0,2},{2,0},{1,3},{3,1},{4,6},{6,4},{5,7},{7,5},{8,10},{10,8},{9,1... | collective-permute-start | bytes 1179656 | tf_op jit(solution)/shard_map/ppermute | solution.py:56
  46.4 16.8 %collective-permute-start.6 = (bf16[128,1536]{1,0:T(8,128)(2,1)S(1)}, bf16[128,1536]{1,0:T(8,128)(2,1)}, u32[]{:S(2)}, u32[]{:S(2)}) collective-permute-start(bf16[128,1536]{1,0:T(8,128)(2,1)S(1)} %collective-permute-done.5.refs_6_.x0_ref), channel_id=1, source_target_pairs={{0,2},{2,0},{1,3},{3,1},{4,6},{6,4},{5,7},{7,5},{8,10},{10,8},{9,1... | collective-permute-start | bytes 1179656 | tf_op jit(solution)/shard_map/ppermute | solution.py:56
  87.7 11.0 %collective-permute-start.11 = (bf16[8,128,128]{2,1,0:T(8,128)(2,1)}, bf16[8,128,128]{2,1,0:T(8,128)(2,1)S(1)}, u32[]{:S(2)}, u32[]{:S(2)}) collective-permute-start(bf16[8,128,128]{2,1,0:T(8,128)(2,1)} %get-tuple-element.127.refs_0_), channel_id=1, source_target_pairs={{0,1},{1,0},{2,3},{3,2},{4,5},{5,4},{6,7},{7,6},{8,9},{9,8},{10,11... | collective-permute-start | bytes 786440 | tf_op jit(solution)/shard_map/ppermute | solution.py:56
  90.1 19.6 %collective-permute-start.7 = (bf16[8,128,128]{2,1,0:T(8,128)(2,1)}, bf16[8,128,128]{2,1,0:T(8,128)(2,1)S(1)}, u32[]{:S(2)}, u32[]{:S(2)}) collective-permute-start(bf16[8,128,128]{2,1,0:T(8,128)(2,1)} %get-tuple-element.127.refs_0_), channel_id=1, source_target_pairs={{0,32},{1,33},{16,48},{17,49},{32,64},{33,65},{48,80},{49,81},{64,... | collective-permute-start | bytes 786440 | tf_op jit(solution)/shard_map/ppermute | solution.py:66
  93.1 20.0 %collective-permute-start.8 = (bf16[8,128,128]{2,1,0:T(8,128)(2,1)}, bf16[8,128,128]{2,1,0:T(8,128)(2,1)S(1)}, u32[]{:S(2)}, u32[]{:S(2)}) collective-permute-start(bf16[8,128,128]{2,1,0:T(8,128)(2,1)} %get-tuple-element.127.refs_0_), channel_id=1, source_target_pairs={{0,33},{1,32},{16,49},{17,48},{32,65},{33,64},{48,81},{49,80},{64,... | collective-permute-start | bytes 786440 | tf_op jit(solution)/shard_map/ppermute | solution.py:66
  96.0 45.0 %collective-permute-start.13 = (bf16[128,1536]{1,0:T(8,128)(2,1)S(1)}, bf16[128,1536]{1,0:T(8,128)(2,1)}, u32[]{:S(2)}, u32[]{:S(2)}) collective-permute-start(bf16[128,1536]{1,0:T(8,128)(2,1)S(1)} %copy-done.18), channel_id=1, source_target_pairs={{4,0},{8,4},{12,8},{0,12},{5,1},{9,5},{13,9},{1,13},{6,2},{10,6},{... | collective-permute-start | bytes 1179656 | tf_op jit(solution)/shard_map/ppermute | solution.py:52
  97.3 44.3 %collective-permute-start.15 = (bf16[128,1536]{1,0:T(8,128)(2,1)S(1)}, bf16[128,1536]{1,0:T(8,128)(2,1)}, u32[]{:S(2)}, u32[]{:S(2)}) collective-permute-start(bf16[128,1536]{1,0:T(8,128)(2,1)S(1)} %copy-done.18), channel_id=1, source_target_pairs={{8,0},{12,4},{0,8},{4,12},{9,1},{13,5},{1,9},{5,13},{10,2},{14,6},... | collective-permute-start | bytes 1179656 | tf_op jit(solution)/shard_map/ppermute | solution.py:52
  98.8 42.9 %collective-permute-start.17 = (bf16[128,1536]{1,0:T(8,128)(2,1)S(1)}, bf16[128,1536]{1,0:T(8,128)(2,1)}, u32[]{:S(2)}, u32[]{:S(2)}) collective-permute-start(bf16[128,1536]{1,0:T(8,128)(2,1)S(1)} %copy-done.18), channel_id=1, source_target_pairs={{12,0},{0,4},{4,8},{8,12},{13,1},{1,5},{5,9},{9,13},{14,2},{2,6},{... | collective-permute-start | bytes 1179656 | tf_op jit(solution)/shard_map/ppermute | solution.py:52
  101.1 62.0 %all-to-all-start.3 = ((bf16[16,192,192]{2,1,0:T(8,128)(2,1)}), bf16[16,192,192]{2,1,0:T(8,128)(2,1)}, u32[]{:S(2)}, u32[]{:S(2)}) async-start(bf16[16,192,192]{2,1,0:T(8,128)(2,1)} %broadcast_in_dim.28), calls=%async_computation.3 | async-start | bytes 3145728 | tf_op jit(solution)/shard_map/all_to_all | solution.py:70
  109.6 390.2 %reduce-scatter.2.cloned.1.call-start = ((), (), s32[]{:S(2)}) async-start(), calls=%async_computation.10 | async-start | bytes 18382848 | tf_op jit(solution)/shard_map/reduce_scatter | solution.py:738
  109.7 31.3 %collective-permute-start.9 = (bf16[8,128,128]{2,1,0:T(8,128)(2,1)}, bf16[8,128,128]{2,1,0:T(8,128)(2,1)S(1)}, u32[]{:S(2)}, u32[]{:S(2)}) collective-permute-start(bf16[8,128,128]{2,1,0:T(8,128)(2,1)} %get-tuple-element.127.refs_0_), channel_id=1, source_target_pairs={{0,16},{1,17},{16,32},{17,33},{32,48},{33,49},{48,64},{49,65},{64,... | collective-permute-start | bytes 786440 | tf_op jit(solution)/shard_map/ppermute | solution.py:66
  113.1 29.0 %collective-permute-start.10 = (bf16[8,128,128]{2,1,0:T(8,128)(2,1)}, bf16[8,128,128]{2,1,0:T(8,128)(2,1)S(1)}, u32[]{:S(2)}, u32[]{:S(2)}) collective-permute-start(bf16[8,128,128]{2,1,0:T(8,128)(2,1)} %get-tuple-element.127.refs_0_), channel_id=1, source_target_pairs={{0,17},{1,16},{16,33},{17,32},{32,49},{33,48},{48,65},{49,64},{64,... | collective-permute-start | bytes 786440 | tf_op jit(solution)/shard_map/ppermute | solution.py:66
  141.0 23.8 %collective-permute-start.12 = (bf16[128,1536]{1,0:T(8,128)(2,1)S(1)}, bf16[128,1536]{1,0:T(8,128)(2,1)}, u32[]{:S(2)}, u32[]{:S(2)}) collective-permute-start(bf16[128,1536]{1,0:T(8,128)(2,1)S(1)} %copy-done.18), channel_id=1, source_target_pairs={{0,2},{2,0},{1,3},{3,1},{4,6},{6,4},{5,7},{7,5},{8,10},{10,8},{9,1... | collective-permute-start | bytes 1179656 | tf_op jit(solution)/shard_map/ppermute | solution.py:56
  141.0 23.8 %collective-permute-start.14 = (bf16[128,1536]{1,0:T(8,128)(2,1)}, bf16[128,1536]{1,0:T(8,128)(2,1)}, u32[]{:S(2)}, u32[]{:S(2)}) collective-permute-start(bf16[128,1536]{1,0:T(8,128)(2,1)} %collective-permute-done.13.c0_ref.refs_10_), channel_id=1, source_target_pairs={{0,2},{2,0},{1,3},{3,1},{4,6},{6,4},{5,7},{7,5},{8,10},{10,8},{9,1... | collective-permute-start | bytes 1179656 | tf_op jit(solution)/shard_map/ppermute | solution.py:56
  141.5 23.3 %collective-permute-start.16 = (bf16[128,1536]{1,0:T(8,128)(2,1)}, bf16[128,1536]{1,0:T(8,128)(2,1)}, u32[]{:S(2)}, u32[]{:S(2)}) collective-permute-start(bf16[128,1536]{1,0:T(8,128)(2,1)} %collective-permute-done.15.c0_ref.refs_12_), channel_id=1, source_target_pairs={{0,2},{2,0},{1,3},{3,1},{4,6},{6,4},{5,7},{7,5},{8,10},{10,8},{9,1... | collective-permute-start | bytes 1179656 | tf_op jit(solution)/shard_map/ppermute | solution.py:56
  141.6 23.2 %collective-permute-start.18 = (bf16[128,1536]{1,0:T(8,128)(2,1)}, bf16[128,1536]{1,0:T(8,128)(2,1)}, u32[]{:S(2)}, u32[]{:S(2)}) collective-permute-start(bf16[128,1536]{1,0:T(8,128)(2,1)} %collective-permute-done.17.c0_ref.refs_14_), channel_id=1, source_target_pairs={{0,2},{2,0},{1,3},{3,1},{4,6},{6,4},{5,7},{7,5},{8,10},{10,8},{9,1... | collective-permute-start | bytes 1179656 | tf_op jit(solution)/shard_map/ppermute | solution.py:56
  168.1 20.8 %collective-permute-start.25 = (bf16[128,1536]{1,0:T(8,128)(2,1)S(1)}, bf16[128,1536]{1,0:T(8,128)(2,1)S(1)}, u32[]{:S(2)}, u32[]{:S(2)}) collective-permute-start(bf16[128,1536]{1,0:T(8,128)(2,1)S(1)} %add_convert_fusion.13), channel_id=1, source_target_pairs={{4,0},{8,4},{12,8},{0,12},{5,1},{9,5},{13,9},{1,13},{6,2},{10,6},{... | collective-permute-start | bytes 1179656 | tf_op jit(solution)/shard_map/ppermute | solution.py:52
  172.0 16.9 %collective-permute-start.23 = (bf16[128,1536]{1,0:T(8,128)(2,1)S(1)}, bf16[128,1536]{1,0:T(8,128)(2,1)S(1)}, u32[]{:S(2)}, u32[]{:S(2)}) collective-permute-start(bf16[128,1536]{1,0:T(8,128)(2,1)S(1)} %add_convert_fusion.14), channel_id=1, source_target_pairs={{8,0},{12,4},{0,8},{4,12},{9,1},{13,5},{1,9},{5,13},{10,2},{14,6},... | collective-permute-start | bytes 1179656 | tf_op jit(solution)/shard_map/ppermute | solution.py:52
  173.3 19.5 %collective-permute-start.21 = (bf16[128,1536]{1,0:T(8,128)(2,1)S(1)}, bf16[128,1536]{1,0:T(8,128)(2,1)S(1)}, u32[]{:S(2)}, u32[]{:S(2)}) collective-permute-start(bf16[128,1536]{1,0:T(8,128)(2,1)S(1)} %add_convert_fusion.15), channel_id=1, source_target_pairs={{12,0},{0,4},{4,8},{8,12},{13,1},{1,5},{5,9},{9,13},{14,2},{2,6},{... | collective-permute-start | bytes 1179656 | tf_op jit(solution)/shard_map/ppermute | solution.py:52
  194.4 17.2 %collective-permute-start.27 = (bf16[128,1536]{1,0:T(8,128)(2,1)}, bf16[128,1536]{1,0:T(8,128)(2,1)}, u32[]{:S(2)}, u32[]{:S(2)}) collective-permute-start(bf16[128,1536]{1,0:T(8,128)(2,1)} %multiply_convert_fusion.x0_ref.refs_0_), channel_id=1, source_target_pairs={{4,0},{8,4},{12,8},{0,12},{5,1},{9,5},{13,9},{1,13},{6,2},{10,6},{... | collective-permute-start | bytes 1179656 | tf_op jit(solution)/shard_map/ppermute | solution.py:52
  194.9 18.1 %collective-permute-start.31 = (bf16[128,1536]{1,0:T(8,128)(2,1)}, bf16[128,1536]{1,0:T(8,128)(2,1)}, u32[]{:S(2)}, u32[]{:S(2)}) collective-permute-start(bf16[128,1536]{1,0:T(8,128)(2,1)} %multiply_convert_fusion.x0_ref.refs_0_), channel_id=1, source_target_pairs={{12,0},{0,4},{4,8},{8,12},{13,1},{1,5},{5,9},{9,13},{14,2},{2,6},{... | collective-permute-start | bytes 1179656 | tf_op jit(solution)/shard_map/ppermute | solution.py:52
  211.6 13.4 %collective-permute-start.29 = (bf16[128,1536]{1,0:T(8,128)(2,1)}, bf16[128,1536]{1,0:T(8,128)(2,1)}, u32[]{:S(2)}, u32[]{:S(2)}) collective-permute-start(bf16[128,1536]{1,0:T(8,128)(2,1)} %multiply_convert_fusion.x0_ref.refs_0_), channel_id=1, source_target_pairs={{8,0},{12,4},{0,8},{4,12},{9,1},{13,5},{1,9},{5,13},{10,2},{14,6},... | collective-permute-start | bytes 1179656 | tf_op jit(solution)/shard_map/ppermute | solution.py:52
  213.0 12.7 %collective-permute-start.32 = (bf16[128,1536]{1,0:T(8,128)(2,1)}, bf16[128,1536]{1,0:T(8,128)(2,1)}, u32[]{:S(2)}, u32[]{:S(2)}) collective-permute-start(bf16[128,1536]{1,0:T(8,128)(2,1)} %collective-permute-done.31.x0_ref.refs_6_), channel_id=1, source_target_pairs={{0,2},{2,0},{1,3},{3,1},{4,6},{6,4},{5,7},{7,5},{8,10},{10,8},{9,1... | collective-permute-start | bytes 1179656 | tf_op jit(solution)/shard_map/ppermute | solution.py:56
  213.2 19.1 %collective-permute-start.33 = (bf16[128,1536]{1,0:T(8,128)(2,1)}, bf16[128,1536]{1,0:T(8,128)(2,1)}, u32[]{:S(2)}, u32[]{:S(2)}) collective-permute-start(bf16[128,1536]{1,0:T(8,128)(2,1)} %get-tuple-element.165), channel_id=1, source_target_pairs={{0,2},{2,0},{1,3},{3,1},{4,6},{6,4},{5,7},{7,5},{8,10},{10,8},{9,1... | collective-permute-start | bytes 1179656 | tf_op jit(solution)/shard_map/ppermute | solution.py:56
  224.8 15.6 %collective-permute-start.34 = (bf16[128,1536]{1,0:T(8,128)(2,1)}, bf16[128,1536]{1,0:T(8,128)(2,1)S(1)}, u32[]{:S(2)}, u32[]{:S(2)}) collective-permute-start(bf16[128,1536]{1,0:T(8,128)(2,1)} %get-tuple-element.166), channel_id=1, source_target_pairs={{0,2},{2,0},{1,3},{3,1},{4,6},{6,4},{5,7},{7,5},{8,10},{10,8},{9,1... | collective-permute-start | bytes 1179656 | tf_op jit(solution)/shard_map/ppermute | solution.py:56
  225.0 8.5 %collective-permute-start.30 = (bf16[128,1536]{1,0:T(8,128)(2,1)}, bf16[128,1536]{1,0:T(8,128)(2,1)S(1)}, u32[]{:S(2)}, u32[]{:S(2)}) collective-permute-start(bf16[128,1536]{1,0:T(8,128)(2,1)} %collective-permute-done.29.x0_ref.refs_4_), channel_id=1, source_target_pairs={{0,2},{2,0},{1,3},{3,1},{4,6},{6,4},{5,7},{7,5},{8,10},{10,8},{9,1... | collective-permute-start | bytes 1179656 | tf_op jit(solution)/shard_map/ppermute | solution.py:56
  232.0 8.4 %collective-permute-start.36 = (bf16[128,1536]{1,0:T(8,128)(2,1)S(1)}, bf16[128,1536]{1,0:T(8,128)(2,1)S(1)}, u32[]{:S(2)}, u32[]{:S(2)}) collective-permute-start(bf16[128,1536]{1,0:T(8,128)(2,1)S(1)} %get-tuple-element.169), channel_id=1, source_target_pairs={{0,2},{2,0},{1,3},{3,1},{4,6},{6,4},{5,7},{7,5},{8,10},{10,8},{9,1... | collective-permute-start | bytes 1179656 | tf_op jit(solution)/shard_map/ppermute | solution.py:56
  241.8 25.4 %collective-permute-start.39 = (bf16[128,1536]{1,0:T(8,128)(2,1)S(1)}, bf16[128,1536]{1,0:T(8,128)(2,1)S(1)}, u32[]{:S(2)}, u32[]{:S(2)}) collective-permute-start(bf16[128,1536]{1,0:T(8,128)(2,1)S(1)} %add_convert_fusion.9), channel_id=1, source_target_pairs={{4,0},{8,4},{12,8},{0,12},{5,1},{9,5},{13,9},{1,13},{6,2},{10,6},{... | collective-permute-start | bytes 1179656 | tf_op jit(solution)/shard_map/ppermute | solution.py:52
  243.5 23.7 %collective-permute-start.38 = (bf16[128,1536]{1,0:T(8,128)(2,1)S(1)}, bf16[128,1536]{1,0:T(8,128)(2,1)S(1)}, u32[]{:S(2)}, u32[]{:S(2)}) collective-permute-start(bf16[128,1536]{1,0:T(8,128)(2,1)S(1)} %add_convert_fusion.10), channel_id=1, source_target_pairs={{8,0},{12,4},{0,8},{4,12},{9,1},{13,5},{1,9},{5,13},{10,2},{14,6},... | collective-permute-start | bytes 1179656 | tf_op jit(solution)/shard_map/ppermute | solution.py:52
  245.1 22.1 %collective-permute-start.37 = (bf16[128,1536]{1,0:T(8,128)(2,1)S(1)}, bf16[128,1536]{1,0:T(8,128)(2,1)S(1)}, u32[]{:S(2)}, u32[]{:S(2)}) collective-permute-start(bf16[128,1536]{1,0:T(8,128)(2,1)S(1)} %add_convert_fusion.11), channel_id=1, source_target_pairs={{12,0},{0,4},{4,8},{8,12},{13,1},{1,5},{5,9},{9,13},{14,2},{2,6},{... | collective-permute-start | bytes 1179656 | tf_op jit(solution)/shard_map/ppermute | solution.py:52
  270.5 19.4 %collective-permute-start.41 = (bf16[128,1536]{1,0:T(8,128)(2,1)S(1)}, bf16[128,1536]{1,0:T(8,128)(2,1)S(1)}, u32[]{:S(2)}, u32[]{:S(2)}) collective-permute-start(bf16[128,1536]{1,0:T(8,128)(2,1)S(1)} %fusion.53.refs_0_), channel_id=1, source_target_pairs={{4,0},{8,4},{12,8},{0,12},{5,1},{9,5},{13,9},{1,13},{6,2},{10,6},{... | collective-permute-start | bytes 1179656 | tf_op jit(solution)/shard_map/ppermute | solution.py:52
  273.4 16.4 %collective-permute-start.43 = (bf16[128,1536]{1,0:T(8,128)(2,1)S(1)}, bf16[128,1536]{1,0:T(8,128)(2,1)S(1)}, u32[]{:S(2)}, u32[]{:S(2)}) collective-permute-start(bf16[128,1536]{1,0:T(8,128)(2,1)S(1)} %fusion.53.refs_0_), channel_id=1, source_target_pairs={{8,0},{12,4},{0,8},{4,12},{9,1},{13,5},{1,9},{5,13},{10,2},{14,6},... | collective-permute-start | bytes 1179656 | tf_op jit(solution)/shard_map/ppermute | solution.py:52
  274.2 19.5 %collective-permute-start.45 = (bf16[128,1536]{1,0:T(8,128)(2,1)S(1)}, bf16[128,1536]{1,0:T(8,128)(2,1)}, u32[]{:S(2)}, u32[]{:S(2)}) collective-permute-start(bf16[128,1536]{1,0:T(8,128)(2,1)S(1)} %fusion.53.refs_0_), channel_id=1, source_target_pairs={{12,0},{0,4},{4,8},{8,12},{13,1},{1,5},{5,9},{9,13},{14,2},{2,6},{... | collective-permute-start | bytes 1179656 | tf_op jit(solution)/shard_map/ppermute | solution.py:52
  274.6 20.1 %collective-permute-start.40 = (bf16[128,1536]{1,0:T(8,128)(2,1)S(1)}, bf16[128,1536]{1,0:T(8,128)(2,1)}, u32[]{:S(2)}, u32[]{:S(2)}) collective-permute-start(bf16[128,1536]{1,0:T(8,128)(2,1)S(1)} %fusion.53.refs_0_), channel_id=1, source_target_pairs={{0,2},{2,0},{1,3},{3,1},{4,6},{6,4},{5,7},{7,5},{8,10},{10,8},{9,1... | collective-permute-start | bytes 1179656 | tf_op jit(solution)/shard_map/ppermute | solution.py:56
  346.1 45.1 %collective-permute-start.54 = (bf16[8,128,128]{2,1,0:T(8,128)(2,1)}, bf16[8,128,128]{2,1,0:T(8,128)(2,1)S(1)}, u32[]{:S(2)}, u32[]{:S(2)}) collective-permute-start(bf16[8,128,128]{2,1,0:T(8,128)(2,1)} %bitcast.20), channel_id=1, source_target_pairs={{0,1},{1,0},{2,3},{3,2},{4,5},{5,4},{6,7},{7,6},{8,9},{9,8},{10,11... | collective-permute-start | bytes 786440 | tf_op jit(solution)/shard_map/ppermute | solution.py:56
  349.5 41.7 %collective-permute-start.55 = (bf16[8,128,128]{2,1,0:T(8,128)(2,1)}, bf16[8,128,128]{2,1,0:T(8,128)(2,1)S(1)}, u32[]{:S(2)}, u32[]{:S(2)}) collective-permute-start(bf16[8,128,128]{2,1,0:T(8,128)(2,1)} %get-tuple-element.262), channel_id=1, source_target_pairs={{16,0},{17,1},{32,16},{33,17},{48,32},{49,33},{64,48},{65,49},{80,... | collective-permute-start | bytes 786440 | tf_op jit(solution)/shard_map/ppermute | solution.py:66
  352.3 39.6 %collective-permute-start.56 = (bf16[8,128,128]{2,1,0:T(8,128)(2,1)}, bf16[8,128,128]{2,1,0:T(8,128)(2,1)S(1)}, u32[]{:S(2)}, u32[]{:S(2)}) collective-permute-start(bf16[8,128,128]{2,1,0:T(8,128)(2,1)} %get-tuple-element.260), channel_id=1, source_target_pairs={{16,1},{17,0},{32,17},{33,16},{48,33},{49,32},{64,49},{65,48},{80,... | collective-permute-start | bytes 786440 | tf_op jit(solution)/shard_map/ppermute | solution.py:66
  354.2 37.8 %collective-permute-start.57 = (bf16[8,128,128]{2,1,0:T(8,128)(2,1)}, bf16[8,128,128]{2,1,0:T(8,128)(2,1)}, u32[]{:S(2)}, u32[]{:S(2)}) collective-permute-start(bf16[8,128,128]{2,1,0:T(8,128)(2,1)} %get-tuple-element.261), channel_id=1, source_target_pairs={{32,0},{33,1},{48,16},{49,17},{64,32},{65,33},{80,48},{81,49},{96,... | collective-permute-start | bytes 786440 | tf_op jit(solution)/shard_map/ppermute | solution.py:66
  360.3 32.1 %collective-permute-start.58 = (bf16[8,128,128]{2,1,0:T(8,128)(2,1)}, bf16[8,128,128]{2,1,0:T(8,128)(2,1)}, u32[]{:S(2)}, u32[]{:S(2)}) collective-permute-start(bf16[8,128,128]{2,1,0:T(8,128)(2,1)} %get-tuple-element.259), channel_id=1, source_target_pairs={{32,1},{33,0},{48,17},{49,16},{64,33},{65,32},{80,49},{81,48},{96,... | collective-permute-start | bytes 786440 | tf_op jit(solution)/shard_map/ppermute | solution.py:66
  368.8 46.5 %all-to-all-start.5 = ((bf16[16,96,192]{2,1,0:T(8,128)(2,1)}), bf16[16,96,192]{2,1,0:T(8,128)(2,1)}, u32[]{:S(2)}, u32[]{:S(2)}) async-start(bf16[16,96,192]{2,1,0:T(8,128)(2,1)} %copy-done.13), calls=%async_computation.5 | async-start | bytes 1572864 | tf_op jit(solution)/shard_map/all_to_all | solution.py:70
  391.2 21.7 %collective-permute-start.52 = (bf16[128,1536]{1,0:T(8,128)(2,1)}, bf16[128,1536]{1,0:T(8,128)(2,1)}, u32[]{:S(2)}, u32[]{:S(2)}) collective-permute-start(bf16[128,1536]{1,0:T(8,128)(2,1)} %get-tuple-element.197), channel_id=1, source_target_pairs={{0,2},{2,0},{1,3},{3,1},{4,6},{6,4},{5,7},{7,5},{8,10},{10,8},{9,1... | collective-permute-start | bytes 1179656 | tf_op jit(solution)/shard_map/ppermute | solution.py:56
  391.2 29.6 %collective-permute-start.50 = (bf16[128,1536]{1,0:T(8,128)(2,1)}, bf16[128,1536]{1,0:T(8,128)(2,1)}, u32[]{:S(2)}, u32[]{:S(2)}) collective-permute-start(bf16[128,1536]{1,0:T(8,128)(2,1)} %get-tuple-element.194), channel_id=1, source_target_pairs={{0,2},{2,0},{1,3},{3,1},{4,6},{6,4},{5,7},{7,5},{8,10},{10,8},{9,1... | collective-permute-start | bytes 1179656 | tf_op jit(solution)/shard_map/ppermute | solution.py:56
  391.9 34.4 %collective-permute-start.48 = (bf16[128,1536]{1,0:T(8,128)(2,1)}, bf16[128,1536]{1,0:T(8,128)(2,1)}, u32[]{:S(2)}, u32[]{:S(2)}) collective-permute-start(bf16[128,1536]{1,0:T(8,128)(2,1)} %get-tuple-element.191), channel_id=1, source_target_pairs={{0,2},{2,0},{1,3},{3,1},{4,6},{6,4},{5,7},{7,5},{8,10},{10,8},{9,1... | collective-permute-start | bytes 1179656 | tf_op jit(solution)/shard_map/ppermute | solution.py:56
  392.0 72.6 %collective-permute-start.47 = (bf16[128,1536]{1,0:T(8,128)(2,1)}, bf16[128,1536]{1,0:T(8,128)(2,1)}, u32[]{:S(2)}, u32[]{:S(2)}) collective-permute-start(bf16[128,1536]{1,0:T(8,128)(2,1)} %get-tuple-element.188), channel_id=1, source_target_pairs={{0,2},{2,0},{1,3},{3,1},{4,6},{6,4},{5,7},{7,5},{8,10},{10,8},{9,1... | collective-permute-start | bytes 1179656 | tf_op jit(solution)/shard_map/ppermute | solution.py:56
  396.6 35.9 %collective-permute-start.59 = (bf16[128,1536]{1,0:T(8,128)(2,1)}, bf16[128,1536]{1,0:T(8,128)(2,1)}, u32[]{:S(2)}, u32[]{:S(2)}) collective-permute-start(bf16[128,1536]{1,0:T(8,128)(2,1)} %get-tuple-element.205), channel_id=1, source_target_pairs={{0,2},{2,0},{1,3},{3,1},{4,6},{6,4},{5,7},{7,5},{8,10},{10,8},{9,1... | collective-permute-start | bytes 1179656 | tf_op jit(solution)/shard_map/ppermute | solution.py:56
  412.9 22.0 %collective-permute-start.60 = (bf16[128,1536]{1,0:T(8,128)(2,1)S(1)}, bf16[128,1536]{1,0:T(8,128)(2,1)}, u32[]{:S(2)}, u32[]{:S(2)}) collective-permute-start(bf16[128,1536]{1,0:T(8,128)(2,1)S(1)} %copy-done.59), channel_id=1, source_target_pairs={{0,2},{2,0},{1,3},{3,1},{4,6},{6,4},{5,7},{7,5},{8,10},{10,8},{9,1... | collective-permute-start | bytes 1179656 | tf_op jit(solution)/shard_map/ppermute | solution.py:56
  417.3 8.9 %all-to-all-start.6 = ((bf16[8,24,96]{2,1,0:T(8,128)(2,1)}), bf16[8,24,96]{2,1,0:T(8,128)(2,1)S(1)}, u32[]{:S(2)}, u32[]{:S(2)}) async-start(bf16[8,24,96]{2,1,0:T(8,128)(2,1)} %bitcast.30), calls=%async_computation.6 | async-start | bytes 98304 | tf_op jit(solution)/shard_map/all_to_all | solution.py:70
  420.8 16.2 %collective-permute-start.61 = (bf16[128,1536]{1,0:T(8,128)(2,1)S(1)}, bf16[128,1536]{1,0:T(8,128)(2,1)}, u32[]{:S(2)}, u32[]{:S(2)}) collective-permute-start(bf16[128,1536]{1,0:T(8,128)(2,1)S(1)} %copy-done.61), channel_id=1, source_target_pairs={{0,2},{2,0},{1,3},{3,1},{4,6},{6,4},{5,7},{7,5},{8,10},{10,8},{9,1... | collective-permute-start | bytes 1179656 | tf_op jit(solution)/shard_map/ppermute | solution.py:56
  432.6 32.0 %collective-permute-start.53 = (bf16[128,1536]{1,0:T(8,128)(2,1)}, bf16[128,1536]{1,0:T(8,128)(2,1)}, u32[]{:S(2)}, u32[]{:S(2)}) collective-permute-start(bf16[128,1536]{1,0:T(8,128)(2,1)} %add_convert_fusion.5), channel_id=1, source_target_pairs={{4,0},{8,4},{12,8},{0,12},{5,1},{9,5},{13,9},{1,13},{6,2},{10,6},{... | collective-permute-start | bytes 1179656 | tf_op jit(solution)/shard_map/ppermute | solution.py:52
  440.7 18.6 %collective-permute-start.65 = (bf16[128,1536]{1,0:T(8,128)(2,1)}, bf16[128,1536]{1,0:T(8,128)(2,1)}, u32[]{:S(2)}, u32[]{:S(2)}) collective-permute-start(bf16[128,1536]{1,0:T(8,128)(2,1)} %add_convert_fusion), channel_id=1, source_target_pairs={{4,0},{8,4},{12,8},{0,12},{5,1},{9,5},{13,9},{1,13},{6,2},{10,6},{... | collective-permute-start | bytes 1179656 | tf_op jit(solution)/shard_map/ppermute | solution.py:52
  441.1 21.2 %collective-permute-start.64 = (bf16[128,1536]{1,0:T(8,128)(2,1)}, bf16[128,1536]{1,0:T(8,128)(2,1)}, u32[]{:S(2)}, u32[]{:S(2)}) collective-permute-start(bf16[128,1536]{1,0:T(8,128)(2,1)} %add_convert_fusion.1), channel_id=1, source_target_pairs={{8,0},{12,4},{0,8},{4,12},{9,1},{13,5},{1,9},{5,13},{10,2},{14,6},... | collective-permute-start | bytes 1179656 | tf_op jit(solution)/shard_map/ppermute | solution.py:52
  443.6 19.3 %collective-permute-start.63 = (bf16[128,1536]{1,0:T(8,128)(2,1)}, bf16[128,1536]{1,0:T(8,128)(2,1)}, u32[]{:S(2)}, u32[]{:S(2)}) collective-permute-start(bf16[128,1536]{1,0:T(8,128)(2,1)} %add_convert_fusion.2), channel_id=1, source_target_pairs={{12,0},{0,4},{4,8},{8,12},{13,1},{1,5},{5,9},{9,13},{14,2},{2,6},{... | collective-permute-start | bytes 1179656 | tf_op jit(solution)/shard_map/ppermute | solution.py:52
  449.8 49.6 %all-to-all-start.4 = ((bf16[128,12,384]{2,1,0:T(8,128)(2,1)}), bf16[128,12,384]{2,1,0:T(8,128)(2,1)S(1)}, u32[]{:S(2)}, u32[]{:S(2)}) async-start(bf16[128,12,384]{2,1,0:T(8,128)(2,1)} %maximum_maximum_fusion), calls=%async_computation.4 | async-start | bytes 3145728 | tf_op jit(solution)/shard_map/all_to_all | solution.py:70
  459.3 29.0 %collective-permute-start.51 = (bf16[128,1536]{1,0:T(8,128)(2,1)}, bf16[128,1536]{1,0:T(8,128)(2,1)S(1)}, u32[]{:S(2)}, u32[]{:S(2)}) collective-permute-start(bf16[128,1536]{1,0:T(8,128)(2,1)} %add_convert_fusion.6), channel_id=1, source_target_pairs={{8,0},{12,4},{0,8},{4,12},{9,1},{13,5},{1,9},{5,13},{10,2},{14,6},... | collective-permute-start | bytes 1179656 | tf_op jit(solution)/shard_map/ppermute | solution.py:52
  462.4 33.6 %collective-permute-start.49 = (bf16[128,1536]{1,0:T(8,128)(2,1)}, bf16[128,1536]{1,0:T(8,128)(2,1)S(1)}, u32[]{:S(2)}, u32[]{:S(2)}) collective-permute-start(bf16[128,1536]{1,0:T(8,128)(2,1)} %add_convert_fusion.7), channel_id=1, source_target_pairs={{12,0},{0,4},{4,8},{8,12},{13,1},{1,5},{5,9},{9,13},{14,2},{2,6},{... | collective-permute-start | bytes 1179656 | tf_op jit(solution)/shard_map/ppermute | solution.py:52
  501.9 14.0 %all-to-all-start.7 = ((bf16[8,24,1296]{2,1,0:T(8,128)(2,1)}), bf16[8,24,1296]{2,1,0:T(8,128)(2,1)S(1)}, u32[]{:S(2)}, u32[]{:S(2)}) async-start(bf16[8,24,1296]{2,1,0:T(8,128)(2,1)} %bitcast.35), calls=%async_computation.8 | async-start | bytes 1081344 | tf_op jit(solution)/shard_map/all_to_all | solution.py:70
  (132 other events, 1203.2 us)
Sparse Core Ops, SparseCore 0:
  87.7 106.6 all-gather.1
  268.5 139.6 reduce-scatter.1

commit v3 on v2

--- a/solution.py
+++ b/solution.py
@@ -164,54 +164,58 @@
             jax.ShapeDtypeStruct((8, ROWS, 2 * HEAD), BF16),
             jax.ShapeDtypeStruct((4, PAIR, 4 * HEAD), F32),
         ),
-        compiler_params=params(0, 32),
+        compiler_params=params(0, 24),
         cost_estimate=cost(8 * PAIR * WIDTH * 384, 1e7),
     )(*xs, w, gain, cos, sin, head_gain)
 
 
-def unproject_kernel(
-    gq_ref, g0_ref, g1_ref, g2_ref, g3_ref, g4_ref, g5_ref, raw_ref, x0_ref, x1_ref, w_ref, cos_ref,
-    sin_ref, head_gain_ref, part0_ref, part1_ref, graw_ref, attn_ref, heads_ref,
-):
-    gq = gq_ref[...].reshape(PAIR, 4 * HEAD).astype(F32)
-    gkv = g0_ref[...]
-    for ref in (g1_ref, g2_ref, g3_ref, g4_ref, g5_ref):
-        gkv = gkv + ref[...].astype(F32)
-    gkv = gkv.reshape(PAIR, 2 * HEAD)
-    lane = lax.broadcasted_iota(jnp.int32, (PAIR, 2 * HEAD), 1)
-    gk = (gkv * HEAD**-0.5).astype(BF16).astype(F32)
-    g = jnp.concatenate([gq[:, : 2 * HEAD], jnp.where(lane < HEAD, gq[:, 2 * HEAD :], gk)], axis=1)
-    g = g * twice(cos_ref[0]) - half_turn(g) * twice(sin_ref[0])
-    raw = raw_ref[0]
-    scale = lax.rsqrt(head_sums(raw * raw) * (1.0 / HEAD) + EPS)
-    heads_ref[...] = jnp.sum(g * raw * scale, axis=0, keepdims=True)
-    e = g * head_gain_ref[...]
-    inner = head_sums(e * raw) * (1.0 / HEAD)
-    graw = scale * (e - raw * scale * scale * inner)
-    graw = jnp.concatenate([graw, jnp.where(lane < HEAD, gkv, 0.0)], axis=1).astype(BF16)
-    graw_ref[...] = graw
-    grad = dot(graw, w_ref[...], NT)
-    x = stacked(x0_ref, x1_ref).astype(F32)
-    attn_ref[...] = jnp.sum(grad * x * rms_scale(x), axis=0, keepdims=True)
-    grad = grad.astype(BF16)
-    part0_ref[...] = grad[:ROWS]
-    part1_ref[...] = grad[ROWS:]
-
-
-def unproject(d, gq, gkvs, raw, x0, x1, w, cos, sin, head_gain):
+def unproject_kernel(*refs):
+    gq_ref, g_refs, raw_ref, xs, (w_ref, cos_ref, sin_ref, head_gain_ref) = (
+        refs[0], refs[1:7], refs[7], refs[8:12], refs[12:16],
+    )
+    parts, (graw_ref, attn_ref, heads_ref) = refs[16:20], refs[20:]
+    attn, sums = 0.0, 0.0
+    for i in range(2):
+        tiles = slice(2 * i, 2 * i + 2)
+        gq = gq_ref[tiles].reshape(PAIR, 4 * HEAD).astype(F32)
+        gkv = g_refs[0][tiles]
+        for ref in g_refs[1:]:
+            gkv = gkv + ref[tiles].astype(F32)
+        gkv = gkv.reshape(PAIR, 2 * HEAD)
+        lane = lax.broadcasted_iota(jnp.int32, (PAIR, 2 * HEAD), 1)
+        gk = (gkv * HEAD**-0.5).astype(BF16).astype(F32)
+        gk = jnp.where(lane < HEAD, gq[:, 2 * HEAD :], gk)
+        g = jnp.concatenate([gq[:, : 2 * HEAD], gk], axis=1)
+        g = g * twice(cos_ref[i]) - half_turn(g) * twice(sin_ref[i])
+        raw = raw_ref[i]
+        scale = lax.rsqrt(head_sums(raw * raw) * (1.0 / HEAD) + EPS)
+        sums = sums + jnp.sum(g * raw * scale, axis=0, keepdims=True)
+        e = g * head_gain_ref[...]
+        inner = head_sums(e * raw) * (1.0 / HEAD)
+        graw = scale * (e - raw * scale * scale * inner)
+        graw = jnp.concatenate([graw, jnp.where(lane < HEAD, gkv, 0.0)], axis=1).astype(BF16)
+        graw_ref[i * PAIR : (i + 1) * PAIR, :] = graw
+        grad = dot(graw, w_ref[...], NT)
+        x = stacked(*xs[tiles]).astype(F32)
+        attn = attn + jnp.sum(grad * x * rms_scale(x), axis=0, keepdims=True)
+        grad = grad.astype(BF16)
+        parts[2 * i][...] = grad[:ROWS]
+        parts[2 * i + 1][...] = grad[ROWS:]
+    attn_ref[...] = attn
+    heads_ref[...] = sums
+
+
+def unproject(half, gq, gkvs, raw, xs, w, cos, sin, head_gain):
     def whole_of(*shape):
         return pl.BlockSpec(shape, lambda i: (0,) * len(shape))
 
-    def at_d(*shape):
-        return pl.BlockSpec(shape, lambda i: (d,) + (0,) * (len(shape) - 1))
+    def at_half(*shape):
+        return pl.BlockSpec(shape, lambda i: (half,) + (0,) * (len(shape) - 1))
 
     rows = whole_of(ROWS, WIDTH)
-    kv = at_d(2, ROWS, 2 * HEAD)
-    table = at_d(1, PAIR, 2 * HEAD)
-    outs = (
-        jax.ShapeDtypeStruct((ROWS, WIDTH), BF16),
-        jax.ShapeDtypeStruct((ROWS, WIDTH), BF16),
-        jax.ShapeDtypeStruct((PAIR, 6 * HEAD), BF16),
+    table = at_half(2, PAIR, 2 * HEAD)
+    outs = (jax.ShapeDtypeStruct((ROWS, WIDTH), BF16),) * 4 + (
+        jax.ShapeDtypeStruct((2 * PAIR, 6 * HEAD), BF16),
         jax.ShapeDtypeStruct((1, WIDTH), F32),
         jax.ShapeDtypeStruct((1, 4 * HEAD), F32),
     )
@@ -219,27 +223,32 @@
         unproject_kernel,
         out_shape=outs,
         grid=(1,),
-        in_specs=[at_d(2, ROWS, 4 * HEAD)] + [kv] * 6 + [at_d(1, PAIR, 4 * HEAD), rows, rows]
+        in_specs=[at_half(4, ROWS, 4 * HEAD)]
+        + [at_half(4, ROWS, 2 * HEAD)] * 6
+        + [at_half(2, PAIR, 4 * HEAD)]
+        + [rows] * 4
         + [whole_of(WIDTH, 6 * HEAD), table, table, whole_of(1, 4 * HEAD)],
         out_specs=tuple(whole_of(*o.shape) for o in outs),
         compiler_params=params(1, 24),
-        cost_estimate=cost(2 * PAIR * WIDTH * 384, 4e6),
-    )(gq, *gkvs, raw, x0, x1, w, cos, sin, head_gain)
-
-
-def ffn_kernel(x0_ref, x1_ref, c0_ref, c1_ref, w_ref, part0_ref, part1_ref, act_ref, gu_ref, total):
+        cost_estimate=cost(4 * PAIR * WIDTH * 384, 8e6),
+    )(gq, *gkvs, raw, *xs, w, cos, sin, head_gain)
+
+
+def ffn_kernel(
+    x0_ref, x1_ref, c0_ref, c1_ref, gu_w_ref, d_w_ref, part0_ref, part1_ref, act_ref, gu_ref, total
+):
     y = pl.program_id(0)
     x = stacked(x0_ref, x1_ref)
-    gate_up = dot(x, w_ref[0, :, : 2 * PADDED])
+    gate_up = dot(x, gu_w_ref[0])
     gate, up = gate_up[:, :PADDED], gate_up[:, PADDED:]
-    grad_act = dot(stacked(c0_ref, c1_ref), w_ref[0, :, 2 * PADDED :])
+    grad_act = dot(stacked(c0_ref, c1_ref), d_w_ref[0])
     sig = 1.0 / (1.0 + jnp.exp(-gate))
     silu = gate * sig
     act_ref[0] = (silu * up).astype(BF16)
     grad_gate = grad_act * up * sig * (1.0 + gate * (1.0 - sig))
     grads = jnp.concatenate([grad_gate, grad_act * silu], axis=1).astype(BF16)
     gu_ref[0] = grads
-    part = dot(grads, w_ref[0, :, : 2 * PADDED], NT)
+    part = dot(grads, gu_w_ref[0], NT)
 
     @pl.when(y == 0)
     def _():
@@ -252,7 +261,7 @@
         part1_ref[...] = whole_part[ROWS:]
 
 
-def ffn(x0, x1, c0, c1, w):
+def ffn(x0, x1, c0, c1, gu_w, d_w):
     rows = pl.BlockSpec((ROWS, WIDTH), lambda y: (0, 0))
     return pl.pallas_call(
         ffn_kernel,
@@ -263,7 +272,8 @@
             jax.ShapeDtypeStruct((2, PAIR, 2 * PADDED), BF16),
         ),
         grid=(2,),
-        in_specs=[rows] * 4 + [pl.BlockSpec((1, WIDTH, 3 * PADDED), lambda y: (y, 0, 0))],
+        in_specs=[rows] * 4
+        + [pl.BlockSpec((1, WIDTH, n * PADDED), lambda y: (y, 0, 0)) for n in (2, 1)],
         out_specs=(
             rows,
             rows,
@@ -271,9 +281,9 @@
             pl.BlockSpec((1, PAIR, 2 * PADDED), lambda y: (y, 0, 0)),
         ),
         scratch_shapes=[pltpu.VMEM((PAIR, WIDTH), F32)],
-        compiler_params=params(1, 40),
+        compiler_params=params(1, 32),
         cost_estimate=cost(2 * 2 * PAIR * WIDTH * 5 * PADDED, 14e6),
-    )(x0, x1, c0, c1, w)
+    )(x0, x1, c0, c1, gu_w, d_w)
 
 
 def down_kernel(act_ref, w_ref, part0_ref, part1_ref, total):
@@ -299,7 +309,7 @@
         grid=(2,),
         in_specs=[
             pl.BlockSpec((1, PAIR, PADDED), lambda y: (y, 0, 0)),
-            pl.BlockSpec((1, WIDTH, PADDED), lambda y: (y, 0, 2)),
+            pl.BlockSpec((1, WIDTH, PADDED), lambda y: (y, 0, 0)),
         ],
         out_specs=(rows, rows),
         scratch_shapes=[pltpu.VMEM((PAIR, WIDTH), F32)],
@@ -310,13 +320,14 @@
 
 def ffn_weights_kernel(*refs):
     xs, cs, gus, acts, out_ref = refs[:8], refs[8:16], refs[16:20], refs[20:24], refs[24]
-    grad_gu, grad_d = 0.0, 0.0
-    for d in range(4):
-        grad_gu = grad_gu + dot(stacked(*xs[2 * d : 2 * d + 2]), gus[d][0], TN)
-        grad_d = grad_d + dot(stacked(*cs[2 * d : 2 * d + 2]), acts[d][0], TN)
-    out_ref[0, :, :PART] = grad_gu[:, :PART]
-    out_ref[0, :, PART : 2 * PART] = grad_gu[:, PADDED : PADDED + PART]
-    out_ref[0, :, 2 * PART :] = grad_d[:, :PART]
+    def all_tokens(refs):
+        return jnp.concatenate([ref[...] for ref in refs], axis=0)
+
+    grad_gu = dot(all_tokens(xs), all_tokens([g.at[0] for g in gus]), TN)
+    grad_d = dot(all_tokens(cs), all_tokens([a.at[0] for a in acts]), TN)
+    out_ref[0, :, :PART] = grad_gu[:, :PART].astype(BF16)
+    out_ref[0, :, PART : 2 * PART] = grad_gu[:, PADDED : PADDED + PART].astype(BF16)
+    out_ref[0, :, 2 * PART :] = grad_d[:, :PART].astype(BF16)
 
 
 def ffn_weights(xs, cs, gus, acts):
@@ -324,13 +335,13 @@
     rows = pl.BlockSpec((ROWS, tall), lambda y, m: (0, m))
     return pl.pallas_call(
         ffn_weights_kernel,
-        out_shape=jax.ShapeDtypeStruct((2, WIDTH, 3 * PART), F32),
+        out_shape=jax.ShapeDtypeStruct((2, WIDTH, 3 * PART), BF16),
         grid=(2, WIDTH // tall),
         in_specs=[rows] * 16
         + [pl.BlockSpec((1, PAIR, 2 * PADDED), lambda y, m: (y, 0, 0))] * 4
         + [pl.BlockSpec((1, PAIR, PADDED), lambda y, m: (y, 0, 0))] * 4,
         out_specs=pl.BlockSpec((1, tall, 3 * PART), lambda y, m: (y, m, 0)),
-        compiler_params=params(2, 40),
+        compiler_params=params(2, 28),
         cost_estimate=cost(2 * 2 * 1024 * WIDTH * 3 * PADDED, 24e6),
     )(*xs, *cs, *gus, *acts)
 
@@ -411,8 +422,13 @@
         key = lax.broadcasted_iota(jnp.int32, (KEY_TILE, LANES), 0) + (j * KEY_TILE + base)
         return visit(j, state, (key >= start) & (key <= place))
 
+    def two(i, state):
+        return visit(m1 + 2 * i + 1, visit(m1 + 2 * i, state, None), None)
+
+    pairs = lax.shift_right_logical(m2 - m1, 1)
     state = lax.fori_loop(lo, m1, masked, state)
-    state = lax.fori_loop(m1, m2, lambda j, s: visit(j, s, None), state)
+    state = lax.fori_loop(0, pairs, two, state)
+    state = lax.fori_loop(m1 + 2 * pairs, m2, lambda j, s: visit(j, s, None), state)
     return lax.fori_loop(m2, hi, masked, state)
 
 
@@ -558,7 +574,7 @@
             out_specs=out_specs,
             scratch_shapes=scratch,
         ),
-        compiler_params=params(1, 32),
+        compiler_params=params(1, 20),
         cost_estimate=cost(flops, 8e6, 1e7),
     )
 
@@ -627,6 +643,7 @@
     ylo, z, x, core, yhi = (lax.axis_index(a) for a in ALL)
     sup = ylo * 4 + z
 
+    token_blocks = near_gather(tokens)
     qkv_own = jnp.concatenate(
         [
             w_query.reshape(12, 8, QUERY),
@@ -638,8 +655,22 @@
         ],
         axis=-1,
     )
-    token_blocks = near_gather(tokens)
-    qkv_rows = exchange(jnp.transpose(qkv_own, (1, 0, 2)), NEAR).reshape(1, 96, 6 * HEAD)
+    qkv_own = jnp.pad(jnp.transpose(qkv_own, (1, 0, 2)), ((0, 0), (0, 12), (0, 0)))
+    out_own = jnp.transpose(w_out.reshape(4, QUERY, 24), (0, 2, 1))
+    rows_own = jnp.concatenate(
+        [
+            jnp.pad(w.reshape(24, 8, PART), ((0, 0), (0, 0), (0, PADDED - PART))).transpose(1, 0, 2)
+            for w in (w_gate, w_up, w_down.T)
+        ]
+        + [jnp.concatenate([out_own, out_own], axis=0), qkv_own],
+        axis=-1,
+    )
+    rows = exchange(rows_own, NEAR)
+    gu_rows = rows[:, :, : 2 * PADDED].reshape(192, 2 * PADDED)
+    d_rows = rows[:, :, 2 * PADDED : 3 * PADDED].reshape(192, PADDED)
+    d_full = lax.all_gather(d_rows, WIDE, axis=0, tiled=True).reshape(2, WIDTH, PADDED)
+    out_rows = rows[:, :, 3 * PADDED : 3 * PADDED + QUERY].reshape(1, 192, QUERY)
+    qkv_rows = rows[:, :12, 3 * PADDED + QUERY :].reshape(1, 96, 6 * HEAD)
     qkv = exchange(jnp.broadcast_to(qkv_rows, (16, 96, 6 * HEAD)), WIDE)
     qkv = jnp.transpose(qkv.reshape(2, 8, 8, 12, 6 * HEAD), (1, 2, 0, 3, 4)).reshape(WIDTH, 6 * HEAD)
     gain_attn = qkv[:, 5 * HEAD].astype(F32)
@@ -682,28 +713,17 @@
         [b for p in token_blocks for b in p], qkv, gain_attn[None], cos, sin, head_gain
     )
 
-    out_own = jnp.transpose(w_out.reshape(4, QUERY, 24), (0, 2, 1))
-    rows_own = jnp.concatenate(
-        [
-            jnp.pad(w.reshape(24, 8, PART), ((0, 0), (0, 0), (0, PADDED - PART))).transpose(1, 0, 2)
-            for w in (w_gate, w_up, w_down.T)
-        ]
-        + [jnp.concatenate([out_own, out_own], axis=0)],
-        axis=-1,
-    )
-    rows_own = exchange(after(rows_own, kv), NEAR).reshape(192, 3 * PADDED + QUERY)
-    ffn_full = lax.all_gather(rows_own[:, : 3 * PADDED], WIDE, axis=0, tiled=True)
-    ffn_full = ffn_full.reshape(2, WIDTH, 3 * PADDED)
-
     kv_own = [kv, swap(kv, "yhi")]
     kv_earlier = [shift_super(kv, 2, 0), shift_super(kv, 2, 1), shift_super(kv, 1, 0), shift_super(kv, 1, 1)]
+    kv_earlier, gu_rows = lax.optimization_barrier((kv_earlier, gu_rows))
+    gu_full = lax.all_gather(gu_rows, WIDE, axis=0, tiled=True).reshape(2, WIDTH, 2 * PADDED)
     state = attend_own(plan, rot_q, start_lanes, kv_own)
-    out_rows = jnp.broadcast_to(rows_own[None, :, 3 * PADDED :], (16, 192, QUERY))
-    out_both = exchange(out_rows, WIDE).reshape(2, WIDTH, QUERY)
-    w_out_t = jnp.where(x < 2, out_both[0], out_both[1])
+    out_both = exchange(jnp.broadcast_to(after(out_rows, kv_own[1]), (16, 192, QUERY)), WIDE)
+    out_both = out_both.reshape(2, WIDTH, QUERY)
+    state, w_out_t = lax.optimization_barrier((state, jnp.where(x < 2, out_both[0], out_both[1])))
     cot_blocks = near_gather(after(cotangent, kv))
     mix, out_tiles, lse = attend_earlier(plan, rot_q, start_lanes, kv_earlier, state)
-    mix, cot_blocks, w_out_t = lax.optimization_barrier((mix, cot_blocks, w_out_t))
+    mix, cot_blocks = lax.optimization_barrier((mix, cot_blocks))
 
     inputs = tokens.astype(F32)
     parts = [None] * 4
@@ -727,7 +747,7 @@
             blocks = after(blocks, ffn_outs[1][0])
         if d == 2:
             blocks = after(blocks, ffn_outs[3][0])
-        ffn_outs[d] = ffn(*blocks, *cot_blocks[d], ffn_full)
+        ffn_outs[d] = ffn(*blocks, *cot_blocks[d], gu_full, d_full)
     acts, gus = [o[2] for o in ffn_outs], [o[3] for o in ffn_outs]
     kept, gus = lax.optimization_barrier((near_keep([o[:2] for o in ffn_outs]), gus))
     pair_total = near_sum(kept)
@@ -744,6 +764,11 @@
     grad_branch = grad_hidden.astype(BF16)
     branches = [b for p in near_gather(grad_branch) for b in p]
     grad_mix = out_back(branches, w_out_t)
+
+    acts, grad_branch = lax.optimization_barrier((acts, grad_branch))
+    out_kept = near_keep([down(a, d_full) for a in acts])
+    grad_mix, out_kept = lax.optimization_barrier((grad_mix, out_kept))
+    grad_out = exchange(out_weights(mix, branches), WIDE)
 
     dqt, mine, theirs = back_earlier(plan, rot_q, start_lanes, kv_earlier, grad_mix, out_tiles, lse)
     mine = mine.astype(BF16)
@@ -753,36 +778,33 @@
         shift_super(mine[0], -2, 0),
         shift_super(theirs[0], -2, 1),
     ]
+    out_total = near_sum(out_kept)
+    dqt, out_total = lax.optimization_barrier((dqt, out_total))
+    output = (hidden + out_total).astype(BF16)
     grad_q, mine, theirs = back_own(
         plan, rot_q, start_lanes, kv_own, grad_mix, out_tiles, lse, dqt
     )
+    grad_q, mine, theirs, sent, grad_out = lax.optimization_barrier(
+        (grad_q, mine, theirs, sent, grad_out)
+    )
     grad_kvs = [mine[0], swap(theirs[0], "yhi")] + sent
-
-    acts, branches, dqt = lax.optimization_barrier((acts, branches, dqt))
-    output = (hidden + near_sum(near_keep([down(a, ffn_full) for a in acts]))).astype(BF16)
-    grad_out = exchange(out_weights(mix, branches), WIDE)
     grad_out = jnp.sum(grad_out.astype(F32), axis=0).astype(BF16)
     grad_out = jnp.transpose(grad_out.reshape(96, 8, 24), (1, 2, 0))
-    grad_out = exchange(grad_out, NEAR).reshape(2, 4, 24, 96)
-    kept = jnp.where(yhi == 0, grad_out[0], grad_out[1])
-    got = swap(jnp.where(yhi == 0, grad_out[1], grad_out[0]), "yhi")
-    w_out_grad = jnp.stack(
-        [jnp.where(yhi == 0, kept, got), jnp.where(yhi == 0, got, kept)], axis=1
-    )
-    w_out_grad = jnp.transpose(w_out_grad, (0, 1, 3, 2)).reshape(768, 24).astype(F32)
-
-    unprojected = [None] * 4
-    for d in (2, 1, 3, 0):
-        unprojected[d] = unproject(
-            d, grad_q, grad_kvs, raw, *token_blocks[d], qkv, cos, sin, head_gain
-        )
-    kept = near_keep([u[:2] for u in unprojected])
+
+    unprojected = [None] * 2
+    for half in (1, 0):
+        xs = [b for p in token_blocks[2 * half : 2 * half + 2] for b in p]
+        unprojected[half] = unproject(half, grad_q, grad_kvs, raw, xs, qkv, cos, sin, head_gain)
+    kept = near_keep([u[2 * i : 2 * i + 2] for u in unprojected for i in (0, 1)])
     kept, normed = lax.optimization_barrier((kept, normed))
     grad_normed = near_sum(kept)
-    qkv_grad = dot(normed, jnp.concatenate([u[2] for u in unprojected], axis=0), TN)
-
-    attn_gain_part = sum(u[3] for u in unprojected).reshape(128, 12, 1)
-    head_part = sum(u[4] for u in unprojected)[0]
+    qkv_grad = dot(normed, jnp.concatenate([u[4] for u in unprojected], axis=0), TN)
+
+    last = jnp.concatenate([ffn_sum.reshape(8, 24, 3 * PART), grad_out], axis=-1)
+    last, qkv_grad = lax.optimization_barrier((exchange(last, NEAR), qkv_grad))
+
+    attn_gain_part = sum(u[5] for u in unprojected).reshape(128, 12, 1)
+    head_part = sum(u[6] for u in unprojected)[0]
     q_gain_part = head_part[:HEAD] + head_part[HEAD : 2 * HEAD] + head_part[2 * HEAD : QUERY]
     head_part = jnp.concatenate([q_gain_part, head_part[QUERY:], jnp.zeros((4,), F32)])
     gain_parts = jnp.concatenate(
@@ -817,7 +839,13 @@
     scale_attn = rms_scale(inputs)
     input_grad = (grad_hidden + rms_back(grad_normed * gain_attn, inputs, scale_attn)).astype(BF16)
 
-    ffn_grad = exchange(ffn_sum.astype(BF16).reshape(8, 24, 3 * PART), NEAR)
+    ffn_grad, grad_out = last[:, :, : 3 * PART], last[:, :, 3 * PART :].reshape(2, 4, 24, 96)
+    kept = jnp.where(yhi == 0, grad_out[0], grad_out[1])
+    got = swap(jnp.where(yhi == 0, grad_out[1], grad_out[0]), "yhi")
+    w_out_grad = jnp.stack(
+        [jnp.where(yhi == 0, kept, got), jnp.where(yhi == 0, got, kept)], axis=1
+    )
+    w_out_grad = jnp.transpose(w_out_grad, (0, 1, 3, 2)).reshape(768, 24).astype(F32)
     ffn_grad = jnp.transpose(ffn_grad, (1, 0, 2)).astype(F32)
     w_gate_grad, w_up_grad, w_down_grad = (
         ffn_grad[:, :, i * PART : (i + 1) * PART].reshape(24, -1) for i in range(3)

time: 537 us -> 502 us (0.935)
  Pallas kernels: 154 us -> 131 us
  starting transfers between devices: 121 us -> 103 us
  waiting for transfers between devices: 110 us -> 128 us
  other arithmetic: 40 us -> 29.7 us
    ppermute x35, waiting for transfers between devices: 3.81 us -> 25.1 us  [swap(): return lax.ppermute(v, axis, [(0, 1), (1, 0)])]
    all_to_all x7 -> x5, starting transfers between devices: 46.7 us -> 35.8 us  [exchange(): return lax.all_to_all(v, axes, split_axis=0, concat_axis=0, tiled=True)]
    convert_element_type x14 -> x15, other arithmetic: 14.1 us -> 3.65 us  [near_keep(): (own.astype(F32) + swap(other, 'core').astype(F32)).astype(BF16)]
    ppermute x8, waiting for transfers between devices: 10.6 us -> 18.1 us  [shift_super(): return lax.ppermute(v, ('ylo', 'z', 'yhi'), pairs)]
    ppermute x24, waiting for transfers between devices: 68 us -> 62.2 us  [shift_x(): return lax.ppermute(v, 'x', [((i + distance) % 4, i) for i in range(4)])]
    all_to_all x7 -> x5, waiting for transfers between devices: 28 us -> 22.7 us  [exchange(): return lax.all_to_all(v, axes, split_axis=0, concat_axis=0, tiled=True)]
    unnamed x241 -> x269, local copies, waits for them, and re-layouts: 37.3 us -> 32.6 us
  transfers between devices with their start and end apart: 76 -> 75, of which waited for: 14 -> 26; matrix products, arithmetic and copies ran while one was open for 12% -> 9% of each run, Pallas kernels for 28% -> 27%
where the time goes in v3:
time: 502 us; the launch traced here: 494 us
  Pallas kernels  131 us (26%)
  waiting for transfers between devices  128 us (25%)
  starting transfers between devices  103 us (21%)
  local copies, waits for them, and re-layouts  63.8 us (13%)
  other arithmetic  29.7 us (6%)
  blocking collectives  18 us (4%)
  between operations  16.4 us (3%)
    ppermute x24, waiting for transfers between devices, shift_x(): return lax.ppermute(v, 'x', [((i + distance) % 4, i) for i in range(4)])  62.2 us
    all_to_all x5, starting transfers between devices, exchange(): return lax.all_to_all(v, axes, split_axis=0, concat_axis=0, tiled=True)  35.8 us
    unnamed x269, local copies, waits for them, and re-layouts  32.6 us
    ppermute x24, starting transfers between devices, shift_x(): return lax.ppermute(v, 'x', [((i + distance) % 4, i) for i in range(4)])  29.7 us
    ppermute x35, waiting for transfers between devices, swap(): return lax.ppermute(v, axis, [(0, 1), (1, 0)])  25.1 us
    pallas_call x4, Pallas kernels, ffn(): pl.pallas_call(ffn_kernel, out_shape=(jax.ShapeDtypeStruct((ROWS, WIDTH),...  25 us
    pallas_call x1, Pallas kernels, back_earlier(): return call(plan, q, start, *kvs, grad, out, lse)  24.3 us
    ppermute x8, starting transfers between devices, shift_super(): return lax.ppermute(v, ('ylo', 'z', 'yhi'), pairs)  24.2 us
  transfers between devices with their start and end apart: 75, of which 26 were waited for; matrix products, arithmetic and copies ran while one was open for 9% of the time, Pallas kernels for 27%

profile of v3, /device:TPU:8, one launch (start us, length us, event | category | flops | bytes accessed | tf_op | source)
XLA Modules:
  0.0 493.7 jit_solution(11055637395654974832)
XLA Ops:
  13.4 18.0 %all_to_all.30 = bf16[8,24,2112]{2,1,0:T(8,128)(2,1)S(1)} all-to-all(bf16[8,24,2112]{2,1,0:T(8,128)(2,1)S(1)} %copy.146), channel_id=1, replica_groups=mesh['ylo'=2,'z'=4,'x'=4,'core'=2,'yhi'=2] {'x','core'}, dimensions={0} | all-to-all | bytes 1622016 | tf_op jit(solution)/shard_map/all_to_all | solution.py:70
  37.6 8.5 %all-to-all-start.1 = ((bf16[16,96,384]{2,1,0:T(8,128)(2,1)}), bf16[16,96,384]{2,1,0:T(8,128)(2,1)S(1)}, u32[]{:S(2)}, u32[]{:S(2)}) async-start(bf16[16,96,384]{2,1,0:T(8,128)(2,1)} %broadcast_in_dim.29), calls=%async_computation.1 | async-start | bytes 2359296 | tf_op jit(solution)/shard_map/all_to_all | solution.py:70
  46.4 1.9 fusion.12
  48.9 5.8 %collective-permute-done.5.refs_6_.refs_10_ = bf16[128,1536]{1,0:T(8,128)(2,1)S(1)} collective-permute-done((bf16[128,1536]{1,0:T(8,128)(2,1)S(1)}, bf16[128,1536]{1,0:T(8,128)(2,1)S(1)}, u32[]{:S(2)}, u32[]{:S(2)}) %collective-permute-start.5) | collective-permute-done | bytes 393248 | tf_op jit(solution)/shard_map/ppermute | solution.py:52
  55.9 8.8 %all-to-all-done.1 = bf16[16,96,384]{2,1,0:T(8,128)(2,1)S(1)} async-done(((bf16[16,96,384]{2,1,0:T(8,128)(2,1)}), bf16[16,96,384]{2,1,0:T(8,128)(2,1)S(1)}, u32[]{:S(2)}, u32[]{:S(2)}) %all-to-all-start.1) | async-done | bytes 1179680 | tf_op jit(solution)/shard_map/all_to_all | solution.py:70
  66.6 2.3 reshape.575.refs_8_.refs_12_
  70.0 4.5 shard_map.237
  78.0 4.0 collective-permute-start.7
  81.9 2.1 collective-permute-start.8
  84.1 2.2 collective-permute-start.9
  86.3 3.5 collective-permute-start.10
  90.6 13.7 %collective-permute-done.7.refs_0_ = bf16[8,128,128]{2,1,0:T(8,128)(2,1)S(1)} collective-permute-done((bf16[8,128,128]{2,1,0:T(8,128)(2,1)S(1)}, bf16[8,128,128]{2,1,0:T(8,128)(2,1)S(1)}, u32[]{:S(2)}, u32[]{:S(2)}) %collective-permute-start.7) | collective-permute-done | bytes 262176 | tf_op jit(solution)/shard_map/ppermute | solution.py:66
  105.0 2.4 collective-permute-done.8.refs_1_
  108.1 2.0 collective-permute-done.9.refs_2_
  111.5 3.1 collective-permute-start.11
  114.7 6.0 %collective-permute-done.11.refs_1_ = bf16[8,128,128]{2,1,0:T(8,128)(2,1)S(1)} collective-permute-done((bf16[8,128,128]{2,1,0:T(8,128)(2,1)}, bf16[8,128,128]{2,1,0:T(8,128)(2,1)S(1)}, u32[]{:S(2)}, u32[]{:S(2)}) %collective-permute-start.11) | collective-permute-done | bytes 262176 | tf_op jit(solution)/shard_map/ppermute | solution.py:56
  122.8 7.0 %all-to-all-start.2 = ((bf16[16,192,192]{2,1,0:T(8,128)(2,1)}), bf16[16,192,192]{2,1,0:T(8,128)(2,1)}, u32[]{:S(2)}, u32[]{:S(2)}) async-start(bf16[16,192,192]{2,1,0:T(8,128)(2,1)} %broadcast_in_dim.31), calls=%async_computation.2 | async-start | bytes 3145728 | tf_op jit(solution)/shard_map/all_to_all | solution.py:70
  129.9 2.8 collective-permute-start.13
  135.6 10.8 %shard_map.238 = (f32[8,64,384]{2,1,0:T(8,128)S(1)}, f32[8,1,384]{2,1,0:T(1,128)S(1)}) custom-call(s32[8,11]{1,0:T(8,128)S(1)} %stack.8.plan, bf16[8,128,192]{2,1,0:T(8,128)(2,1)S(1)} %copy-done.55, s32[8,1,384]{2,1,0:T(1,128)S(1)} %copy.150.start_ref, bf16[8,128,128]{2,1,0:T(8,128)(2,1)S(1)} %copy-done.75, bf16[8,128,128]{2,1,0:T(8,128)(2,1)S(1)} %copy-done.78), custom_call_target="tpu_custom_call" | custom-call | flops 4000000000 | bytes 8000000 | tf_op jit(solution)/shard_map/pallas_call | solution.py:589
  148.7 3.2 collective-permute-done.17.c0_ref.refs_14_
  155.7 15.0 %shard_map.239 = (bf16[8,128,192]{2,1,0:T(8,128)(2,1)S(1)}, f32[8,64,384]{2,1,0:T(8,128)S(1)}, f32[8,1,384]{2,1,0:T(1,128)S(1)}) custom-call(s32[8,11]{1,0:T(8,128)S(1)} %stack.8.plan, bf16[8,128,192]{2,1,0:T(8,128)(2,1)S(1)} %copy-done.55, s32[8,1,384]{2,1,0:T(1,128)S(1)} %copy.150.start_ref, bf16[8,128,128]{2,1,0:T(8,128)(2,1)S(1)} %copy-done.81, ...), custom_call_target="tpu_custom_call" | custom-call | flops 8000000000 | bytes 8000000 | tf_op jit(solution)/shard_map/pallas_call | solution.py:596
  174.0 2.8 collective-permute-start.25
  178.8 15.0 %collective-permute-done.25 = bf16[128,1536]{1,0:T(8,128)(2,1)S(1)} collective-permute-done((bf16[128,1536]{1,0:T(8,128)(2,1)S(1)}, bf16[128,1536]{1,0:T(8,128)(2,1)S(1)}, u32[]{:S(2)}, u32[]{:S(2)}) %collective-permute-start.25) | collective-permute-done | bytes 393248 | tf_op jit(solution)/shard_map/ppermute | solution.py:52
  193.8 3.8 collective-permute-done.21
  201.6 2.0 copy-done
  203.6 2.8 copy-done.51
  206.4 6.2 %shard_map.244 = (bf16[128,1536]{1,0:T(8,128)(2,1)S(1)}, bf16[128,1536]{1,0:T(8,128)(2,1)S(1)}, bf16[2,256,512]{2,1,0:T(8,128)(2,1)S(1)}, bf16[2,256,1024]{2,1,0:T(8,128)(2,1)S(1)}) custom-call(bf16[128,1536]{1,0:T(8,128)(2,1)} %multiply_convert_fusion.x0_ref.refs_0_, bf16[128,1536]{1,0:T(8,128)(2,1)S(1)} %collective-permute-done.26.x1_ref.refs_1_, ...), custom_call_target="tpu_custom_call" | custom-call | flops 4026531840 | bytes 14000000 | tf_op jit(solution)/shard_map/pallas_call | solution.py:266
  214.7 6.6 %shard_map.245 = (bf16[128,1536]{1,0:T(8,128)(2,1)S(1)}, bf16[128,1536]{1,0:T(8,128)(2,1)S(1)}, bf16[2,256,512]{2,1,0:T(8,128)(2,1)S(1)}, bf16[2,256,1024]{2,1,0:T(8,128)(2,1)S(1)}) custom-call(bf16[128,1536]{1,0:T(8,128)(2,1)} %collective-permute-done.28.x0_ref.refs_2_, bf16[128,1536]{1,0:T(8,128)(2,1)S(1)} %collective-permute-done.29.x1_ref.refs_3_, ...), custom_call_target="tpu_custom_call" | custom-call | flops 4026531840 | bytes 14000000 | tf_op jit(solution)/shard_map/pallas_call | solution.py:266
  221.4 4.6 collective-permute-done.31.x0_ref.refs_4_
  226.0 6.2 %shard_map.246 = (bf16[128,1536]{1,0:T(8,128)(2,1)S(1)}, bf16[128,1536]{1,0:T(8,128)(2,1)S(1)}, bf16[2,256,512]{2,1,0:T(8,128)(2,1)S(1)}, bf16[2,256,1024]{2,1,0:T(8,128)(2,1)S(1)}) custom-call(bf16[128,1536]{1,0:T(8,128)(2,1)} %collective-permute-done.33.x0_ref.refs_6_, bf16[128,1536]{1,0:T(8,128)(2,1)S(1)} %collective-permute-done.34.x1_ref.refs_7_, ...), custom_call_target="tpu_custom_call" | custom-call | flops 4026531840 | bytes 14000000 | tf_op jit(solution)/shard_map/pallas_call | solution.py:266
  232.9 6.0 %shard_map.247 = (bf16[128,1536]{1,0:T(8,128)(2,1)S(1)}, bf16[128,1536]{1,0:T(8,128)(2,1)S(1)}, bf16[2,256,512]{2,1,0:T(8,128)(2,1)S(1)}, bf16[2,256,1024]{2,1,0:T(8,128)(2,1)S(1)}) custom-call(bf16[128,1536]{1,0:T(8,128)(2,1)S(1)} %collective-permute-done.31.x0_ref.refs_4_, bf16[128,1536]{1,0:T(8,128)(2,1)S(1)} %collective-permute-done.32.x1_ref.refs_5_, ...), custom_call_target="tpu_custom_call" | custom-call | flops 4026531840 | bytes 14000000 | tf_op jit(solution)/shard_map/pallas_call | solution.py:266
  240.9 1.9 collective-permute-start.39
  243.8 15.3 %shard_map.248 = bf16[2,1536,1296]{2,1,0:T(8,128)(2,1)S(1)} custom-call(bf16[128,1536]{1,0:T(8,128)(2,1)} %multiply_convert_fusion.x0_ref.refs_0_, bf16[128,1536]{1,0:T(8,128)(2,1)S(1)} %copy-done.69, bf16[128,1536]{1,0:T(8,128)(2,1)} %collective-permute-done.28.x0_ref.refs_2_, bf16[128,1536]{1,0:T(8,128)(2,1)S(1)} %collective-permute-done.29.x1_ref.refs_3_, ...), custom_call_target="tpu_custom_call" | custom-call | flops 9663676416 | bytes 24000000 | tf_op jit(solution)/shard_map/pallas_call | solution.py:336
  259.1 3.3 copy-done.9
  264.4 2.2 multiply_reduce_fusion
  270.3 1.9 collective-permute-start.41
  272.2 2.1 collective-permute-start.43
  282.5 3.3 collective-permute-done.43.refs_4_
  285.7 7.2 %collective-permute-done.45.refs_6_ = bf16[128,1536]{1,0:T(8,128)(2,1)S(1)} collective-permute-done((bf16[128,1536]{1,0:T(8,128)(2,1)S(1)}, bf16[128,1536]{1,0:T(8,128)(2,1)S(1)}, u32[]{:S(2)}, u32[]{:S(2)}) %collective-permute-start.45) | collective-permute-done | bytes 393248 | tf_op jit(solution)/shard_map/ppermute | solution.py:52
  299.5 24.3 %shard_map.254 = (f32[8,64,384]{2,1,0:T(8,128)S(1)}, f32[2,8,128,128]{3,2,1,0:T(8,128)S(1)}, bf16[2,8,128,128]{3,2,1,0:T(8,128)(2,1)S(1)}) custom-call(s32[8,11]{1,0:T(8,128)S(1)} %copy-done.50, bf16[8,128,192]{2,1,0:T(8,128)(2,1)S(1)} %copy-done.56, s32[8,1,384]{2,1,0:T(1,128)S(1)} %copy.150.start_ref, bf16[8,128,128]{2,1,0:T(8,128)(2,1)S(1)} %copy-done.82, ...), custom_call_target="tpu_custom_call" | custom-call | flops 20000000000 | bytes 8000000 | tf_op jit(solution)/shard_map/pallas_call | solution.py:610
  325.7 1.9 collective-permute-start.54
  328.4 2.1 collective-permute-start.55
  330.6 1.8 shard_map.256
  332.4 8.9 %all-to-all-start.3 = ((bf16[16,96,192]{2,1,0:T(8,128)(2,1)}), bf16[16,96,192]{2,1,0:T(8,128)(2,1)}, u32[]{:S(2)}, u32[]{:S(2)}) async-start(bf16[16,96,192]{2,1,0:T(8,128)(2,1)} %shard_map.256), calls=%async_computation.3 | async-start | bytes 1572864 | tf_op jit(solution)/shard_map/all_to_all | solution.py:70
  341.3 5.0 %collective-permute-start.56 = (bf16[8,128,128]{2,1,0:T(8,128)(2,1)}, bf16[8,128,128]{2,1,0:T(8,128)(2,1)S(1)}, u32[]{:S(2)}, u32[]{:S(2)}) collective-permute-start(bf16[8,128,128]{2,1,0:T(8,128)(2,1)} %get-tuple-element.283), channel_id=1, source_target_pairs={{32,0},{33,1},{48,16},{49,17},{64,32},{65,33},{80,48},{81,49},{96,... | collective-permute-start | bytes 786440 | tf_op jit(solution)/shard_map/ppermute | solution.py:66
  346.4 3.4 collective-permute-start.57
  352.0 18.3 %shard_map.255 = (bf16[8,128,256]{2,1,0:T(8,128)(2,1)S(1)}, f32[1,8,128,128]{3,2,1,0:T(8,128)S(1)}, bf16[1,8,128,128]{3,2,1,0:T(8,128)(2,1)S(1)}) custom-call(s32[8,11]{1,0:T(8,128)S(1)} %copy-done.50, bf16[8,128,192]{2,1,0:T(8,128)(2,1)S(1)} %copy-done.57, s32[8,1,384]{2,1,0:T(1,128)S(1)} %copy.150.start_ref, bf16[8,128,128]{2,1,0:T(8,128)(2,1)S(1)} %copy-done.76, ...), custom_call_target="tpu_custom_call" | custom-call | flops 10000000000 | bytes 8000000 | tf_op jit(solution)/shard_map/pallas_call | solution.py:620
  376.4 5.0 %collective-permute-done.58.refs_2_ = bf16[8,128,128]{2,1,0:T(8,128)(2,1)} collective-permute-done((bf16[8,128,128]{2,1,0:T(8,128)(2,1)}, bf16[8,128,128]{2,1,0:T(8,128)(2,1)}, u32[]{:S(2)}, u32[]{:S(2)}) %collective-permute-start.58) | collective-permute-done | bytes 262176 | tf_op jit(solution)/shard_map/ppermute | solution.py:56
  385.6 4.0 shard_map.257
  392.5 3.9 shard_map.258
  405.0 3.1 collective-permute-start.65
  409.7 2.9 fusion.8
  412.6 12.5 %collective-permute-done.65 = bf16[128,1536]{1,0:T(8,128)(2,1)S(1)} collective-permute-done((bf16[128,1536]{1,0:T(8,128)(2,1)S(1)}, bf16[128,1536]{1,0:T(8,128)(2,1)S(1)}, u32[]{:S(2)}, u32[]{:S(2)}) %collective-permute-start.65) | collective-permute-done | bytes 393248 | tf_op jit(solution)/shard_map/ppermute | solution.py:52
  425.1 3.7 collective-permute-done.63
  430.6 2.0 pad_maximum_fusion
  432.6 4.2 all-to-all-start.4
  436.9 2.7 fusion.6
  439.6 7.7 %all-to-all-done.4 = bf16[8,24,1392]{2,1,0:T(8,128)(2,1)} async-done(((bf16[8,24,1392]{2,1,0:T(8,128)(2,1)}), bf16[8,24,1392]{2,1,0:T(8,128)(2,1)}, u32[]{:S(2)}, u32[]{:S(2)}) %all-to-all-start.4) | async-done | bytes 534560 | tf_op jit(solution)/shard_map/all_to_all | solution.py:70
  447.3 2.4 reshape.585
  449.7 1.9 maximum_maximum_fusion
  451.7 7.1 %all-to-all-start.5 = ((bf16[128,12,384]{2,1,0:T(8,128)(2,1)}), bf16[128,12,384]{2,1,0:T(8,128)(2,1)S(1)}, u32[]{:S(2)}, u32[]{:S(2)}) async-start(bf16[128,12,384]{2,1,0:T(8,128)(2,1)} %maximum_maximum_fusion), calls=%async_computation.6 | async-start | bytes 3145728 | tf_op jit(solution)/shard_map/all_to_all | solution.py:70
  459.6 2.2 collective-permute-start.66
  466.8 9.4 %collective-permute-done.66 = bf16[4,24,96]{2,1,0:T(8,128)(2,1)S(1)} collective-permute-done((bf16[4,24,96]{2,1,0:T(8,128)(2,1)S(1)}, bf16[4,24,96]{2,1,0:T(8,128)(2,1)S(1)}, u32[]{:S(2)}, u32[]{:S(2)}) %collective-permute-start.66) | collective-permute-done | bytes 18464 | tf_op jit(solution)/shard_map/ppermute | solution.py:56
  478.0 4.6 all-to-all-done.5
  (524 shorter events, 111.7 us)
Async XLA Ops:
  7.2 194.3 %all-gather.5.cloned.1.call-start = ((), (), s32[]{:S(2)}) async-start(), calls=%async_computation.8 | async-start | bytes 3342336 | tf_op jit(solution)/shard_map/all_gather | solution.py:671
  32.2 37.2 %collective-permute-start = (bf16[128,1536]{1,0:T(8,128)(2,1)S(1)}, bf16[128,1536]{1,0:T(8,128)(2,1)}, u32[]{:S(2)}, u32[]{:S(2)}) collective-permute-start(bf16[128,1536]{1,0:T(8,128)(2,1)S(1)} %copy-done.8), channel_id=1, source_target_pairs={{0,2},{2,0},{1,3},{3,1},{4,6},{6,4},{5,7},{7,5},{8,10},{10,8},{9,1... | collective-permute-start | bytes 1179656 | tf_op jit(solution)/shard_map/ppermute | solution.py:56
  32.3 16.0 %collective-permute-start.1 = (bf16[128,1536]{1,0:T(8,128)(2,1)S(1)}, bf16[128,1536]{1,0:T(8,128)(2,1)}, u32[]{:S(2)}, u32[]{:S(2)}) collective-permute-start(bf16[128,1536]{1,0:T(8,128)(2,1)S(1)} %copy-done.8), channel_id=1, source_target_pairs={{4,0},{8,4},{12,8},{0,12},{5,1},{9,5},{13,9},{1,13},{6,2},{10,6},{... | collective-permute-start | bytes 1179656 | tf_op jit(solution)/shard_map/ppermute | solution.py:52
  33.6 14.8 %collective-permute-start.3 = (bf16[128,1536]{1,0:T(8,128)(2,1)S(1)}, bf16[128,1536]{1,0:T(8,128)(2,1)S(1)}, u32[]{:S(2)}, u32[]{:S(2)}) collective-permute-start(bf16[128,1536]{1,0:T(8,128)(2,1)S(1)} %copy-done.8), channel_id=1, source_target_pairs={{8,0},{12,4},{0,8},{4,12},{9,1},{13,5},{1,9},{5,13},{10,2},{14,6},... | collective-permute-start | bytes 1179656 | tf_op jit(solution)/shard_map/ppermute | solution.py:52
  35.0 19.6 %collective-permute-start.5 = (bf16[128,1536]{1,0:T(8,128)(2,1)S(1)}, bf16[128,1536]{1,0:T(8,128)(2,1)S(1)}, u32[]{:S(2)}, u32[]{:S(2)}) collective-permute-start(bf16[128,1536]{1,0:T(8,128)(2,1)S(1)} %copy-done.8), channel_id=1, source_target_pairs={{12,0},{0,4},{4,8},{8,12},{13,1},{1,5},{5,9},{9,13},{14,2},{2,6},{... | collective-permute-start | bytes 1179656 | tf_op jit(solution)/shard_map/ppermute | solution.py:52
  37.6 27.1 %all-to-all-start.1 = ((bf16[16,96,384]{2,1,0:T(8,128)(2,1)}), bf16[16,96,384]{2,1,0:T(8,128)(2,1)S(1)}, u32[]{:S(2)}, u32[]{:S(2)}) async-start(bf16[16,96,384]{2,1,0:T(8,128)(2,1)} %broadcast_in_dim.29), calls=%async_computation.1 | async-start | bytes 2359296 | tf_op jit(solution)/shard_map/all_to_all | solution.py:70
  46.1 155.5 %all-gather.3.cloned.1.call-start = ((), (), s32[]{:S(2)}) async-start(), calls=%async_computation.7 | async-start | bytes 6684672 | tf_op jit(solution)/shard_map/all_gather | solution.py:719
  48.3 21.2 %collective-permute-start.2 = (bf16[128,1536]{1,0:T(8,128)(2,1)}, bf16[128,1536]{1,0:T(8,128)(2,1)}, u32[]{:S(2)}, u32[]{:S(2)}) collective-permute-start(bf16[128,1536]{1,0:T(8,128)(2,1)} %collective-permute-done.1.refs_2_.refs_10_), channel_id=1, source_target_pairs={{0,2},{2,0},{1,3},{3,1},{4,6},{6,4},{5,7},{7,5},{8,10},{10,8},{9,1... | collective-permute-start | bytes 1179656 | tf_op jit(solution)/shard_map/ppermute | solution.py:56
  48.4 21.1 %collective-permute-start.4 = (bf16[128,1536]{1,0:T(8,128)(2,1)S(1)}, bf16[128,1536]{1,0:T(8,128)(2,1)}, u32[]{:S(2)}, u32[]{:S(2)}) collective-permute-start(bf16[128,1536]{1,0:T(8,128)(2,1)S(1)} %collective-permute-done.3.refs_4_.refs_8_), channel_id=1, source_target_pairs={{0,2},{2,0},{1,3},{3,1},{4,6},{6,4},{5,7},{7,5},{8,10},{10,8},{9,1... | collective-permute-start | bytes 1179656 | tf_op jit(solution)/shard_map/ppermute | solution.py:56
  54.7 14.8 %collective-permute-start.6 = (bf16[128,1536]{1,0:T(8,128)(2,1)S(1)}, bf16[128,1536]{1,0:T(8,128)(2,1)}, u32[]{:S(2)}, u32[]{:S(2)}) collective-permute-start(bf16[128,1536]{1,0:T(8,128)(2,1)S(1)} %collective-permute-done.5.refs_6_.refs_10_), channel_id=1, source_target_pairs={{0,2},{2,0},{1,3},{3,1},{4,6},{6,4},{5,7},{7,5},{8,10},{10,8},{9,1... | collective-permute-start | bytes 1179656 | tf_op jit(solution)/shard_map/ppermute | solution.py:56
  78.0 26.3 %collective-permute-start.7 = (bf16[8,128,128]{2,1,0:T(8,128)(2,1)S(1)}, bf16[8,128,128]{2,1,0:T(8,128)(2,1)S(1)}, u32[]{:S(2)}, u32[]{:S(2)}) collective-permute-start(bf16[8,128,128]{2,1,0:T(8,128)(2,1)S(1)} %get-tuple-element.137.refs_0_), channel_id=1, source_target_pairs={{0,32},{1,33},{16,48},{17,49},{32,64},{33,65},{48,80},{49,81},{64,... | collective-permute-start | bytes 786440 | tf_op jit(solution)/shard_map/ppermute | solution.py:66
  81.9 25.4 %collective-permute-start.8 = (bf16[8,128,128]{2,1,0:T(8,128)(2,1)S(1)}, bf16[8,128,128]{2,1,0:T(8,128)(2,1)S(1)}, u32[]{:S(2)}, u32[]{:S(2)}) collective-permute-start(bf16[8,128,128]{2,1,0:T(8,128)(2,1)S(1)} %get-tuple-element.137.refs_0_), channel_id=1, source_target_pairs={{0,33},{1,32},{16,49},{17,48},{32,65},{33,64},{48,81},{49,80},{64,... | collective-permute-start | bytes 786440 | tf_op jit(solution)/shard_map/ppermute | solution.py:66
  84.1 26.1 %collective-permute-start.9 = (bf16[8,128,128]{2,1,0:T(8,128)(2,1)S(1)}, bf16[8,128,128]{2,1,0:T(8,128)(2,1)S(1)}, u32[]{:S(2)}, u32[]{:S(2)}) collective-permute-start(bf16[8,128,128]{2,1,0:T(8,128)(2,1)S(1)} %get-tuple-element.137.refs_0_), channel_id=1, source_target_pairs={{0,16},{1,17},{16,32},{17,33},{32,48},{33,49},{48,64},{49,65},{64,... | collective-permute-start | bytes 786440 | tf_op jit(solution)/shard_map/ppermute | solution.py:66
  86.3 24.5 %collective-permute-start.10 = (bf16[8,128,128]{2,1,0:T(8,128)(2,1)S(1)}, bf16[8,128,128]{2,1,0:T(8,128)(2,1)S(1)}, u32[]{:S(2)}, u32[]{:S(2)}) collective-permute-start(bf16[8,128,128]{2,1,0:T(8,128)(2,1)S(1)} %get-tuple-element.137.refs_0_), channel_id=1, source_target_pairs={{0,17},{1,16},{16,33},{17,32},{32,49},{33,48},{48,65},{49,64},{64,... | collective-permute-start | bytes 786440 | tf_op jit(solution)/shard_map/ppermute | solution.py:66
  111.5 9.2 %collective-permute-start.11 = (bf16[8,128,128]{2,1,0:T(8,128)(2,1)}, bf16[8,128,128]{2,1,0:T(8,128)(2,1)S(1)}, u32[]{:S(2)}, u32[]{:S(2)}) collective-permute-start(bf16[8,128,128]{2,1,0:T(8,128)(2,1)} %copy-done.74), channel_id=1, source_target_pairs={{0,1},{1,0},{2,3},{3,2},{4,5},{5,4},{6,7},{7,6},{8,9},{9,8},{10,11... | collective-permute-start | bytes 786440 | tf_op jit(solution)/shard_map/ppermute | solution.py:56
  122.8 31.0 %all-to-all-start.2 = ((bf16[16,192,192]{2,1,0:T(8,128)(2,1)}), bf16[16,192,192]{2,1,0:T(8,128)(2,1)}, u32[]{:S(2)}, u32[]{:S(2)}) async-start(bf16[16,192,192]{2,1,0:T(8,128)(2,1)} %broadcast_in_dim.31), calls=%async_computation.2 | async-start | bytes 3145728 | tf_op jit(solution)/shard_map/all_to_all | solution.py:70
  129.8 300.9 %reduce-scatter.2.cloned.1.call-start = ((), (), s32[]{:S(2)}) async-start(), calls=%async_computation.9 | async-start | bytes 9191424 | tf_op jit(solution)/shard_map/reduce_scatter | solution.py:758
  129.9 18.3 %collective-permute-start.13 = (bf16[128,1536]{1,0:T(8,128)(2,1)S(1)}, bf16[128,1536]{1,0:T(8,128)(2,1)S(1)}, u32[]{:S(2)}, u32[]{:S(2)}) collective-permute-start(bf16[128,1536]{1,0:T(8,128)(2,1)S(1)} %copy-done.18), channel_id=1, source_target_pairs={{4,0},{8,4},{12,8},{0,12},{5,1},{9,5},{13,9},{1,13},{6,2},{10,6},{... | collective-permute-start | bytes 1179656 | tf_op jit(solution)/shard_map/ppermute | solution.py:52
  132.6 15.5 %collective-permute-start.15 = (bf16[128,1536]{1,0:T(8,128)(2,1)S(1)}, bf16[128,1536]{1,0:T(8,128)(2,1)S(1)}, u32[]{:S(2)}, u32[]{:S(2)}) collective-permute-start(bf16[128,1536]{1,0:T(8,128)(2,1)S(1)} %copy-done.18), channel_id=1, source_target_pairs={{8,0},{12,4},{0,8},{4,12},{9,1},{13,5},{1,9},{5,13},{10,2},{14,6},... | collective-permute-start | bytes 1179656 | tf_op jit(solution)/shard_map/ppermute | solution.py:52
  133.5 18.3 %collective-permute-start.17 = (bf16[128,1536]{1,0:T(8,128)(2,1)S(1)}, bf16[128,1536]{1,0:T(8,128)(2,1)S(1)}, u32[]{:S(2)}, u32[]{:S(2)}) collective-permute-start(bf16[128,1536]{1,0:T(8,128)(2,1)S(1)} %copy-done.18), channel_id=1, source_target_pairs={{12,0},{0,4},{4,8},{8,12},{13,1},{1,5},{5,9},{9,13},{14,2},{2,6},{... | collective-permute-start | bytes 1179656 | tf_op jit(solution)/shard_map/ppermute | solution.py:52
  134.5 36.3 %collective-permute-start.12 = (bf16[128,1536]{1,0:T(8,128)(2,1)S(1)}, bf16[128,1536]{1,0:T(8,128)(2,1)S(1)}, u32[]{:S(2)}, u32[]{:S(2)}) collective-permute-start(bf16[128,1536]{1,0:T(8,128)(2,1)S(1)} %copy-done.18), channel_id=1, source_target_pairs={{0,2},{2,0},{1,3},{3,1},{4,6},{6,4},{5,7},{7,5},{8,10},{10,8},{9,1... | collective-permute-start | bytes 1179656 | tf_op jit(solution)/shard_map/ppermute | solution.py:56
  148.1 22.7 %collective-permute-start.14 = (bf16[128,1536]{1,0:T(8,128)(2,1)S(1)}, bf16[128,1536]{1,0:T(8,128)(2,1)S(1)}, u32[]{:S(2)}, u32[]{:S(2)}) collective-permute-start(bf16[128,1536]{1,0:T(8,128)(2,1)S(1)} %collective-permute-done.13.c0_ref.refs_10_), channel_id=1, source_target_pairs={{0,2},{2,0},{1,3},{3,1},{4,6},{6,4},{5,7},{7,5},{8,10},{10,8},{9,1... | collective-permute-start | bytes 1179656 | tf_op jit(solution)/shard_map/ppermute | solution.py:56
  148.1 22.7 %collective-permute-start.16 = (bf16[128,1536]{1,0:T(8,128)(2,1)S(1)}, bf16[128,1536]{1,0:T(8,128)(2,1)}, u32[]{:S(2)}, u32[]{:S(2)}) collective-permute-start(bf16[128,1536]{1,0:T(8,128)(2,1)S(1)} %collective-permute-done.15.c0_ref.refs_12_), channel_id=1, source_target_pairs={{0,2},{2,0},{1,3},{3,1},{4,6},{6,4},{5,7},{7,5},{8,10},{10,8},{9,1... | collective-permute-start | bytes 1179656 | tf_op jit(solution)/shard_map/ppermute | solution.py:56
  151.8 19.0 %collective-permute-start.18 = (bf16[128,1536]{1,0:T(8,128)(2,1)S(1)}, bf16[128,1536]{1,0:T(8,128)(2,1)}, u32[]{:S(2)}, u32[]{:S(2)}) collective-permute-start(bf16[128,1536]{1,0:T(8,128)(2,1)S(1)} %collective-permute-done.17.c0_ref.refs_14_), channel_id=1, source_target_pairs={{0,2},{2,0},{1,3},{3,1},{4,6},{6,4},{5,7},{7,5},{8,10},{10,8},{9,1... | collective-permute-start | bytes 1179656 | tf_op jit(solution)/shard_map/ppermute | solution.py:56
  174.0 19.8 %collective-permute-start.25 = (bf16[128,1536]{1,0:T(8,128)(2,1)S(1)}, bf16[128,1536]{1,0:T(8,128)(2,1)S(1)}, u32[]{:S(2)}, u32[]{:S(2)}) collective-permute-start(bf16[128,1536]{1,0:T(8,128)(2,1)S(1)} %add_convert_fusion.13), channel_id=1, source_target_pairs={{4,0},{8,4},{12,8},{0,12},{5,1},{9,5},{13,9},{1,13},{6,2},{10,6},{... | collective-permute-start | bytes 1179656 | tf_op jit(solution)/shard_map/ppermute | solution.py:52
  176.8 16.9 %collective-permute-start.23 = (bf16[128,1536]{1,0:T(8,128)(2,1)S(1)}, bf16[128,1536]{1,0:T(8,128)(2,1)S(1)}, u32[]{:S(2)}, u32[]{:S(2)}) collective-permute-start(bf16[128,1536]{1,0:T(8,128)(2,1)S(1)} %add_convert_fusion.14), channel_id=1, source_target_pairs={{8,0},{12,4},{0,8},{4,12},{9,1},{13,5},{1,9},{5,13},{10,2},{14,6},... | collective-permute-start | bytes 1179656 | tf_op jit(solution)/shard_map/ppermute | solution.py:52
  177.9 19.8 %collective-permute-start.21 = (bf16[128,1536]{1,0:T(8,128)(2,1)S(1)}, bf16[128,1536]{1,0:T(8,128)(2,1)S(1)}, u32[]{:S(2)}, u32[]{:S(2)}) collective-permute-start(bf16[128,1536]{1,0:T(8,128)(2,1)S(1)} %add_convert_fusion.15), channel_id=1, source_target_pairs={{12,0},{0,4},{4,8},{8,12},{13,1},{1,5},{5,9},{9,13},{14,2},{2,6},{... | collective-permute-start | bytes 1179656 | tf_op jit(solution)/shard_map/ppermute | solution.py:52
  199.5 13.1 %collective-permute-start.28 = (bf16[128,1536]{1,0:T(8,128)(2,1)}, bf16[128,1536]{1,0:T(8,128)(2,1)}, u32[]{:S(2)}, u32[]{:S(2)}) collective-permute-start(bf16[128,1536]{1,0:T(8,128)(2,1)} %multiply_convert_fusion.x0_ref.refs_0_), channel_id=1, source_target_pairs={{4,0},{8,4},{12,8},{0,12},{5,1},{9,5},{13,9},{1,13},{6,2},{10,6},{... | collective-permute-start | bytes 1179656 | tf_op jit(solution)/shard_map/ppermute | solution.py:52
  200.1 13.5 %collective-permute-start.33 = (bf16[128,1536]{1,0:T(8,128)(2,1)}, bf16[128,1536]{1,0:T(8,128)(2,1)}, u32[]{:S(2)}, u32[]{:S(2)}) collective-permute-start(bf16[128,1536]{1,0:T(8,128)(2,1)} %multiply_convert_fusion.x0_ref.refs_0_), channel_id=1, source_target_pairs={{12,0},{0,4},{4,8},{8,12},{13,1},{1,5},{5,9},{9,13},{14,2},{2,6},{... | collective-permute-start | bytes 1179656 | tf_op jit(solution)/shard_map/ppermute | solution.py:52
  212.7 13.2 %collective-permute-start.31 = (bf16[128,1536]{1,0:T(8,128)(2,1)}, bf16[128,1536]{1,0:T(8,128)(2,1)S(1)}, u32[]{:S(2)}, u32[]{:S(2)}) collective-permute-start(bf16[128,1536]{1,0:T(8,128)(2,1)} %multiply_convert_fusion.x0_ref.refs_0_), channel_id=1, source_target_pairs={{8,0},{12,4},{0,8},{4,12},{9,1},{13,5},{1,9},{5,13},{10,2},{14,6},... | collective-permute-start | bytes 1179656 | tf_op jit(solution)/shard_map/ppermute | solution.py:52
  213.6 12.3 %collective-permute-start.34 = (bf16[128,1536]{1,0:T(8,128)(2,1)}, bf16[128,1536]{1,0:T(8,128)(2,1)S(1)}, u32[]{:S(2)}, u32[]{:S(2)}) collective-permute-start(bf16[128,1536]{1,0:T(8,128)(2,1)} %collective-permute-done.33.x0_ref.refs_6_), channel_id=1, source_target_pairs={{0,2},{2,0},{1,3},{3,1},{4,6},{6,4},{5,7},{7,5},{8,10},{10,8},{9,1... | collective-permute-start | bytes 1179656 | tf_op jit(solution)/shard_map/ppermute | solution.py:56
  213.8 19.0 %collective-permute-start.27 = (bf16[128,1536]{1,0:T(8,128)(2,1)S(1)}, bf16[128,1536]{1,0:T(8,128)(2,1)S(1)}, u32[]{:S(2)}, u32[]{:S(2)}) collective-permute-start(bf16[128,1536]{1,0:T(8,128)(2,1)S(1)} %get-tuple-element.163), channel_id=1, source_target_pairs={{0,2},{2,0},{1,3},{3,1},{4,6},{6,4},{5,7},{7,5},{8,10},{10,8},{9,1... | collective-permute-start | bytes 1179656 | tf_op jit(solution)/shard_map/ppermute | solution.py:56
  221.3 17.9 %collective-permute-start.30 = (bf16[128,1536]{1,0:T(8,128)(2,1)S(1)}, bf16[128,1536]{1,0:T(8,128)(2,1)S(1)}, u32[]{:S(2)}, u32[]{:S(2)}) collective-permute-start(bf16[128,1536]{1,0:T(8,128)(2,1)S(1)} %get-tuple-element.168), channel_id=1, source_target_pairs={{0,2},{2,0},{1,3},{3,1},{4,6},{6,4},{5,7},{7,5},{8,10},{10,8},{9,1... | collective-permute-start | bytes 1179656 | tf_op jit(solution)/shard_map/ppermute | solution.py:56
  226.0 7.0 %collective-permute-start.32 = (bf16[128,1536]{1,0:T(8,128)(2,1)S(1)}, bf16[128,1536]{1,0:T(8,128)(2,1)S(1)}, u32[]{:S(2)}, u32[]{:S(2)}) collective-permute-start(bf16[128,1536]{1,0:T(8,128)(2,1)S(1)} %collective-permute-done.31.x0_ref.refs_4_), channel_id=1, source_target_pairs={{0,2},{2,0},{1,3},{3,1},{4,6},{6,4},{5,7},{7,5},{8,10},{10,8},{9,1... | collective-permute-start | bytes 1179656 | tf_op jit(solution)/shard_map/ppermute | solution.py:56
  232.3 7.0 %collective-permute-start.36 = (bf16[128,1536]{1,0:T(8,128)(2,1)S(1)}, bf16[128,1536]{1,0:T(8,128)(2,1)S(1)}, u32[]{:S(2)}, u32[]{:S(2)}) collective-permute-start(bf16[128,1536]{1,0:T(8,128)(2,1)S(1)} %get-tuple-element.182), channel_id=1, source_target_pairs={{0,2},{2,0},{1,3},{3,1},{4,6},{6,4},{5,7},{7,5},{8,10},{10,8},{9,1... | collective-permute-start | bytes 1179656 | tf_op jit(solution)/shard_map/ppermute | solution.py:56
  240.9 21.5 %collective-permute-start.39 = (bf16[128,1536]{1,0:T(8,128)(2,1)S(1)}, bf16[128,1536]{1,0:T(8,128)(2,1)S(1)}, u32[]{:S(2)}, u32[]{:S(2)}) collective-permute-start(bf16[128,1536]{1,0:T(8,128)(2,1)S(1)} %add_convert_fusion.9), channel_id=1, source_target_pairs={{4,0},{8,4},{12,8},{0,12},{5,1},{9,5},{13,9},{1,13},{6,2},{10,6},{... | collective-permute-start | bytes 1179656 | tf_op jit(solution)/shard_map/ppermute | solution.py:52
  242.8 19.7 %collective-permute-start.38 = (bf16[128,1536]{1,0:T(8,128)(2,1)S(1)}, bf16[128,1536]{1,0:T(8,128)(2,1)S(1)}, u32[]{:S(2)}, u32[]{:S(2)}) collective-permute-start(bf16[128,1536]{1,0:T(8,128)(2,1)S(1)} %add_convert_fusion.10), channel_id=1, source_target_pairs={{8,0},{12,4},{0,8},{4,12},{9,1},{13,5},{1,9},{5,13},{10,2},{14,6},... | collective-permute-start | bytes 1179656 | tf_op jit(solution)/shard_map/ppermute | solution.py:52
  243.0 20.3 %collective-permute-start.37 = (bf16[128,1536]{1,0:T(8,128)(2,1)S(1)}, bf16[128,1536]{1,0:T(8,128)(2,1)S(1)}, u32[]{:S(2)}, u32[]{:S(2)}) collective-permute-start(bf16[128,1536]{1,0:T(8,128)(2,1)S(1)} %add_convert_fusion.11), channel_id=1, source_target_pairs={{12,0},{0,4},{4,8},{8,12},{13,1},{1,5},{5,9},{9,13},{14,2},{2,6},{... | collective-permute-start | bytes 1179656 | tf_op jit(solution)/shard_map/ppermute | solution.py:52
  269.7 9.2 %collective-permute-start.47 = (bf16[128,1536]{1,0:T(8,128)(2,1)S(1)}, bf16[128,1536]{1,0:T(8,128)(2,1)S(1)}, u32[]{:S(2)}, u32[]{:S(2)}) collective-permute-start(bf16[128,1536]{1,0:T(8,128)(2,1)S(1)} %get-tuple-element.202), channel_id=1, source_target_pairs={{0,2},{2,0},{1,3},{3,1},{4,6},{6,4},{5,7},{7,5},{8,10},{10,8},{9,1... | collective-permute-start | bytes 1179656 | tf_op jit(solution)/shard_map/ppermute | solution.py:56
  269.8 24.0 %collective-permute-start.40 = (bf16[128,1536]{1,0:T(8,128)(2,1)S(1)}, bf16[128,1536]{1,0:T(8,128)(2,1)S(1)}, u32[]{:S(2)}, u32[]{:S(2)}) collective-permute-start(bf16[128,1536]{1,0:T(8,128)(2,1)S(1)} %fusion.49.refs_0_), channel_id=1, source_target_pairs={{0,2},{2,0},{1,3},{3,1},{4,6},{6,4},{5,7},{7,5},{8,10},{10,8},{9,1... | collective-permute-start | bytes 1179656 | tf_op jit(solution)/shard_map/ppermute | solution.py:56
  270.3 12.2 %collective-permute-start.41 = (bf16[128,1536]{1,0:T(8,128)(2,1)S(1)}, bf16[128,1536]{1,0:T(8,128)(2,1)S(1)}, u32[]{:S(2)}, u32[]{:S(2)}) collective-permute-start(bf16[128,1536]{1,0:T(8,128)(2,1)S(1)} %fusion.49.refs_0_), channel_id=1, source_target_pairs={{4,0},{8,4},{12,8},{0,12},{5,1},{9,5},{13,9},{1,13},{6,2},{10,6},{... | collective-permute-start | bytes 1179656 | tf_op jit(solution)/shard_map/ppermute | solution.py:52
  272.2 13.6 %collective-permute-start.43 = (bf16[128,1536]{1,0:T(8,128)(2,1)S(1)}, bf16[128,1536]{1,0:T(8,128)(2,1)S(1)}, u32[]{:S(2)}, u32[]{:S(2)}) collective-permute-start(bf16[128,1536]{1,0:T(8,128)(2,1)S(1)} %fusion.49.refs_0_), channel_id=1, source_target_pairs={{8,0},{12,4},{0,8},{4,12},{9,1},{13,5},{1,9},{5,13},{10,2},{14,6},... | collective-permute-start | bytes 1179656 | tf_op jit(solution)/shard_map/ppermute | solution.py:52
  274.3 18.7 %collective-permute-start.45 = (bf16[128,1536]{1,0:T(8,128)(2,1)S(1)}, bf16[128,1536]{1,0:T(8,128)(2,1)S(1)}, u32[]{:S(2)}, u32[]{:S(2)}) collective-permute-start(bf16[128,1536]{1,0:T(8,128)(2,1)S(1)} %fusion.49.refs_0_), channel_id=1, source_target_pairs={{12,0},{0,4},{4,8},{8,12},{13,1},{1,5},{5,9},{9,13},{14,2},{2,6},{... | collective-permute-start | bytes 1179656 | tf_op jit(solution)/shard_map/ppermute | solution.py:52
  280.7 12.3 %collective-permute-start.49 = (bf16[128,1536]{1,0:T(8,128)(2,1)S(1)}, bf16[128,1536]{1,0:T(8,128)(2,1)S(1)}, u32[]{:S(2)}, u32[]{:S(2)}) collective-permute-start(bf16[128,1536]{1,0:T(8,128)(2,1)S(1)} %get-tuple-element.208), channel_id=1, source_target_pairs={{0,2},{2,0},{1,3},{3,1},{4,6},{6,4},{5,7},{7,5},{8,10},{10,8},{9,1... | collective-permute-start | bytes 1179656 | tf_op jit(solution)/shard_map/ppermute | solution.py:56
  282.5 11.1 %collective-permute-start.50 = (bf16[128,1536]{1,0:T(8,128)(2,1)S(1)}, bf16[128,1536]{1,0:T(8,128)(2,1)S(1)}, u32[]{:S(2)}, u32[]{:S(2)}) collective-permute-start(bf16[128,1536]{1,0:T(8,128)(2,1)S(1)} %get-tuple-element.211), channel_id=1, source_target_pairs={{0,2},{2,0},{1,3},{3,1},{4,6},{6,4},{5,7},{7,5},{8,10},{10,8},{9,1... | collective-permute-start | bytes 1179656 | tf_op jit(solution)/shard_map/ppermute | solution.py:56
  285.7 8.0 %collective-permute-start.42 = (bf16[128,1536]{1,0:T(8,128)(2,1)S(1)}, bf16[128,1536]{1,0:T(8,128)(2,1)S(1)}, u32[]{:S(2)}, u32[]{:S(2)}) collective-permute-start(bf16[128,1536]{1,0:T(8,128)(2,1)S(1)} %collective-permute-done.41.refs_2_), channel_id=1, source_target_pairs={{0,2},{2,0},{1,3},{3,1},{4,6},{6,4},{5,7},{7,5},{8,10},{10,8},{9,1... | collective-permute-start | bytes 1179656 | tf_op jit(solution)/shard_map/ppermute | solution.py:56
  296.2 45.1 %collective-permute-start.53 = (bf16[128,1536]{1,0:T(8,128)(2,1)S(1)}, bf16[128,1536]{1,0:T(8,128)(2,1)S(1)}, u32[]{:S(2)}, u32[]{:S(2)}) collective-permute-start(bf16[128,1536]{1,0:T(8,128)(2,1)S(1)} %add_convert_fusion.5), channel_id=1, source_target_pairs={{4,0},{8,4},{12,8},{0,12},{5,1},{9,5},{13,9},{1,13},{6,2},{10,6},{... | collective-permute-start | bytes 1179656 | tf_op jit(solution)/shard_map/ppermute | solution.py:52
  297.4 49.0 %collective-permute-start.52 = (bf16[128,1536]{1,0:T(8,128)(2,1)S(1)}, bf16[128,1536]{1,0:T(8,128)(2,1)S(1)}, u32[]{:S(2)}, u32[]{:S(2)}) collective-permute-start(bf16[128,1536]{1,0:T(8,128)(2,1)S(1)} %add_convert_fusion.6), channel_id=1, source_target_pairs={{8,0},{12,4},{0,8},{4,12},{9,1},{13,5},{1,9},{5,13},{10,2},{14,6},... | collective-permute-start | bytes 1179656 | tf_op jit(solution)/shard_map/ppermute | solution.py:52
  299.0 50.7 %collective-permute-start.51 = (bf16[128,1536]{1,0:T(8,128)(2,1)S(1)}, bf16[128,1536]{1,0:T(8,128)(2,1)S(1)}, u32[]{:S(2)}, u32[]{:S(2)}) collective-permute-start(bf16[128,1536]{1,0:T(8,128)(2,1)S(1)} %add_convert_fusion.7), channel_id=1, source_target_pairs={{12,0},{0,4},{4,8},{8,12},{13,1},{1,5},{5,9},{9,13},{14,2},{2,6},{... | collective-permute-start | bytes 1179656 | tf_op jit(solution)/shard_map/ppermute | solution.py:52
  325.7 46.1 %collective-permute-start.54 = (bf16[8,128,128]{2,1,0:T(8,128)(2,1)}, bf16[8,128,128]{2,1,0:T(8,128)(2,1)S(1)}, u32[]{:S(2)}, u32[]{:S(2)}) collective-permute-start(bf16[8,128,128]{2,1,0:T(8,128)(2,1)} %get-tuple-element.284), channel_id=1, source_target_pairs={{16,0},{17,1},{32,16},{33,17},{48,32},{49,33},{64,48},{65,49},{80,... | collective-permute-start | bytes 786440 | tf_op jit(solution)/shard_map/ppermute | solution.py:66
  328.4 43.3 %collective-permute-start.55 = (bf16[8,128,128]{2,1,0:T(8,128)(2,1)}, bf16[8,128,128]{2,1,0:T(8,128)(2,1)}, u32[]{:S(2)}, u32[]{:S(2)}) collective-permute-start(bf16[8,128,128]{2,1,0:T(8,128)(2,1)} %get-tuple-element.282), channel_id=1, source_target_pairs={{16,1},{17,0},{32,17},{33,16},{48,33},{49,32},{64,49},{65,48},{80,... | collective-permute-start | bytes 786440 | tf_op jit(solution)/shard_map/ppermute | solution.py:66
  332.4 40.8 %all-to-all-start.3 = ((bf16[16,96,192]{2,1,0:T(8,128)(2,1)}), bf16[16,96,192]{2,1,0:T(8,128)(2,1)}, u32[]{:S(2)}, u32[]{:S(2)}) async-start(bf16[16,96,192]{2,1,0:T(8,128)(2,1)} %shard_map.256), calls=%async_computation.3 | async-start | bytes 1572864 | tf_op jit(solution)/shard_map/all_to_all | solution.py:70
  341.3 30.4 %collective-permute-start.56 = (bf16[8,128,128]{2,1,0:T(8,128)(2,1)}, bf16[8,128,128]{2,1,0:T(8,128)(2,1)S(1)}, u32[]{:S(2)}, u32[]{:S(2)}) collective-permute-start(bf16[8,128,128]{2,1,0:T(8,128)(2,1)} %get-tuple-element.283), channel_id=1, source_target_pairs={{32,0},{33,1},{48,16},{49,17},{64,32},{65,33},{80,48},{81,49},{96,... | collective-permute-start | bytes 786440 | tf_op jit(solution)/shard_map/ppermute | solution.py:66
  346.4 26.1 %collective-permute-start.57 = (bf16[8,128,128]{2,1,0:T(8,128)(2,1)}, bf16[8,128,128]{2,1,0:T(8,128)(2,1)S(1)}, u32[]{:S(2)}, u32[]{:S(2)}) collective-permute-start(bf16[8,128,128]{2,1,0:T(8,128)(2,1)} %get-tuple-element.281), channel_id=1, source_target_pairs={{32,1},{33,0},{48,17},{49,16},{64,33},{65,32},{80,49},{81,48},{96,... | collective-permute-start | bytes 786440 | tf_op jit(solution)/shard_map/ppermute | solution.py:66
  373.2 8.2 %collective-permute-start.58 = (bf16[8,128,128]{2,1,0:T(8,128)(2,1)}, bf16[8,128,128]{2,1,0:T(8,128)(2,1)}, u32[]{:S(2)}, u32[]{:S(2)}) collective-permute-start(bf16[8,128,128]{2,1,0:T(8,128)(2,1)} %bitcast.95), channel_id=1, source_target_pairs={{0,1},{1,0},{2,3},{3,2},{4,5},{5,4},{6,7},{7,6},{8,9},{9,8},{10,11... | collective-permute-start | bytes 786440 | tf_op jit(solution)/shard_map/ppermute | solution.py:56
  392.0 10.3 %collective-permute-start.59 = (bf16[128,1536]{1,0:T(8,128)(2,1)}, bf16[128,1536]{1,0:T(8,128)(2,1)}, u32[]{:S(2)}, u32[]{:S(2)}) collective-permute-start(bf16[128,1536]{1,0:T(8,128)(2,1)} %get-tuple-element.236), channel_id=1, source_target_pairs={{0,2},{2,0},{1,3},{3,1},{4,6},{6,4},{5,7},{7,5},{8,10},{10,8},{9,1... | collective-permute-start | bytes 1179656 | tf_op jit(solution)/shard_map/ppermute | solution.py:56
  392.0 11.5 %collective-permute-start.60 = (bf16[128,1536]{1,0:T(8,128)(2,1)}, bf16[128,1536]{1,0:T(8,128)(2,1)}, u32[]{:S(2)}, u32[]{:S(2)}) collective-permute-start(bf16[128,1536]{1,0:T(8,128)(2,1)} %get-tuple-element.238), channel_id=1, source_target_pairs={{0,2},{2,0},{1,3},{3,1},{4,6},{6,4},{5,7},{7,5},{8,10},{10,8},{9,1... | collective-permute-start | bytes 1179656 | tf_op jit(solution)/shard_map/ppermute | solution.py:56
  398.7 6.2 %collective-permute-start.62 = (bf16[128,1536]{1,0:T(8,128)(2,1)}, bf16[128,1536]{1,0:T(8,128)(2,1)S(1)}, u32[]{:S(2)}, u32[]{:S(2)}) collective-permute-start(bf16[128,1536]{1,0:T(8,128)(2,1)} %get-tuple-element.242), channel_id=1, source_target_pairs={{0,2},{2,0},{1,3},{3,1},{4,6},{6,4},{5,7},{7,5},{8,10},{10,8},{9,1... | collective-permute-start | bytes 1179656 | tf_op jit(solution)/shard_map/ppermute | solution.py:56
  405.0 20.1 %collective-permute-start.65 = (bf16[128,1536]{1,0:T(8,128)(2,1)S(1)}, bf16[128,1536]{1,0:T(8,128)(2,1)S(1)}, u32[]{:S(2)}, u32[]{:S(2)}) collective-permute-start(bf16[128,1536]{1,0:T(8,128)(2,1)S(1)} %add_convert_fusion), channel_id=1, source_target_pairs={{4,0},{8,4},{12,8},{0,12},{5,1},{9,5},{13,9},{1,13},{6,2},{10,6},{... | collective-permute-start | bytes 1179656 | tf_op jit(solution)/shard_map/ppermute | solution.py:52
  408.1 17.0 %collective-permute-start.64 = (bf16[128,1536]{1,0:T(8,128)(2,1)S(1)}, bf16[128,1536]{1,0:T(8,128)(2,1)S(1)}, u32[]{:S(2)}, u32[]{:S(2)}) collective-permute-start(bf16[128,1536]{1,0:T(8,128)(2,1)S(1)} %add_convert_fusion.1), channel_id=1, source_target_pairs={{8,0},{12,4},{0,8},{4,12},{9,1},{13,5},{1,9},{5,13},{10,2},{14,6},... | collective-permute-start | bytes 1179656 | tf_op jit(solution)/shard_map/ppermute | solution.py:52
  408.8 20.0 %collective-permute-start.63 = (bf16[128,1536]{1,0:T(8,128)(2,1)S(1)}, bf16[128,1536]{1,0:T(8,128)(2,1)S(1)}, u32[]{:S(2)}, u32[]{:S(2)}) collective-permute-start(bf16[128,1536]{1,0:T(8,128)(2,1)S(1)} %add_convert_fusion.2), channel_id=1, source_target_pairs={{12,0},{0,4},{4,8},{8,12},{13,1},{1,5},{5,9},{9,13},{14,2},{2,6},{... | collective-permute-start | bytes 1179656 | tf_op jit(solution)/shard_map/ppermute | solution.py:52
  432.6 14.7 %all-to-all-start.4 = ((bf16[8,24,1392]{2,1,0:T(8,128)(2,1)}), bf16[8,24,1392]{2,1,0:T(8,128)(2,1)}, u32[]{:S(2)}, u32[]{:S(2)}) async-start(bf16[8,24,1392]{2,1,0:T(8,128)(2,1)} %pad_maximum_fusion), calls=%async_computation.5 | async-start | bytes 1081344 | tf_op jit(solution)/shard_map/all_to_all | solution.py:70
  451.7 30.9 %all-to-all-start.5 = ((bf16[128,12,384]{2,1,0:T(8,128)(2,1)}), bf16[128,12,384]{2,1,0:T(8,128)(2,1)S(1)}, u32[]{:S(2)}, u32[]{:S(2)}) async-start(bf16[128,12,384]{2,1,0:T(8,128)(2,1)} %maximum_maximum_fusion), calls=%async_computation.6 | async-start | bytes 3145728 | tf_op jit(solution)/shard_map/all_to_all | solution.py:70
  459.6 16.6 %collective-permute-start.66 = (bf16[4,24,96]{2,1,0:T(8,128)(2,1)S(1)}, bf16[4,24,96]{2,1,0:T(8,128)(2,1)S(1)}, u32[]{:S(2)}, u32[]{:S(2)}) collective-permute-start(bf16[4,24,96]{2,1,0:T(8,128)(2,1)S(1)} %broadcast_select_fusion), channel_id=1, source_target_pairs={{0,1},{1,0},{2,3},{3,2},{4,5},{5,4},{6,7},{7,6},{8,9},{9,8},{10,11... | collective-permute-start | bytes 55304 | tf_op jit(solution)/shard_map/ppermute | solution.py:56
  (146 other events, 1233.5 us)
Sparse Core Ops, SparseCore 0:
  32.3 79.4 all-gather.4
  114.0 71.8 all-gather.2
  264.5 100.3 reduce-scatter.1

commit v4 on v3

--- a/solution.py
+++ b/solution.py
@@ -108,6 +108,13 @@
     return pl.CostEstimate(flops=int(flops), bytes_accessed=int(moved), transcendentals=int(exps))
 
 
+def all_of(*shape):
+    return pl.BlockSpec(shape, lambda *i: (0,) * len(shape))
+
+
+ROWS_OF = pl.BlockSpec((ROWS, WIDTH), lambda *i: (0, 0))
+
+
 def stacked(a_ref, b_ref):
     return jnp.concatenate([a_ref[...], b_ref[...]], axis=0)
 
@@ -164,7 +171,18 @@
             jax.ShapeDtypeStruct((8, ROWS, 2 * HEAD), BF16),
             jax.ShapeDtypeStruct((4, PAIR, 4 * HEAD), F32),
         ),
-        compiler_params=params(0, 24),
+        grid=(1,),
+        in_specs=[ROWS_OF] * 8
+        + [all_of(WIDTH, 384), all_of(1, WIDTH)]
+        + [all_of(4, PAIR, 2 * HEAD)] * 2
+        + [all_of(1, 4 * HEAD)],
+        out_specs=(
+            all_of(4 * PAIR, WIDTH),
+            all_of(8, ROWS, QUERY),
+            all_of(8, ROWS, 2 * HEAD),
+            all_of(4, PAIR, 4 * HEAD),
+        ),
+        compiler_params=params(1, 40),
         cost_estimate=cost(8 * PAIR * WIDTH * 384, 1e7),
     )(*xs, w, gain, cos, sin, head_gain)
 
@@ -178,7 +196,7 @@
     for i in range(2):
         tiles = slice(2 * i, 2 * i + 2)
         gq = gq_ref[tiles].reshape(PAIR, 4 * HEAD).astype(F32)
-        gkv = g_refs[0][tiles]
+        gkv = g_refs[0][tiles].astype(F32)
         for ref in g_refs[1:]:
             gkv = gkv + ref[tiles].astype(F32)
         gkv = gkv.reshape(PAIR, 2 * HEAD)
@@ -206,13 +224,9 @@
 
 
 def unproject(half, gq, gkvs, raw, xs, w, cos, sin, head_gain):
-    def whole_of(*shape):
-        return pl.BlockSpec(shape, lambda i: (0,) * len(shape))
-
     def at_half(*shape):
         return pl.BlockSpec(shape, lambda i: (half,) + (0,) * (len(shape) - 1))
 
-    rows = whole_of(ROWS, WIDTH)
     table = at_half(2, PAIR, 2 * HEAD)
     outs = (jax.ShapeDtypeStruct((ROWS, WIDTH), BF16),) * 4 + (
         jax.ShapeDtypeStruct((2 * PAIR, 6 * HEAD), BF16),
@@ -226,16 +240,17 @@
         in_specs=[at_half(4, ROWS, 4 * HEAD)]
         + [at_half(4, ROWS, 2 * HEAD)] * 6
         + [at_half(2, PAIR, 4 * HEAD)]
-        + [rows] * 4
-        + [whole_of(WIDTH, 6 * HEAD), table, table, whole_of(1, 4 * HEAD)],
-        out_specs=tuple(whole_of(*o.shape) for o in outs),
-        compiler_params=params(1, 24),
+        + [ROWS_OF] * 4
+        + [all_of(WIDTH, 6 * HEAD), table, table, all_of(1, 4 * HEAD)],
+        out_specs=tuple(all_of(*o.shape) for o in outs),
+        compiler_params=params(1, 28),
         cost_estimate=cost(4 * PAIR * WIDTH * 384, 8e6),
     )(gq, *gkvs, raw, *xs, w, cos, sin, head_gain)
 
 
 def ffn_kernel(
-    x0_ref, x1_ref, c0_ref, c1_ref, gu_w_ref, d_w_ref, part0_ref, part1_ref, act_ref, gu_ref, total
+    x0_ref, x1_ref, c0_ref, c1_ref, gu_w_ref, d_w_ref,
+    part0_ref, part1_ref, out0_ref, out1_ref, act_ref, gu_ref, total, out_total,
 ):
     y = pl.program_id(0)
     x = stacked(x0_ref, x1_ref)
@@ -244,7 +259,9 @@
     grad_act = dot(stacked(c0_ref, c1_ref), d_w_ref[0])
     sig = 1.0 / (1.0 + jnp.exp(-gate))
     silu = gate * sig
-    act_ref[0] = (silu * up).astype(BF16)
+    act = (silu * up).astype(BF16)
+    act_ref[0] = act
+    out_part = dot(act, d_w_ref[0], NT)
     grad_gate = grad_act * up * sig * (1.0 + gate * (1.0 - sig))
     grads = jnp.concatenate([grad_gate, grad_act * silu], axis=1).astype(BF16)
     gu_ref[0] = grads
@@ -253,69 +270,39 @@
     @pl.when(y == 0)
     def _():
         total[...] = part
+        out_total[...] = out_part
 
     @pl.when(y == 1)
     def _():
         whole_part = (total[...] + part).astype(BF16)
         part0_ref[...] = whole_part[:ROWS]
         part1_ref[...] = whole_part[ROWS:]
-
-
-def ffn(x0, x1, c0, c1, gu_w, d_w):
-    rows = pl.BlockSpec((ROWS, WIDTH), lambda y: (0, 0))
+        whole_part = (out_total[...] + out_part).astype(BF16)
+        out0_ref[...] = whole_part[:ROWS]
+        out1_ref[...] = whole_part[ROWS:]
+
+
+def ffn(x0, x1, c0, c1, w):
+    rows = ROWS_OF
     return pl.pallas_call(
         ffn_kernel,
-        out_shape=(
-            jax.ShapeDtypeStruct((ROWS, WIDTH), BF16),
-            jax.ShapeDtypeStruct((ROWS, WIDTH), BF16),
+        out_shape=(jax.ShapeDtypeStruct((ROWS, WIDTH), BF16),) * 4
+        + (
             jax.ShapeDtypeStruct((2, PAIR, PADDED), BF16),
             jax.ShapeDtypeStruct((2, PAIR, 2 * PADDED), BF16),
         ),
         grid=(2,),
         in_specs=[rows] * 4
-        + [pl.BlockSpec((1, WIDTH, n * PADDED), lambda y: (y, 0, 0)) for n in (2, 1)],
-        out_specs=(
-            rows,
-            rows,
+        + [pl.BlockSpec((1, WIDTH, n * PADDED), lambda y, c=c: (y, 0, c)) for n, c in ((2, 0), (1, 2))],
+        out_specs=(rows,) * 4
+        + (
             pl.BlockSpec((1, PAIR, PADDED), lambda y: (y, 0, 0)),
             pl.BlockSpec((1, PAIR, 2 * PADDED), lambda y: (y, 0, 0)),
         ),
-        scratch_shapes=[pltpu.VMEM((PAIR, WIDTH), F32)],
+        scratch_shapes=[pltpu.VMEM((PAIR, WIDTH), F32)] * 2,
         compiler_params=params(1, 32),
-        cost_estimate=cost(2 * 2 * PAIR * WIDTH * 5 * PADDED, 14e6),
-    )(x0, x1, c0, c1, gu_w, d_w)
-
-
-def down_kernel(act_ref, w_ref, part0_ref, part1_ref, total):
-    y = pl.program_id(0)
-    part = dot(act_ref[0], w_ref[0], NT)
-
-    @pl.when(y == 0)
-    def _():
-        total[...] = part
-
-    @pl.when(y == 1)
-    def _():
-        whole_part = (total[...] + part).astype(BF16)
-        part0_ref[...] = whole_part[:ROWS]
-        part1_ref[...] = whole_part[ROWS:]
-
-
-def down(act, w):
-    rows = pl.BlockSpec((ROWS, WIDTH), lambda y: (0, 0))
-    return pl.pallas_call(
-        down_kernel,
-        out_shape=(jax.ShapeDtypeStruct((ROWS, WIDTH), BF16),) * 2,
-        grid=(2,),
-        in_specs=[
-            pl.BlockSpec((1, PAIR, PADDED), lambda y: (y, 0, 0)),
-            pl.BlockSpec((1, WIDTH, PADDED), lambda y: (y, 0, 0)),
-        ],
-        out_specs=(rows, rows),
-        scratch_shapes=[pltpu.VMEM((PAIR, WIDTH), F32)],
-        compiler_params=params(1, 24),
-        cost_estimate=cost(2 * 2 * PAIR * WIDTH * PADDED, 5e6),
-    )(act, w)
+        cost_estimate=cost(2 * 2 * PAIR * WIDTH * 6 * PADDED, 14e6),
+    )(x0, x1, c0, c1, w, w)
 
 
 def ffn_weights_kernel(*refs):
@@ -383,26 +370,47 @@
 
 
 def out_weights_kernel(mix_ref, *refs):
-    branches, (out_ref, total) = refs[:8], refs[8:]
-    grad = 0.0
-    for d in range(4):
-        mix = mix_ref[2 * d : 2 * d + 2].reshape(PAIR, QUERY)
-        grad = grad + dot(mix, stacked(*branches[2 * d : 2 * d + 2]), TN)
-    total[...] = grad
-    for half in (0, 1):
-        for s in range(8):
-            piece = total[half * 96 : half * 96 + 96, s * 192 : s * 192 + 192]
-            out_ref[half * 8 + s] = piece.astype(BF16)
+    branch = jnp.concatenate([b[...] for b in refs[:8]], axis=0)
+    refs[8][...] = dot(branch, mix_ref[...].reshape(8 * ROWS, QUERY), TN)
 
 
 def out_weights(mix, branches):
     return pl.pallas_call(
         out_weights_kernel,
-        out_shape=jax.ShapeDtypeStruct((16, 96, 192), BF16),
-        scratch_shapes=[pltpu.VMEM((QUERY, WIDTH), F32)],
+        out_shape=jax.ShapeDtypeStruct((WIDTH, QUERY), F32),
         compiler_params=params(0, 24),
         cost_estimate=cost(2 * 1024 * WIDTH * QUERY, 4e6),
     )(mix, *branches)
+
+
+def pack_kernel(normed_ref, graw0_ref, graw1_ref, gains_ref, out_grad_ref, sent_ref):
+    graw = jnp.concatenate([graw0_ref[...], graw1_ref[...]], axis=0)
+    grad = dot(normed_ref[...], graw, TN)
+    gains = gains_ref[...]
+    high = gains.astype(BF16).astype(F32)
+    gains = jnp.concatenate([high, gains - high, jnp.zeros((HEAD - 32, gains.shape[1]), F32)], axis=0)
+    sent_ref[:, : 5 * HEAD] = grad[:, : 5 * HEAD].astype(BF16)
+    sent_ref[:, 5 * HEAD : 6 * HEAD] = gains.T.astype(BF16)
+    sent_ref[:, 6 * HEAD :] = out_grad_ref[...].astype(BF16)
+
+
+def pack(normed, graws, gains, out_grad):
+    tall = 256
+    return pl.pallas_call(
+        pack_kernel,
+        out_shape=jax.ShapeDtypeStruct((WIDTH, 9 * HEAD), BF16),
+        grid=(WIDTH // tall,),
+        in_specs=[
+            pl.BlockSpec((8 * ROWS, tall), lambda m: (0, m)),
+            all_of(4 * ROWS, 6 * HEAD),
+            all_of(4 * ROWS, 6 * HEAD),
+            pl.BlockSpec((16, tall), lambda m: (0, m)),
+            pl.BlockSpec((tall, QUERY), lambda m: (m, 0)),
+        ],
+        out_specs=pl.BlockSpec((tall, 9 * HEAD), lambda m: (m, 0)),
+        compiler_params=params(1, 24),
+        cost_estimate=cost(2 * 1024 * WIDTH * 384, 8e6),
+    )(normed, *graws, gains, out_grad)
 
 
 def side_by_side(t):
@@ -488,7 +496,12 @@
     lse_ref[0] = jnp.log2(total)
 
 
-def back_body(at, base, plan, q_ref, start_ref, g_ref, out_ref, lse_ref, kv, kvt, dkv, dqt):
+def back_kernel(plan, q_ref, start_ref, *refs):
+    kv_refs, (g_ref, out_ref, lse_ref, dq_ref), sent_refs, (kv, kvt, dkv) = (
+        refs[:6], refs[6:10], refs[10:16], refs[16:],
+    )
+    line_up(plan, kv_refs, kv, kvt)
+
     @pl.when(pl.program_id(0) == 0)
     def _():
         dkv[...] = jnp.zeros_like(dkv)
@@ -513,37 +526,14 @@
         dkv[rows_of(j), :] += dot(sides, both)
         return dqt + dot(kvt[HEAD:, rows_of(j)], grads)
 
-    return key_loops(plan, at, base, start_ref[0], visit, dqt)
-
-
-def hand_out(plan, supers, dkv, mine_ref, theirs_ref):
+    dqt = key_loops(plan, 11, 0, start_ref[0], visit, jnp.zeros((HEAD, LANES), F32))
+    dq = on_top(dqt * HEAD**-0.5).T
+    dq_ref[0] = jnp.concatenate([dq, jnp.zeros((ROWS, HEAD), F32)], axis=1).astype(BF16)
+
     @pl.when(pl.program_id(0) == 7)
     def _():
-        for b, half, place, sent in chunks(plan, supers):
-            ref = (mine_ref, theirs_ref)[half]
-            ref[b, sent] = dkv[pl.ds(place, ROWS), :].astype(ref.dtype)
-
-
-def back_earlier_kernel(plan, q_ref, start_ref, *refs):
-    kv_refs, (g_ref, out_ref, lse_ref, dqt_ref, mine_ref, theirs_ref, kv, kvt, dkv) = refs[:4], refs[4:]
-    line_up(plan, kv_refs, kv, kvt)
-    dqt = jnp.zeros((HEAD, LANES), F32)
-    dqt_ref[0] = back_body(
-        2, 0, plan, q_ref, start_ref, g_ref, out_ref, lse_ref, kv, kvt, dkv, dqt
-    )
-    hand_out(plan, 2, dkv, mine_ref, theirs_ref)
-
-
-def back_own_kernel(plan, q_ref, start_ref, *refs):
-    kv_refs, (g_ref, out_ref, lse_ref, dqt_ref) = refs[:2], refs[2:6]
-    dq_ref, mine_ref, theirs_ref, kv, kvt, dkv = refs[6:]
-    line_up(plan, kv_refs, kv, kvt)
-    dqt = back_body(
-        6, EARLIER, plan, q_ref, start_ref, g_ref, out_ref, lse_ref, kv, kvt, dkv, dqt_ref[0]
-    )
-    dq = on_top(dqt * HEAD**-0.5).T
-    dq_ref[0] = jnp.concatenate([dq, jnp.zeros((ROWS, HEAD), F32)], axis=1).astype(BF16)
-    hand_out(plan, 1, dkv, mine_ref, theirs_ref)
+        for b, half, place, sent in chunks(plan, 3):
+            sent_refs[2 * b + half][sent] = dkv[pl.ds(place, ROWS), :].astype(BF16)
 
 
 def whole(*shape):
@@ -596,28 +586,18 @@
     return call(plan, q, start, *kvs, *state)
 
 
-def sent_back(supers):
-    shape = (supers, 8, ROWS, 2 * HEAD)
-    return [jax.ShapeDtypeStruct(shape, F32), jax.ShapeDtypeStruct(shape, BF16)], [whole(*shape)] * 2
-
-
-def back_earlier(plan, q, start, kvs, grad, out, lse):
-    shapes, specs = sent_back(2)
+def back(plan, q, start, kvs, grad, out, lse):
+    sent = jax.ShapeDtypeStruct((8, ROWS, 2 * HEAD), BF16)
     call = tiles_call(
-        back_earlier_kernel, 2, [TILE_T] + shapes, [placed(ROWS, QUERY)] + STATE,
-        [tile(HEAD, LANES)] + specs, 20e9, True,
+        back_kernel,
+        3,
+        [jax.ShapeDtypeStruct((8, ROWS, 4 * HEAD), BF16)] + [sent] * 6,
+        [placed(ROWS, QUERY)] + STATE,
+        [placed(ROWS, 4 * HEAD)] + [whole(*sent.shape)] * 6,
+        30e9,
+        True,
     )
     return call(plan, q, start, *kvs, grad, out, lse)
-
-
-def back_own(plan, q, start, kvs, grad, out, lse, dqt):
-    shapes, specs = sent_back(1)
-    dq = jax.ShapeDtypeStruct((8, ROWS, 4 * HEAD), BF16)
-    call = tiles_call(
-        back_own_kernel, 1, [dq] + shapes, [placed(ROWS, QUERY)] + STATE + [tile(HEAD, LANES)],
-        [placed(ROWS, 4 * HEAD)] + specs, 10e9, True,
-    )
-    return call(plan, q, start, *kvs, grad, out, lse, dqt)
 
 
 def after(v, *others):
@@ -643,7 +623,9 @@
     ylo, z, x, core, yhi = (lax.axis_index(a) for a in ALL)
     sup = ylo * 4 + z
 
-    token_blocks = near_gather(tokens)
+    token_shifts = [shift_x(tokens, d) for d in (1, 2, 3)]
+    token_blocks = [[b, swap(b, "core")] for b in [tokens] + token_shifts]
+    all_tokens = [b for p in token_blocks for b in p]
     qkv_own = jnp.concatenate(
         [
             w_query.reshape(12, 8, QUERY),
@@ -666,13 +648,13 @@
         axis=-1,
     )
     rows = exchange(rows_own, NEAR)
-    gu_rows = rows[:, :, : 2 * PADDED].reshape(192, 2 * PADDED)
-    d_rows = rows[:, :, 2 * PADDED : 3 * PADDED].reshape(192, PADDED)
-    d_full = lax.all_gather(d_rows, WIDE, axis=0, tiled=True).reshape(2, WIDTH, PADDED)
+    ffn_rows = rows[:, :, : 3 * PADDED].reshape(192, 3 * PADDED)
     out_rows = rows[:, :, 3 * PADDED : 3 * PADDED + QUERY].reshape(1, 192, QUERY)
     qkv_rows = rows[:, :12, 3 * PADDED + QUERY :].reshape(1, 96, 6 * HEAD)
     qkv = exchange(jnp.broadcast_to(qkv_rows, (16, 96, 6 * HEAD)), WIDE)
     qkv = jnp.transpose(qkv.reshape(2, 8, 8, 12, 6 * HEAD), (1, 2, 0, 3, 4)).reshape(WIDTH, 6 * HEAD)
+    qkv, ffn_rows = lax.optimization_barrier((qkv, ffn_rows))
+    ffn_full = lax.all_gather(ffn_rows, WIDE, axis=0, tiled=True).reshape(2, WIDTH, 3 * PADDED)
     gain_attn = qkv[:, 5 * HEAD].astype(F32)
     gain_ffn = qkv[:, 5 * HEAD + 1].astype(F32)
 
@@ -704,26 +686,30 @@
         [first - window, relative]
         + [jnp.minimum(v, edge) for v in (lo, m1, m2, hi)]
         + [jnp.maximum(v - edge, 0) for v in (lo, m1, m2, hi)]
-        + [jnp.broadcast_to(yhi, (8,))],
+        + [jnp.broadcast_to(yhi, (8,)), lo, m1, m2, hi],
         axis=1,
     ).astype(jnp.int32)
     start_lanes = jnp.tile(own_starts - window, (1, GROUP)).reshape(8, 1, LANES)
 
     normed, rot_q, kv, raw = project(
-        [b for p in token_blocks for b in p], qkv, gain_attn[None], cos, sin, head_gain
+        all_tokens, qkv, gain_attn[None], cos, sin, head_gain
     )
 
     kv_own = [kv, swap(kv, "yhi")]
-    kv_earlier = [shift_super(kv, 2, 0), shift_super(kv, 2, 1), shift_super(kv, 1, 0), shift_super(kv, 1, 1)]
-    kv_earlier, gu_rows = lax.optimization_barrier((kv_earlier, gu_rows))
-    gu_full = lax.all_gather(gu_rows, WIDE, axis=0, tiled=True).reshape(2, WIDTH, 2 * PADDED)
+    kv_sent = after(kv, kv_own[1])
+    kv_earlier = [shift_super(kv_sent, a, b) for a, b in ((2, 0), (2, 1), (1, 0), (1, 1))]
     state = attend_own(plan, rot_q, start_lanes, kv_own)
-    out_both = exchange(jnp.broadcast_to(after(out_rows, kv_own[1]), (16, 192, QUERY)), WIDE)
+    state, kv_earlier, out_rows, cot_sent = lax.optimization_barrier(
+        (state, kv_earlier, out_rows, cotangent)
+    )
+    cot_shifts = [shift_x(cot_sent, d) for d in (1, 2, 3)]
+    out_both = exchange(jnp.broadcast_to(out_rows, (16, 192, QUERY)), WIDE)
     out_both = out_both.reshape(2, WIDTH, QUERY)
-    state, w_out_t = lax.optimization_barrier((state, jnp.where(x < 2, out_both[0], out_both[1])))
-    cot_blocks = near_gather(after(cotangent, kv))
     mix, out_tiles, lse = attend_earlier(plan, rot_q, start_lanes, kv_earlier, state)
-    mix, cot_blocks = lax.optimization_barrier((mix, cot_blocks))
+    w_out_t = jnp.where(x < 2, out_both[0], out_both[1])
+    mix, w_out_t, cot_shifts = lax.optimization_barrier((mix, w_out_t, cot_shifts))
+    cot_blocks = [[b, swap(b, "core")] for b in [cotangent] + cot_shifts]
+    all_cot = [b for p in cot_blocks for b in p]
 
     inputs = tokens.astype(F32)
     parts = [None] * 4
@@ -747,14 +733,18 @@
             blocks = after(blocks, ffn_outs[1][0])
         if d == 2:
             blocks = after(blocks, ffn_outs[3][0])
-        ffn_outs[d] = ffn(*blocks, *cot_blocks[d], gu_full, d_full)
-    acts, gus = [o[2] for o in ffn_outs], [o[3] for o in ffn_outs]
-    kept, gus = lax.optimization_barrier((near_keep([o[:2] for o in ffn_outs]), gus))
+        ffn_outs[d] = ffn(*blocks, *cot_blocks[d], ffn_full)
+    acts, gus = [o[4] for o in ffn_outs], [o[5] for o in ffn_outs]
+    kept, gus, out_own, out_other = lax.optimization_barrier(
+        (near_keep([o[:2] for o in ffn_outs]), gus, [o[2] for o in ffn_outs], [o[3] for o in ffn_outs])
+    )
+    out_kept = jnp.stack(out_own).astype(F32) + swap(jnp.stack(out_other), "core").astype(F32)
+    out_kept = out_kept.astype(BF16)
     pair_total = near_sum(kept)
     weight_grads = ffn_weights(
-        [b for p in ffn_blocks for b in p], [b for p in cot_blocks for b in p], gus, acts
-    )
-    pair_total, weight_grads = lax.optimization_barrier((pair_total, weight_grads))
+        [b for p in ffn_blocks for b in p], all_cot, gus, acts
+    )
+    pair_total, weight_grads, out_kept = lax.optimization_barrier((pair_total, weight_grads, out_kept))
     ffn_sum = lax.psum_scatter(
         weight_grads.reshape(2 * WIDTH, 3 * PART), WIDE, scatter_dimension=0, tiled=True
     )
@@ -764,88 +754,75 @@
     grad_branch = grad_hidden.astype(BF16)
     branches = [b for p in near_gather(grad_branch) for b in p]
     grad_mix = out_back(branches, w_out_t)
-
-    acts, grad_branch = lax.optimization_barrier((acts, grad_branch))
-    out_kept = near_keep([down(a, d_full) for a in acts])
-    grad_mix, out_kept = lax.optimization_barrier((grad_mix, out_kept))
-    grad_out = exchange(out_weights(mix, branches), WIDE)
-
-    dqt, mine, theirs = back_earlier(plan, rot_q, start_lanes, kv_earlier, grad_mix, out_tiles, lse)
-    mine = mine.astype(BF16)
-    sent = [
-        shift_super(mine[1], -1, 0),
-        shift_super(theirs[1], -1, 1),
-        shift_super(mine[0], -2, 0),
-        shift_super(theirs[0], -2, 1),
+    out_total = near_sum(after([out_kept[d] for d in range(4)], branches))
+
+    back_outs = back(plan, rot_q, start_lanes, kv_earlier + kv_own, grad_mix, out_tiles, lse)
+    back_outs, out_total = lax.optimization_barrier((back_outs, out_total))
+    grad_q, two_mine, two_theirs, one_mine, one_theirs, mine, theirs = back_outs
+    grad_kvs = [
+        mine,
+        swap(theirs, "yhi"),
+        shift_super(one_mine, -1, 0),
+        shift_super(one_theirs, -1, 1),
+        shift_super(two_mine, -2, 0),
+        shift_super(two_theirs, -2, 1),
     ]
-    out_total = near_sum(out_kept)
-    dqt, out_total = lax.optimization_barrier((dqt, out_total))
-    output = (hidden + out_total).astype(BF16)
-    grad_q, mine, theirs = back_own(
-        plan, rot_q, start_lanes, kv_own, grad_mix, out_tiles, lse, dqt
-    )
-    grad_q, mine, theirs, sent, grad_out = lax.optimization_barrier(
-        (grad_q, mine, theirs, sent, grad_out)
-    )
-    grad_kvs = [mine[0], swap(theirs[0], "yhi")] + sent
-    grad_out = jnp.sum(grad_out.astype(F32), axis=0).astype(BF16)
-    grad_out = jnp.transpose(grad_out.reshape(96, 8, 24), (1, 2, 0))
+
+    grad_out = out_weights(after(mix, grad_q), branches)
+    grad_kvs, grad_out = lax.optimization_barrier((grad_kvs, grad_out))
 
     unprojected = [None] * 2
     for half in (1, 0):
-        xs = [b for p in token_blocks[2 * half : 2 * half + 2] for b in p]
+        xs = all_tokens[4 * half : 4 * half + 4]
         unprojected[half] = unproject(half, grad_q, grad_kvs, raw, xs, qkv, cos, sin, head_gain)
-    kept = near_keep([u[2 * i : 2 * i + 2] for u in unprojected for i in (0, 1)])
-    kept, normed = lax.optimization_barrier((kept, normed))
-    grad_normed = near_sum(kept)
-    qkv_grad = dot(normed, jnp.concatenate([u[4] for u in unprojected], axis=0), TN)
-
-    last = jnp.concatenate([ffn_sum.reshape(8, 24, 3 * PART), grad_out], axis=-1)
-    last, qkv_grad = lax.optimization_barrier((exchange(last, NEAR), qkv_grad))
-
-    attn_gain_part = sum(u[5] for u in unprojected).reshape(128, 12, 1)
     head_part = sum(u[6] for u in unprojected)[0]
     q_gain_part = head_part[:HEAD] + head_part[HEAD : 2 * HEAD] + head_part[2 * HEAD : QUERY]
     head_part = jnp.concatenate([q_gain_part, head_part[QUERY:], jnp.zeros((4,), F32)])
     gain_parts = jnp.concatenate(
         [
-            attn_gain_part,
-            ffn_gain_part.reshape(128, 12, 1),
-            jnp.broadcast_to(head_part.reshape(1, 12, 11), (128, 12, 11)),
+            sum(u[5] for u in unprojected),
+            ffn_gain_part[None],
+            jnp.tile(head_part.reshape(12, 11).T, (1, 128)),
+            jnp.zeros((3, WIDTH), F32),
         ],
-        axis=2,
-    )
-    gain_high = gain_parts.astype(BF16)
-    gain_low = (gain_parts - gain_high.astype(F32)).astype(BF16)
-    qkv_grad = jnp.concatenate(
-        [
-            qkv_grad[:, : 5 * HEAD].astype(BF16).reshape(128, 12, 5 * HEAD),
-            gain_high,
-            gain_low,
-            jnp.zeros((128, 12, HEAD - 26), BF16),
-        ],
-        axis=2,
-    )
-    qkv_grad = exchange(qkv_grad, ALL).reshape(8, 8, 2, 12, 6 * HEAD).astype(F32)
-    qkv_grad = jnp.sum(qkv_grad, axis=(0, 2))
+        axis=0,
+    )
+    sent = pack(normed, [u[4] for u in unprojected], gain_parts, grad_out)
+    parts = [u[2 * i : 2 * i + 2] for u in unprojected for i in (0, 1)]
+    parts, sent = lax.optimization_barrier((parts, sent))
+    grad_normed = near_sum(near_keep(parts))
+    got = exchange(sent.reshape(8, 192, 9 * HEAD), ("ylo", "z"))
+    got = jnp.sum(got.astype(F32), axis=0).astype(BF16)
+    last = jnp.concatenate(
+        [ffn_sum.reshape(8, 24, 3 * PART), got.reshape(8, 24, 9 * HEAD)], axis=-1
+    )
+    last = exchange(last, NEAR)
+    ffn_grad, got = last[:, :, : 3 * PART], last[:, :, 3 * PART :].astype(F32)
+
+    qkv_grad, grad_out = got[:, :, : 6 * HEAD], got[:, :, 6 * HEAD :]
+    here, there = jnp.where(yhi == 0, 0, 1), jnp.where(yhi == 0, 1, 0)
+
+    def half_of(v, axis, which):
+        size = v.shape[axis] // 2
+        return lax.dynamic_slice_in_dim(v, which * size, size, axis)
+
+    qkv_other = swap(half_of(qkv_grad, 1, there).astype(BF16), "yhi").astype(F32)
+    out_other = swap(half_of(grad_out, 0, there).astype(BF16), "yhi").astype(F32)
+    qkv_grad = half_of(qkv_grad, 1, here) + qkv_other
+    grad_out = half_of(grad_out, 0, here) + out_other
     gains = jnp.sum(qkv_grad[:, :, 5 * HEAD :], axis=0)
-    gains = gains[:, :13] + gains[:, 13:26]
-    head_gains = gains[:, 2:].reshape(-1)
+    gains = gains[:, :16] + gains[:, 16:32]
+    head_gains = gains[:, 2:13].reshape(-1)
     qkv_grad = jnp.transpose(qkv_grad, (1, 0, 2))
+    w_out_grad = jnp.transpose(grad_out, (0, 2, 1)).reshape(768, 24)
     w_query_grad = qkv_grad[:, :, :QUERY].reshape(12, -1)
     w_key_grad = qkv_grad[:, :, QUERY : QUERY + HEAD].reshape(12, -1)
     w_value_grad = qkv_grad[:, :, QUERY + HEAD : QUERY + 2 * HEAD].reshape(12, -1)
 
+    output = (hidden + out_total).astype(BF16)
     scale_attn = rms_scale(inputs)
     input_grad = (grad_hidden + rms_back(grad_normed * gain_attn, inputs, scale_attn)).astype(BF16)
 
-    ffn_grad, grad_out = last[:, :, : 3 * PART], last[:, :, 3 * PART :].reshape(2, 4, 24, 96)
-    kept = jnp.where(yhi == 0, grad_out[0], grad_out[1])
-    got = swap(jnp.where(yhi == 0, grad_out[1], grad_out[0]), "yhi")
-    w_out_grad = jnp.stack(
-        [jnp.where(yhi == 0, kept, got), jnp.where(yhi == 0, got, kept)], axis=1
-    )
-    w_out_grad = jnp.transpose(w_out_grad, (0, 1, 3, 2)).reshape(768, 24).astype(F32)
     ffn_grad = jnp.transpose(ffn_grad, (1, 0, 2)).astype(F32)
     w_gate_grad, w_up_grad, w_down_grad = (
         ffn_grad[:, :, i * PART : (i + 1) * PART].reshape(24, -1) for i in range(3)

time: 502 us -> 490 us (0.976)
  local copies, waits for them, and re-layouts: 63.8 us -> 53.4 us
  waiting for transfers between devices: 128 us -> 138 us
  starting transfers between devices: 103 us -> 97.3 us
    ppermute x24, waiting for transfers between devices: 62.2 us -> 71.7 us  [shift_x(): return lax.ppermute(v, 'x', [((i + distance) % 4, i) for i in range(4)])]
    ppermute x35 -> x33, waiting for transfers between devices: 25.1 us -> 17.6 us  [swap(): return lax.ppermute(v, axis, [(0, 1), (1, 0)])]
    all_to_all x5 -> x4, starting transfers between devices: 35.8 us -> 29.2 us  [exchange(): return lax.all_to_all(v, axes, split_axis=0, concat_axis=0, tiled=True)]
    pallas_call x4, Pallas kernels: 25 us -> 30.4 us  [ffn(): pl.pallas_call(ffn_kernel, out_shape=(jax.ShapeDtypeStruct((ROWS, WIDTH),...]
    ppermute x8, waiting for transfers between devices: 18.1 us -> 23.3 us  [shift_super(): return lax.ppermute(v, ('ylo', 'z', 'yhi'), pairs)]
    pallas_call x7 -> x3, Pallas kernels: 50.2 us -> 45.8 us  [the longest x1 40.5 us: back(): return call(plan, q, start, *kvs, grad, out, lse)]
    all_to_all x5 -> x4, waiting for transfers between devices: 22.7 us -> 25.1 us  [exchange(): return lax.all_to_all(v, axes, split_axis=0, concat_axis=0, tiled=True)]
    ppermute x35 -> x33, starting transfers between devices: 13.6 us -> 14.9 us  [swap(): return lax.ppermute(v, axis, [(0, 1), (1, 0)])]
  transfers between devices with their start and end apart: 75 -> 71, of which waited for: 26 -> 23; matrix products, arithmetic and copies ran while one was open for 9% -> 6% of each run, Pallas kernels for 27% -> 27%
where the time goes in v4:
time: 490 us; the launch traced here: 481 us
  waiting for transfers between devices  138 us (28%)
  Pallas kernels  131 us (27%)
  starting transfers between devices  97.3 us (20%)
  local copies, waits for them, and re-layouts  53.4 us (11%)
  other arithmetic  27.1 us (6%)
  blocking collectives  17.9 us (4%)
  between operations  16.1 us (3%)
    ppermute x24, waiting for transfers between devices, shift_x(): return lax.ppermute(v, 'x', [((i + distance) % 4, i) for i in range(4)])  71.7 us
    pallas_call x1, Pallas kernels, back(): return call(plan, q, start, *kvs, grad, out, lse)  40.5 us
    unnamed x187, local copies, waits for them, and re-layouts  32.9 us
    pallas_call x4, Pallas kernels, ffn(): pl.pallas_call(ffn_kernel, out_shape=(jax.ShapeDtypeStruct((ROWS, WIDTH),...  30.4 us
    all_to_all x4, starting transfers between devices, exchange(): return lax.all_to_all(v, axes, split_axis=0, concat_axis=0, tiled=True)  29.2 us
    ppermute x24, starting transfers between devices, shift_x(): return lax.ppermute(v, 'x', [((i + distance) % 4, i) for i in range(4)])  28.3 us
    all_to_all x4, waiting for transfers between devices, exchange(): return lax.all_to_all(v, axes, split_axis=0, concat_axis=0, tiled=True)  25.1 us
    ppermute x8, starting transfers between devices, shift_super(): return lax.ppermute(v, ('ylo', 'z', 'yhi'), pairs)  24.8 us
  transfers between devices with their start and end apart: 71, of which 23 were waited for; matrix products, arithmetic and copies ran while one was open for 6% of the time, Pallas kernels for 27%

profile of v4, /device:TPU:8, one launch (start us, length us, event | category | flops | bytes accessed | tf_op | source)
XLA Modules:
  0.0 481.0 jit_solution(15662636337303673407)
XLA Ops:
  13.4 17.9 %all_to_all.25 = bf16[8,24,2112]{2,1,0:T(8,128)(2,1)S(1)} all-to-all(bf16[8,24,2112]{2,1,0:T(8,128)(2,1)S(1)} %copy.84), channel_id=1, replica_groups=mesh['ylo'=2,'z'=4,'x'=4,'core'=2,'yhi'=2] {'x','core'}, dimensions={0} | all-to-all | bytes 1622016 | tf_op jit(solution)/shard_map/all_to_all | solution.py:70
  32.6 8.4 %all-to-all-start.1 = ((bf16[16,96,384]{2,1,0:T(8,128)(2,1)}), bf16[16,96,384]{2,1,0:T(8,128)(2,1)S(1)}, u32[]{:S(2)}, u32[]{:S(2)}) async-start(bf16[16,96,384]{2,1,0:T(8,128)(2,1)} %broadcast_in_dim.27), calls=%async_computation.1 | async-start | bytes 2359296 | tf_op jit(solution)/shard_map/all_to_all | solution.py:70
  42.0 15.6 %all-to-all-done.1 = bf16[16,96,384]{2,1,0:T(8,128)(2,1)S(1)} async-done(((bf16[16,96,384]{2,1,0:T(8,128)(2,1)}), bf16[16,96,384]{2,1,0:T(8,128)(2,1)S(1)}, u32[]{:S(2)}, u32[]{:S(2)}) %all-to-all-start.1) | async-done | bytes 1179680 | tf_op jit(solution)/shard_map/all_to_all | solution.py:70
  63.5 1.9 fusion.8
  66.4 4.9 %collective-permute-done.1.refs_2_.refs_10_ = bf16[128,1536]{1,0:T(8,128)(2,1)} collective-permute-done((bf16[128,1536]{1,0:T(8,128)(2,1)S(1)}, bf16[128,1536]{1,0:T(8,128)(2,1)}, u32[]{:S(2)}, u32[]{:S(2)}) %collective-permute-start.1) | collective-permute-done | bytes 393248 | tf_op jit(solution)/shard_map/ppermute | solution.py:52
  71.3 2.6 collective-permute-done.3.refs_4_.refs_8_
  73.9 7.7 %collective-permute-done.5.refs_6_.refs_10_ = bf16[128,1536]{1,0:T(8,128)(2,1)S(1)} collective-permute-done((bf16[128,1536]{1,0:T(8,128)(2,1)S(1)}, bf16[128,1536]{1,0:T(8,128)(2,1)S(1)}, u32[]{:S(2)}, u32[]{:S(2)}) %collective-permute-start.5) | collective-permute-done | bytes 393248 | tf_op jit(solution)/shard_map/ppermute | solution.py:52
  83.5 4.5 shard_map.237
  89.0 1.7 copy-done.9
  91.5 2.4 collective-permute-start.7
  94.1 13.6 %collective-permute-done.7.refs_1_.refs_5_ = bf16[8,128,128]{2,1,0:T(8,128)(2,1)S(1)} collective-permute-done((bf16[8,128,128]{2,1,0:T(8,128)(2,1)}, bf16[8,128,128]{2,1,0:T(8,128)(2,1)S(1)}, u32[]{:S(2)}, u32[]{:S(2)}) %collective-permute-start.7) | collective-permute-done | bytes 262176 | tf_op jit(solution)/shard_map/ppermute | solution.py:56
  107.7 3.9 collective-permute-start.8
  111.6 2.0 collective-permute-start.9
  113.7 2.1 collective-permute-start.10
  115.8 3.6 collective-permute-start.11
  120.4 11.7 %shard_map.238 = (f32[8,64,384]{2,1,0:T(8,128)S(1)}, f32[8,1,384]{2,1,0:T(1,128)S(1)}) custom-call(s32[8,15]{1,0:T(8,128)S(1)} %stack.22.plan, bf16[8,128,192]{2,1,0:T(8,128)(2,1)S(1)} %copy-done.42, s32[8,1,384]{2,1,0:T(1,128)S(1)} %copy.88.start_ref, bf16[8,128,128]{2,1,0:T(8,128)(2,1)} %get-tuple-element.151.refs_0_.refs_4_, ...), custom_call_target="tpu_custom_call" | custom-call | flops 4000000000 | bytes 8000000 | tf_op jit(solution)/shard_map/pallas_call | solution.py:579
  133.1 4.7 collective-permute-done.9.refs_1_
  138.5 7.6 %collective-permute-done.10.refs_2_ = bf16[8,128,128]{2,1,0:T(8,128)(2,1)S(1)} collective-permute-done((bf16[8,128,128]{2,1,0:T(8,128)(2,1)}, bf16[8,128,128]{2,1,0:T(8,128)(2,1)S(1)}, u32[]{:S(2)}, u32[]{:S(2)}) %collective-permute-start.10) | collective-permute-done | bytes 262176 | tf_op jit(solution)/shard_map/ppermute | solution.py:66
  148.1 6.7 %all-to-all-start.2 = ((bf16[16,192,192]{2,1,0:T(8,128)(2,1)}), bf16[16,192,192]{2,1,0:T(8,128)(2,1)}, u32[]{:S(2)}, u32[]{:S(2)}) async-start(bf16[16,192,192]{2,1,0:T(8,128)(2,1)} %broadcast_in_dim.29), calls=%async_computation.2 | async-start | bytes 3145728 | tf_op jit(solution)/shard_map/all_to_all | solution.py:70
  155.4 1.6 collective-permute-start.13
  161.7 15.0 %shard_map.239 = (bf16[8,128,192]{2,1,0:T(8,128)(2,1)S(1)}, f32[8,64,384]{2,1,0:T(8,128)S(1)}, f32[8,1,384]{2,1,0:T(1,128)S(1)}) custom-call(s32[8,15]{1,0:T(8,128)S(1)} %stack.22.plan, bf16[8,128,192]{2,1,0:T(8,128)(2,1)S(1)} %copy-done.43, s32[8,1,384]{2,1,0:T(1,128)S(1)} %copy.88.start_ref, bf16[8,128,128]{2,1,0:T(8,128)(2,1)S(1)} %collective-permute-done.8.refs_0_, ...), custom_call_target="tpu_custom_call" | custom-call | flops 8000000000 | bytes 8000000 | tf_op jit(solution)/shard_map/pallas_call | solution.py:586
  182.7 2.5 collective-permute-start.21
  187.9 14.3 %collective-permute-done.21 = bf16[128,1536]{1,0:T(8,128)(2,1)S(1)} collective-permute-done((bf16[128,1536]{1,0:T(8,128)(2,1)S(1)}, bf16[128,1536]{1,0:T(8,128)(2,1)S(1)}, u32[]{:S(2)}, u32[]{:S(2)}) %collective-permute-start.21) | collective-permute-done | bytes 393248 | tf_op jit(solution)/shard_map/ppermute | solution.py:52
  202.2 3.8 collective-permute-done.17
  211.5 3.7 copy-done
  217.2 7.5 %shard_map.244 = (bf16[128,1536]{1,0:T(8,128)(2,1)S(1)}, bf16[128,1536]{1,0:T(8,128)(2,1)S(1)}, bf16[128,1536]{1,0:T(8,128)(2,1)S(1)}, bf16[128,1536]{1,0:T(8,12...) custom-call(bf16[128,1536]{1,0:T(8,128)(2,1)} %multiply_convert_fusion.x0_ref.refs_0_, ...), custom_call_target="tpu_custom_call" | custom-call | flops 4831838208 | bytes 14000000 | tf_op jit(solution)/shard_map/pallas_call | solution.py:287
  227.3 8.0 %shard_map.245 = (bf16[128,1536]{1,0:T(8,128)(2,1)S(1)}, bf16[128,1536]{1,0:T(8,128)(2,1)S(1)}, bf16[128,1536]{1,0:T(8,128)(2,1)S(1)}, bf16[128,1536]{1,0:T(8,12...) custom-call(bf16[128,1536]{1,0:T(8,128)(2,1)} %collective-permute-done.25.x0_ref.refs_2_, ...), custom_call_target="tpu_custom_call" | custom-call | flops 4831838208 | bytes 14000000 | tf_op jit(solution)/shard_map/pallas_call | solution.py:287
  235.3 3.2 collective-permute-done.29.x0_ref.refs_4_
  239.2 7.5 %shard_map.246 = (bf16[128,1536]{1,0:T(8,128)(2,1)S(1)}, bf16[128,1536]{1,0:T(8,128)(2,1)S(1)}, bf16[128,1536]{1,0:T(8,128)(2,1)S(1)}, bf16[128,1536]{1,0:T(8,12...) custom-call(bf16[128,1536]{1,0:T(8,128)(2,1)} %collective-permute-done.31.x0_ref.refs_6_, ...), custom_call_target="tpu_custom_call" | custom-call | flops 4831838208 | bytes 14000000 | tf_op jit(solution)/shard_map/pallas_call | solution.py:287
  248.0 7.4 %shard_map.247 = (bf16[128,1536]{1,0:T(8,128)(2,1)S(1)}, bf16[128,1536]{1,0:T(8,128)(2,1)S(1)}, bf16[128,1536]{1,0:T(8,128)(2,1)S(1)}, bf16[128,1536]{1,0:T(8,12...) custom-call(bf16[128,1536]{1,0:T(8,128)(2,1)S(1)} %collective-permute-done.29.x0_ref.refs_4_, ...), custom_call_target="tpu_custom_call" | custom-call | flops 4831838208 | bytes 14000000 | tf_op jit(solution)/shard_map/pallas_call | solution.py:287
  258.1 1.8 collective-permute-start.39
  260.7 15.2 %shard_map.248 = bf16[2,1536,1296]{2,1,0:T(8,128)(2,1)S(1)} custom-call(bf16[128,1536]{1,0:T(8,128)(2,1)} %multiply_convert_fusion.x0_ref.refs_0_, bf16[128,1536]{1,0:T(8,128)(2,1)S(1)} %copy-done.36, bf16[128,1536]{1,0:T(8,128)(2,1)} %collective-permute-done.25.x0_ref.refs_2_, bf16[128,1536]{1,0:T(8,128)(2,1)S(1)} %collective-permute-done.26.x1_ref.refs_3_, ...), custom_call_target="tpu_custom_call" | custom-call | flops 9663676416 | bytes 24000000 | tf_op jit(solution)/shard_map/pallas_call | solution.py:323
  275.9 3.5 copy-done.2
  283.1 1.7 multiply_reduce_fusion
  286.2 1.8 collective-permute-start.42
  288.0 2.0 collective-permute-start.44
  290.5 7.9 %collective-permute-done.42.refs_2_ = bf16[128,1536]{1,0:T(8,128)(2,1)S(1)} collective-permute-done((bf16[128,1536]{1,0:T(8,128)(2,1)S(1)}, bf16[128,1536]{1,0:T(8,128)(2,1)S(1)}, u32[]{:S(2)}, u32[]{:S(2)}) %collective-permute-start.42) | collective-permute-done | bytes 393248 | tf_op jit(solution)/shard_map/ppermute | solution.py:52
  298.3 3.3 collective-permute-done.44.refs_4_
  301.6 6.4 %collective-permute-done.46.refs_6_ = bf16[128,1536]{1,0:T(8,128)(2,1)S(1)} collective-permute-done((bf16[128,1536]{1,0:T(8,128)(2,1)S(1)}, bf16[128,1536]{1,0:T(8,128)(2,1)S(1)}, u32[]{:S(2)}, u32[]{:S(2)}) %collective-permute-start.46) | collective-permute-done | bytes 393248 | tf_op jit(solution)/shard_map/ppermute | solution.py:52
  308.1 1.6 collective-permute-done.47.refs_7_
  310.5 2.0 collective-permute-start.49
  314.0 40.5 %shard_map.250 = (bf16[8,128,256]{2,1,0:T(8,128)(2,1)S(1)}, bf16[8,128,128]{2,1,0:T(8,128)(2,1)S(1)}, bf16[8,128,128]{2,1,0:T(8,128)(2,1)S(1)}, bf16[8,128,128]{...) custom-call(s32[8,15]{1,0:T(8,128)S(1)} %stack.22.plan, ...), custom_call_target="tpu_custom_call" | custom-call | flops 30000001024 | bytes 8000000 | tf_op jit(solution)/shard_map/pallas_call | solution.py:600
  355.7 2.1 collective-permute-start.51
  357.7 1.9 collective-permute-start.52
  359.6 1.9 collective-permute-start.53
  361.6 6.3 %collective-permute-start.54 = (bf16[8,128,128]{2,1,0:T(8,128)(2,1)S(1)}, bf16[8,128,128]{2,1,0:T(8,128)(2,1)S(1)}, u32[]{:S(2)}, u32[]{:S(2)}) collective-permute-start(bf16[8,128,128]{2,1,0:T(8,128)(2,1)S(1)} %get-tuple-element.243), channel_id=1, source_target_pairs={{32,0},{33,1},{48,16},{49,17},{64,32},{65,33},{80,48},{81,49},{96,... | collective-permute-start | bytes 786440 | tf_op jit(solution)/shard_map/ppermute | solution.py:66
  367.9 3.1 collective-permute-start.55
  373.3 6.1 %collective-permute-done.52.refs_3_ = bf16[8,128,128]{2,1,0:T(8,128)(2,1)S(1)} collective-permute-done((bf16[8,128,128]{2,1,0:T(8,128)(2,1)S(1)}, bf16[8,128,128]{2,1,0:T(8,128)(2,1)S(1)}, u32[]{:S(2)}, u32[]{:S(2)}) %collective-permute-start.52) | collective-permute-done | bytes 262176 | tf_op jit(solution)/shard_map/ppermute | solution.py:66
  379.4 4.9 %collective-permute-done.54.refs_5_ = bf16[8,128,128]{2,1,0:T(8,128)(2,1)S(1)} collective-permute-done((bf16[8,128,128]{2,1,0:T(8,128)(2,1)S(1)}, bf16[8,128,128]{2,1,0:T(8,128)(2,1)S(1)}, u32[]{:S(2)}, u32[]{:S(2)}) %collective-permute-start.54) | collective-permute-done | bytes 262176 | tf_op jit(solution)/shard_map/ppermute | solution.py:66
  384.4 3.7 shard_map.252
  389.6 2.6 shard_map.253
  395.9 1.9 copy-done.10
  399.8 4.3 shard_map.254
  405.1 10.4 %all-to-all-start.3 = ((bf16[8,192,576]{2,1,0:T(8,128)(2,1)}), bf16[8,192,576]{2,1,0:T(8,128)(2,1)}, u32[]{:S(2)}, u32[]{:S(2)}) async-start(bf16[8,192,576]{2,1,0:T(8,128)(2,1)} %bitcast.38), calls=%async_computation.4 | async-start | bytes 3932160 | tf_op jit(solution)/shard_map/all_to_all | solution.py:70
  415.6 2.8 collective-permute-start.62
  420.4 1.8 add_convert_fusion.3
  423.1 11.7 %collective-permute-done.62 = bf16[128,1536]{1,0:T(8,128)(2,1)S(1)} collective-permute-done((bf16[128,1536]{1,0:T(8,128)(2,1)S(1)}, bf16[128,1536]{1,0:T(8,128)(2,1)S(1)}, u32[]{:S(2)}, u32[]{:S(2)}) %collective-permute-start.62) | collective-permute-done | bytes 393248 | tf_op jit(solution)/shard_map/ppermute | solution.py:52
  434.8 4.8 %collective-permute-done.58 = bf16[128,1536]{1,0:T(8,128)(2,1)S(1)} collective-permute-done((bf16[128,1536]{1,0:T(8,128)(2,1)}, bf16[128,1536]{1,0:T(8,128)(2,1)S(1)}, u32[]{:S(2)}, u32[]{:S(2)}) %collective-permute-start.58) | collective-permute-done | bytes 393248 | tf_op jit(solution)/shard_map/ppermute | solution.py:52
  440.4 1.9 reduce_sum.71
  442.4 2.2 pad_maximum_fusion.1
  444.6 3.7 all-to-all-start.4
  448.4 3.1 fusion.6
  451.5 9.5 %all-to-all-done.4 = bf16[8,24,1872]{2,1,0:T(8,128)(2,1)S(1)} async-done(((bf16[8,24,1872]{2,1,0:T(8,128)(2,1)}), bf16[8,24,1872]{2,1,0:T(8,128)(2,1)S(1)}, u32[]{:S(2)}, u32[]{:S(2)}) %all-to-all-start.4) | async-done | bytes 718880 | tf_op jit(solution)/shard_map/all_to_all | solution.py:70
  461.2 2.2 collective-permute-start.63
  (418 shorter events, 86.5 us)
Async XLA Ops:
  32.6 24.9 %all-to-all-start.1 = ((bf16[16,96,384]{2,1,0:T(8,128)(2,1)}), bf16[16,96,384]{2,1,0:T(8,128)(2,1)S(1)}, u32[]{:S(2)}, u32[]{:S(2)}) async-start(bf16[16,96,384]{2,1,0:T(8,128)(2,1)} %broadcast_in_dim.27), calls=%async_computation.1 | async-start | bytes 2359296 | tf_op jit(solution)/shard_map/all_to_all | solution.py:70
  41.0 170.5 %all-gather.2.cloned.1.call-start = ((), (), s32[]{:S(2)}) async-start(), calls=%async_computation.6 | async-start | bytes 10027008 | tf_op jit(solution)/shard_map/all_gather | solution.py:657
  59.2 23.2 %collective-permute-start = (bf16[128,1536]{1,0:T(8,128)(2,1)S(1)}, bf16[128,1536]{1,0:T(8,128)(2,1)S(1)}, u32[]{:S(2)}, u32[]{:S(2)}) collective-permute-start(bf16[128,1536]{1,0:T(8,128)(2,1)S(1)} %copy-done.1), channel_id=1, source_target_pairs={{0,2},{2,0},{1,3},{3,1},{4,6},{6,4},{5,7},{7,5},{8,10},{10,8},{9,1... | collective-permute-start | bytes 1179656 | tf_op jit(solution)/shard_map/ppermute | solution.py:56
  59.2 12.0 %collective-permute-start.1 = (bf16[128,1536]{1,0:T(8,128)(2,1)S(1)}, bf16[128,1536]{1,0:T(8,128)(2,1)}, u32[]{:S(2)}, u32[]{:S(2)}) collective-permute-start(bf16[128,1536]{1,0:T(8,128)(2,1)S(1)} %copy-done.1), channel_id=1, source_target_pairs={{4,0},{8,4},{12,8},{0,12},{5,1},{9,5},{13,9},{1,13},{6,2},{10,6},{... | collective-permute-start | bytes 1179656 | tf_op jit(solution)/shard_map/ppermute | solution.py:52
  60.4 13.5 %collective-permute-start.3 = (bf16[128,1536]{1,0:T(8,128)(2,1)S(1)}, bf16[128,1536]{1,0:T(8,128)(2,1)S(1)}, u32[]{:S(2)}, u32[]{:S(2)}) collective-permute-start(bf16[128,1536]{1,0:T(8,128)(2,1)S(1)} %copy-done.1), channel_id=1, source_target_pairs={{8,0},{12,4},{0,8},{4,12},{9,1},{13,5},{1,9},{5,13},{10,2},{14,6},... | collective-permute-start | bytes 1179656 | tf_op jit(solution)/shard_map/ppermute | solution.py:52
  61.9 19.7 %collective-permute-start.5 = (bf16[128,1536]{1,0:T(8,128)(2,1)S(1)}, bf16[128,1536]{1,0:T(8,128)(2,1)S(1)}, u32[]{:S(2)}, u32[]{:S(2)}) collective-permute-start(bf16[128,1536]{1,0:T(8,128)(2,1)S(1)} %copy-done.1), channel_id=1, source_target_pairs={{12,0},{0,4},{4,8},{8,12},{13,1},{1,5},{5,9},{9,13},{14,2},{2,6},{... | collective-permute-start | bytes 1179656 | tf_op jit(solution)/shard_map/ppermute | solution.py:52
  71.3 11.2 %collective-permute-start.2 = (bf16[128,1536]{1,0:T(8,128)(2,1)}, bf16[128,1536]{1,0:T(8,128)(2,1)S(1)}, u32[]{:S(2)}, u32[]{:S(2)}) collective-permute-start(bf16[128,1536]{1,0:T(8,128)(2,1)} %collective-permute-done.1.refs_2_.refs_10_), channel_id=1, source_target_pairs={{0,2},{2,0},{1,3},{3,1},{4,6},{6,4},{5,7},{7,5},{8,10},{10,8},{9,1... | collective-permute-start | bytes 1179656 | tf_op jit(solution)/shard_map/ppermute | solution.py:56
  73.9 8.6 %collective-permute-start.4 = (bf16[128,1536]{1,0:T(8,128)(2,1)S(1)}, bf16[128,1536]{1,0:T(8,128)(2,1)S(1)}, u32[]{:S(2)}, u32[]{:S(2)}) collective-permute-start(bf16[128,1536]{1,0:T(8,128)(2,1)S(1)} %collective-permute-done.3.refs_4_.refs_8_), channel_id=1, source_target_pairs={{0,2},{2,0},{1,3},{3,1},{4,6},{6,4},{5,7},{7,5},{8,10},{10,8},{9,1... | collective-permute-start | bytes 1179656 | tf_op jit(solution)/shard_map/ppermute | solution.py:56
  91.5 16.2 %collective-permute-start.7 = (bf16[8,128,128]{2,1,0:T(8,128)(2,1)}, bf16[8,128,128]{2,1,0:T(8,128)(2,1)S(1)}, u32[]{:S(2)}, u32[]{:S(2)}) collective-permute-start(bf16[8,128,128]{2,1,0:T(8,128)(2,1)} %get-tuple-element.151.refs_0_.refs_4_), channel_id=1, source_target_pairs={{0,1},{1,0},{2,3},{3,2},{4,5},{5,4},{6,7},{7,6},{8,9},{9,8},{10,11... | collective-permute-start | bytes 786440 | tf_op jit(solution)/shard_map/ppermute | solution.py:56
  107.7 25.3 %collective-permute-start.8 = (bf16[8,128,128]{2,1,0:T(8,128)(2,1)}, bf16[8,128,128]{2,1,0:T(8,128)(2,1)S(1)}, u32[]{:S(2)}, u32[]{:S(2)}) collective-permute-start(bf16[8,128,128]{2,1,0:T(8,128)(2,1)} %get-tuple-element.151.refs_0_.refs_4_), channel_id=1, source_target_pairs={{0,32},{1,33},{16,48},{17,49},{32,64},{33,65},{48,80},{49,81},{64,... | collective-permute-start | bytes 786440 | tf_op jit(solution)/shard_map/ppermute | solution.py:66
  111.6 26.2 %collective-permute-start.9 = (bf16[8,128,128]{2,1,0:T(8,128)(2,1)}, bf16[8,128,128]{2,1,0:T(8,128)(2,1)S(1)}, u32[]{:S(2)}, u32[]{:S(2)}) collective-permute-start(bf16[8,128,128]{2,1,0:T(8,128)(2,1)} %get-tuple-element.151.refs_0_.refs_4_), channel_id=1, source_target_pairs={{0,33},{1,32},{16,49},{17,48},{32,65},{33,64},{48,81},{49,80},{64,... | collective-permute-start | bytes 786440 | tf_op jit(solution)/shard_map/ppermute | solution.py:66
  113.7 32.4 %collective-permute-start.10 = (bf16[8,128,128]{2,1,0:T(8,128)(2,1)}, bf16[8,128,128]{2,1,0:T(8,128)(2,1)S(1)}, u32[]{:S(2)}, u32[]{:S(2)}) collective-permute-start(bf16[8,128,128]{2,1,0:T(8,128)(2,1)} %get-tuple-element.151.refs_0_.refs_4_), channel_id=1, source_target_pairs={{0,16},{1,17},{16,32},{17,33},{32,48},{33,49},{48,64},{49,65},{64,... | collective-permute-start | bytes 786440 | tf_op jit(solution)/shard_map/ppermute | solution.py:66
  115.8 30.3 %collective-permute-start.11 = (bf16[8,128,128]{2,1,0:T(8,128)(2,1)}, bf16[8,128,128]{2,1,0:T(8,128)(2,1)S(1)}, u32[]{:S(2)}, u32[]{:S(2)}) collective-permute-start(bf16[8,128,128]{2,1,0:T(8,128)(2,1)} %get-tuple-element.151.refs_0_.refs_4_), channel_id=1, source_target_pairs={{0,17},{1,16},{16,33},{17,32},{32,49},{33,48},{48,65},{49,64},{64,... | collective-permute-start | bytes 786440 | tf_op jit(solution)/shard_map/ppermute | solution.py:66
  148.1 29.5 %all-to-all-start.2 = ((bf16[16,192,192]{2,1,0:T(8,128)(2,1)}), bf16[16,192,192]{2,1,0:T(8,128)(2,1)}, u32[]{:S(2)}, u32[]{:S(2)}) async-start(bf16[16,192,192]{2,1,0:T(8,128)(2,1)} %broadcast_in_dim.29), calls=%async_computation.2 | async-start | bytes 3145728 | tf_op jit(solution)/shard_map/all_to_all | solution.py:70
  154.8 287.6 %reduce-scatter.2.cloned.1.call-start = ((), (), s32[]{:S(2)}) async-start(), calls=%async_computation.7 | async-start | bytes 9191424 | tf_op jit(solution)/shard_map/reduce_scatter | solution.py:748
  154.9 24.2 %collective-permute-start.12 = (bf16[128,1536]{1,0:T(8,128)(2,1)}, bf16[128,1536]{1,0:T(8,128)(2,1)}, u32[]{:S(2)}, u32[]{:S(2)}) collective-permute-start(bf16[128,1536]{1,0:T(8,128)(2,1)} %refs_8_.2), channel_id=1, source_target_pairs={{4,0},{8,4},{12,8},{0,12},{5,1},{9,5},{13,9},{1,13},{6,2},{10,6},{... | collective-permute-start | bytes 1179656 | tf_op jit(solution)/shard_map/ppermute | solution.py:52
  155.4 23.7 %collective-permute-start.13 = (bf16[128,1536]{1,0:T(8,128)(2,1)}, bf16[128,1536]{1,0:T(8,128)(2,1)}, u32[]{:S(2)}, u32[]{:S(2)}) collective-permute-start(bf16[128,1536]{1,0:T(8,128)(2,1)} %refs_8_.2), channel_id=1, source_target_pairs={{8,0},{12,4},{0,8},{4,12},{9,1},{13,5},{1,9},{5,13},{10,2},{14,6},... | collective-permute-start | bytes 1179656 | tf_op jit(solution)/shard_map/ppermute | solution.py:52
  156.9 22.2 %collective-permute-start.14 = (bf16[128,1536]{1,0:T(8,128)(2,1)}, bf16[128,1536]{1,0:T(8,128)(2,1)}, u32[]{:S(2)}, u32[]{:S(2)}) collective-permute-start(bf16[128,1536]{1,0:T(8,128)(2,1)} %refs_8_.2), channel_id=1, source_target_pairs={{12,0},{0,4},{4,8},{8,12},{13,1},{1,5},{5,9},{9,13},{14,2},{2,6},{... | collective-permute-start | bytes 1179656 | tf_op jit(solution)/shard_map/ppermute | solution.py:52
  181.0 5.3 %collective-permute-start.16 = (bf16[128,1536]{1,0:T(8,128)(2,1)S(1)}, bf16[128,1536]{1,0:T(8,128)(2,1)S(1)}, u32[]{:S(2)}, u32[]{:S(2)}) collective-permute-start(bf16[128,1536]{1,0:T(8,128)(2,1)S(1)} %get-tuple-element.166), channel_id=1, source_target_pairs={{0,2},{2,0},{1,3},{3,1},{4,6},{6,4},{5,7},{7,5},{8,10},{10,8},{9,1... | collective-permute-start | bytes 1179656 | tf_op jit(solution)/shard_map/ppermute | solution.py:56
  181.5 6.4 %collective-permute-start.15 = (bf16[128,1536]{1,0:T(8,128)(2,1)S(1)}, bf16[128,1536]{1,0:T(8,128)(2,1)S(1)}, u32[]{:S(2)}, u32[]{:S(2)}) collective-permute-start(bf16[128,1536]{1,0:T(8,128)(2,1)S(1)} %get-tuple-element.164), channel_id=1, source_target_pairs={{0,2},{2,0},{1,3},{3,1},{4,6},{6,4},{5,7},{7,5},{8,10},{10,8},{9,1... | collective-permute-start | bytes 1179656 | tf_op jit(solution)/shard_map/ppermute | solution.py:56
  182.7 19.5 %collective-permute-start.21 = (bf16[128,1536]{1,0:T(8,128)(2,1)S(1)}, bf16[128,1536]{1,0:T(8,128)(2,1)S(1)}, u32[]{:S(2)}, u32[]{:S(2)}) collective-permute-start(bf16[128,1536]{1,0:T(8,128)(2,1)S(1)} %add_convert_fusion.10), channel_id=1, source_target_pairs={{4,0},{8,4},{12,8},{0,12},{5,1},{9,5},{13,9},{1,13},{6,2},{10,6},{... | collective-permute-start | bytes 1179656 | tf_op jit(solution)/shard_map/ppermute | solution.py:52
  185.3 16.9 %collective-permute-start.19 = (bf16[128,1536]{1,0:T(8,128)(2,1)S(1)}, bf16[128,1536]{1,0:T(8,128)(2,1)S(1)}, u32[]{:S(2)}, u32[]{:S(2)}) collective-permute-start(bf16[128,1536]{1,0:T(8,128)(2,1)S(1)} %add_convert_fusion.11), channel_id=1, source_target_pairs={{8,0},{12,4},{0,8},{4,12},{9,1},{13,5},{1,9},{5,13},{10,2},{14,6},... | collective-permute-start | bytes 1179656 | tf_op jit(solution)/shard_map/ppermute | solution.py:52
  186.4 19.6 %collective-permute-start.17 = (bf16[128,1536]{1,0:T(8,128)(2,1)S(1)}, bf16[128,1536]{1,0:T(8,128)(2,1)S(1)}, u32[]{:S(2)}, u32[]{:S(2)}) collective-permute-start(bf16[128,1536]{1,0:T(8,128)(2,1)S(1)} %add_convert_fusion.12), channel_id=1, source_target_pairs={{12,0},{0,4},{4,8},{8,12},{13,1},{1,5},{5,9},{9,13},{14,2},{2,6},{... | collective-permute-start | bytes 1179656 | tf_op jit(solution)/shard_map/ppermute | solution.py:52
  187.9 22.1 %collective-permute-start.23 = (bf16[128,1536]{1,0:T(8,128)(2,1)}, bf16[128,1536]{1,0:T(8,128)(2,1)S(1)}, u32[]{:S(2)}, u32[]{:S(2)}) collective-permute-start(bf16[128,1536]{1,0:T(8,128)(2,1)} %refs_8_.2), channel_id=1, source_target_pairs={{0,2},{2,0},{1,3},{3,1},{4,6},{6,4},{5,7},{7,5},{8,10},{10,8},{9,1... | collective-permute-start | bytes 1179656 | tf_op jit(solution)/shard_map/ppermute | solution.py:56
  207.5 19.2 %collective-permute-start.27 = (bf16[128,1536]{1,0:T(8,128)(2,1)}, bf16[128,1536]{1,0:T(8,128)(2,1)}, u32[]{:S(2)}, u32[]{:S(2)}) collective-permute-start(bf16[128,1536]{1,0:T(8,128)(2,1)} %collective-permute-done.12.c0_ref.refs_10_), channel_id=1, source_target_pairs={{0,2},{2,0},{1,3},{3,1},{4,6},{6,4},{5,7},{7,5},{8,10},{10,8},{9,1... | collective-permute-start | bytes 1179656 | tf_op jit(solution)/shard_map/ppermute | solution.py:56
  208.0 16.7 %collective-permute-start.25 = (bf16[128,1536]{1,0:T(8,128)(2,1)}, bf16[128,1536]{1,0:T(8,128)(2,1)}, u32[]{:S(2)}, u32[]{:S(2)}) collective-permute-start(bf16[128,1536]{1,0:T(8,128)(2,1)} %multiply_convert_fusion.x0_ref.refs_0_), channel_id=1, source_target_pairs={{4,0},{8,4},{12,8},{0,12},{5,1},{9,5},{13,9},{1,13},{6,2},{10,6},{... | collective-permute-start | bytes 1179656 | tf_op jit(solution)/shard_map/ppermute | solution.py:52
  208.6 16.8 %collective-permute-start.31 = (bf16[128,1536]{1,0:T(8,128)(2,1)}, bf16[128,1536]{1,0:T(8,128)(2,1)}, u32[]{:S(2)}, u32[]{:S(2)}) collective-permute-start(bf16[128,1536]{1,0:T(8,128)(2,1)} %multiply_convert_fusion.x0_ref.refs_0_), channel_id=1, source_target_pairs={{12,0},{0,4},{4,8},{8,12},{13,1},{1,5},{5,9},{9,13},{14,2},{2,6},{... | collective-permute-start | bytes 1179656 | tf_op jit(solution)/shard_map/ppermute | solution.py:52
  224.8 14.4 %collective-permute-start.33 = (bf16[128,1536]{1,0:T(8,128)(2,1)}, bf16[128,1536]{1,0:T(8,128)(2,1)S(1)}, u32[]{:S(2)}, u32[]{:S(2)}) collective-permute-start(bf16[128,1536]{1,0:T(8,128)(2,1)} %collective-permute-done.14.c0_ref.refs_14_), channel_id=1, source_target_pairs={{0,2},{2,0},{1,3},{3,1},{4,6},{6,4},{5,7},{7,5},{8,10},{10,8},{9,1... | collective-permute-start | bytes 1179656 | tf_op jit(solution)/shard_map/ppermute | solution.py:56
  225.3 22.7 %collective-permute-start.34 = (bf16[128,1536]{1,0:T(8,128)(2,1)}, bf16[128,1536]{1,0:T(8,128)(2,1)S(1)}, u32[]{:S(2)}, u32[]{:S(2)}) collective-permute-start(bf16[128,1536]{1,0:T(8,128)(2,1)} %collective-permute-done.13.c0_ref.refs_12_), channel_id=1, source_target_pairs={{0,2},{2,0},{1,3},{3,1},{4,6},{6,4},{5,7},{7,5},{8,10},{10,8},{9,1... | collective-permute-start | bytes 1179656 | tf_op jit(solution)/shard_map/ppermute | solution.py:56
  225.4 13.2 %collective-permute-start.29 = (bf16[128,1536]{1,0:T(8,128)(2,1)}, bf16[128,1536]{1,0:T(8,128)(2,1)S(1)}, u32[]{:S(2)}, u32[]{:S(2)}) collective-permute-start(bf16[128,1536]{1,0:T(8,128)(2,1)} %multiply_convert_fusion.x0_ref.refs_0_), channel_id=1, source_target_pairs={{8,0},{12,4},{0,8},{4,12},{9,1},{13,5},{1,9},{5,13},{10,2},{14,6},... | collective-permute-start | bytes 1179656 | tf_op jit(solution)/shard_map/ppermute | solution.py:52
  226.7 20.2 %collective-permute-start.24 = (bf16[128,1536]{1,0:T(8,128)(2,1)S(1)}, bf16[128,1536]{1,0:T(8,128)(2,1)}, u32[]{:S(2)}, u32[]{:S(2)}) collective-permute-start(bf16[128,1536]{1,0:T(8,128)(2,1)S(1)} %get-tuple-element.173), channel_id=1, source_target_pairs={{0,2},{2,0},{1,3},{3,1},{4,6},{6,4},{5,7},{7,5},{8,10},{10,8},{9,1... | collective-permute-start | bytes 1179656 | tf_op jit(solution)/shard_map/ppermute | solution.py:56
  226.9 11.7 %collective-permute-start.32 = (bf16[128,1536]{1,0:T(8,128)(2,1)}, bf16[128,1536]{1,0:T(8,128)(2,1)S(1)}, u32[]{:S(2)}, u32[]{:S(2)}) collective-permute-start(bf16[128,1536]{1,0:T(8,128)(2,1)} %collective-permute-done.31.x0_ref.refs_6_), channel_id=1, source_target_pairs={{0,2},{2,0},{1,3},{3,1},{4,6},{6,4},{5,7},{7,5},{8,10},{10,8},{9,1... | collective-permute-start | bytes 1179656 | tf_op jit(solution)/shard_map/ppermute | solution.py:56
  238.6 17.4 %collective-permute-start.28 = (bf16[128,1536]{1,0:T(8,128)(2,1)S(1)}, bf16[128,1536]{1,0:T(8,128)(2,1)S(1)}, u32[]{:S(2)}, u32[]{:S(2)}) collective-permute-start(bf16[128,1536]{1,0:T(8,128)(2,1)S(1)} %get-tuple-element.177), channel_id=1, source_target_pairs={{0,2},{2,0},{1,3},{3,1},{4,6},{6,4},{5,7},{7,5},{8,10},{10,8},{9,1... | collective-permute-start | bytes 1179656 | tf_op jit(solution)/shard_map/ppermute | solution.py:56
  238.6 9.4 %collective-permute-start.30 = (bf16[128,1536]{1,0:T(8,128)(2,1)S(1)}, bf16[128,1536]{1,0:T(8,128)(2,1)S(1)}, u32[]{:S(2)}, u32[]{:S(2)}) collective-permute-start(bf16[128,1536]{1,0:T(8,128)(2,1)S(1)} %collective-permute-done.29.x0_ref.refs_4_), channel_id=1, source_target_pairs={{0,2},{2,0},{1,3},{3,1},{4,6},{6,4},{5,7},{7,5},{8,10},{10,8},{9,1... | collective-permute-start | bytes 1179656 | tf_op jit(solution)/shard_map/ppermute | solution.py:56
  246.8 9.3 %collective-permute-start.36 = (bf16[128,1536]{1,0:T(8,128)(2,1)S(1)}, bf16[128,1536]{1,0:T(8,128)(2,1)S(1)}, u32[]{:S(2)}, u32[]{:S(2)}) collective-permute-start(bf16[128,1536]{1,0:T(8,128)(2,1)S(1)} %get-tuple-element.189), channel_id=1, source_target_pairs={{0,2},{2,0},{1,3},{3,1},{4,6},{6,4},{5,7},{7,5},{8,10},{10,8},{9,1... | collective-permute-start | bytes 1179656 | tf_op jit(solution)/shard_map/ppermute | solution.py:56
  257.6 23.9 %collective-permute-start.40 = (bf16[4,128,1536]{2,1,0:T(8,128)(2,1)S(1)}, bf16[4,128,1536]{2,1,0:T(8,128)(2,1)S(1)}, u32[]{:S(2)}, u32[]{:S(2)}) collective-permute-start(bf16[4,128,1536]{2,1,0:T(8,128)(2,1)S(1)} %pad_maximum_fusion), channel_id=1, source_target_pairs={{0,2},{2,0},{1,3},{3,1},{4,6},{6,4},{5,7},{7,5},{8,10},{10,8},{9,1... | collective-permute-start | bytes 4718600 | tf_op jit(solution)/shard_map/ppermute | solution.py:56
  258.1 21.4 %collective-permute-start.39 = (bf16[128,1536]{1,0:T(8,128)(2,1)S(1)}, bf16[128,1536]{1,0:T(8,128)(2,1)S(1)}, u32[]{:S(2)}, u32[]{:S(2)}) collective-permute-start(bf16[128,1536]{1,0:T(8,128)(2,1)S(1)} %add_convert_fusion.6), channel_id=1, source_target_pairs={{4,0},{8,4},{12,8},{0,12},{5,1},{9,5},{13,9},{1,13},{6,2},{10,6},{... | collective-permute-start | bytes 1179656 | tf_op jit(solution)/shard_map/ppermute | solution.py:52
  259.9 19.6 %collective-permute-start.38 = (bf16[128,1536]{1,0:T(8,128)(2,1)S(1)}, bf16[128,1536]{1,0:T(8,128)(2,1)S(1)}, u32[]{:S(2)}, u32[]{:S(2)}) collective-permute-start(bf16[128,1536]{1,0:T(8,128)(2,1)S(1)} %add_convert_fusion.7), channel_id=1, source_target_pairs={{8,0},{12,4},{0,8},{4,12},{9,1},{13,5},{1,9},{5,13},{10,2},{14,6},... | collective-permute-start | bytes 1179656 | tf_op jit(solution)/shard_map/ppermute | solution.py:52
  260.1 20.3 %collective-permute-start.37 = (bf16[128,1536]{1,0:T(8,128)(2,1)S(1)}, bf16[128,1536]{1,0:T(8,128)(2,1)S(1)}, u32[]{:S(2)}, u32[]{:S(2)}) collective-permute-start(bf16[128,1536]{1,0:T(8,128)(2,1)S(1)} %add_convert_fusion.8), channel_id=1, source_target_pairs={{12,0},{0,4},{4,8},{8,12},{13,1},{1,5},{5,9},{9,13},{14,2},{2,6},{... | collective-permute-start | bytes 1179656 | tf_op jit(solution)/shard_map/ppermute | solution.py:52
  286.2 12.1 %collective-permute-start.42 = (bf16[128,1536]{1,0:T(8,128)(2,1)S(1)}, bf16[128,1536]{1,0:T(8,128)(2,1)S(1)}, u32[]{:S(2)}, u32[]{:S(2)}) collective-permute-start(bf16[128,1536]{1,0:T(8,128)(2,1)S(1)} %fusion.41.refs_0_), channel_id=1, source_target_pairs={{4,0},{8,4},{12,8},{0,12},{5,1},{9,5},{13,9},{1,13},{6,2},{10,6},{... | collective-permute-start | bytes 1179656 | tf_op jit(solution)/shard_map/ppermute | solution.py:52
  288.0 13.6 %collective-permute-start.44 = (bf16[128,1536]{1,0:T(8,128)(2,1)S(1)}, bf16[128,1536]{1,0:T(8,128)(2,1)S(1)}, u32[]{:S(2)}, u32[]{:S(2)}) collective-permute-start(bf16[128,1536]{1,0:T(8,128)(2,1)S(1)} %fusion.41.refs_0_), channel_id=1, source_target_pairs={{8,0},{12,4},{0,8},{4,12},{9,1},{13,5},{1,9},{5,13},{10,2},{14,6},... | collective-permute-start | bytes 1179656 | tf_op jit(solution)/shard_map/ppermute | solution.py:52
  290.0 17.9 %collective-permute-start.46 = (bf16[128,1536]{1,0:T(8,128)(2,1)S(1)}, bf16[128,1536]{1,0:T(8,128)(2,1)S(1)}, u32[]{:S(2)}, u32[]{:S(2)}) collective-permute-start(bf16[128,1536]{1,0:T(8,128)(2,1)S(1)} %fusion.41.refs_0_), channel_id=1, source_target_pairs={{12,0},{0,4},{4,8},{8,12},{13,1},{1,5},{5,9},{9,13},{14,2},{2,6},{... | collective-permute-start | bytes 1179656 | tf_op jit(solution)/shard_map/ppermute | solution.py:52
  290.3 17.8 %collective-permute-start.41 = (bf16[128,1536]{1,0:T(8,128)(2,1)S(1)}, bf16[128,1536]{1,0:T(8,128)(2,1)S(1)}, u32[]{:S(2)}, u32[]{:S(2)}) collective-permute-start(bf16[128,1536]{1,0:T(8,128)(2,1)S(1)} %fusion.41.refs_0_), channel_id=1, source_target_pairs={{0,2},{2,0},{1,3},{3,1},{4,6},{6,4},{5,7},{7,5},{8,10},{10,8},{9,1... | collective-permute-start | bytes 1179656 | tf_op jit(solution)/shard_map/ppermute | solution.py:56
  298.3 9.8 %collective-permute-start.43 = (bf16[128,1536]{1,0:T(8,128)(2,1)S(1)}, bf16[128,1536]{1,0:T(8,128)(2,1)S(1)}, u32[]{:S(2)}, u32[]{:S(2)}) collective-permute-start(bf16[128,1536]{1,0:T(8,128)(2,1)S(1)} %collective-permute-done.42.refs_2_), channel_id=1, source_target_pairs={{0,2},{2,0},{1,3},{3,1},{4,6},{6,4},{5,7},{7,5},{8,10},{10,8},{9,1... | collective-permute-start | bytes 1179656 | tf_op jit(solution)/shard_map/ppermute | solution.py:56
  301.6 6.5 %collective-permute-start.45 = (bf16[128,1536]{1,0:T(8,128)(2,1)S(1)}, bf16[128,1536]{1,0:T(8,128)(2,1)S(1)}, u32[]{:S(2)}, u32[]{:S(2)}) collective-permute-start(bf16[128,1536]{1,0:T(8,128)(2,1)S(1)} %collective-permute-done.44.refs_4_), channel_id=1, source_target_pairs={{0,2},{2,0},{1,3},{3,1},{4,6},{6,4},{5,7},{7,5},{8,10},{10,8},{9,1... | collective-permute-start | bytes 1179656 | tf_op jit(solution)/shard_map/ppermute | solution.py:56
  309.7 44.8 %collective-permute-start.50 = (bf16[128,1536]{1,0:T(8,128)(2,1)S(1)}, bf16[128,1536]{1,0:T(8,128)(2,1)S(1)}, u32[]{:S(2)}, u32[]{:S(2)}) collective-permute-start(bf16[128,1536]{1,0:T(8,128)(2,1)S(1)} %get-tuple-element.236), channel_id=1, source_target_pairs={{4,0},{8,4},{12,8},{0,12},{5,1},{9,5},{13,9},{1,13},{6,2},{10,6},{... | collective-permute-start | bytes 1179656 | tf_op jit(solution)/shard_map/ppermute | solution.py:52
  310.5 44.1 %collective-permute-start.49 = (bf16[128,1536]{1,0:T(8,128)(2,1)S(1)}, bf16[128,1536]{1,0:T(8,128)(2,1)S(1)}, u32[]{:S(2)}, u32[]{:S(2)}) collective-permute-start(bf16[128,1536]{1,0:T(8,128)(2,1)S(1)} %get-tuple-element.235), channel_id=1, source_target_pairs={{8,0},{12,4},{0,8},{4,12},{9,1},{13,5},{1,9},{5,13},{10,2},{14,6},... | collective-permute-start | bytes 1179656 | tf_op jit(solution)/shard_map/ppermute | solution.py:52
  312.5 42.1 %collective-permute-start.48 = (bf16[128,1536]{1,0:T(8,128)(2,1)S(1)}, bf16[128,1536]{1,0:T(8,128)(2,1)S(1)}, u32[]{:S(2)}, u32[]{:S(2)}) collective-permute-start(bf16[128,1536]{1,0:T(8,128)(2,1)S(1)} %get-tuple-element.234), channel_id=1, source_target_pairs={{12,0},{0,4},{4,8},{8,12},{13,1},{1,5},{5,9},{9,13},{14,2},{2,6},{... | collective-permute-start | bytes 1179656 | tf_op jit(solution)/shard_map/ppermute | solution.py:52
  355.7 17.7 %collective-permute-start.51 = (bf16[8,128,128]{2,1,0:T(8,128)(2,1)S(1)}, bf16[8,128,128]{2,1,0:T(8,128)(2,1)S(1)}, u32[]{:S(2)}, u32[]{:S(2)}) collective-permute-start(bf16[8,128,128]{2,1,0:T(8,128)(2,1)S(1)} %get-tuple-element.240), channel_id=1, source_target_pairs={{0,1},{1,0},{2,3},{3,2},{4,5},{5,4},{6,7},{7,6},{8,9},{9,8},{10,11... | collective-permute-start | bytes 786440 | tf_op jit(solution)/shard_map/ppermute | solution.py:56
  357.7 21.7 %collective-permute-start.52 = (bf16[8,128,128]{2,1,0:T(8,128)(2,1)S(1)}, bf16[8,128,128]{2,1,0:T(8,128)(2,1)S(1)}, u32[]{:S(2)}, u32[]{:S(2)}) collective-permute-start(bf16[8,128,128]{2,1,0:T(8,128)(2,1)S(1)} %get-tuple-element.241), channel_id=1, source_target_pairs={{16,0},{17,1},{32,16},{33,17},{48,32},{49,33},{64,48},{65,49},{80,... | collective-permute-start | bytes 786440 | tf_op jit(solution)/shard_map/ppermute | solution.py:66
  359.6 19.8 %collective-permute-start.53 = (bf16[8,128,128]{2,1,0:T(8,128)(2,1)S(1)}, bf16[8,128,128]{2,1,0:T(8,128)(2,1)S(1)}, u32[]{:S(2)}, u32[]{:S(2)}) collective-permute-start(bf16[8,128,128]{2,1,0:T(8,128)(2,1)S(1)} %get-tuple-element.242), channel_id=1, source_target_pairs={{16,1},{17,0},{32,17},{33,16},{48,33},{49,32},{64,49},{65,48},{80,... | collective-permute-start | bytes 786440 | tf_op jit(solution)/shard_map/ppermute | solution.py:66
  361.6 22.8 %collective-permute-start.54 = (bf16[8,128,128]{2,1,0:T(8,128)(2,1)S(1)}, bf16[8,128,128]{2,1,0:T(8,128)(2,1)S(1)}, u32[]{:S(2)}, u32[]{:S(2)}) collective-permute-start(bf16[8,128,128]{2,1,0:T(8,128)(2,1)S(1)} %get-tuple-element.243), channel_id=1, source_target_pairs={{32,0},{33,1},{48,16},{49,17},{64,32},{65,33},{80,48},{81,49},{96,... | collective-permute-start | bytes 786440 | tf_op jit(solution)/shard_map/ppermute | solution.py:66
  367.9 16.4 %collective-permute-start.55 = (bf16[8,128,128]{2,1,0:T(8,128)(2,1)S(1)}, bf16[8,128,128]{2,1,0:T(8,128)(2,1)S(1)}, u32[]{:S(2)}, u32[]{:S(2)}) collective-permute-start(bf16[8,128,128]{2,1,0:T(8,128)(2,1)S(1)} %get-tuple-element.244), channel_id=1, source_target_pairs={{32,1},{33,0},{48,17},{49,16},{64,33},{65,32},{80,49},{81,48},{96,... | collective-permute-start | bytes 786440 | tf_op jit(solution)/shard_map/ppermute | solution.py:66
  404.1 11.4 %collective-permute-start.61 = (bf16[128,1536]{1,0:T(8,128)(2,1)}, bf16[128,1536]{1,0:T(8,128)(2,1)S(1)}, u32[]{:S(2)}, u32[]{:S(2)}) collective-permute-start(bf16[128,1536]{1,0:T(8,128)(2,1)} %get-tuple-element.276), channel_id=1, source_target_pairs={{0,2},{2,0},{1,3},{3,1},{4,6},{6,4},{5,7},{7,5},{8,10},{10,8},{9,1... | collective-permute-start | bytes 1179656 | tf_op jit(solution)/shard_map/ppermute | solution.py:56
  404.1 14.3 %collective-permute-start.59 = (bf16[128,1536]{1,0:T(8,128)(2,1)}, bf16[128,1536]{1,0:T(8,128)(2,1)}, u32[]{:S(2)}, u32[]{:S(2)}) collective-permute-start(bf16[128,1536]{1,0:T(8,128)(2,1)} %get-tuple-element.274), channel_id=1, source_target_pairs={{0,2},{2,0},{1,3},{3,1},{4,6},{6,4},{5,7},{7,5},{8,10},{10,8},{9,1... | collective-permute-start | bytes 1179656 | tf_op jit(solution)/shard_map/ppermute | solution.py:56
  404.6 15.8 %collective-permute-start.57 = (bf16[128,1536]{1,0:T(8,128)(2,1)}, bf16[128,1536]{1,0:T(8,128)(2,1)}, u32[]{:S(2)}, u32[]{:S(2)}) collective-permute-start(bf16[128,1536]{1,0:T(8,128)(2,1)} %get-tuple-element.272), channel_id=1, source_target_pairs={{0,2},{2,0},{1,3},{3,1},{4,6},{6,4},{5,7},{7,5},{8,10},{10,8},{9,1... | collective-permute-start | bytes 1179656 | tf_op jit(solution)/shard_map/ppermute | solution.py:56
  404.6 18.5 %collective-permute-start.56 = (bf16[128,1536]{1,0:T(8,128)(2,1)S(1)}, bf16[128,1536]{1,0:T(8,128)(2,1)S(1)}, u32[]{:S(2)}, u32[]{:S(2)}) collective-permute-start(bf16[128,1536]{1,0:T(8,128)(2,1)S(1)} %copy-done.48), channel_id=1, source_target_pairs={{0,2},{2,0},{1,3},{3,1},{4,6},{6,4},{5,7},{7,5},{8,10},{10,8},{9,1... | collective-permute-start | bytes 1179656 | tf_op jit(solution)/shard_map/ppermute | solution.py:56
  405.1 35.1 %all-to-all-start.3 = ((bf16[8,192,576]{2,1,0:T(8,128)(2,1)}), bf16[8,192,576]{2,1,0:T(8,128)(2,1)}, u32[]{:S(2)}, u32[]{:S(2)}) async-start(bf16[8,192,576]{2,1,0:T(8,128)(2,1)} %bitcast.38), calls=%async_computation.4 | async-start | bytes 3932160 | tf_op jit(solution)/shard_map/all_to_all | solution.py:70
  415.6 19.2 %collective-permute-start.62 = (bf16[128,1536]{1,0:T(8,128)(2,1)S(1)}, bf16[128,1536]{1,0:T(8,128)(2,1)S(1)}, u32[]{:S(2)}, u32[]{:S(2)}) collective-permute-start(bf16[128,1536]{1,0:T(8,128)(2,1)S(1)} %add_convert_fusion.1), channel_id=1, source_target_pairs={{4,0},{8,4},{12,8},{0,12},{5,1},{9,5},{13,9},{1,13},{6,2},{10,6},{... | collective-permute-start | bytes 1179656 | tf_op jit(solution)/shard_map/ppermute | solution.py:52
  419.5 15.4 %collective-permute-start.60 = (bf16[128,1536]{1,0:T(8,128)(2,1)S(1)}, bf16[128,1536]{1,0:T(8,128)(2,1)S(1)}, u32[]{:S(2)}, u32[]{:S(2)}) collective-permute-start(bf16[128,1536]{1,0:T(8,128)(2,1)S(1)} %add_convert_fusion.2), channel_id=1, source_target_pairs={{8,0},{12,4},{0,8},{4,12},{9,1},{13,5},{1,9},{5,13},{10,2},{14,6},... | collective-permute-start | bytes 1179656 | tf_op jit(solution)/shard_map/ppermute | solution.py:52
  422.2 17.5 %collective-permute-start.58 = (bf16[128,1536]{1,0:T(8,128)(2,1)}, bf16[128,1536]{1,0:T(8,128)(2,1)S(1)}, u32[]{:S(2)}, u32[]{:S(2)}) collective-permute-start(bf16[128,1536]{1,0:T(8,128)(2,1)} %add_convert_fusion.3), channel_id=1, source_target_pairs={{12,0},{0,4},{4,8},{8,12},{13,1},{1,5},{5,9},{9,13},{14,2},{2,6},{... | collective-permute-start | bytes 1179656 | tf_op jit(solution)/shard_map/ppermute | solution.py:52
  444.6 16.3 %all-to-all-start.4 = ((bf16[8,24,1872]{2,1,0:T(8,128)(2,1)}), bf16[8,24,1872]{2,1,0:T(8,128)(2,1)S(1)}, u32[]{:S(2)}, u32[]{:S(2)}) async-start(bf16[8,24,1872]{2,1,0:T(8,128)(2,1)} %pad_maximum_fusion.1), calls=%async_computation.5 | async-start | bytes 1474560 | tf_op jit(solution)/shard_map/all_to_all | solution.py:70
  461.2 8.6 %collective-permute-start.63 = (bf16[8,12,384]{2,1,0:T(8,128)(2,1)S(1)}, bf16[8,12,384]{2,1,0:T(8,128)(2,1)S(1)}, u32[]{:S(2)}, u32[]{:S(2)}) collective-permute-start(bf16[8,12,384]{2,1,0:T(8,128)(2,1)S(1)} %dynamic-slice_convert_fusion), channel_id=1, source_target_pairs={{0,1},{1,0},{2,3},{3,2},{4,5},{5,4},{6,7},{7,6},{8,9},{9,8},{10,11... | collective-permute-start | bytes 221192 | tf_op jit(solution)/shard_map/ppermute | solution.py:56
  463.4 5.6 %collective-permute-start.64 = (bf16[4,24,192]{2,1,0:T(8,128)(2,1)S(1)}, bf16[4,24,192]{2,1,0:T(8,128)(2,1)S(1)}, u32[]{:S(2)}, u32[]{:S(2)}) collective-permute-start(bf16[4,24,192]{2,1,0:T(8,128)(2,1)S(1)} %dynamic-slice_convert_fusion.1), channel_id=1, source_target_pairs={{0,1},{1,0},{2,3},{3,2},{4,5},{5,4},{6,7},{7,6},{8,9},{9,8},{10,11... | collective-permute-start | bytes 110600 | tf_op jit(solution)/shard_map/ppermute | solution.py:56
  (101 other events, 691.1 us)
Sparse Core Ops, SparseCore 0:
  58.7 96.2 all-gather.1
  283.2 96.2 reduce-scatter.1

commit v5 on v4

--- a/solution.py
+++ b/solution.py
@@ -18,10 +18,12 @@
 QUERY = GROUP * HEAD
 LANES = ROWS * GROUP
 KEY_TILE = 512
+UNROLL = 4
 SUPER = 2048
 EARLIER = 2 * SUPER
 PART = 432
 PADDED = 512
+FREE = PADDED - PART
 WIDTH = 1536
 ALL = ("ylo", "z", "x", "core", "yhi")
 BLK = ("ylo", "z", "x", "core")
@@ -243,7 +245,7 @@
         + [ROWS_OF] * 4
         + [all_of(WIDTH, 6 * HEAD), table, table, all_of(1, 4 * HEAD)],
         out_specs=tuple(all_of(*o.shape) for o in outs),
-        compiler_params=params(1, 28),
+        compiler_params=params(1, 20),
         cost_estimate=cost(4 * PAIR * WIDTH * 384, 8e6),
     )(gq, *gkvs, raw, *xs, w, cos, sin, head_gain)
 
@@ -257,13 +259,15 @@
     gate_up = dot(x, gu_w_ref[0])
     gate, up = gate_up[:, :PADDED], gate_up[:, PADDED:]
     grad_act = dot(stacked(c0_ref, c1_ref), d_w_ref[0])
+    own = lax.broadcasted_iota(jnp.int32, (PAIR, PADDED), 1) < PART
     sig = 1.0 / (1.0 + jnp.exp(-gate))
     silu = gate * sig
-    act = (silu * up).astype(BF16)
+    act = jnp.where(own, silu * up, 0.0).astype(BF16)
     act_ref[0] = act
     out_part = dot(act, d_w_ref[0], NT)
-    grad_gate = grad_act * up * sig * (1.0 + gate * (1.0 - sig))
-    grads = jnp.concatenate([grad_gate, grad_act * silu], axis=1).astype(BF16)
+    grad_act = jnp.where(own, grad_act, 0.0)
+    grad_gate = jnp.where(own, grad_act * up * sig * (1.0 + gate * (1.0 - sig)), 0.0)
+    grads = jnp.concatenate([grad_gate, jnp.where(own, grad_act * silu, 0.0)], axis=1).astype(BF16)
     gu_ref[0] = grads
     part = dot(grads, gu_w_ref[0], NT)
 
@@ -430,13 +434,15 @@
         key = lax.broadcasted_iota(jnp.int32, (KEY_TILE, LANES), 0) + (j * KEY_TILE + base)
         return visit(j, state, (key >= start) & (key <= place))
 
-    def two(i, state):
-        return visit(m1 + 2 * i + 1, visit(m1 + 2 * i, state, None), None)
-
-    pairs = lax.shift_right_logical(m2 - m1, 1)
+    def several(i, state):
+        for k in range(UNROLL):
+            state = visit(m1 + UNROLL * i + k, state, None)
+        return state
+
+    steps = lax.div(m2 - m1, UNROLL)
     state = lax.fori_loop(lo, m1, masked, state)
-    state = lax.fori_loop(0, pairs, two, state)
-    state = lax.fori_loop(m1 + 2 * pairs, m2, lambda j, s: visit(j, s, None), state)
+    state = lax.fori_loop(0, steps, several, state)
+    state = lax.fori_loop(m1 + UNROLL * steps, m2, lambda j, s: visit(j, s, None), state)
     return lax.fori_loop(m2, hi, masked, state)
 
 
@@ -639,21 +645,24 @@
     )
     qkv_own = jnp.pad(jnp.transpose(qkv_own, (1, 0, 2)), ((0, 0), (0, 12), (0, 0)))
     out_own = jnp.transpose(w_out.reshape(4, QUERY, 24), (0, 2, 1))
+    out_own = jnp.pad(jnp.concatenate([out_own, out_own], axis=0), ((0, 0), (0, 0), (0, 3 * FREE - QUERY)))
     rows_own = jnp.concatenate(
         [
-            jnp.pad(w.reshape(24, 8, PART), ((0, 0), (0, 0), (0, PADDED - PART))).transpose(1, 0, 2)
-            for w in (w_gate, w_up, w_down.T)
+            part
+            for i, w in enumerate((w_gate, w_up, w_down.T))
+            for part in (
+                w.reshape(24, 8, PART).transpose(1, 0, 2),
+                out_own[:, :, i * FREE : (i + 1) * FREE],
+            )
         ]
-        + [jnp.concatenate([out_own, out_own], axis=0), qkv_own],
+        + [qkv_own],
         axis=-1,
     )
     rows = exchange(rows_own, NEAR)
     ffn_rows = rows[:, :, : 3 * PADDED].reshape(192, 3 * PADDED)
-    out_rows = rows[:, :, 3 * PADDED : 3 * PADDED + QUERY].reshape(1, 192, QUERY)
-    qkv_rows = rows[:, :12, 3 * PADDED + QUERY :].reshape(1, 96, 6 * HEAD)
+    qkv_rows = rows[:, :12, 3 * PADDED :].reshape(1, 96, 6 * HEAD)
     qkv = exchange(jnp.broadcast_to(qkv_rows, (16, 96, 6 * HEAD)), WIDE)
     qkv = jnp.transpose(qkv.reshape(2, 8, 8, 12, 6 * HEAD), (1, 2, 0, 3, 4)).reshape(WIDTH, 6 * HEAD)
-    qkv, ffn_rows = lax.optimization_barrier((qkv, ffn_rows))
     ffn_full = lax.all_gather(ffn_rows, WIDE, axis=0, tiled=True).reshape(2, WIDTH, 3 * PADDED)
     gain_attn = qkv[:, 5 * HEAD].astype(F32)
     gain_ffn = qkv[:, 5 * HEAD + 1].astype(F32)
@@ -699,15 +708,15 @@
     kv_sent = after(kv, kv_own[1])
     kv_earlier = [shift_super(kv_sent, a, b) for a, b in ((2, 0), (2, 1), (1, 0), (1, 1))]
     state = attend_own(plan, rot_q, start_lanes, kv_own)
-    state, kv_earlier, out_rows, cot_sent = lax.optimization_barrier(
-        (state, kv_earlier, out_rows, cotangent)
-    )
+    state, kv_earlier, cot_sent = lax.optimization_barrier((state, kv_earlier, cotangent))
     cot_shifts = [shift_x(cot_sent, d) for d in (1, 2, 3)]
-    out_both = exchange(jnp.broadcast_to(out_rows, (16, 192, QUERY)), WIDE)
-    out_both = out_both.reshape(2, WIDTH, QUERY)
     mix, out_tiles, lse = attend_earlier(plan, rot_q, start_lanes, kv_earlier, state)
-    w_out_t = jnp.where(x < 2, out_both[0], out_both[1])
-    mix, w_out_t, cot_shifts = lax.optimization_barrier((mix, w_out_t, cot_shifts))
+    mix, cot_shifts = lax.optimization_barrier((mix, cot_shifts))
+    out_half = lax.dynamic_index_in_dim(ffn_full, x // 2, 0, keepdims=False)
+    w_out_t = jnp.concatenate(
+        [out_half[:, i * PADDED + PART : (i + 1) * PADDED] for i in range(3)], axis=1
+    )[:, :QUERY]
+    w_out_t, mix = lax.optimization_barrier((w_out_t, mix))
     cot_blocks = [[b, swap(b, "core")] for b in [cotangent] + cot_shifts]
     all_cot = [b for p in cot_blocks for b in p]
 
@@ -741,14 +750,11 @@
     out_kept = jnp.stack(out_own).astype(F32) + swap(jnp.stack(out_other), "core").astype(F32)
     out_kept = out_kept.astype(BF16)
     pair_total = near_sum(kept)
-    weight_grads = ffn_weights(
-        [b for p in ffn_blocks for b in p], all_cot, gus, acts
-    )
+    weight_grads = ffn_weights([b for p in ffn_blocks for b in p], all_cot, gus, acts)
     pair_total, weight_grads, out_kept = lax.optimization_barrier((pair_total, weight_grads, out_kept))
     ffn_sum = lax.psum_scatter(
         weight_grads.reshape(2 * WIDTH, 3 * PART), WIDE, scatter_dimension=0, tiled=True
     )
-
     ffn_gain_part = jnp.sum(pair_total * scaled_ffn, axis=0)
     grad_hidden = cotangent.astype(F32) + rms_back(pair_total * gain_ffn, hidden, scale_ffn)
     grad_branch = grad_hidden.astype(BF16)

time: 490 us -> 464 us (0.947)
  starting transfers between devices: 97.3 us -> 89.7 us
  Pallas kernels: 131 us -> 124 us
  local copies, waits for them, and re-layouts: 53.4 us -> 46.8 us
    unnamed x187 -> x175, local copies, waits for them, and re-layouts: 32.9 us -> 22.2 us
    all_to_all x4 -> x3, starting transfers between devices: 29.2 us -> 22.8 us  [exchange(): return lax.all_to_all(v, axes, split_axis=0, concat_axis=0, tiled=True)]
    all_to_all x4 -> x3, waiting for transfers between devices: 25.1 us -> 24.6 us  [exchange(): return lax.all_to_all(v, axes, split_axis=0, concat_axis=0, tiled=True)]
  transfers between devices with their start and end apart: 71 -> 70, of which waited for: 23 -> 25; matrix products, arithmetic and copies ran while one was open for 6% -> 8% of each run, Pallas kernels for 27% -> 27%
where the time goes in v5:
time: 464 us; the launch traced here: 456 us
  waiting for transfers between devices  134 us (29%)
  Pallas kernels  124 us (27%)
  starting transfers between devices  89.7 us (19%)
  local copies, waits for them, and re-layouts  46.8 us (10%)
  other arithmetic  28.3 us (6%)
  blocking collectives  17 us (4%)
  between operations  16.1 us (3%)
    ppermute x24, waiting for transfers between devices, shift_x(): return lax.ppermute(v, 'x', [((i + distance) % 4, i) for i in range(4)])  69.2 us
    pallas_call x1, Pallas kernels, back(): return call(plan, q, start, *kvs, grad, out, lse)  38.5 us
    ppermute x24, starting transfers between devices, shift_x(): return lax.ppermute(v, 'x', [((i + distance) % 4, i) for i in range(4)])  27.4 us
    ppermute x8, starting transfers between devices, shift_super(): return lax.ppermute(v, ('ylo', 'z', 'yhi'), pairs)  26.6 us
    pallas_call x4, Pallas kernels, ffn(): pl.pallas_call(ffn_kernel, out_shape=(jax.ShapeDtypeStruct((ROWS, WIDTH),...  26.5 us
    all_to_all x3, waiting for transfers between devices, exchange(): return lax.all_to_all(v, axes, split_axis=0, concat_axis=0, tiled=True)  24.6 us
    ppermute x8, waiting for transfers between devices, shift_super(): return lax.ppermute(v, ('ylo', 'z', 'yhi'), pairs)  22.9 us
    all_to_all x3, starting transfers between devices, exchange(): return lax.all_to_all(v, axes, split_axis=0, concat_axis=0, tiled=True)  22.8 us
  transfers between devices with their start and end apart: 70, of which 25 were waited for; matrix products, arithmetic and copies ran while one was open for 8% of the time, Pallas kernels for 27%

profile of v5, /device:TPU:8, one launch (start us, length us, event | category | flops | bytes accessed | tf_op | source)
XLA Modules:
  0.0 456.3 jit_solution(3332170713748318401)
XLA Ops:
  12.7 17.0 %all_to_all.20 = bf16[8,24,1920]{2,1,0:T(8,128)(2,1)S(1)} all-to-all(bf16[8,24,1920]{2,1,0:T(8,128)(2,1)S(1)} %concatenate.51), channel_id=1, replica_groups=mesh['ylo'=2,'z'=4,'x'=4,'core'=2,'yhi'=2] {'x','core'}, dimensions={0} | all-to-all | bytes 1474560 | tf_op jit(solution)/shard_map/all_to_all | solution.py:72
  36.2 8.4 %all-to-all-start.1 = ((bf16[16,96,384]{2,1,0:T(8,128)(2,1)}), bf16[16,96,384]{2,1,0:T(8,128)(2,1)S(1)}, u32[]{:S(2)}, u32[]{:S(2)}) async-start(bf16[16,96,384]{2,1,0:T(8,128)(2,1)} %broadcast_in_dim.23), calls=%async_computation.1 | async-start | bytes 2359296 | tf_op jit(solution)/shard_map/all_to_all | solution.py:72
  44.6 1.9 fusion.8
  48.1 5.0 %collective-permute-done.5.refs_6_.refs_10_ = bf16[128,1536]{1,0:T(8,128)(2,1)} collective-permute-done((bf16[128,1536]{1,0:T(8,128)(2,1)S(1)}, bf16[128,1536]{1,0:T(8,128)(2,1)}, u32[]{:S(2)}, u32[]{:S(2)}) %collective-permute-start.5) | collective-permute-done | bytes 393248 | tf_op jit(solution)/shard_map/ppermute | solution.py:54
  53.3 15.2 %all-to-all-done.1 = bf16[16,96,384]{2,1,0:T(8,128)(2,1)S(1)} async-done(((bf16[16,96,384]{2,1,0:T(8,128)(2,1)}), bf16[16,96,384]{2,1,0:T(8,128)(2,1)S(1)}, u32[]{:S(2)}, u32[]{:S(2)}) %all-to-all-start.1) | async-done | bytes 1179680 | tf_op jit(solution)/shard_map/all_to_all | solution.py:72
  70.4 2.3 reshape.555.refs_8_.refs_12_
  73.3 4.9 %shard_map.237 = (bf16[1024,1536]{1,0:T(8,128)(2,1)S(1)}, bf16[8,128,192]{2,1,0:T(8,128)(2,1)S(1)}, bf16[8,128,128]{2,1,0:T(8,128)(2,1)}, f32[4,256,256]{2,1,0:T(8,128)S(1)}) custom-call(bf16[128,1536]{1,0:T(8,128)(2,1)S(1)} %copy-done, bf16[128,1536]{1,0:T(8,128)(2,1)S(1)} %collective-permute-done.refs_1_.refs_9_, ...), custom_call_target="tpu_custom_call" | custom-call | flops 1207959552 | bytes 10000000 | tf_op jit(solution)/shard_map/pallas_call | solution.py:168
  79.2 1.6 copy-done.12
  81.7 1.7 collective-permute-start.7
  83.5 13.9 %collective-permute-done.7.refs_1_.refs_5_ = bf16[8,128,128]{2,1,0:T(8,128)(2,1)S(1)} collective-permute-done((bf16[8,128,128]{2,1,0:T(8,128)(2,1)}, bf16[8,128,128]{2,1,0:T(8,128)(2,1)S(1)}, u32[]{:S(2)}, u32[]{:S(2)}) %collective-permute-start.7) | collective-permute-done | bytes 262176 | tf_op jit(solution)/shard_map/ppermute | solution.py:58
  97.4 3.4 collective-permute-start.8
  100.8 1.9 collective-permute-start.9
  102.7 2.1 collective-permute-start.10
  104.9 3.7 collective-permute-start.11
  109.6 12.4 %shard_map.238 = (f32[8,64,384]{2,1,0:T(8,128)S(1)}, f32[8,1,384]{2,1,0:T(1,128)S(1)}) custom-call(s32[8,15]{1,0:T(8,128)S(1)} %stack.22.plan, bf16[8,128,192]{2,1,0:T(8,128)(2,1)S(1)} %copy-done.37, s32[8,1,384]{2,1,0:T(1,128)S(1)} %copy.80.start_ref, bf16[8,128,128]{2,1,0:T(8,128)(2,1)} %get-tuple-element.148.refs_0_.refs_4_, ...), custom_call_target="tpu_custom_call" | custom-call | flops 4000000000 | bytes 8000000 | tf_op jit(solution)/shard_map/pallas_call | solution.py:585
  122.1 4.1 collective-permute-done.9.refs_1_
  126.2 8.7 %collective-permute-done.10.refs_2_ = bf16[8,128,128]{2,1,0:T(8,128)(2,1)S(1)} collective-permute-done((bf16[8,128,128]{2,1,0:T(8,128)(2,1)}, bf16[8,128,128]{2,1,0:T(8,128)(2,1)S(1)}, u32[]{:S(2)}, u32[]{:S(2)}) %collective-permute-start.10) | collective-permute-done | bytes 262176 | tf_op jit(solution)/shard_map/ppermute | solution.py:68
  134.9 2.9 collective-permute-start.12
  139.8 13.1 %shard_map.239 = (bf16[8,128,192]{2,1,0:T(8,128)(2,1)S(1)}, f32[8,64,384]{2,1,0:T(8,128)S(1)}, f32[8,1,384]{2,1,0:T(1,128)S(1)}) custom-call(s32[8,15]{1,0:T(8,128)S(1)} %stack.22.plan, bf16[8,128,192]{2,1,0:T(8,128)(2,1)S(1)} %copy-done.38, s32[8,1,384]{2,1,0:T(1,128)S(1)} %copy.80.start_ref, bf16[8,128,128]{2,1,0:T(8,128)(2,1)S(1)} %collective-permute-done.8.refs_0_, ...), custom_call_target="tpu_custom_call" | custom-call | flops 8000000000 | bytes 8000000 | tf_op jit(solution)/shard_map/pallas_call | solution.py:592
  153.9 2.2 collective-permute-done.14.c0_ref.refs_14_
  156.8 2.8 dynamic-slice_bitcast_fusion
  164.7 1.6 collective-permute-start.19
  166.5 9.1 %collective-permute-done.21 = bf16[128,1536]{1,0:T(8,128)(2,1)S(1)} collective-permute-done((bf16[128,1536]{1,0:T(8,128)(2,1)S(1)}, bf16[128,1536]{1,0:T(8,128)(2,1)S(1)}, u32[]{:S(2)}, u32[]{:S(2)}) %collective-permute-start.21) | collective-permute-done | bytes 393248 | tf_op jit(solution)/shard_map/ppermute | solution.py:54
  175.6 2.7 collective-permute-done.19
  178.3 7.1 %collective-permute-done.17 = bf16[128,1536]{1,0:T(8,128)(2,1)S(1)} collective-permute-done((bf16[128,1536]{1,0:T(8,128)(2,1)S(1)}, bf16[128,1536]{1,0:T(8,128)(2,1)S(1)}, u32[]{:S(2)}, u32[]{:S(2)}) %collective-permute-start.17) | collective-permute-done | bytes 393248 | tf_op jit(solution)/shard_map/ppermute | solution.py:54
  189.2 1.8 collective-permute-start.31
  191.0 6.6 %shard_map.244 = (bf16[128,1536]{1,0:T(8,128)(2,1)S(1)}, bf16[128,1536]{1,0:T(8,128)(2,1)S(1)}, bf16[128,1536]{1,0:T(8,128)(2,1)S(1)}, bf16[128,1536]{1,0:T(8,12...) custom-call(bf16[128,1536]{1,0:T(8,128)(2,1)S(1)} %multiply_convert_fusion.x0_ref.refs_0_, ...), custom_call_target="tpu_custom_call" | custom-call | flops 4831838208 | bytes 14000000 | tf_op jit(solution)/shard_map/pallas_call | solution.py:291
  197.7 2.0 collective-permute-done.25.x0_ref.refs_2_
  202.7 6.6 %shard_map.245 = (bf16[128,1536]{1,0:T(8,128)(2,1)S(1)}, bf16[128,1536]{1,0:T(8,128)(2,1)S(1)}, bf16[128,1536]{1,0:T(8,128)(2,1)S(1)}, bf16[128,1536]{1,0:T(8,12...) custom-call(bf16[128,1536]{1,0:T(8,128)(2,1)S(1)} %collective-permute-done.25.x0_ref.refs_2_, ...), custom_call_target="tpu_custom_call" | custom-call | flops 4831838208 | bytes 14000000 | tf_op jit(solution)/shard_map/pallas_call | solution.py:291
  209.3 3.9 collective-permute-done.29.x0_ref.refs_4_
  213.8 6.6 %shard_map.246 = (bf16[128,1536]{1,0:T(8,128)(2,1)S(1)}, bf16[128,1536]{1,0:T(8,128)(2,1)S(1)}, bf16[128,1536]{1,0:T(8,128)(2,1)S(1)}, bf16[128,1536]{1,0:T(8,12...) custom-call(bf16[128,1536]{1,0:T(8,128)(2,1)S(1)} %collective-permute-done.31.x0_ref.refs_6_, ...), custom_call_target="tpu_custom_call" | custom-call | flops 4831838208 | bytes 14000000 | tf_op jit(solution)/shard_map/pallas_call | solution.py:291
  221.5 6.6 %shard_map.247 = (bf16[128,1536]{1,0:T(8,128)(2,1)S(1)}, bf16[128,1536]{1,0:T(8,128)(2,1)S(1)}, bf16[128,1536]{1,0:T(8,128)(2,1)S(1)}, bf16[128,1536]{1,0:T(8,12...) custom-call(bf16[128,1536]{1,0:T(8,128)(2,1)S(1)} %collective-permute-done.29.x0_ref.refs_4_, ...), custom_call_target="tpu_custom_call" | custom-call | flops 4831838208 | bytes 14000000 | tf_op jit(solution)/shard_map/pallas_call | solution.py:291
  230.9 1.8 collective-permute-start.39
  233.8 14.7 %shard_map.248 = bf16[2,1536,1296]{2,1,0:T(8,128)(2,1)S(1)} custom-call(bf16[128,1536]{1,0:T(8,128)(2,1)S(1)} %multiply_convert_fusion.x0_ref.refs_0_, bf16[128,1536]{1,0:T(8,128)(2,1)S(1)} %collective-permute-done.22.x1_ref.refs_1_, bf16[128,1536]{1,0:T(8,128)(2,1)S(1)} %collective-permute-done.25.x0_ref.refs_2_, ...), custom_call_target="tpu_custom_call" | custom-call | flops 9663676416 | bytes 24000000 | tf_op jit(solution)/shard_map/pallas_call | solution.py:327
  248.5 3.3 copy-done.1
  254.3 1.6 add_convert_fusion
  255.9 1.6 multiply_reduce_fusion
  260.3 2.0 collective-permute-start.44
  262.5 8.7 %collective-permute-done.42.refs_2_ = bf16[128,1536]{1,0:T(8,128)(2,1)S(1)} collective-permute-done((bf16[128,1536]{1,0:T(8,128)(2,1)S(1)}, bf16[128,1536]{1,0:T(8,128)(2,1)S(1)}, u32[]{:S(2)}, u32[]{:S(2)}) %collective-permute-start.42) | collective-permute-done | bytes 393248 | tf_op jit(solution)/shard_map/ppermute | solution.py:54
  271.2 2.6 collective-permute-done.44.refs_4_
  273.9 6.4 %collective-permute-done.46.refs_6_ = bf16[128,1536]{1,0:T(8,128)(2,1)S(1)} collective-permute-done((bf16[128,1536]{1,0:T(8,128)(2,1)S(1)}, bf16[128,1536]{1,0:T(8,128)(2,1)S(1)}, u32[]{:S(2)}, u32[]{:S(2)}) %collective-permute-start.46) | collective-permute-done | bytes 393248 | tf_op jit(solution)/shard_map/ppermute | solution.py:54
  280.4 1.6 collective-permute-done.47.refs_7_
  286.5 38.5 %shard_map.250 = (bf16[8,128,256]{2,1,0:T(8,128)(2,1)S(1)}, bf16[8,128,128]{2,1,0:T(8,128)(2,1)S(1)}, bf16[8,128,128]{2,1,0:T(8,128)(2,1)S(1)}, bf16[8,128,128]{...) custom-call(s32[8,15]{1,0:T(8,128)S(1)} %stack.22.plan, ...), custom_call_target="tpu_custom_call" | custom-call | flops 30000001024 | bytes 8000000 | tf_op jit(solution)/shard_map/pallas_call | solution.py:606
  326.9 1.9 collective-permute-start.52
  328.8 1.9 collective-permute-start.53
  330.7 9.4 %collective-permute-start.54 = (bf16[8,128,128]{2,1,0:T(8,128)(2,1)S(1)}, bf16[8,128,128]{2,1,0:T(8,128)(2,1)S(1)}, u32[]{:S(2)}, u32[]{:S(2)}) collective-permute-start(bf16[8,128,128]{2,1,0:T(8,128)(2,1)S(1)} %get-tuple-element.239), channel_id=1, source_target_pairs={{32,0},{33,1},{48,16},{49,17},{64,32},{65,33},{80,48},{81,49},{96,... | collective-permute-start | bytes 786440 | tf_op jit(solution)/shard_map/ppermute | solution.py:68
  340.1 2.3 collective-permute-start.55
  344.7 3.7 collective-permute-done.52.refs_3_
  348.4 5.0 %collective-permute-done.54.refs_5_ = bf16[8,128,128]{2,1,0:T(8,128)(2,1)S(1)} collective-permute-done((bf16[8,128,128]{2,1,0:T(8,128)(2,1)S(1)}, bf16[8,128,128]{2,1,0:T(8,128)(2,1)S(1)}, u32[]{:S(2)}, u32[]{:S(2)}) %collective-permute-start.54) | collective-permute-done | bytes 262176 | tf_op jit(solution)/shard_map/ppermute | solution.py:68
  354.8 3.0 shard_map.252
  360.8 3.2 shard_map.253
  369.2 1.9 copy-done.13
  373.1 4.3 shard_map.254
  378.4 10.8 %all-to-all-start.2 = ((bf16[8,192,576]{2,1,0:T(8,128)(2,1)}), bf16[8,192,576]{2,1,0:T(8,128)(2,1)}, u32[]{:S(2)}, u32[]{:S(2)}) async-start(bf16[8,192,576]{2,1,0:T(8,128)(2,1)} %bitcast.36), calls=%async_computation.3 | async-start | bytes 3932160 | tf_op jit(solution)/shard_map/all_to_all | solution.py:72
  390.4 2.9 collective-permute-start.62
  395.4 1.8 add_convert_fusion.3
  398.0 11.8 %collective-permute-done.62 = bf16[128,1536]{1,0:T(8,128)(2,1)S(1)} collective-permute-done((bf16[128,1536]{1,0:T(8,128)(2,1)S(1)}, bf16[128,1536]{1,0:T(8,128)(2,1)S(1)}, u32[]{:S(2)}, u32[]{:S(2)}) %collective-permute-start.62) | collective-permute-done | bytes 393248 | tf_op jit(solution)/shard_map/ppermute | solution.py:54
  409.8 4.9 %collective-permute-done.58 = bf16[128,1536]{1,0:T(8,128)(2,1)S(1)} collective-permute-done((bf16[128,1536]{1,0:T(8,128)(2,1)}, bf16[128,1536]{1,0:T(8,128)(2,1)S(1)}, u32[]{:S(2)}, u32[]{:S(2)}) %collective-permute-start.58) | collective-permute-done | bytes 393248 | tf_op jit(solution)/shard_map/ppermute | solution.py:54
  415.4 1.9 reduce_sum.71
  417.4 2.2 pad_maximum_fusion.3
  419.6 3.5 all-to-all-start.3
  423.2 3.1 fusion.6
  426.3 9.4 %all-to-all-done.3 = bf16[8,24,1872]{2,1,0:T(8,128)(2,1)S(1)} async-done(((bf16[8,24,1872]{2,1,0:T(8,128)(2,1)}), bf16[8,24,1872]{2,1,0:T(8,128)(2,1)S(1)}, u32[]{:S(2)}, u32[]{:S(2)}) %all-to-all-start.3) | async-done | bytes 718880 | tf_op jit(solution)/shard_map/all_to_all | solution.py:72
  435.9 2.7 collective-permute-start.63
  (407 shorter events, 81.6 us)
Async XLA Ops:
  7.2 149.6 %all-gather.2.cloned.1.call-start = ((), (), s32[]{:S(2)}) async-start(), calls=%async_computation.5 | async-start | bytes 10027008 | tf_op jit(solution)/shard_map/all_gather | solution.py:666
  30.6 42.7 %collective-permute-start = (bf16[128,1536]{1,0:T(8,128)(2,1)S(1)}, bf16[128,1536]{1,0:T(8,128)(2,1)S(1)}, u32[]{:S(2)}, u32[]{:S(2)}) collective-permute-start(bf16[128,1536]{1,0:T(8,128)(2,1)S(1)} %copy-done), channel_id=1, source_target_pairs={{0,2},{2,0},{1,3},{3,1},{4,6},{6,4},{5,7},{7,5},{8,10},{10,8},{9,1... | collective-permute-start | bytes 1179656 | tf_op jit(solution)/shard_map/ppermute | solution.py:58
  30.7 16.8 %collective-permute-start.1 = (bf16[128,1536]{1,0:T(8,128)(2,1)S(1)}, bf16[128,1536]{1,0:T(8,128)(2,1)}, u32[]{:S(2)}, u32[]{:S(2)}) collective-permute-start(bf16[128,1536]{1,0:T(8,128)(2,1)S(1)} %copy-done), channel_id=1, source_target_pairs={{4,0},{8,4},{12,8},{0,12},{5,1},{9,5},{13,9},{1,13},{6,2},{10,6},{... | collective-permute-start | bytes 1179656 | tf_op jit(solution)/shard_map/ppermute | solution.py:54
  31.9 15.8 %collective-permute-start.3 = (bf16[128,1536]{1,0:T(8,128)(2,1)S(1)}, bf16[128,1536]{1,0:T(8,128)(2,1)S(1)}, u32[]{:S(2)}, u32[]{:S(2)}) collective-permute-start(bf16[128,1536]{1,0:T(8,128)(2,1)S(1)} %copy-done), channel_id=1, source_target_pairs={{8,0},{12,4},{0,8},{4,12},{9,1},{13,5},{1,9},{5,13},{10,2},{14,6},... | collective-permute-start | bytes 1179656 | tf_op jit(solution)/shard_map/ppermute | solution.py:54
  33.4 19.7 %collective-permute-start.5 = (bf16[128,1536]{1,0:T(8,128)(2,1)S(1)}, bf16[128,1536]{1,0:T(8,128)(2,1)}, u32[]{:S(2)}, u32[]{:S(2)}) collective-permute-start(bf16[128,1536]{1,0:T(8,128)(2,1)S(1)} %copy-done), channel_id=1, source_target_pairs={{12,0},{0,4},{4,8},{8,12},{13,1},{1,5},{5,9},{9,13},{14,2},{2,6},{... | collective-permute-start | bytes 1179656 | tf_op jit(solution)/shard_map/ppermute | solution.py:54
  36.2 32.4 %all-to-all-start.1 = ((bf16[16,96,384]{2,1,0:T(8,128)(2,1)}), bf16[16,96,384]{2,1,0:T(8,128)(2,1)S(1)}, u32[]{:S(2)}, u32[]{:S(2)}) async-start(bf16[16,96,384]{2,1,0:T(8,128)(2,1)} %broadcast_in_dim.23), calls=%async_computation.1 | async-start | bytes 2359296 | tf_op jit(solution)/shard_map/all_to_all | solution.py:72
  44.6 372.8 %reduce-scatter.2.cloned.1.call-start = ((), (), s32[]{:S(2)}) async-start(), calls=%async_computation.6 | async-start | bytes 9191424 | tf_op jit(solution)/shard_map/reduce_scatter | solution.py:755
  47.5 25.7 %collective-permute-start.2 = (bf16[128,1536]{1,0:T(8,128)(2,1)}, bf16[128,1536]{1,0:T(8,128)(2,1)}, u32[]{:S(2)}, u32[]{:S(2)}) collective-permute-start(bf16[128,1536]{1,0:T(8,128)(2,1)} %collective-permute-done.1.refs_2_.refs_10_), channel_id=1, source_target_pairs={{0,2},{2,0},{1,3},{3,1},{4,6},{6,4},{5,7},{7,5},{8,10},{10,8},{9,1... | collective-permute-start | bytes 1179656 | tf_op jit(solution)/shard_map/ppermute | solution.py:58
  47.6 25.6 %collective-permute-start.4 = (bf16[128,1536]{1,0:T(8,128)(2,1)S(1)}, bf16[128,1536]{1,0:T(8,128)(2,1)}, u32[]{:S(2)}, u32[]{:S(2)}) collective-permute-start(bf16[128,1536]{1,0:T(8,128)(2,1)S(1)} %collective-permute-done.3.refs_4_.refs_8_), channel_id=1, source_target_pairs={{0,2},{2,0},{1,3},{3,1},{4,6},{6,4},{5,7},{7,5},{8,10},{10,8},{9,1... | collective-permute-start | bytes 1179656 | tf_op jit(solution)/shard_map/ppermute | solution.py:58
  53.1 20.2 %collective-permute-start.6 = (bf16[128,1536]{1,0:T(8,128)(2,1)}, bf16[128,1536]{1,0:T(8,128)(2,1)}, u32[]{:S(2)}, u32[]{:S(2)}) collective-permute-start(bf16[128,1536]{1,0:T(8,128)(2,1)} %collective-permute-done.5.refs_6_.refs_10_), channel_id=1, source_target_pairs={{0,2},{2,0},{1,3},{3,1},{4,6},{6,4},{5,7},{7,5},{8,10},{10,8},{9,1... | collective-permute-start | bytes 1179656 | tf_op jit(solution)/shard_map/ppermute | solution.py:58
  81.7 15.8 %collective-permute-start.7 = (bf16[8,128,128]{2,1,0:T(8,128)(2,1)}, bf16[8,128,128]{2,1,0:T(8,128)(2,1)S(1)}, u32[]{:S(2)}, u32[]{:S(2)}) collective-permute-start(bf16[8,128,128]{2,1,0:T(8,128)(2,1)} %get-tuple-element.148.refs_0_.refs_4_), channel_id=1, source_target_pairs={{0,1},{1,0},{2,3},{3,2},{4,5},{5,4},{6,7},{7,6},{8,9},{9,8},{10,11... | collective-permute-start | bytes 786440 | tf_op jit(solution)/shard_map/ppermute | solution.py:58
  97.4 24.6 %collective-permute-start.8 = (bf16[8,128,128]{2,1,0:T(8,128)(2,1)}, bf16[8,128,128]{2,1,0:T(8,128)(2,1)S(1)}, u32[]{:S(2)}, u32[]{:S(2)}) collective-permute-start(bf16[8,128,128]{2,1,0:T(8,128)(2,1)} %get-tuple-element.148.refs_0_.refs_4_), channel_id=1, source_target_pairs={{0,32},{1,33},{16,48},{17,49},{32,64},{33,65},{48,80},{49,81},{64,... | collective-permute-start | bytes 786440 | tf_op jit(solution)/shard_map/ppermute | solution.py:68
  100.8 25.4 %collective-permute-start.9 = (bf16[8,128,128]{2,1,0:T(8,128)(2,1)}, bf16[8,128,128]{2,1,0:T(8,128)(2,1)S(1)}, u32[]{:S(2)}, u32[]{:S(2)}) collective-permute-start(bf16[8,128,128]{2,1,0:T(8,128)(2,1)} %get-tuple-element.148.refs_0_.refs_4_), channel_id=1, source_target_pairs={{0,33},{1,32},{16,49},{17,48},{32,65},{33,64},{48,81},{49,80},{64,... | collective-permute-start | bytes 786440 | tf_op jit(solution)/shard_map/ppermute | solution.py:68
  102.7 32.2 %collective-permute-start.10 = (bf16[8,128,128]{2,1,0:T(8,128)(2,1)}, bf16[8,128,128]{2,1,0:T(8,128)(2,1)S(1)}, u32[]{:S(2)}, u32[]{:S(2)}) collective-permute-start(bf16[8,128,128]{2,1,0:T(8,128)(2,1)} %get-tuple-element.148.refs_0_.refs_4_), channel_id=1, source_target_pairs={{0,16},{1,17},{16,32},{17,33},{32,48},{33,49},{48,64},{49,65},{64,... | collective-permute-start | bytes 786440 | tf_op jit(solution)/shard_map/ppermute | solution.py:68
  104.9 30.1 %collective-permute-start.11 = (bf16[8,128,128]{2,1,0:T(8,128)(2,1)}, bf16[8,128,128]{2,1,0:T(8,128)(2,1)S(1)}, u32[]{:S(2)}, u32[]{:S(2)}) collective-permute-start(bf16[8,128,128]{2,1,0:T(8,128)(2,1)} %get-tuple-element.148.refs_0_.refs_4_), channel_id=1, source_target_pairs={{0,17},{1,16},{16,33},{17,32},{32,49},{33,48},{48,65},{49,64},{64,... | collective-permute-start | bytes 786440 | tf_op jit(solution)/shard_map/ppermute | solution.py:68
  134.9 18.9 %collective-permute-start.12 = (bf16[128,1536]{1,0:T(8,128)(2,1)S(1)}, bf16[128,1536]{1,0:T(8,128)(2,1)S(1)}, u32[]{:S(2)}, u32[]{:S(2)}) collective-permute-start(bf16[128,1536]{1,0:T(8,128)(2,1)S(1)} %copy-done.8), channel_id=1, source_target_pairs={{4,0},{8,4},{12,8},{0,12},{5,1},{9,5},{13,9},{1,13},{6,2},{10,6},{... | collective-permute-start | bytes 1179656 | tf_op jit(solution)/shard_map/ppermute | solution.py:54
  137.9 16.0 %collective-permute-start.13 = (bf16[128,1536]{1,0:T(8,128)(2,1)S(1)}, bf16[128,1536]{1,0:T(8,128)(2,1)S(1)}, u32[]{:S(2)}, u32[]{:S(2)}) collective-permute-start(bf16[128,1536]{1,0:T(8,128)(2,1)S(1)} %copy-done.8), channel_id=1, source_target_pairs={{8,0},{12,4},{0,8},{4,12},{9,1},{13,5},{1,9},{5,13},{10,2},{14,6},... | collective-permute-start | bytes 1179656 | tf_op jit(solution)/shard_map/ppermute | solution.py:54
  138.7 17.4 %collective-permute-start.14 = (bf16[128,1536]{1,0:T(8,128)(2,1)S(1)}, bf16[128,1536]{1,0:T(8,128)(2,1)S(1)}, u32[]{:S(2)}, u32[]{:S(2)}) collective-permute-start(bf16[128,1536]{1,0:T(8,128)(2,1)S(1)} %copy-done.8), channel_id=1, source_target_pairs={{12,0},{0,4},{4,8},{8,12},{13,1},{1,5},{5,9},{9,13},{14,2},{2,6},{... | collective-permute-start | bytes 1179656 | tf_op jit(solution)/shard_map/ppermute | solution.py:54
  162.4 3.8 collective-permute-start.16
  162.9 3.6 collective-permute-start.15
  163.6 12.0 %collective-permute-start.21 = (bf16[128,1536]{1,0:T(8,128)(2,1)S(1)}, bf16[128,1536]{1,0:T(8,128)(2,1)S(1)}, u32[]{:S(2)}, u32[]{:S(2)}) collective-permute-start(bf16[128,1536]{1,0:T(8,128)(2,1)S(1)} %add_convert_fusion.10), channel_id=1, source_target_pairs={{4,0},{8,4},{12,8},{0,12},{5,1},{9,5},{13,9},{1,13},{6,2},{10,6},{... | collective-permute-start | bytes 1179656 | tf_op jit(solution)/shard_map/ppermute | solution.py:54
  164.7 13.6 %collective-permute-start.19 = (bf16[128,1536]{1,0:T(8,128)(2,1)S(1)}, bf16[128,1536]{1,0:T(8,128)(2,1)S(1)}, u32[]{:S(2)}, u32[]{:S(2)}) collective-permute-start(bf16[128,1536]{1,0:T(8,128)(2,1)S(1)} %add_convert_fusion.11), channel_id=1, source_target_pairs={{8,0},{12,4},{0,8},{4,12},{9,1},{13,5},{1,9},{5,13},{10,2},{14,6},... | collective-permute-start | bytes 1179656 | tf_op jit(solution)/shard_map/ppermute | solution.py:54
  166.4 19.1 %collective-permute-start.17 = (bf16[128,1536]{1,0:T(8,128)(2,1)S(1)}, bf16[128,1536]{1,0:T(8,128)(2,1)S(1)}, u32[]{:S(2)}, u32[]{:S(2)}) collective-permute-start(bf16[128,1536]{1,0:T(8,128)(2,1)S(1)} %add_convert_fusion.12), channel_id=1, source_target_pairs={{12,0},{0,4},{4,8},{8,12},{13,1},{1,5},{5,9},{9,13},{14,2},{2,6},{... | collective-permute-start | bytes 1179656 | tf_op jit(solution)/shard_map/ppermute | solution.py:54
  166.4 24.6 %collective-permute-start.23 = (bf16[128,1536]{1,0:T(8,128)(2,1)S(1)}, bf16[128,1536]{1,0:T(8,128)(2,1)S(1)}, u32[]{:S(2)}, u32[]{:S(2)}) collective-permute-start(bf16[128,1536]{1,0:T(8,128)(2,1)S(1)} %copy-done.9), channel_id=1, source_target_pairs={{0,2},{2,0},{1,3},{3,1},{4,6},{6,4},{5,7},{7,5},{8,10},{10,8},{9,1... | collective-permute-start | bytes 1179656 | tf_op jit(solution)/shard_map/ppermute | solution.py:58
  188.1 14.1 %collective-permute-start.27 = (bf16[128,1536]{1,0:T(8,128)(2,1)S(1)}, bf16[128,1536]{1,0:T(8,128)(2,1)S(1)}, u32[]{:S(2)}, u32[]{:S(2)}) collective-permute-start(bf16[128,1536]{1,0:T(8,128)(2,1)S(1)} %copy-done.27), channel_id=1, source_target_pairs={{0,2},{2,0},{1,3},{3,1},{4,6},{6,4},{5,7},{7,5},{8,10},{10,8},{9,1... | collective-permute-start | bytes 1179656 | tf_op jit(solution)/shard_map/ppermute | solution.py:58
  188.6 11.1 %collective-permute-start.25 = (bf16[128,1536]{1,0:T(8,128)(2,1)S(1)}, bf16[128,1536]{1,0:T(8,128)(2,1)S(1)}, u32[]{:S(2)}, u32[]{:S(2)}) collective-permute-start(bf16[128,1536]{1,0:T(8,128)(2,1)S(1)} %multiply_convert_fusion.x0_ref.refs_0_), channel_id=1, source_target_pairs={{4,0},{8,4},{12,8},{0,12},{5,1},{9,5},{13,9},{1,13},{6,2},{10,6},{... | collective-permute-start | bytes 1179656 | tf_op jit(solution)/shard_map/ppermute | solution.py:54
  189.2 12.4 %collective-permute-start.31 = (bf16[128,1536]{1,0:T(8,128)(2,1)S(1)}, bf16[128,1536]{1,0:T(8,128)(2,1)S(1)}, u32[]{:S(2)}, u32[]{:S(2)}) collective-permute-start(bf16[128,1536]{1,0:T(8,128)(2,1)S(1)} %multiply_convert_fusion.x0_ref.refs_0_), channel_id=1, source_target_pairs={{12,0},{0,4},{4,8},{8,12},{13,1},{1,5},{5,9},{9,13},{14,2},{2,6},{... | collective-permute-start | bytes 1179656 | tf_op jit(solution)/shard_map/ppermute | solution.py:54
  199.7 14.1 %collective-permute-start.33 = (bf16[128,1536]{1,0:T(8,128)(2,1)S(1)}, bf16[128,1536]{1,0:T(8,128)(2,1)S(1)}, u32[]{:S(2)}, u32[]{:S(2)}) collective-permute-start(bf16[128,1536]{1,0:T(8,128)(2,1)S(1)} %copy-done.31), channel_id=1, source_target_pairs={{0,2},{2,0},{1,3},{3,1},{4,6},{6,4},{5,7},{7,5},{8,10},{10,8},{9,1... | collective-permute-start | bytes 1179656 | tf_op jit(solution)/shard_map/ppermute | solution.py:58
  200.2 21.3 %collective-permute-start.34 = (bf16[128,1536]{1,0:T(8,128)(2,1)S(1)}, bf16[128,1536]{1,0:T(8,128)(2,1)S(1)}, u32[]{:S(2)}, u32[]{:S(2)}) collective-permute-start(bf16[128,1536]{1,0:T(8,128)(2,1)S(1)} %copy-done.29), channel_id=1, source_target_pairs={{0,2},{2,0},{1,3},{3,1},{4,6},{6,4},{5,7},{7,5},{8,10},{10,8},{9,1... | collective-permute-start | bytes 1179656 | tf_op jit(solution)/shard_map/ppermute | solution.py:58
  201.6 11.6 %collective-permute-start.29 = (bf16[128,1536]{1,0:T(8,128)(2,1)S(1)}, bf16[128,1536]{1,0:T(8,128)(2,1)S(1)}, u32[]{:S(2)}, u32[]{:S(2)}) collective-permute-start(bf16[128,1536]{1,0:T(8,128)(2,1)S(1)} %multiply_convert_fusion.x0_ref.refs_0_), channel_id=1, source_target_pairs={{8,0},{12,4},{0,8},{4,12},{9,1},{13,5},{1,9},{5,13},{10,2},{14,6},... | collective-permute-start | bytes 1179656 | tf_op jit(solution)/shard_map/ppermute | solution.py:54
  202.2 18.5 %collective-permute-start.24 = (bf16[128,1536]{1,0:T(8,128)(2,1)S(1)}, bf16[128,1536]{1,0:T(8,128)(2,1)S(1)}, u32[]{:S(2)}, u32[]{:S(2)}) collective-permute-start(bf16[128,1536]{1,0:T(8,128)(2,1)S(1)} %get-tuple-element.169), channel_id=1, source_target_pairs={{0,2},{2,0},{1,3},{3,1},{4,6},{6,4},{5,7},{7,5},{8,10},{10,8},{9,1... | collective-permute-start | bytes 1179656 | tf_op jit(solution)/shard_map/ppermute | solution.py:58
  202.2 11.1 %collective-permute-start.32 = (bf16[128,1536]{1,0:T(8,128)(2,1)S(1)}, bf16[128,1536]{1,0:T(8,128)(2,1)S(1)}, u32[]{:S(2)}, u32[]{:S(2)}) collective-permute-start(bf16[128,1536]{1,0:T(8,128)(2,1)S(1)} %collective-permute-done.31.x0_ref.refs_6_), channel_id=1, source_target_pairs={{0,2},{2,0},{1,3},{3,1},{4,6},{6,4},{5,7},{7,5},{8,10},{10,8},{9,1... | collective-permute-start | bytes 1179656 | tf_op jit(solution)/shard_map/ppermute | solution.py:58
  213.3 15.5 %collective-permute-start.28 = (bf16[128,1536]{1,0:T(8,128)(2,1)S(1)}, bf16[128,1536]{1,0:T(8,128)(2,1)S(1)}, u32[]{:S(2)}, u32[]{:S(2)}) collective-permute-start(bf16[128,1536]{1,0:T(8,128)(2,1)S(1)} %get-tuple-element.173), channel_id=1, source_target_pairs={{0,2},{2,0},{1,3},{3,1},{4,6},{6,4},{5,7},{7,5},{8,10},{10,8},{9,1... | collective-permute-start | bytes 1179656 | tf_op jit(solution)/shard_map/ppermute | solution.py:58
  213.3 8.3 %collective-permute-start.30 = (bf16[128,1536]{1,0:T(8,128)(2,1)S(1)}, bf16[128,1536]{1,0:T(8,128)(2,1)S(1)}, u32[]{:S(2)}, u32[]{:S(2)}) collective-permute-start(bf16[128,1536]{1,0:T(8,128)(2,1)S(1)} %collective-permute-done.29.x0_ref.refs_4_), channel_id=1, source_target_pairs={{0,2},{2,0},{1,3},{3,1},{4,6},{6,4},{5,7},{7,5},{8,10},{10,8},{9,1... | collective-permute-start | bytes 1179656 | tf_op jit(solution)/shard_map/ppermute | solution.py:58
  220.4 8.4 %collective-permute-start.36 = (bf16[128,1536]{1,0:T(8,128)(2,1)S(1)}, bf16[128,1536]{1,0:T(8,128)(2,1)S(1)}, u32[]{:S(2)}, u32[]{:S(2)}) collective-permute-start(bf16[128,1536]{1,0:T(8,128)(2,1)S(1)} %get-tuple-element.185), channel_id=1, source_target_pairs={{0,2},{2,0},{1,3},{3,1},{4,6},{6,4},{5,7},{7,5},{8,10},{10,8},{9,1... | collective-permute-start | bytes 1179656 | tf_op jit(solution)/shard_map/ppermute | solution.py:58
  230.4 23.9 %collective-permute-start.40 = (bf16[4,128,1536]{2,1,0:T(8,128)(2,1)S(1)}, bf16[4,128,1536]{2,1,0:T(8,128)(2,1)S(1)}, u32[]{:S(2)}, u32[]{:S(2)}) collective-permute-start(bf16[4,128,1536]{2,1,0:T(8,128)(2,1)S(1)} %pad_maximum_fusion), channel_id=1, source_target_pairs={{0,2},{2,0},{1,3},{3,1},{4,6},{6,4},{5,7},{7,5},{8,10},{10,8},{9,1... | collective-permute-start | bytes 4718600 | tf_op jit(solution)/shard_map/ppermute | solution.py:58
  230.9 21.0 %collective-permute-start.39 = (bf16[128,1536]{1,0:T(8,128)(2,1)S(1)}, bf16[128,1536]{1,0:T(8,128)(2,1)S(1)}, u32[]{:S(2)}, u32[]{:S(2)}) collective-permute-start(bf16[128,1536]{1,0:T(8,128)(2,1)S(1)} %add_convert_fusion.6), channel_id=1, source_target_pairs={{4,0},{8,4},{12,8},{0,12},{5,1},{9,5},{13,9},{1,13},{6,2},{10,6},{... | collective-permute-start | bytes 1179656 | tf_op jit(solution)/shard_map/ppermute | solution.py:54
  232.7 19.1 %collective-permute-start.38 = (bf16[128,1536]{1,0:T(8,128)(2,1)S(1)}, bf16[128,1536]{1,0:T(8,128)(2,1)S(1)}, u32[]{:S(2)}, u32[]{:S(2)}) collective-permute-start(bf16[128,1536]{1,0:T(8,128)(2,1)S(1)} %add_convert_fusion.7), channel_id=1, source_target_pairs={{8,0},{12,4},{0,8},{4,12},{9,1},{13,5},{1,9},{5,13},{10,2},{14,6},... | collective-permute-start | bytes 1179656 | tf_op jit(solution)/shard_map/ppermute | solution.py:54
  233.0 20.2 %collective-permute-start.37 = (bf16[128,1536]{1,0:T(8,128)(2,1)S(1)}, bf16[128,1536]{1,0:T(8,128)(2,1)S(1)}, u32[]{:S(2)}, u32[]{:S(2)}) collective-permute-start(bf16[128,1536]{1,0:T(8,128)(2,1)S(1)} %add_convert_fusion.8), channel_id=1, source_target_pairs={{12,0},{0,4},{4,8},{8,12},{13,1},{1,5},{5,9},{9,13},{14,2},{2,6},{... | collective-permute-start | bytes 1179656 | tf_op jit(solution)/shard_map/ppermute | solution.py:54
  259.1 12.1 %collective-permute-start.42 = (bf16[128,1536]{1,0:T(8,128)(2,1)S(1)}, bf16[128,1536]{1,0:T(8,128)(2,1)S(1)}, u32[]{:S(2)}, u32[]{:S(2)}) collective-permute-start(bf16[128,1536]{1,0:T(8,128)(2,1)S(1)} %fusion.43.refs_0_), channel_id=1, source_target_pairs={{4,0},{8,4},{12,8},{0,12},{5,1},{9,5},{13,9},{1,13},{6,2},{10,6},{... | collective-permute-start | bytes 1179656 | tf_op jit(solution)/shard_map/ppermute | solution.py:54
  260.3 13.6 %collective-permute-start.44 = (bf16[128,1536]{1,0:T(8,128)(2,1)S(1)}, bf16[128,1536]{1,0:T(8,128)(2,1)S(1)}, u32[]{:S(2)}, u32[]{:S(2)}) collective-permute-start(bf16[128,1536]{1,0:T(8,128)(2,1)S(1)} %fusion.43.refs_0_), channel_id=1, source_target_pairs={{8,0},{12,4},{0,8},{4,12},{9,1},{13,5},{1,9},{5,13},{10,2},{14,6},... | collective-permute-start | bytes 1179656 | tf_op jit(solution)/shard_map/ppermute | solution.py:54
  262.3 17.9 %collective-permute-start.46 = (bf16[128,1536]{1,0:T(8,128)(2,1)S(1)}, bf16[128,1536]{1,0:T(8,128)(2,1)S(1)}, u32[]{:S(2)}, u32[]{:S(2)}) collective-permute-start(bf16[128,1536]{1,0:T(8,128)(2,1)S(1)} %fusion.43.refs_0_), channel_id=1, source_target_pairs={{12,0},{0,4},{4,8},{8,12},{13,1},{1,5},{5,9},{9,13},{14,2},{2,6},{... | collective-permute-start | bytes 1179656 | tf_op jit(solution)/shard_map/ppermute | solution.py:54
  262.5 17.9 %collective-permute-start.41 = (bf16[128,1536]{1,0:T(8,128)(2,1)S(1)}, bf16[128,1536]{1,0:T(8,128)(2,1)S(1)}, u32[]{:S(2)}, u32[]{:S(2)}) collective-permute-start(bf16[128,1536]{1,0:T(8,128)(2,1)S(1)} %fusion.43.refs_0_), channel_id=1, source_target_pairs={{0,2},{2,0},{1,3},{3,1},{4,6},{6,4},{5,7},{7,5},{8,10},{10,8},{9,1... | collective-permute-start | bytes 1179656 | tf_op jit(solution)/shard_map/ppermute | solution.py:58
  271.2 9.2 %collective-permute-start.43 = (bf16[128,1536]{1,0:T(8,128)(2,1)S(1)}, bf16[128,1536]{1,0:T(8,128)(2,1)S(1)}, u32[]{:S(2)}, u32[]{:S(2)}) collective-permute-start(bf16[128,1536]{1,0:T(8,128)(2,1)S(1)} %collective-permute-done.42.refs_2_), channel_id=1, source_target_pairs={{0,2},{2,0},{1,3},{3,1},{4,6},{6,4},{5,7},{7,5},{8,10},{10,8},{9,1... | collective-permute-start | bytes 1179656 | tf_op jit(solution)/shard_map/ppermute | solution.py:58
  273.9 6.5 %collective-permute-start.45 = (bf16[128,1536]{1,0:T(8,128)(2,1)S(1)}, bf16[128,1536]{1,0:T(8,128)(2,1)S(1)}, u32[]{:S(2)}, u32[]{:S(2)}) collective-permute-start(bf16[128,1536]{1,0:T(8,128)(2,1)S(1)} %collective-permute-done.44.refs_4_), channel_id=1, source_target_pairs={{0,2},{2,0},{1,3},{3,1},{4,6},{6,4},{5,7},{7,5},{8,10},{10,8},{9,1... | collective-permute-start | bytes 1179656 | tf_op jit(solution)/shard_map/ppermute | solution.py:58
  282.0 43.0 %collective-permute-start.50 = (bf16[128,1536]{1,0:T(8,128)(2,1)S(1)}, bf16[128,1536]{1,0:T(8,128)(2,1)S(1)}, u32[]{:S(2)}, u32[]{:S(2)}) collective-permute-start(bf16[128,1536]{1,0:T(8,128)(2,1)S(1)} %get-tuple-element.232), channel_id=1, source_target_pairs={{4,0},{8,4},{12,8},{0,12},{5,1},{9,5},{13,9},{1,13},{6,2},{10,6},{... | collective-permute-start | bytes 1179656 | tf_op jit(solution)/shard_map/ppermute | solution.py:54
  283.4 41.6 %collective-permute-start.49 = (bf16[128,1536]{1,0:T(8,128)(2,1)S(1)}, bf16[128,1536]{1,0:T(8,128)(2,1)S(1)}, u32[]{:S(2)}, u32[]{:S(2)}) collective-permute-start(bf16[128,1536]{1,0:T(8,128)(2,1)S(1)} %get-tuple-element.231), channel_id=1, source_target_pairs={{8,0},{12,4},{0,8},{4,12},{9,1},{13,5},{1,9},{5,13},{10,2},{14,6},... | collective-permute-start | bytes 1179656 | tf_op jit(solution)/shard_map/ppermute | solution.py:54
  284.7 40.3 %collective-permute-start.48 = (bf16[128,1536]{1,0:T(8,128)(2,1)S(1)}, bf16[128,1536]{1,0:T(8,128)(2,1)S(1)}, u32[]{:S(2)}, u32[]{:S(2)}) collective-permute-start(bf16[128,1536]{1,0:T(8,128)(2,1)S(1)} %get-tuple-element.230), channel_id=1, source_target_pairs={{12,0},{0,4},{4,8},{8,12},{13,1},{1,5},{5,9},{9,13},{14,2},{2,6},{... | collective-permute-start | bytes 1179656 | tf_op jit(solution)/shard_map/ppermute | solution.py:54
  326.1 18.6 %collective-permute-start.51 = (bf16[8,128,128]{2,1,0:T(8,128)(2,1)S(1)}, bf16[8,128,128]{2,1,0:T(8,128)(2,1)S(1)}, u32[]{:S(2)}, u32[]{:S(2)}) collective-permute-start(bf16[8,128,128]{2,1,0:T(8,128)(2,1)S(1)} %get-tuple-element.236), channel_id=1, source_target_pairs={{0,1},{1,0},{2,3},{3,2},{4,5},{5,4},{6,7},{7,6},{8,9},{9,8},{10,11... | collective-permute-start | bytes 786440 | tf_op jit(solution)/shard_map/ppermute | solution.py:58
  326.9 21.5 %collective-permute-start.52 = (bf16[8,128,128]{2,1,0:T(8,128)(2,1)S(1)}, bf16[8,128,128]{2,1,0:T(8,128)(2,1)S(1)}, u32[]{:S(2)}, u32[]{:S(2)}) collective-permute-start(bf16[8,128,128]{2,1,0:T(8,128)(2,1)S(1)} %get-tuple-element.237), channel_id=1, source_target_pairs={{16,0},{17,1},{32,16},{33,17},{48,32},{49,33},{64,48},{65,49},{80,... | collective-permute-start | bytes 786440 | tf_op jit(solution)/shard_map/ppermute | solution.py:68
  328.8 19.6 %collective-permute-start.53 = (bf16[8,128,128]{2,1,0:T(8,128)(2,1)S(1)}, bf16[8,128,128]{2,1,0:T(8,128)(2,1)S(1)}, u32[]{:S(2)}, u32[]{:S(2)}) collective-permute-start(bf16[8,128,128]{2,1,0:T(8,128)(2,1)S(1)} %get-tuple-element.238), channel_id=1, source_target_pairs={{16,1},{17,0},{32,17},{33,16},{48,33},{49,32},{64,49},{65,48},{80,... | collective-permute-start | bytes 786440 | tf_op jit(solution)/shard_map/ppermute | solution.py:68
  330.7 22.7 %collective-permute-start.54 = (bf16[8,128,128]{2,1,0:T(8,128)(2,1)S(1)}, bf16[8,128,128]{2,1,0:T(8,128)(2,1)S(1)}, u32[]{:S(2)}, u32[]{:S(2)}) collective-permute-start(bf16[8,128,128]{2,1,0:T(8,128)(2,1)S(1)} %get-tuple-element.239), channel_id=1, source_target_pairs={{32,0},{33,1},{48,16},{49,17},{64,32},{65,33},{80,48},{81,49},{96,... | collective-permute-start | bytes 786440 | tf_op jit(solution)/shard_map/ppermute | solution.py:68
  340.1 14.7 %collective-permute-start.55 = (bf16[8,128,128]{2,1,0:T(8,128)(2,1)S(1)}, bf16[8,128,128]{2,1,0:T(8,128)(2,1)S(1)}, u32[]{:S(2)}, u32[]{:S(2)}) collective-permute-start(bf16[8,128,128]{2,1,0:T(8,128)(2,1)S(1)} %get-tuple-element.240), channel_id=1, source_target_pairs={{32,1},{33,0},{48,17},{49,16},{64,33},{65,32},{80,49},{81,48},{96,... | collective-permute-start | bytes 786440 | tf_op jit(solution)/shard_map/ppermute | solution.py:68
  377.4 11.9 %collective-permute-start.61 = (bf16[128,1536]{1,0:T(8,128)(2,1)S(1)}, bf16[128,1536]{1,0:T(8,128)(2,1)}, u32[]{:S(2)}, u32[]{:S(2)}) collective-permute-start(bf16[128,1536]{1,0:T(8,128)(2,1)S(1)} %copy-done.49), channel_id=1, source_target_pairs={{0,2},{2,0},{1,3},{3,1},{4,6},{6,4},{5,7},{7,5},{8,10},{10,8},{9,1... | collective-permute-start | bytes 1179656 | tf_op jit(solution)/shard_map/ppermute | solution.py:58
  377.4 15.9 %collective-permute-start.59 = (bf16[128,1536]{1,0:T(8,128)(2,1)S(1)}, bf16[128,1536]{1,0:T(8,128)(2,1)}, u32[]{:S(2)}, u32[]{:S(2)}) collective-permute-start(bf16[128,1536]{1,0:T(8,128)(2,1)S(1)} %copy-done.47), channel_id=1, source_target_pairs={{0,2},{2,0},{1,3},{3,1},{4,6},{6,4},{5,7},{7,5},{8,10},{10,8},{9,1... | collective-permute-start | bytes 1179656 | tf_op jit(solution)/shard_map/ppermute | solution.py:58
  377.9 17.5 %collective-permute-start.57 = (bf16[128,1536]{1,0:T(8,128)(2,1)S(1)}, bf16[128,1536]{1,0:T(8,128)(2,1)}, u32[]{:S(2)}, u32[]{:S(2)}) collective-permute-start(bf16[128,1536]{1,0:T(8,128)(2,1)S(1)} %copy-done.45), channel_id=1, source_target_pairs={{0,2},{2,0},{1,3},{3,1},{4,6},{6,4},{5,7},{7,5},{8,10},{10,8},{9,1... | collective-permute-start | bytes 1179656 | tf_op jit(solution)/shard_map/ppermute | solution.py:58
  378.0 20.0 %collective-permute-start.56 = (bf16[128,1536]{1,0:T(8,128)(2,1)S(1)}, bf16[128,1536]{1,0:T(8,128)(2,1)S(1)}, u32[]{:S(2)}, u32[]{:S(2)}) collective-permute-start(bf16[128,1536]{1,0:T(8,128)(2,1)S(1)} %copy-done.43), channel_id=1, source_target_pairs={{0,2},{2,0},{1,3},{3,1},{4,6},{6,4},{5,7},{7,5},{8,10},{10,8},{9,1... | collective-permute-start | bytes 1179656 | tf_op jit(solution)/shard_map/ppermute | solution.py:58
  378.4 36.7 %all-to-all-start.2 = ((bf16[8,192,576]{2,1,0:T(8,128)(2,1)}), bf16[8,192,576]{2,1,0:T(8,128)(2,1)}, u32[]{:S(2)}, u32[]{:S(2)}) async-start(bf16[8,192,576]{2,1,0:T(8,128)(2,1)} %bitcast.36), calls=%async_computation.3 | async-start | bytes 3932160 | tf_op jit(solution)/shard_map/all_to_all | solution.py:72
  390.4 19.4 %collective-permute-start.62 = (bf16[128,1536]{1,0:T(8,128)(2,1)S(1)}, bf16[128,1536]{1,0:T(8,128)(2,1)S(1)}, u32[]{:S(2)}, u32[]{:S(2)}) collective-permute-start(bf16[128,1536]{1,0:T(8,128)(2,1)S(1)} %add_convert_fusion.1), channel_id=1, source_target_pairs={{4,0},{8,4},{12,8},{0,12},{5,1},{9,5},{13,9},{1,13},{6,2},{10,6},{... | collective-permute-start | bytes 1179656 | tf_op jit(solution)/shard_map/ppermute | solution.py:54
  394.4 15.4 %collective-permute-start.60 = (bf16[128,1536]{1,0:T(8,128)(2,1)S(1)}, bf16[128,1536]{1,0:T(8,128)(2,1)S(1)}, u32[]{:S(2)}, u32[]{:S(2)}) collective-permute-start(bf16[128,1536]{1,0:T(8,128)(2,1)S(1)} %add_convert_fusion.2), channel_id=1, source_target_pairs={{8,0},{12,4},{0,8},{4,12},{9,1},{13,5},{1,9},{5,13},{10,2},{14,6},... | collective-permute-start | bytes 1179656 | tf_op jit(solution)/shard_map/ppermute | solution.py:54
  397.2 17.5 %collective-permute-start.58 = (bf16[128,1536]{1,0:T(8,128)(2,1)}, bf16[128,1536]{1,0:T(8,128)(2,1)S(1)}, u32[]{:S(2)}, u32[]{:S(2)}) collective-permute-start(bf16[128,1536]{1,0:T(8,128)(2,1)} %add_convert_fusion.3), channel_id=1, source_target_pairs={{12,0},{0,4},{4,8},{8,12},{13,1},{1,5},{5,9},{9,13},{14,2},{2,6},{... | collective-permute-start | bytes 1179656 | tf_op jit(solution)/shard_map/ppermute | solution.py:54
  419.6 16.1 %all-to-all-start.3 = ((bf16[8,24,1872]{2,1,0:T(8,128)(2,1)}), bf16[8,24,1872]{2,1,0:T(8,128)(2,1)S(1)}, u32[]{:S(2)}, u32[]{:S(2)}) async-start(bf16[8,24,1872]{2,1,0:T(8,128)(2,1)} %pad_maximum_fusion.3), calls=%async_computation.4 | async-start | bytes 1474560 | tf_op jit(solution)/shard_map/all_to_all | solution.py:72
  435.9 9.1 %collective-permute-start.63 = (bf16[8,12,384]{2,1,0:T(8,128)(2,1)S(1)}, bf16[8,12,384]{2,1,0:T(8,128)(2,1)S(1)}, u32[]{:S(2)}, u32[]{:S(2)}) collective-permute-start(bf16[8,12,384]{2,1,0:T(8,128)(2,1)S(1)} %dynamic-slice_convert_fusion), channel_id=1, source_target_pairs={{0,1},{1,0},{2,3},{3,2},{4,5},{5,4},{6,7},{7,6},{8,9},{9,8},{10,11... | collective-permute-start | bytes 221192 | tf_op jit(solution)/shard_map/ppermute | solution.py:58
  438.7 5.6 %collective-permute-start.64 = (bf16[4,24,192]{2,1,0:T(8,128)(2,1)S(1)}, bf16[4,24,192]{2,1,0:T(8,128)(2,1)S(1)}, u32[]{:S(2)}, u32[]{:S(2)}) collective-permute-start(bf16[4,24,192]{2,1,0:T(8,128)(2,1)S(1)} %dynamic-slice_convert_fusion.1), channel_id=1, source_target_pairs={{0,1},{1,0},{2,3},{3,2},{4,5},{5,4},{6,7},{7,6},{8,9},{9,8},{10,11... | collective-permute-start | bytes 110600 | tf_op jit(solution)/shard_map/ppermute | solution.py:58
  (93 other events, 836.5 us)
Sparse Core Ops, SparseCore 0:
  30.7 109.0 all-gather.1
  256.0 99.0 reduce-scatter.1

commit v6 on v5

--- a/solution.py
+++ b/solution.py
@@ -16,9 +16,8 @@
 PAIR = 2 * ROWS
 GROUP = 3
 QUERY = GROUP * HEAD
-LANES = ROWS * GROUP
+LANES = PAIR * GROUP
 KEY_TILE = 512
-UNROLL = 4
 SUPER = 2048
 EARLIER = 2 * SUPER
 PART = 432
@@ -122,8 +121,9 @@
 
 
 def head_sums(v):
-    lane = lax.shift_right_logical(lax.broadcasted_iota(jnp.int32, (4 * HEAD, 4 * HEAD), 1), 6)
-    row = lax.shift_right_logical(lax.broadcasted_iota(jnp.int32, (4 * HEAD, 4 * HEAD), 0), 6)
+    shape = (v.shape[1], v.shape[1])
+    lane = lax.shift_right_logical(lax.broadcasted_iota(jnp.int32, shape, 1), 6)
+    row = lax.shift_right_logical(lax.broadcasted_iota(jnp.int32, shape, 0), 6)
     ones = jnp.where(lane == row, 1.0, 0.0).astype(BF16)
     high = v.astype(BF16)
     low = (v - high.astype(F32)).astype(BF16)
@@ -189,57 +189,90 @@
     )(*xs, w, gain, cos, sin, head_gain)
 
 
+def turned_back(g, raw, cos, sin, head_gain):
+    width = g.shape[1]
+    g = g * cos - half_turn(g) * sin
+    scale = lax.rsqrt(head_sums(raw * raw) * (1.0 / HEAD) + EPS)
+    gain = jnp.sum(g * raw * scale, axis=0, keepdims=True)
+    e = g * head_gain[:, -width:]
+    inner = head_sums(e * raw) * (1.0 / HEAD)
+    return scale * (e - raw * scale * scale * inner), gain
+
+
+def unproject_q_kernel(gq_ref, raw_ref, cos_ref, sin_ref, head_gain_ref, graw_ref, gain_ref):
+    gains = 0.0
+    for d in range(4):
+        g = gq_ref[2 * d : 2 * d + 2].reshape(PAIR, 4 * HEAD).astype(F32)
+        graw, gain = turned_back(
+            g, raw_ref[d], twice(cos_ref[d]), twice(sin_ref[d]), head_gain_ref[...]
+        )
+        graw_ref[d] = graw.astype(BF16)
+        gains = gains + gain
+    gain_ref[...] = gains
+
+
+def unproject_q(gq, raw, cos, sin, head_gain):
+    return pl.pallas_call(
+        unproject_q_kernel,
+        out_shape=(
+            jax.ShapeDtypeStruct((4, PAIR, 4 * HEAD), BF16),
+            jax.ShapeDtypeStruct((1, 4 * HEAD), F32),
+        ),
+        compiler_params=params(0, 20),
+        cost_estimate=cost(1e8, 4e6),
+    )(gq, raw, cos, sin, head_gain)
+
+
 def unproject_kernel(*refs):
-    gq_ref, g_refs, raw_ref, xs, (w_ref, cos_ref, sin_ref, head_gain_ref) = (
+    graw_q_ref, g_refs, raw_ref, xs, (w_ref, cos_ref, sin_ref, head_gain_ref) = (
         refs[0], refs[1:7], refs[7], refs[8:12], refs[12:16],
     )
-    parts, (graw_ref, attn_ref, heads_ref) = refs[16:20], refs[20:]
-    attn, sums = 0.0, 0.0
+    parts, (gkv_ref, attn_ref, gain_ref) = refs[16:20], refs[20:]
+    attn, gains = 0.0, 0.0
+    lane = lax.broadcasted_iota(jnp.int32, (PAIR, 2 * HEAD), 1)
     for i in range(2):
         tiles = slice(2 * i, 2 * i + 2)
-        gq = gq_ref[tiles].reshape(PAIR, 4 * HEAD).astype(F32)
         gkv = g_refs[0][tiles].astype(F32)
         for ref in g_refs[1:]:
             gkv = gkv + ref[tiles].astype(F32)
         gkv = gkv.reshape(PAIR, 2 * HEAD)
-        lane = lax.broadcasted_iota(jnp.int32, (PAIR, 2 * HEAD), 1)
-        gk = (gkv * HEAD**-0.5).astype(BF16).astype(F32)
-        gk = jnp.where(lane < HEAD, gq[:, 2 * HEAD :], gk)
-        g = jnp.concatenate([gq[:, : 2 * HEAD], gk], axis=1)
-        g = g * twice(cos_ref[i]) - half_turn(g) * twice(sin_ref[i])
-        raw = raw_ref[i]
-        scale = lax.rsqrt(head_sums(raw * raw) * (1.0 / HEAD) + EPS)
-        sums = sums + jnp.sum(g * raw * scale, axis=0, keepdims=True)
-        e = g * head_gain_ref[...]
-        inner = head_sums(e * raw) * (1.0 / HEAD)
-        graw = scale * (e - raw * scale * scale * inner)
-        graw = jnp.concatenate([graw, jnp.where(lane < HEAD, gkv, 0.0)], axis=1).astype(BF16)
-        graw_ref[i * PAIR : (i + 1) * PAIR, :] = graw
-        grad = dot(graw, w_ref[...], NT)
+        gk = jnp.where(lane < HEAD, 0.0, (gkv * HEAD**-0.5).astype(BF16).astype(F32))
+        graw_k, gain = turned_back(
+            gk, raw_ref[i][:, 2 * HEAD :], cos_ref[i], sin_ref[i], head_gain_ref[...]
+        )
+        gains = gains + gain
+        graw_q = graw_q_ref[i].astype(F32)
+        graw = [
+            graw_q[:, : 2 * HEAD],
+            jnp.where(lane < HEAD, graw_q[:, 2 * HEAD :], graw_k),
+            jnp.where(lane < HEAD, gkv, 0.0),
+        ]
+        gkv_ref[i * PAIR : (i + 1) * PAIR, :] = jnp.where(lane < HEAD, gkv, graw_k).astype(BF16)
+        grad = dot(jnp.concatenate(graw, axis=1).astype(BF16), w_ref[...], NT)
         x = stacked(*xs[tiles]).astype(F32)
         attn = attn + jnp.sum(grad * x * rms_scale(x), axis=0, keepdims=True)
         grad = grad.astype(BF16)
         parts[2 * i][...] = grad[:ROWS]
         parts[2 * i + 1][...] = grad[ROWS:]
     attn_ref[...] = attn
-    heads_ref[...] = sums
-
-
-def unproject(half, gq, gkvs, raw, xs, w, cos, sin, head_gain):
+    gain_ref[...] = gains
+
+
+def unproject(half, graw_q, gkvs, raw, xs, w, cos, sin, head_gain):
     def at_half(*shape):
         return pl.BlockSpec(shape, lambda i: (half,) + (0,) * (len(shape) - 1))
 
     table = at_half(2, PAIR, 2 * HEAD)
     outs = (jax.ShapeDtypeStruct((ROWS, WIDTH), BF16),) * 4 + (
-        jax.ShapeDtypeStruct((2 * PAIR, 6 * HEAD), BF16),
+        jax.ShapeDtypeStruct((2 * PAIR, 2 * HEAD), BF16),
         jax.ShapeDtypeStruct((1, WIDTH), F32),
-        jax.ShapeDtypeStruct((1, 4 * HEAD), F32),
+        jax.ShapeDtypeStruct((1, 2 * HEAD), F32),
     )
     return pl.pallas_call(
         unproject_kernel,
         out_shape=outs,
         grid=(1,),
-        in_specs=[at_half(4, ROWS, 4 * HEAD)]
+        in_specs=[at_half(2, PAIR, 4 * HEAD)]
         + [at_half(4, ROWS, 2 * HEAD)] * 6
         + [at_half(2, PAIR, 4 * HEAD)]
         + [ROWS_OF] * 4
@@ -247,7 +280,7 @@
         out_specs=tuple(all_of(*o.shape) for o in outs),
         compiler_params=params(1, 20),
         cost_estimate=cost(4 * PAIR * WIDTH * 384, 8e6),
-    )(gq, *gkvs, raw, *xs, w, cos, sin, head_gain)
+    )(graw_q, *gkvs, raw, *xs, w, cos, sin, head_gain)
 
 
 def ffn_kernel(
@@ -387,62 +420,93 @@
     )(mix, *branches)
 
 
-def pack_kernel(normed_ref, graw0_ref, graw1_ref, gains_ref, out_grad_ref, sent_ref):
-    graw = jnp.concatenate([graw0_ref[...], graw1_ref[...]], axis=0)
-    grad = dot(normed_ref[...], graw, TN)
+def pack_q_kernel(normed_ref, graw_ref, out_grad_ref, sent_ref):
+    graw = graw_ref[...].reshape(8 * ROWS, 4 * HEAD)
+    sent_ref[:, :QUERY] = dot(normed_ref[...], graw, TN)[:, :QUERY].astype(BF16)
+    sent_ref[:, QUERY:] = out_grad_ref[...].astype(BF16)
+
+
+def pack_q(normed, graw, out_grad):
+    tall = 256
+    return pl.pallas_call(
+        pack_q_kernel,
+        out_shape=jax.ShapeDtypeStruct((WIDTH, 2 * QUERY), BF16),
+        grid=(WIDTH // tall,),
+        in_specs=[
+            pl.BlockSpec((8 * ROWS, tall), lambda m: (0, m)),
+            all_of(4, PAIR, 4 * HEAD),
+            pl.BlockSpec((tall, QUERY), lambda m: (m, 0)),
+        ],
+        out_specs=pl.BlockSpec((tall, 2 * QUERY), lambda m: (m, 0)),
+        compiler_params=params(1, 16),
+        cost_estimate=cost(2 * 1024 * WIDTH * 256, 8e6),
+    )(normed, graw, out_grad)
+
+
+def pack_kv_kernel(normed_ref, gkv0_ref, gkv1_ref, gains_ref, sent_ref):
+    grad = dot(normed_ref[...], stacked(gkv0_ref, gkv1_ref), TN)
     gains = gains_ref[...]
     high = gains.astype(BF16).astype(F32)
     gains = jnp.concatenate([high, gains - high, jnp.zeros((HEAD - 32, gains.shape[1]), F32)], axis=0)
-    sent_ref[:, : 5 * HEAD] = grad[:, : 5 * HEAD].astype(BF16)
-    sent_ref[:, 5 * HEAD : 6 * HEAD] = gains.T.astype(BF16)
-    sent_ref[:, 6 * HEAD :] = out_grad_ref[...].astype(BF16)
-
-
-def pack(normed, graws, gains, out_grad):
+    sent_ref[:, : 2 * HEAD] = grad.astype(BF16)
+    sent_ref[:, 2 * HEAD :] = gains.T.astype(BF16)
+
+
+def pack_kv(normed, gkvs, gains):
     tall = 256
     return pl.pallas_call(
-        pack_kernel,
-        out_shape=jax.ShapeDtypeStruct((WIDTH, 9 * HEAD), BF16),
+        pack_kv_kernel,
+        out_shape=jax.ShapeDtypeStruct((WIDTH, QUERY), BF16),
         grid=(WIDTH // tall,),
         in_specs=[
             pl.BlockSpec((8 * ROWS, tall), lambda m: (0, m)),
-            all_of(4 * ROWS, 6 * HEAD),
-            all_of(4 * ROWS, 6 * HEAD),
+            all_of(4 * ROWS, 2 * HEAD),
+            all_of(4 * ROWS, 2 * HEAD),
             pl.BlockSpec((16, tall), lambda m: (0, m)),
-            pl.BlockSpec((tall, QUERY), lambda m: (m, 0)),
         ],
-        out_specs=pl.BlockSpec((tall, 9 * HEAD), lambda m: (m, 0)),
-        compiler_params=params(1, 24),
-        cost_estimate=cost(2 * 1024 * WIDTH * 384, 8e6),
-    )(normed, *graws, gains, out_grad)
-
-
-def side_by_side(t):
-    return jnp.concatenate([t[g * HEAD : (g + 1) * HEAD] for g in range(GROUP)], axis=1)
-
-
-def on_top(t):
-    return jnp.concatenate([t[:, g * ROWS : (g + 1) * ROWS] for g in range(GROUP)], axis=0)
-
-
-def key_loops(plan, at, base, start, visit, state):
-    f = pl.program_id(0)
-    lo, m1, m2, hi = (plan[f, at + i] for i in range(4))
-    place = lax.rem(lax.broadcasted_iota(jnp.int32, (1, LANES), 1), ROWS) + plan[f, 0]
+        out_specs=pl.BlockSpec((tall, QUERY), lambda m: (m, 0)),
+        compiler_params=params(1, 16),
+        cost_estimate=cost(2 * 1024 * WIDTH * 128, 6e6),
+    )(normed, *gkvs, gains)
+
+
+def to_lanes(v):
+    parts = []
+    for c in (0, 1):
+        t = v[c].astype(F32).T
+        parts += [t[g * HEAD : (g + 1) * HEAD] for g in range(GROUP)]
+    return jnp.concatenate(parts, axis=1)
+
+
+def from_lanes(t, c):
+    at = [(c * GROUP + g) * ROWS for g in range(GROUP)]
+    return jnp.concatenate([t[:, i : i + ROWS] for i in at], axis=0).T
+
+
+def key_loops(plan, at, base, unrolls, start, visit, state):
+    p = 2 * pl.program_id(0)
+    lo, m1, hi = plan[p, at], plan[p + 1, at + 1], plan[p + 1, at + 3]
+    m2 = jnp.maximum(plan[p, at + 2], m1)
+    core = plan[0, 15]
+    lane = lax.broadcasted_iota(jnp.int32, (1, LANES), 1)
+    place = lax.rem(lane, ROWS) + jnp.where(lane < LANES // 2, plan[p + core, 0], plan[p + 1 - core, 0])
 
     def masked(j, state):
         key = lax.broadcasted_iota(jnp.int32, (KEY_TILE, LANES), 0) + (j * KEY_TILE + base)
         return visit(j, state, (key >= start) & (key <= place))
 
-    def several(i, state):
-        for k in range(UNROLL):
-            state = visit(m1 + UNROLL * i + k, state, None)
-        return state
-
-    steps = lax.div(m2 - m1, UNROLL)
     state = lax.fori_loop(lo, m1, masked, state)
-    state = lax.fori_loop(0, steps, several, state)
-    state = lax.fori_loop(m1 + UNROLL * steps, m2, lambda j, s: visit(j, s, None), state)
+    done = m1
+    for unroll in unrolls:
+        steps = lax.div(m2 - done, unroll)
+
+        def several(i, state, done=done, unroll=unroll):
+            for k in range(unroll):
+                state = visit(done + unroll * i + k, state, None)
+            return state
+
+        state = lax.fori_loop(0, steps, several, state)
+        done = done + unroll * steps
     return lax.fori_loop(m2, hi, masked, state)
 
 
@@ -468,7 +532,7 @@
 
 
 def attend_body(at, base, plan, q_ref, start_ref, kv, kvt, state):
-    qt = side_by_side(q_ref[0].astype(F32).T)
+    qt = to_lanes(q_ref)
     qt = jnp.concatenate([jnp.zeros_like(qt), qt], axis=0).astype(BF16)
 
     def visit(j, state, mask):
@@ -479,7 +543,7 @@
         total = total + jnp.sum(weights, axis=0, keepdims=True)
         return total, accum + dot(kvt[:HEAD, rows_of(j)], weights.astype(BF16))
 
-    return key_loops(plan, at, base, start_ref[0], visit, state)
+    return key_loops(plan, at, base, (4, 2, 1), start_ref[0], visit, state)
 
 
 def attend_own_kernel(plan, q_ref, start_ref, *refs):
@@ -498,7 +562,8 @@
     total, accum = attend_body(2, 0, plan, q_ref, start_ref, kv, kvt, state)
     out = accum / total
     out_ref[0] = out
-    mix_ref[0] = on_top(out).T.astype(BF16)
+    for c in (0, 1):
+        mix_ref[c] = from_lanes(out, c).astype(BF16)
     lse_ref[0] = jnp.log2(total)
 
 
@@ -512,8 +577,8 @@
     def _():
         dkv[...] = jnp.zeros_like(dkv)
 
-    qt = side_by_side(q_ref[0].astype(F32).T)
-    gt = side_by_side(g_ref[0].astype(F32).T)
+    qt = to_lanes(q_ref)
+    gt = to_lanes(g_ref)
     delta = jnp.sum(gt * out_ref[0], axis=0, keepdims=True)
     zero = jnp.zeros_like(qt)
     gt = jnp.concatenate([gt, zero], axis=0)
@@ -532,11 +597,12 @@
         dkv[rows_of(j), :] += dot(sides, both)
         return dqt + dot(kvt[HEAD:, rows_of(j)], grads)
 
-    dqt = key_loops(plan, 11, 0, start_ref[0], visit, jnp.zeros((HEAD, LANES), F32))
-    dq = on_top(dqt * HEAD**-0.5).T
-    dq_ref[0] = jnp.concatenate([dq, jnp.zeros((ROWS, HEAD), F32)], axis=1).astype(BF16)
-
-    @pl.when(pl.program_id(0) == 7)
+    dqt = key_loops(plan, 11, 0, (2, 1), start_ref[0], visit, jnp.zeros((HEAD, LANES), F32))
+    for c in (0, 1):
+        dq = from_lanes(dqt * HEAD**-0.5, c)
+        dq_ref[c] = jnp.concatenate([dq, jnp.zeros((ROWS, HEAD), F32)], axis=1).astype(BF16)
+
+    @pl.when(pl.program_id(0) == 3)
     def _():
         for b, half, place, sent in chunks(plan, 3):
             sent_refs[2 * b + half][sent] = dkv[pl.ds(place, ROWS), :].astype(BF16)
@@ -551,7 +617,7 @@
 
 
 def placed(*shape):
-    return pl.BlockSpec((1,) + shape, lambda f, plan: (plan[f, 1],) + (0,) * len(shape))
+    return pl.BlockSpec((2,) + shape, lambda f, plan: (plan[2 * f, 16],) + (0,) * len(shape))
 
 
 def tiles_call(kernel, supers, outs, more_ins, out_specs, flops, back):
@@ -565,18 +631,18 @@
         out_shape=outs,
         grid_spec=pltpu.PrefetchScalarGridSpec(
             num_scalar_prefetch=1,
-            grid=(8,),
+            grid=(4,),
             in_specs=ins + more_ins,
             out_specs=out_specs,
             scratch_shapes=scratch,
         ),
-        compiler_params=params(1, 20),
+        compiler_params=params(1, 36 if back else 28),
         cost_estimate=cost(flops, 8e6, 1e7),
     )
 
 
-TILE_T = jax.ShapeDtypeStruct((8, HEAD, LANES), F32)
-TILE_ROW = jax.ShapeDtypeStruct((8, 1, LANES), F32)
+TILE_T = jax.ShapeDtypeStruct((4, HEAD, LANES), F32)
+TILE_ROW = jax.ShapeDtypeStruct((4, 1, LANES), F32)
 STATE = [tile(HEAD, LANES), tile(1, LANES)]
 
 
@@ -695,10 +761,13 @@
         [first - window, relative]
         + [jnp.minimum(v, edge) for v in (lo, m1, m2, hi)]
         + [jnp.maximum(v - edge, 0) for v in (lo, m1, m2, hi)]
-        + [jnp.broadcast_to(yhi, (8,)), lo, m1, m2, hi],
+        + [jnp.broadcast_to(yhi, (8,)), lo, m1, m2, hi]
+        + [jnp.broadcast_to(core, (8,)), (order // 2 - x) % 4],
         axis=1,
     ).astype(jnp.int32)
-    start_lanes = jnp.tile(own_starts - window, (1, GROUP)).reshape(8, 1, LANES)
+    pair_starts = (own_starts - window).reshape(4, 2, 1, ROWS)
+    pair_starts = jnp.where(core == 0, pair_starts, pair_starts[:, ::-1])
+    start_lanes = jnp.broadcast_to(pair_starts, (4, 2, GROUP, ROWS)).reshape(4, 1, LANES)
 
     normed, rot_q, kv, raw = project(
         all_tokens, qkv, gain_attn[None], cos, sin, head_gain
@@ -775,15 +844,18 @@
     ]
 
     grad_out = out_weights(after(mix, grad_q), branches)
-    grad_kvs, grad_out = lax.optimization_barrier((grad_kvs, grad_out))
+    graw_q, q_gain_part = unproject_q(grad_q, raw, cos, sin, head_gain)
+    sent_q = pack_q(normed, graw_q, grad_out)
+    grad_kvs, sent_q = lax.optimization_barrier((grad_kvs, sent_q))
+    got_q = exchange(sent_q.reshape(8, 192, 2 * QUERY), ("ylo", "z"))
 
     unprojected = [None] * 2
     for half in (1, 0):
         xs = all_tokens[4 * half : 4 * half + 4]
-        unprojected[half] = unproject(half, grad_q, grad_kvs, raw, xs, qkv, cos, sin, head_gain)
-    head_part = sum(u[6] for u in unprojected)[0]
-    q_gain_part = head_part[:HEAD] + head_part[HEAD : 2 * HEAD] + head_part[2 * HEAD : QUERY]
-    head_part = jnp.concatenate([q_gain_part, head_part[QUERY:], jnp.zeros((4,), F32)])
+        unprojected[half] = unproject(half, graw_q, grad_kvs, raw, xs, qkv, cos, sin, head_gain)
+    q_gain_part = q_gain_part[0, :HEAD] + q_gain_part[0, HEAD : 2 * HEAD] + q_gain_part[0, 2 * HEAD : QUERY]
+    k_gain_part = (unprojected[0][6] + unprojected[1][6])[0, HEAD:]
+    head_part = jnp.concatenate([q_gain_part, k_gain_part, jnp.zeros((4,), F32)])
     gain_parts = jnp.concatenate(
         [
             sum(u[5] for u in unprojected),
@@ -793,19 +865,21 @@
         ],
         axis=0,
     )
-    sent = pack(normed, [u[4] for u in unprojected], gain_parts, grad_out)
+    sent = pack_kv(normed, [u[4] for u in unprojected], gain_parts)
     parts = [u[2 * i : 2 * i + 2] for u in unprojected for i in (0, 1)]
     parts, sent = lax.optimization_barrier((parts, sent))
     grad_normed = near_sum(near_keep(parts))
-    got = exchange(sent.reshape(8, 192, 9 * HEAD), ("ylo", "z"))
-    got = jnp.sum(got.astype(F32), axis=0).astype(BF16)
-    last = jnp.concatenate(
-        [ffn_sum.reshape(8, 24, 3 * PART), got.reshape(8, 24, 9 * HEAD)], axis=-1
-    )
+    got = exchange(sent.reshape(8, 192, QUERY), ("ylo", "z"))
+
+    def added(v):
+        return jnp.sum(v.astype(F32), axis=0).astype(BF16).reshape(8, 24, -1)
+
+    last = jnp.concatenate([ffn_sum.reshape(8, 24, 3 * PART), added(got_q), added(got)], axis=-1)
     last = exchange(last, NEAR)
     ffn_grad, got = last[:, :, : 3 * PART], last[:, :, 3 * PART :].astype(F32)
 
-    qkv_grad, grad_out = got[:, :, : 6 * HEAD], got[:, :, 6 * HEAD :]
+    grad_out = got[:, :, QUERY : 2 * QUERY]
+    qkv_grad = jnp.concatenate([got[:, :, :QUERY], got[:, :, 2 * QUERY :]], axis=-1)
     here, there = jnp.where(yhi == 0, 0, 1), jnp.where(yhi == 0, 1, 0)
 
     def half_of(v, axis, which):
@@ -822,8 +896,8 @@
     qkv_grad = jnp.transpose(qkv_grad, (1, 0, 2))
     w_out_grad = jnp.transpose(grad_out, (0, 2, 1)).reshape(768, 24)
     w_query_grad = qkv_grad[:, :, :QUERY].reshape(12, -1)
-    w_key_grad = qkv_grad[:, :, QUERY : QUERY + HEAD].reshape(12, -1)
-    w_value_grad = qkv_grad[:, :, QUERY + HEAD : QUERY + 2 * HEAD].reshape(12, -1)
+    w_value_grad = qkv_grad[:, :, QUERY : QUERY + HEAD].reshape(12, -1)
+    w_key_grad = qkv_grad[:, :, QUERY + HEAD : QUERY + 2 * HEAD].reshape(12, -1)
 
     output = (hidden + out_total).astype(BF16)
     scale_attn = rms_scale(inputs)

time: 464 us -> 459 us (0.989)
  Pallas kernels: 124 us -> 116 us
    all_to_all x3 -> x4, waiting for transfers between devices: 24.6 us -> 30.8 us  [exchange(): return lax.all_to_all(v, axes, split_axis=0, concat_axis=0, tiled=True)]
    pallas_call x1, Pallas kernels: 38.5 us -> 33.3 us  [back(): return call(plan, q, start, *kvs, grad, out, lse)]
    all_to_all x3 -> x4, starting transfers between devices: 22.8 us -> 27.6 us  [exchange(): return lax.all_to_all(v, axes, split_axis=0, concat_axis=0, tiled=True)]
    unnamed x175 -> x177, local copies, waits for them, and re-layouts: 22.2 us -> 18.3 us
  transfers between devices with their start and end apart: 70 -> 71, of which waited for: 25 -> 26; matrix products, arithmetic and copies ran while one was open for 8% -> 8% of each run, Pallas kernels for 27% -> 26%
where the time goes in v6:
time: 459 us; the launch traced here: 451 us
  waiting for transfers between devices  134 us (29%)
  Pallas kernels  116 us (25%)
  starting transfers between devices  94.2 us (21%)
  local copies, waits for them, and re-layouts  46.3 us (10%)
  other arithmetic  27.4 us (6%)
  blocking collectives  17 us (4%)
  between operations  16.2 us (4%)
    ppermute x24, waiting for transfers between devices, shift_x(): return lax.ppermute(v, 'x', [((i + distance) % 4, i) for i in range(4)])  65 us
    pallas_call x1, Pallas kernels, back(): return call(plan, q, start, *kvs, grad, out, lse)  33.3 us
    all_to_all x4, waiting for transfers between devices, exchange(): return lax.all_to_all(v, axes, split_axis=0, concat_axis=0, tiled=True)  30.8 us
    all_to_all x4, starting transfers between devices, exchange(): return lax.all_to_all(v, axes, split_axis=0, concat_axis=0, tiled=True)  27.6 us
    ppermute x24, starting transfers between devices, shift_x(): return lax.ppermute(v, 'x', [((i + distance) % 4, i) for i in range(4)])  26.8 us
    ppermute x8, starting transfers between devices, shift_super(): return lax.ppermute(v, ('ylo', 'z', 'yhi'), pairs)  26.8 us
    pallas_call x4, Pallas kernels, ffn(): pl.pallas_call(ffn_kernel, out_shape=(jax.ShapeDtypeStruct((ROWS, WIDTH),...  26.7 us
    ppermute x8, waiting for transfers between devices, shift_super(): return lax.ppermute(v, ('ylo', 'z', 'yhi'), pairs)  21.7 us
  transfers between devices with their start and end apart: 71, of which 26 were waited for; matrix products, arithmetic and copies ran while one was open for 8% of the time, Pallas kernels for 26%

profile of v6, /device:TPU:8, one launch (start us, length us, event | category | flops | bytes accessed | tf_op | source)
XLA Modules:
  0.0 451.4 jit_solution(610409714476157901)
XLA Ops:
  12.7 17.0 %all_to_all.25 = bf16[8,24,1920]{2,1,0:T(8,128)(2,1)S(1)} all-to-all(bf16[8,24,1920]{2,1,0:T(8,128)(2,1)S(1)} %concatenate.54), channel_id=1, replica_groups=mesh['ylo'=2,'z'=4,'x'=4,'core'=2,'yhi'=2] {'x','core'}, dimensions={0} | all-to-all | bytes 1474560 | tf_op jit(solution)/shard_map/all_to_all | solution.py:71
  36.2 8.4 %all-to-all-start.1 = ((bf16[16,96,384]{2,1,0:T(8,128)(2,1)}), bf16[16,96,384]{2,1,0:T(8,128)(2,1)S(1)}, u32[]{:S(2)}, u32[]{:S(2)}) async-start(bf16[16,96,384]{2,1,0:T(8,128)(2,1)} %broadcast_in_dim.27), calls=%async_computation.1 | async-start | bytes 2359296 | tf_op jit(solution)/shard_map/all_to_all | solution.py:71
  44.7 1.9 fusion.12
  48.1 4.9 %collective-permute-done.5.refs_6_.refs_10_ = bf16[128,1536]{1,0:T(8,128)(2,1)} collective-permute-done((bf16[128,1536]{1,0:T(8,128)(2,1)S(1)}, bf16[128,1536]{1,0:T(8,128)(2,1)}, u32[]{:S(2)}, u32[]{:S(2)}) %collective-permute-start.5) | collective-permute-done | bytes 393248 | tf_op jit(solution)/shard_map/ppermute | solution.py:53
  53.4 15.2 %all-to-all-done.1 = bf16[16,96,384]{2,1,0:T(8,128)(2,1)S(1)} async-done(((bf16[16,96,384]{2,1,0:T(8,128)(2,1)}), bf16[16,96,384]{2,1,0:T(8,128)(2,1)S(1)}, u32[]{:S(2)}, u32[]{:S(2)}) %all-to-all-start.1) | async-done | bytes 1179680 | tf_op jit(solution)/shard_map/all_to_all | solution.py:71
  70.5 2.3 reshape.569.refs_8_.refs_12_
  74.4 5.1 %shard_map.237 = (bf16[1024,1536]{1,0:T(8,128)(2,1)S(1)}, bf16[8,128,192]{2,1,0:T(8,128)(2,1)S(1)}, bf16[8,128,128]{2,1,0:T(8,128)(2,1)}, f32[4,256,256]{2,1,0:T(8,128)S(1)}) custom-call(bf16[128,1536]{1,0:T(8,128)(2,1)S(1)} %copy-done.3, bf16[128,1536]{1,0:T(8,128)(2,1)S(1)} %collective-permute-done.refs_1_.refs_9_, ...), custom_call_target="tpu_custom_call" | custom-call | flops 1207959552 | bytes 10000000 | tf_op jit(solution)/shard_map/pallas_call | solution.py:168
  84.9 13.9 %collective-permute-done.7.refs_1_.refs_5_ = bf16[8,128,128]{2,1,0:T(8,128)(2,1)S(1)} collective-permute-done((bf16[8,128,128]{2,1,0:T(8,128)(2,1)}, bf16[8,128,128]{2,1,0:T(8,128)(2,1)S(1)}, u32[]{:S(2)}, u32[]{:S(2)}) %collective-permute-start.7) | collective-permute-done | bytes 262176 | tf_op jit(solution)/shard_map/ppermute | solution.py:57
  98.7 3.4 collective-permute-start.8
  102.1 1.9 collective-permute-start.9
  104.1 2.1 collective-permute-start.10
  106.2 3.7 collective-permute-start.11
  111.0 8.6 %shard_map.238 = (f32[4,64,768]{2,1,0:T(8,128)S(1)}, f32[4,1,768]{2,1,0:T(1,128)S(1)}) custom-call(s32[8,17]{1,0:T(8,128)S(1)} %stack.22.plan, bf16[8,128,192]{2,1,0:T(8,128)(2,1)S(1)} %copy-done.34, s32[4,1,768]{2,1,0:T(1,128)S(1)} %copy.103.start_ref, bf16[8,128,128]{2,1,0:T(8,128)(2,1)} %get-tuple-element.150.refs_0_.refs_4_, ...), custom_call_target="tpu_custom_call" | custom-call | flops 4000000000 | bytes 8000000 | tf_op jit(solution)/shard_map/pallas_call | solution.py:651
  119.5 3.3 collective-permute-done.8.refs_0_
  122.8 4.8 %collective-permute-done.9.refs_1_ = bf16[8,128,128]{2,1,0:T(8,128)(2,1)S(1)} collective-permute-done((bf16[8,128,128]{2,1,0:T(8,128)(2,1)}, bf16[8,128,128]{2,1,0:T(8,128)(2,1)S(1)}, u32[]{:S(2)}, u32[]{:S(2)}) %collective-permute-start.9) | collective-permute-done | bytes 262176 | tf_op jit(solution)/shard_map/ppermute | solution.py:67
  127.6 8.3 %collective-permute-done.10.refs_2_ = bf16[8,128,128]{2,1,0:T(8,128)(2,1)S(1)} collective-permute-done((bf16[8,128,128]{2,1,0:T(8,128)(2,1)}, bf16[8,128,128]{2,1,0:T(8,128)(2,1)S(1)}, u32[]{:S(2)}, u32[]{:S(2)}) %collective-permute-start.10) | collective-permute-done | bytes 262176 | tf_op jit(solution)/shard_map/ppermute | solution.py:67
  135.9 2.8 collective-permute-start.12
  140.6 9.2 %shard_map.239 = (bf16[8,128,192]{2,1,0:T(8,128)(2,1)S(1)}, f32[4,64,768]{2,1,0:T(8,128)S(1)}, f32[4,1,768]{2,1,0:T(1,128)S(1)}) custom-call(s32[8,17]{1,0:T(8,128)S(1)} %stack.22.plan, bf16[8,128,192]{2,1,0:T(8,128)(2,1)S(1)} %copy-done.35, s32[4,1,768]{2,1,0:T(1,128)S(1)} %copy.103.start_ref, bf16[8,128,128]{2,1,0:T(8,128)(2,1)S(1)} %collective-permute-done.8.refs_0_, ...), custom_call_target="tpu_custom_call" | custom-call | flops 8000000000 | bytes 8000000 | tf_op jit(solution)/shard_map/pallas_call | solution.py:658
  151.3 2.5 collective-permute-done.12.c0_ref.refs_10_
  153.8 3.7 collective-permute-done.14.c0_ref.refs_14_
  158.2 2.8 dynamic-slice_bitcast_fusion
  167.6 9.4 %collective-permute-done.21 = bf16[128,1536]{1,0:T(8,128)(2,1)S(1)} collective-permute-done((bf16[128,1536]{1,0:T(8,128)(2,1)S(1)}, bf16[128,1536]{1,0:T(8,128)(2,1)S(1)}, u32[]{:S(2)}, u32[]{:S(2)}) %collective-permute-start.21) | collective-permute-done | bytes 393248 | tf_op jit(solution)/shard_map/ppermute | solution.py:53
  177.0 2.6 collective-permute-done.19
  179.6 7.2 %collective-permute-done.17 = bf16[128,1536]{1,0:T(8,128)(2,1)S(1)} collective-permute-done((bf16[128,1536]{1,0:T(8,128)(2,1)S(1)}, bf16[128,1536]{1,0:T(8,128)(2,1)S(1)}, u32[]{:S(2)}, u32[]{:S(2)}) %collective-permute-start.17) | collective-permute-done | bytes 393248 | tf_op jit(solution)/shard_map/ppermute | solution.py:53
  189.5 1.8 collective-permute-start.31
  191.4 6.6 %shard_map.244 = (bf16[128,1536]{1,0:T(8,128)(2,1)S(1)}, bf16[128,1536]{1,0:T(8,128)(2,1)S(1)}, bf16[128,1536]{1,0:T(8,128)(2,1)S(1)}, bf16[128,1536]{1,0:T(8,12...) custom-call(bf16[128,1536]{1,0:T(8,128)(2,1)S(1)} %multiply_convert_fusion.x0_ref.refs_0_, ...), custom_call_target="tpu_custom_call" | custom-call | flops 4831838208 | bytes 14000000 | tf_op jit(solution)/shard_map/pallas_call | solution.py:324
  198.0 2.0 collective-permute-done.25.x0_ref.refs_2_
  203.0 6.7 %shard_map.245 = (bf16[128,1536]{1,0:T(8,128)(2,1)S(1)}, bf16[128,1536]{1,0:T(8,128)(2,1)S(1)}, bf16[128,1536]{1,0:T(8,128)(2,1)S(1)}, bf16[128,1536]{1,0:T(8,12...) custom-call(bf16[128,1536]{1,0:T(8,128)(2,1)S(1)} %collective-permute-done.25.x0_ref.refs_2_, ...), custom_call_target="tpu_custom_call" | custom-call | flops 4831838208 | bytes 14000000 | tf_op jit(solution)/shard_map/pallas_call | solution.py:324
  209.7 3.9 collective-permute-done.29.x0_ref.refs_4_
  214.1 6.7 %shard_map.246 = (bf16[128,1536]{1,0:T(8,128)(2,1)S(1)}, bf16[128,1536]{1,0:T(8,128)(2,1)S(1)}, bf16[128,1536]{1,0:T(8,128)(2,1)S(1)}, bf16[128,1536]{1,0:T(8,12...) custom-call(bf16[128,1536]{1,0:T(8,128)(2,1)S(1)} %collective-permute-done.31.x0_ref.refs_6_, ...), custom_call_target="tpu_custom_call" | custom-call | flops 4831838208 | bytes 14000000 | tf_op jit(solution)/shard_map/pallas_call | solution.py:324
  221.2 6.7 %shard_map.247 = (bf16[128,1536]{1,0:T(8,128)(2,1)S(1)}, bf16[128,1536]{1,0:T(8,128)(2,1)S(1)}, bf16[128,1536]{1,0:T(8,128)(2,1)S(1)}, bf16[128,1536]{1,0:T(8,12...) custom-call(bf16[128,1536]{1,0:T(8,128)(2,1)S(1)} %collective-permute-done.29.x0_ref.refs_4_, ...), custom_call_target="tpu_custom_call" | custom-call | flops 4831838208 | bytes 14000000 | tf_op jit(solution)/shard_map/pallas_call | solution.py:324
  230.6 1.8 collective-permute-start.39
  233.3 14.7 %shard_map.248 = bf16[2,1536,1296]{2,1,0:T(8,128)(2,1)S(1)} custom-call(bf16[128,1536]{1,0:T(8,128)(2,1)S(1)} %multiply_convert_fusion.x0_ref.refs_0_, bf16[128,1536]{1,0:T(8,128)(2,1)S(1)} %collective-permute-done.22.x1_ref.refs_1_, bf16[128,1536]{1,0:T(8,128)(2,1)S(1)} %collective-permute-done.25.x0_ref.refs_2_, ...), custom_call_target="tpu_custom_call" | custom-call | flops 9663676416 | bytes 24000000 | tf_op jit(solution)/shard_map/pallas_call | solution.py:360
  248.0 3.5 copy-done.8
  260.2 2.0 collective-permute-start.44
  263.6 7.4 %collective-permute-done.42.refs_2_ = bf16[128,1536]{1,0:T(8,128)(2,1)S(1)} collective-permute-done((bf16[128,1536]{1,0:T(8,128)(2,1)S(1)}, bf16[128,1536]{1,0:T(8,128)(2,1)S(1)}, u32[]{:S(2)}, u32[]{:S(2)}) %collective-permute-start.42) | collective-permute-done | bytes 393248 | tf_op jit(solution)/shard_map/ppermute | solution.py:53
  271.0 2.8 collective-permute-done.44.refs_4_
  273.8 6.4 %collective-permute-done.46.refs_6_ = bf16[128,1536]{1,0:T(8,128)(2,1)S(1)} collective-permute-done((bf16[128,1536]{1,0:T(8,128)(2,1)S(1)}, bf16[128,1536]{1,0:T(8,128)(2,1)S(1)}, u32[]{:S(2)}, u32[]{:S(2)}) %collective-permute-start.46) | collective-permute-done | bytes 393248 | tf_op jit(solution)/shard_map/ppermute | solution.py:53
  286.5 33.3 %shard_map.250 = (bf16[8,128,256]{2,1,0:T(8,128)(2,1)S(1)}, bf16[8,128,128]{2,1,0:T(8,128)(2,1)S(1)}, bf16[8,128,128]{2,1,0:T(8,128)(2,1)S(1)}, bf16[8,128,128]{...) custom-call(s32[8,17]{1,0:T(8,128)S(1)} %copy-done.32, ...), custom_call_target="tpu_custom_call" | custom-call | flops 30000001024 | bytes 8000000 | tf_op jit(solution)/shard_map/pallas_call | solution.py:672
  321.5 1.9 collective-permute-start.52
  323.4 1.9 collective-permute-start.53
  325.4 9.4 %collective-permute-start.54 = (bf16[8,128,128]{2,1,0:T(8,128)(2,1)S(1)}, bf16[8,128,128]{2,1,0:T(8,128)(2,1)S(1)}, u32[]{:S(2)}, u32[]{:S(2)}) collective-permute-start(bf16[8,128,128]{2,1,0:T(8,128)(2,1)S(1)} %get-tuple-element.243), channel_id=1, source_target_pairs={{32,0},{33,1},{48,16},{49,17},{64,32},{65,33},{80,48},{81,49},{96,... | collective-permute-start | bytes 786440 | tf_op jit(solution)/shard_map/ppermute | solution.py:67
  334.8 2.4 collective-permute-start.55
  340.4 3.6 shard_map.253
  344.1 5.3 %collective-permute-done.54.refs_5_ = bf16[8,128,128]{2,1,0:T(8,128)(2,1)S(1)} collective-permute-done((bf16[8,128,128]{2,1,0:T(8,128)(2,1)S(1)}, bf16[8,128,128]{2,1,0:T(8,128)(2,1)S(1)}, u32[]{:S(2)}, u32[]{:S(2)}) %collective-permute-start.54) | collective-permute-done | bytes 262176 | tf_op jit(solution)/shard_map/ppermute | solution.py:67
  349.4 2.7 shard_map.254
  352.2 3.8 shard_map.255
  360.5 1.9 copy-done.2
  362.4 3.5 shard_map.256
  367.0 10.6 %all-to-all-start.3 = ((bf16[8,192,192]{2,1,0:T(8,128)(2,1)}), bf16[8,192,192]{2,1,0:T(8,128)(2,1)}, u32[]{:S(2)}, u32[]{:S(2)}) async-start(bf16[8,192,192]{2,1,0:T(8,128)(2,1)} %bitcast.39), calls=%async_computation.4 | async-start | bytes 1572864 | tf_op jit(solution)/shard_map/all_to_all | solution.py:71
  377.6 1.8 add_convert_fusion.1
  379.5 2.7 collective-permute-start.62
  382.2 1.8 add_convert_fusion.2
  386.9 2.8 all-to-all-done.3
  389.7 4.3 all-to-all-start.2
  395.3 4.0 collective-permute-done.62
  399.3 5.4 %collective-permute-done.58 = bf16[128,1536]{1,0:T(8,128)(2,1)S(1)} collective-permute-done((bf16[128,1536]{1,0:T(8,128)(2,1)S(1)}, bf16[128,1536]{1,0:T(8,128)(2,1)S(1)}, u32[]{:S(2)}, u32[]{:S(2)}) %collective-permute-start.58) | collective-permute-done | bytes 393248 | tf_op jit(solution)/shard_map/ppermute | solution.py:53
  404.7 1.7 fusion
  406.5 3.2 all-to-all-done.2
  409.9 2.1 concatenate.66
  412.0 4.3 all-to-all-start.4
  416.3 3.0 fusion.6
  419.3 9.7 %all-to-all-done.4 = bf16[8,24,1872]{2,1,0:T(8,128)(2,1)} async-done(((bf16[8,24,1872]{2,1,0:T(8,128)(2,1)}), bf16[8,24,1872]{2,1,0:T(8,128)(2,1)}, u32[]{:S(2)}, u32[]{:S(2)}) %all-to-all-start.4) | async-done | bytes 718880 | tf_op jit(solution)/shard_map/all_to_all | solution.py:71
  430.9 3.4 collective-permute-start.64
  (419 shorter events, 86.7 us)
Async XLA Ops:
  7.2 151.0 %all-gather.2.cloned.1.call-start = ((), (), s32[]{:S(2)}) async-start(), calls=%async_computation.6 | async-start | bytes 10027008 | tf_op jit(solution)/shard_map/all_gather | solution.py:732
  30.6 43.2 %collective-permute-start = (bf16[128,1536]{1,0:T(8,128)(2,1)S(1)}, bf16[128,1536]{1,0:T(8,128)(2,1)S(1)}, u32[]{:S(2)}, u32[]{:S(2)}) collective-permute-start(bf16[128,1536]{1,0:T(8,128)(2,1)S(1)} %copy-done.3), channel_id=1, source_target_pairs={{0,2},{2,0},{1,3},{3,1},{4,6},{6,4},{5,7},{7,5},{8,10},{10,8},{9,1... | collective-permute-start | bytes 1179656 | tf_op jit(solution)/shard_map/ppermute | solution.py:57
  30.7 16.9 %collective-permute-start.1 = (bf16[128,1536]{1,0:T(8,128)(2,1)S(1)}, bf16[128,1536]{1,0:T(8,128)(2,1)}, u32[]{:S(2)}, u32[]{:S(2)}) collective-permute-start(bf16[128,1536]{1,0:T(8,128)(2,1)S(1)} %copy-done.3), channel_id=1, source_target_pairs={{4,0},{8,4},{12,8},{0,12},{5,1},{9,5},{13,9},{1,13},{6,2},{10,6},{... | collective-permute-start | bytes 1179656 | tf_op jit(solution)/shard_map/ppermute | solution.py:53
  31.9 15.8 %collective-permute-start.3 = (bf16[128,1536]{1,0:T(8,128)(2,1)S(1)}, bf16[128,1536]{1,0:T(8,128)(2,1)S(1)}, u32[]{:S(2)}, u32[]{:S(2)}) collective-permute-start(bf16[128,1536]{1,0:T(8,128)(2,1)S(1)} %copy-done.3), channel_id=1, source_target_pairs={{8,0},{12,4},{0,8},{4,12},{9,1},{13,5},{1,9},{5,13},{10,2},{14,6},... | collective-permute-start | bytes 1179656 | tf_op jit(solution)/shard_map/ppermute | solution.py:53
  33.4 19.7 %collective-permute-start.5 = (bf16[128,1536]{1,0:T(8,128)(2,1)S(1)}, bf16[128,1536]{1,0:T(8,128)(2,1)}, u32[]{:S(2)}, u32[]{:S(2)}) collective-permute-start(bf16[128,1536]{1,0:T(8,128)(2,1)S(1)} %copy-done.3), channel_id=1, source_target_pairs={{12,0},{0,4},{4,8},{8,12},{13,1},{1,5},{5,9},{9,13},{14,2},{2,6},{... | collective-permute-start | bytes 1179656 | tf_op jit(solution)/shard_map/ppermute | solution.py:53
  36.2 32.4 %all-to-all-start.1 = ((bf16[16,96,384]{2,1,0:T(8,128)(2,1)}), bf16[16,96,384]{2,1,0:T(8,128)(2,1)S(1)}, u32[]{:S(2)}, u32[]{:S(2)}) async-start(bf16[16,96,384]{2,1,0:T(8,128)(2,1)} %broadcast_in_dim.27), calls=%async_computation.1 | async-start | bytes 2359296 | tf_op jit(solution)/shard_map/all_to_all | solution.py:71
  44.6 365.3 %reduce-scatter.2.cloned.1.call-start = ((), (), s32[]{:S(2)}) async-start(), calls=%async_computation.7 | async-start | bytes 9191424 | tf_op jit(solution)/shard_map/reduce_scatter | solution.py:824
  47.5 26.3 %collective-permute-start.2 = (bf16[128,1536]{1,0:T(8,128)(2,1)}, bf16[128,1536]{1,0:T(8,128)(2,1)}, u32[]{:S(2)}, u32[]{:S(2)}) collective-permute-start(bf16[128,1536]{1,0:T(8,128)(2,1)} %collective-permute-done.1.refs_2_.refs_10_), channel_id=1, source_target_pairs={{0,2},{2,0},{1,3},{3,1},{4,6},{6,4},{5,7},{7,5},{8,10},{10,8},{9,1... | collective-permute-start | bytes 1179656 | tf_op jit(solution)/shard_map/ppermute | solution.py:57
  47.6 26.2 %collective-permute-start.4 = (bf16[128,1536]{1,0:T(8,128)(2,1)S(1)}, bf16[128,1536]{1,0:T(8,128)(2,1)}, u32[]{:S(2)}, u32[]{:S(2)}) collective-permute-start(bf16[128,1536]{1,0:T(8,128)(2,1)S(1)} %collective-permute-done.3.refs_4_.refs_8_), channel_id=1, source_target_pairs={{0,2},{2,0},{1,3},{3,1},{4,6},{6,4},{5,7},{7,5},{8,10},{10,8},{9,1... | collective-permute-start | bytes 1179656 | tf_op jit(solution)/shard_map/ppermute | solution.py:57
  53.1 20.8 %collective-permute-start.6 = (bf16[128,1536]{1,0:T(8,128)(2,1)}, bf16[128,1536]{1,0:T(8,128)(2,1)}, u32[]{:S(2)}, u32[]{:S(2)}) collective-permute-start(bf16[128,1536]{1,0:T(8,128)(2,1)} %collective-permute-done.5.refs_6_.refs_10_), channel_id=1, source_target_pairs={{0,2},{2,0},{1,3},{3,1},{4,6},{6,4},{5,7},{7,5},{8,10},{10,8},{9,1... | collective-permute-start | bytes 1179656 | tf_op jit(solution)/shard_map/ppermute | solution.py:57
  83.0 15.7 %collective-permute-start.7 = (bf16[8,128,128]{2,1,0:T(8,128)(2,1)}, bf16[8,128,128]{2,1,0:T(8,128)(2,1)S(1)}, u32[]{:S(2)}, u32[]{:S(2)}) collective-permute-start(bf16[8,128,128]{2,1,0:T(8,128)(2,1)} %get-tuple-element.150.refs_0_.refs_4_), channel_id=1, source_target_pairs={{0,1},{1,0},{2,3},{3,2},{4,5},{5,4},{6,7},{7,6},{8,9},{9,8},{10,11... | collective-permute-start | bytes 786440 | tf_op jit(solution)/shard_map/ppermute | solution.py:57
  98.7 24.1 %collective-permute-start.8 = (bf16[8,128,128]{2,1,0:T(8,128)(2,1)}, bf16[8,128,128]{2,1,0:T(8,128)(2,1)S(1)}, u32[]{:S(2)}, u32[]{:S(2)}) collective-permute-start(bf16[8,128,128]{2,1,0:T(8,128)(2,1)} %get-tuple-element.150.refs_0_.refs_4_), channel_id=1, source_target_pairs={{0,32},{1,33},{16,48},{17,49},{32,64},{33,65},{48,80},{49,81},{64,... | collective-permute-start | bytes 786440 | tf_op jit(solution)/shard_map/ppermute | solution.py:67
  102.1 25.5 %collective-permute-start.9 = (bf16[8,128,128]{2,1,0:T(8,128)(2,1)}, bf16[8,128,128]{2,1,0:T(8,128)(2,1)S(1)}, u32[]{:S(2)}, u32[]{:S(2)}) collective-permute-start(bf16[8,128,128]{2,1,0:T(8,128)(2,1)} %get-tuple-element.150.refs_0_.refs_4_), channel_id=1, source_target_pairs={{0,33},{1,32},{16,49},{17,48},{32,65},{33,64},{48,81},{49,80},{64,... | collective-permute-start | bytes 786440 | tf_op jit(solution)/shard_map/ppermute | solution.py:67
  104.1 31.9 %collective-permute-start.10 = (bf16[8,128,128]{2,1,0:T(8,128)(2,1)}, bf16[8,128,128]{2,1,0:T(8,128)(2,1)S(1)}, u32[]{:S(2)}, u32[]{:S(2)}) collective-permute-start(bf16[8,128,128]{2,1,0:T(8,128)(2,1)} %get-tuple-element.150.refs_0_.refs_4_), channel_id=1, source_target_pairs={{0,16},{1,17},{16,32},{17,33},{32,48},{33,49},{48,64},{49,65},{64,... | collective-permute-start | bytes 786440 | tf_op jit(solution)/shard_map/ppermute | solution.py:67
  106.2 29.7 %collective-permute-start.11 = (bf16[8,128,128]{2,1,0:T(8,128)(2,1)}, bf16[8,128,128]{2,1,0:T(8,128)(2,1)S(1)}, u32[]{:S(2)}, u32[]{:S(2)}) collective-permute-start(bf16[8,128,128]{2,1,0:T(8,128)(2,1)} %get-tuple-element.150.refs_0_.refs_4_), channel_id=1, source_target_pairs={{0,17},{1,16},{16,33},{17,32},{32,49},{33,48},{48,65},{49,64},{64,... | collective-permute-start | bytes 786440 | tf_op jit(solution)/shard_map/ppermute | solution.py:67
  135.9 17.8 %collective-permute-start.12 = (bf16[128,1536]{1,0:T(8,128)(2,1)S(1)}, bf16[128,1536]{1,0:T(8,128)(2,1)S(1)}, u32[]{:S(2)}, u32[]{:S(2)}) collective-permute-start(bf16[128,1536]{1,0:T(8,128)(2,1)S(1)} %copy-done.9), channel_id=1, source_target_pairs={{4,0},{8,4},{12,8},{0,12},{5,1},{9,5},{13,9},{1,13},{6,2},{10,6},{... | collective-permute-start | bytes 1179656 | tf_op jit(solution)/shard_map/ppermute | solution.py:53
  138.7 15.1 %collective-permute-start.13 = (bf16[128,1536]{1,0:T(8,128)(2,1)S(1)}, bf16[128,1536]{1,0:T(8,128)(2,1)S(1)}, u32[]{:S(2)}, u32[]{:S(2)}) collective-permute-start(bf16[128,1536]{1,0:T(8,128)(2,1)S(1)} %copy-done.9), channel_id=1, source_target_pairs={{8,0},{12,4},{0,8},{4,12},{9,1},{13,5},{1,9},{5,13},{10,2},{14,6},... | collective-permute-start | bytes 1179656 | tf_op jit(solution)/shard_map/ppermute | solution.py:53
  139.5 17.9 %collective-permute-start.14 = (bf16[128,1536]{1,0:T(8,128)(2,1)S(1)}, bf16[128,1536]{1,0:T(8,128)(2,1)S(1)}, u32[]{:S(2)}, u32[]{:S(2)}) collective-permute-start(bf16[128,1536]{1,0:T(8,128)(2,1)S(1)} %copy-done.9), channel_id=1, source_target_pairs={{12,0},{0,4},{4,8},{8,12},{13,1},{1,5},{5,9},{9,13},{14,2},{2,6},{... | collective-permute-start | bytes 1179656 | tf_op jit(solution)/shard_map/ppermute | solution.py:53
  164.3 3.3 collective-permute-start.15
  165.0 12.0 %collective-permute-start.21 = (bf16[128,1536]{1,0:T(8,128)(2,1)S(1)}, bf16[128,1536]{1,0:T(8,128)(2,1)S(1)}, u32[]{:S(2)}, u32[]{:S(2)}) collective-permute-start(bf16[128,1536]{1,0:T(8,128)(2,1)S(1)} %add_convert_fusion.10), channel_id=1, source_target_pairs={{4,0},{8,4},{12,8},{0,12},{5,1},{9,5},{13,9},{1,13},{6,2},{10,6},{... | collective-permute-start | bytes 1179656 | tf_op jit(solution)/shard_map/ppermute | solution.py:53
  166.0 13.6 %collective-permute-start.19 = (bf16[128,1536]{1,0:T(8,128)(2,1)S(1)}, bf16[128,1536]{1,0:T(8,128)(2,1)S(1)}, u32[]{:S(2)}, u32[]{:S(2)}) collective-permute-start(bf16[128,1536]{1,0:T(8,128)(2,1)S(1)} %add_convert_fusion.11), channel_id=1, source_target_pairs={{8,0},{12,4},{0,8},{4,12},{9,1},{13,5},{1,9},{5,13},{10,2},{14,6},... | collective-permute-start | bytes 1179656 | tf_op jit(solution)/shard_map/ppermute | solution.py:53
  166.7 20.1 %collective-permute-start.17 = (bf16[128,1536]{1,0:T(8,128)(2,1)S(1)}, bf16[128,1536]{1,0:T(8,128)(2,1)S(1)}, u32[]{:S(2)}, u32[]{:S(2)}) collective-permute-start(bf16[128,1536]{1,0:T(8,128)(2,1)S(1)} %add_convert_fusion.12), channel_id=1, source_target_pairs={{12,0},{0,4},{4,8},{8,12},{13,1},{1,5},{5,9},{9,13},{14,2},{2,6},{... | collective-permute-start | bytes 1179656 | tf_op jit(solution)/shard_map/ppermute | solution.py:53
  167.6 23.7 %collective-permute-start.23 = (bf16[128,1536]{1,0:T(8,128)(2,1)S(1)}, bf16[128,1536]{1,0:T(8,128)(2,1)S(1)}, u32[]{:S(2)}, u32[]{:S(2)}) collective-permute-start(bf16[128,1536]{1,0:T(8,128)(2,1)S(1)} %copy-done.10), channel_id=1, source_target_pairs={{0,2},{2,0},{1,3},{3,1},{4,6},{6,4},{5,7},{7,5},{8,10},{10,8},{9,1... | collective-permute-start | bytes 1179656 | tf_op jit(solution)/shard_map/ppermute | solution.py:57
  188.4 14.1 %collective-permute-start.27 = (bf16[128,1536]{1,0:T(8,128)(2,1)S(1)}, bf16[128,1536]{1,0:T(8,128)(2,1)S(1)}, u32[]{:S(2)}, u32[]{:S(2)}) collective-permute-start(bf16[128,1536]{1,0:T(8,128)(2,1)S(1)} %copy-done.22), channel_id=1, source_target_pairs={{0,2},{2,0},{1,3},{3,1},{4,6},{6,4},{5,7},{7,5},{8,10},{10,8},{9,1... | collective-permute-start | bytes 1179656 | tf_op jit(solution)/shard_map/ppermute | solution.py:57
  188.9 11.1 %collective-permute-start.25 = (bf16[128,1536]{1,0:T(8,128)(2,1)S(1)}, bf16[128,1536]{1,0:T(8,128)(2,1)S(1)}, u32[]{:S(2)}, u32[]{:S(2)}) collective-permute-start(bf16[128,1536]{1,0:T(8,128)(2,1)S(1)} %multiply_convert_fusion.x0_ref.refs_0_), channel_id=1, source_target_pairs={{4,0},{8,4},{12,8},{0,12},{5,1},{9,5},{13,9},{1,13},{6,2},{10,6},{... | collective-permute-start | bytes 1179656 | tf_op jit(solution)/shard_map/ppermute | solution.py:53
  189.5 12.4 %collective-permute-start.31 = (bf16[128,1536]{1,0:T(8,128)(2,1)S(1)}, bf16[128,1536]{1,0:T(8,128)(2,1)S(1)}, u32[]{:S(2)}, u32[]{:S(2)}) collective-permute-start(bf16[128,1536]{1,0:T(8,128)(2,1)S(1)} %multiply_convert_fusion.x0_ref.refs_0_), channel_id=1, source_target_pairs={{12,0},{0,4},{4,8},{8,12},{13,1},{1,5},{5,9},{9,13},{14,2},{2,6},{... | collective-permute-start | bytes 1179656 | tf_op jit(solution)/shard_map/ppermute | solution.py:53
  200.0 14.1 %collective-permute-start.33 = (bf16[128,1536]{1,0:T(8,128)(2,1)S(1)}, bf16[128,1536]{1,0:T(8,128)(2,1)S(1)}, u32[]{:S(2)}, u32[]{:S(2)}) collective-permute-start(bf16[128,1536]{1,0:T(8,128)(2,1)S(1)} %copy-done.26), channel_id=1, source_target_pairs={{0,2},{2,0},{1,3},{3,1},{4,6},{6,4},{5,7},{7,5},{8,10},{10,8},{9,1... | collective-permute-start | bytes 1179656 | tf_op jit(solution)/shard_map/ppermute | solution.py:57
  200.6 20.6 %collective-permute-start.34 = (bf16[128,1536]{1,0:T(8,128)(2,1)S(1)}, bf16[128,1536]{1,0:T(8,128)(2,1)S(1)}, u32[]{:S(2)}, u32[]{:S(2)}) collective-permute-start(bf16[128,1536]{1,0:T(8,128)(2,1)S(1)} %copy-done.24), channel_id=1, source_target_pairs={{0,2},{2,0},{1,3},{3,1},{4,6},{6,4},{5,7},{7,5},{8,10},{10,8},{9,1... | collective-permute-start | bytes 1179656 | tf_op jit(solution)/shard_map/ppermute | solution.py:57
  202.0 11.6 %collective-permute-start.29 = (bf16[128,1536]{1,0:T(8,128)(2,1)S(1)}, bf16[128,1536]{1,0:T(8,128)(2,1)S(1)}, u32[]{:S(2)}, u32[]{:S(2)}) collective-permute-start(bf16[128,1536]{1,0:T(8,128)(2,1)S(1)} %multiply_convert_fusion.x0_ref.refs_0_), channel_id=1, source_target_pairs={{8,0},{12,4},{0,8},{4,12},{9,1},{13,5},{1,9},{5,13},{10,2},{14,6},... | collective-permute-start | bytes 1179656 | tf_op jit(solution)/shard_map/ppermute | solution.py:53
  202.5 18.6 %collective-permute-start.24 = (bf16[128,1536]{1,0:T(8,128)(2,1)S(1)}, bf16[128,1536]{1,0:T(8,128)(2,1)S(1)}, u32[]{:S(2)}, u32[]{:S(2)}) collective-permute-start(bf16[128,1536]{1,0:T(8,128)(2,1)S(1)} %get-tuple-element.171), channel_id=1, source_target_pairs={{0,2},{2,0},{1,3},{3,1},{4,6},{6,4},{5,7},{7,5},{8,10},{10,8},{9,1... | collective-permute-start | bytes 1179656 | tf_op jit(solution)/shard_map/ppermute | solution.py:57
  202.5 11.1 %collective-permute-start.32 = (bf16[128,1536]{1,0:T(8,128)(2,1)S(1)}, bf16[128,1536]{1,0:T(8,128)(2,1)S(1)}, u32[]{:S(2)}, u32[]{:S(2)}) collective-permute-start(bf16[128,1536]{1,0:T(8,128)(2,1)S(1)} %collective-permute-done.31.x0_ref.refs_6_), channel_id=1, source_target_pairs={{0,2},{2,0},{1,3},{3,1},{4,6},{6,4},{5,7},{7,5},{8,10},{10,8},{9,1... | collective-permute-start | bytes 1179656 | tf_op jit(solution)/shard_map/ppermute | solution.py:57
  213.6 14.9 %collective-permute-start.28 = (bf16[128,1536]{1,0:T(8,128)(2,1)S(1)}, bf16[128,1536]{1,0:T(8,128)(2,1)S(1)}, u32[]{:S(2)}, u32[]{:S(2)}) collective-permute-start(bf16[128,1536]{1,0:T(8,128)(2,1)S(1)} %get-tuple-element.175), channel_id=1, source_target_pairs={{0,2},{2,0},{1,3},{3,1},{4,6},{6,4},{5,7},{7,5},{8,10},{10,8},{9,1... | collective-permute-start | bytes 1179656 | tf_op jit(solution)/shard_map/ppermute | solution.py:57
  213.6 7.6 %collective-permute-start.30 = (bf16[128,1536]{1,0:T(8,128)(2,1)S(1)}, bf16[128,1536]{1,0:T(8,128)(2,1)S(1)}, u32[]{:S(2)}, u32[]{:S(2)}) collective-permute-start(bf16[128,1536]{1,0:T(8,128)(2,1)S(1)} %collective-permute-done.29.x0_ref.refs_4_), channel_id=1, source_target_pairs={{0,2},{2,0},{1,3},{3,1},{4,6},{6,4},{5,7},{7,5},{8,10},{10,8},{9,1... | collective-permute-start | bytes 1179656 | tf_op jit(solution)/shard_map/ppermute | solution.py:57
  220.8 7.8 %collective-permute-start.36 = (bf16[128,1536]{1,0:T(8,128)(2,1)S(1)}, bf16[128,1536]{1,0:T(8,128)(2,1)S(1)}, u32[]{:S(2)}, u32[]{:S(2)}) collective-permute-start(bf16[128,1536]{1,0:T(8,128)(2,1)S(1)} %get-tuple-element.187), channel_id=1, source_target_pairs={{0,2},{2,0},{1,3},{3,1},{4,6},{6,4},{5,7},{7,5},{8,10},{10,8},{9,1... | collective-permute-start | bytes 1179656 | tf_op jit(solution)/shard_map/ppermute | solution.py:57
  230.2 23.9 %collective-permute-start.40 = (bf16[4,128,1536]{2,1,0:T(8,128)(2,1)S(1)}, bf16[4,128,1536]{2,1,0:T(8,128)(2,1)S(1)}, u32[]{:S(2)}, u32[]{:S(2)}) collective-permute-start(bf16[4,128,1536]{2,1,0:T(8,128)(2,1)S(1)} %pad_maximum_fusion), channel_id=1, source_target_pairs={{0,2},{2,0},{1,3},{3,1},{4,6},{6,4},{5,7},{7,5},{8,10},{10,8},{9,1... | collective-permute-start | bytes 4718600 | tf_op jit(solution)/shard_map/ppermute | solution.py:57
  230.6 20.9 %collective-permute-start.39 = (bf16[128,1536]{1,0:T(8,128)(2,1)S(1)}, bf16[128,1536]{1,0:T(8,128)(2,1)S(1)}, u32[]{:S(2)}, u32[]{:S(2)}) collective-permute-start(bf16[128,1536]{1,0:T(8,128)(2,1)S(1)} %add_convert_fusion.6), channel_id=1, source_target_pairs={{4,0},{8,4},{12,8},{0,12},{5,1},{9,5},{13,9},{1,13},{6,2},{10,6},{... | collective-permute-start | bytes 1179656 | tf_op jit(solution)/shard_map/ppermute | solution.py:53
  232.4 19.1 %collective-permute-start.38 = (bf16[128,1536]{1,0:T(8,128)(2,1)S(1)}, bf16[128,1536]{1,0:T(8,128)(2,1)S(1)}, u32[]{:S(2)}, u32[]{:S(2)}) collective-permute-start(bf16[128,1536]{1,0:T(8,128)(2,1)S(1)} %add_convert_fusion.7), channel_id=1, source_target_pairs={{8,0},{12,4},{0,8},{4,12},{9,1},{13,5},{1,9},{5,13},{10,2},{14,6},... | collective-permute-start | bytes 1179656 | tf_op jit(solution)/shard_map/ppermute | solution.py:53
  232.7 20.2 %collective-permute-start.37 = (bf16[128,1536]{1,0:T(8,128)(2,1)S(1)}, bf16[128,1536]{1,0:T(8,128)(2,1)S(1)}, u32[]{:S(2)}, u32[]{:S(2)}) collective-permute-start(bf16[128,1536]{1,0:T(8,128)(2,1)S(1)} %add_convert_fusion.8), channel_id=1, source_target_pairs={{12,0},{0,4},{4,8},{8,12},{13,1},{1,5},{5,9},{9,13},{14,2},{2,6},{... | collective-permute-start | bytes 1179656 | tf_op jit(solution)/shard_map/ppermute | solution.py:53
  258.9 12.1 %collective-permute-start.42 = (bf16[128,1536]{1,0:T(8,128)(2,1)S(1)}, bf16[128,1536]{1,0:T(8,128)(2,1)S(1)}, u32[]{:S(2)}, u32[]{:S(2)}) collective-permute-start(bf16[128,1536]{1,0:T(8,128)(2,1)S(1)} %fusion.45.refs_0_), channel_id=1, source_target_pairs={{4,0},{8,4},{12,8},{0,12},{5,1},{9,5},{13,9},{1,13},{6,2},{10,6},{... | collective-permute-start | bytes 1179656 | tf_op jit(solution)/shard_map/ppermute | solution.py:53
  260.2 13.6 %collective-permute-start.44 = (bf16[128,1536]{1,0:T(8,128)(2,1)S(1)}, bf16[128,1536]{1,0:T(8,128)(2,1)S(1)}, u32[]{:S(2)}, u32[]{:S(2)}) collective-permute-start(bf16[128,1536]{1,0:T(8,128)(2,1)S(1)} %fusion.45.refs_0_), channel_id=1, source_target_pairs={{8,0},{12,4},{0,8},{4,12},{9,1},{13,5},{1,9},{5,13},{10,2},{14,6},... | collective-permute-start | bytes 1179656 | tf_op jit(solution)/shard_map/ppermute | solution.py:53
  262.2 18.0 %collective-permute-start.46 = (bf16[128,1536]{1,0:T(8,128)(2,1)S(1)}, bf16[128,1536]{1,0:T(8,128)(2,1)S(1)}, u32[]{:S(2)}, u32[]{:S(2)}) collective-permute-start(bf16[128,1536]{1,0:T(8,128)(2,1)S(1)} %fusion.45.refs_0_), channel_id=1, source_target_pairs={{12,0},{0,4},{4,8},{8,12},{13,1},{1,5},{5,9},{9,13},{14,2},{2,6},{... | collective-permute-start | bytes 1179656 | tf_op jit(solution)/shard_map/ppermute | solution.py:53
  263.0 17.3 %collective-permute-start.41 = (bf16[128,1536]{1,0:T(8,128)(2,1)S(1)}, bf16[128,1536]{1,0:T(8,128)(2,1)S(1)}, u32[]{:S(2)}, u32[]{:S(2)}) collective-permute-start(bf16[128,1536]{1,0:T(8,128)(2,1)S(1)} %fusion.45.refs_0_), channel_id=1, source_target_pairs={{0,2},{2,0},{1,3},{3,1},{4,6},{6,4},{5,7},{7,5},{8,10},{10,8},{9,1... | collective-permute-start | bytes 1179656 | tf_op jit(solution)/shard_map/ppermute | solution.py:57
  271.0 9.3 %collective-permute-start.43 = (bf16[128,1536]{1,0:T(8,128)(2,1)S(1)}, bf16[128,1536]{1,0:T(8,128)(2,1)S(1)}, u32[]{:S(2)}, u32[]{:S(2)}) collective-permute-start(bf16[128,1536]{1,0:T(8,128)(2,1)S(1)} %collective-permute-done.42.refs_2_), channel_id=1, source_target_pairs={{0,2},{2,0},{1,3},{3,1},{4,6},{6,4},{5,7},{7,5},{8,10},{10,8},{9,1... | collective-permute-start | bytes 1179656 | tf_op jit(solution)/shard_map/ppermute | solution.py:57
  273.8 6.5 %collective-permute-start.45 = (bf16[128,1536]{1,0:T(8,128)(2,1)S(1)}, bf16[128,1536]{1,0:T(8,128)(2,1)S(1)}, u32[]{:S(2)}, u32[]{:S(2)}) collective-permute-start(bf16[128,1536]{1,0:T(8,128)(2,1)S(1)} %collective-permute-done.44.refs_4_), channel_id=1, source_target_pairs={{0,2},{2,0},{1,3},{3,1},{4,6},{6,4},{5,7},{7,5},{8,10},{10,8},{9,1... | collective-permute-start | bytes 1179656 | tf_op jit(solution)/shard_map/ppermute | solution.py:57
  282.0 37.8 %collective-permute-start.50 = (bf16[128,1536]{1,0:T(8,128)(2,1)S(1)}, bf16[128,1536]{1,0:T(8,128)(2,1)S(1)}, u32[]{:S(2)}, u32[]{:S(2)}) collective-permute-start(bf16[128,1536]{1,0:T(8,128)(2,1)S(1)} %get-tuple-element.234), channel_id=1, source_target_pairs={{4,0},{8,4},{12,8},{0,12},{5,1},{9,5},{13,9},{1,13},{6,2},{10,6},{... | collective-permute-start | bytes 1179656 | tf_op jit(solution)/shard_map/ppermute | solution.py:53
  283.2 36.5 %collective-permute-start.49 = (bf16[128,1536]{1,0:T(8,128)(2,1)S(1)}, bf16[128,1536]{1,0:T(8,128)(2,1)S(1)}, u32[]{:S(2)}, u32[]{:S(2)}) collective-permute-start(bf16[128,1536]{1,0:T(8,128)(2,1)S(1)} %get-tuple-element.233), channel_id=1, source_target_pairs={{8,0},{12,4},{0,8},{4,12},{9,1},{13,5},{1,9},{5,13},{10,2},{14,6},... | collective-permute-start | bytes 1179656 | tf_op jit(solution)/shard_map/ppermute | solution.py:53
  284.7 35.1 %collective-permute-start.48 = (bf16[128,1536]{1,0:T(8,128)(2,1)S(1)}, bf16[128,1536]{1,0:T(8,128)(2,1)S(1)}, u32[]{:S(2)}, u32[]{:S(2)}) collective-permute-start(bf16[128,1536]{1,0:T(8,128)(2,1)S(1)} %get-tuple-element.232), channel_id=1, source_target_pairs={{12,0},{0,4},{4,8},{8,12},{13,1},{1,5},{5,9},{9,13},{14,2},{2,6},{... | collective-permute-start | bytes 1179656 | tf_op jit(solution)/shard_map/ppermute | solution.py:53
  320.9 23.2 %collective-permute-start.51 = (bf16[8,128,128]{2,1,0:T(8,128)(2,1)S(1)}, bf16[8,128,128]{2,1,0:T(8,128)(2,1)S(1)}, u32[]{:S(2)}, u32[]{:S(2)}) collective-permute-start(bf16[8,128,128]{2,1,0:T(8,128)(2,1)S(1)} %get-tuple-element.240), channel_id=1, source_target_pairs={{0,1},{1,0},{2,3},{3,2},{4,5},{5,4},{6,7},{7,6},{8,9},{9,8},{10,11... | collective-permute-start | bytes 786440 | tf_op jit(solution)/shard_map/ppermute | solution.py:57
  321.5 22.6 %collective-permute-start.52 = (bf16[8,128,128]{2,1,0:T(8,128)(2,1)S(1)}, bf16[8,128,128]{2,1,0:T(8,128)(2,1)S(1)}, u32[]{:S(2)}, u32[]{:S(2)}) collective-permute-start(bf16[8,128,128]{2,1,0:T(8,128)(2,1)S(1)} %get-tuple-element.241), channel_id=1, source_target_pairs={{16,0},{17,1},{32,16},{33,17},{48,32},{49,33},{64,48},{65,49},{80,... | collective-permute-start | bytes 786440 | tf_op jit(solution)/shard_map/ppermute | solution.py:67
  323.4 20.7 %collective-permute-start.53 = (bf16[8,128,128]{2,1,0:T(8,128)(2,1)S(1)}, bf16[8,128,128]{2,1,0:T(8,128)(2,1)S(1)}, u32[]{:S(2)}, u32[]{:S(2)}) collective-permute-start(bf16[8,128,128]{2,1,0:T(8,128)(2,1)S(1)} %get-tuple-element.242), channel_id=1, source_target_pairs={{16,1},{17,0},{32,17},{33,16},{48,33},{49,32},{64,49},{65,48},{80,... | collective-permute-start | bytes 786440 | tf_op jit(solution)/shard_map/ppermute | solution.py:67
  325.4 24.0 %collective-permute-start.54 = (bf16[8,128,128]{2,1,0:T(8,128)(2,1)S(1)}, bf16[8,128,128]{2,1,0:T(8,128)(2,1)S(1)}, u32[]{:S(2)}, u32[]{:S(2)}) collective-permute-start(bf16[8,128,128]{2,1,0:T(8,128)(2,1)S(1)} %get-tuple-element.243), channel_id=1, source_target_pairs={{32,0},{33,1},{48,16},{49,17},{64,32},{65,33},{80,48},{81,49},{96,... | collective-permute-start | bytes 786440 | tf_op jit(solution)/shard_map/ppermute | solution.py:67
  334.8 14.6 %collective-permute-start.55 = (bf16[8,128,128]{2,1,0:T(8,128)(2,1)S(1)}, bf16[8,128,128]{2,1,0:T(8,128)(2,1)S(1)}, u32[]{:S(2)}, u32[]{:S(2)}) collective-permute-start(bf16[8,128,128]{2,1,0:T(8,128)(2,1)S(1)} %get-tuple-element.244), channel_id=1, source_target_pairs={{32,1},{33,0},{48,17},{49,16},{64,33},{65,32},{80,49},{81,48},{96,... | collective-permute-start | bytes 786440 | tf_op jit(solution)/shard_map/ppermute | solution.py:67
  366.0 11.7 %collective-permute-start.61 = (bf16[128,1536]{1,0:T(8,128)(2,1)}, bf16[128,1536]{1,0:T(8,128)(2,1)}, u32[]{:S(2)}, u32[]{:S(2)}) collective-permute-start(bf16[128,1536]{1,0:T(8,128)(2,1)} %get-tuple-element.275), channel_id=1, source_target_pairs={{0,2},{2,0},{1,3},{3,1},{4,6},{6,4},{5,7},{7,5},{8,10},{10,8},{9,1... | collective-permute-start | bytes 1179656 | tf_op jit(solution)/shard_map/ppermute | solution.py:57
  366.0 16.2 %collective-permute-start.59 = (bf16[128,1536]{1,0:T(8,128)(2,1)S(1)}, bf16[128,1536]{1,0:T(8,128)(2,1)}, u32[]{:S(2)}, u32[]{:S(2)}) collective-permute-start(bf16[128,1536]{1,0:T(8,128)(2,1)S(1)} %copy-done.44), channel_id=1, source_target_pairs={{0,2},{2,0},{1,3},{3,1},{4,6},{6,4},{5,7},{7,5},{8,10},{10,8},{9,1... | collective-permute-start | bytes 1179656 | tf_op jit(solution)/shard_map/ppermute | solution.py:57
  366.5 18.4 %collective-permute-start.57 = (bf16[128,1536]{1,0:T(8,128)(2,1)S(1)}, bf16[128,1536]{1,0:T(8,128)(2,1)}, u32[]{:S(2)}, u32[]{:S(2)}) collective-permute-start(bf16[128,1536]{1,0:T(8,128)(2,1)S(1)} %copy-done.42), channel_id=1, source_target_pairs={{0,2},{2,0},{1,3},{3,1},{4,6},{6,4},{5,7},{7,5},{8,10},{10,8},{9,1... | collective-permute-start | bytes 1179656 | tf_op jit(solution)/shard_map/ppermute | solution.py:57
  366.6 28.7 %collective-permute-start.56 = (bf16[128,1536]{1,0:T(8,128)(2,1)S(1)}, bf16[128,1536]{1,0:T(8,128)(2,1)}, u32[]{:S(2)}, u32[]{:S(2)}) collective-permute-start(bf16[128,1536]{1,0:T(8,128)(2,1)S(1)} %copy-done.40), channel_id=1, source_target_pairs={{0,2},{2,0},{1,3},{3,1},{4,6},{6,4},{5,7},{7,5},{8,10},{10,8},{9,1... | collective-permute-start | bytes 1179656 | tf_op jit(solution)/shard_map/ppermute | solution.py:57
  367.0 22.7 %all-to-all-start.3 = ((bf16[8,192,192]{2,1,0:T(8,128)(2,1)}), bf16[8,192,192]{2,1,0:T(8,128)(2,1)}, u32[]{:S(2)}, u32[]{:S(2)}) async-start(bf16[8,192,192]{2,1,0:T(8,128)(2,1)} %bitcast.39), calls=%async_computation.4 | async-start | bytes 1572864 | tf_op jit(solution)/shard_map/all_to_all | solution.py:71
  379.5 19.8 %collective-permute-start.62 = (bf16[128,1536]{1,0:T(8,128)(2,1)}, bf16[128,1536]{1,0:T(8,128)(2,1)}, u32[]{:S(2)}, u32[]{:S(2)}) collective-permute-start(bf16[128,1536]{1,0:T(8,128)(2,1)} %add_convert_fusion.1), channel_id=1, source_target_pairs={{4,0},{8,4},{12,8},{0,12},{5,1},{9,5},{13,9},{1,13},{6,2},{10,6},{... | collective-permute-start | bytes 1179656 | tf_op jit(solution)/shard_map/ppermute | solution.py:53
  384.0 15.3 %collective-permute-start.60 = (bf16[128,1536]{1,0:T(8,128)(2,1)}, bf16[128,1536]{1,0:T(8,128)(2,1)}, u32[]{:S(2)}, u32[]{:S(2)}) collective-permute-start(bf16[128,1536]{1,0:T(8,128)(2,1)} %add_convert_fusion.2), channel_id=1, source_target_pairs={{8,0},{12,4},{0,8},{4,12},{9,1},{13,5},{1,9},{5,13},{10,2},{14,6},... | collective-permute-start | bytes 1179656 | tf_op jit(solution)/shard_map/ppermute | solution.py:53
  386.0 18.8 %collective-permute-start.58 = (bf16[128,1536]{1,0:T(8,128)(2,1)S(1)}, bf16[128,1536]{1,0:T(8,128)(2,1)S(1)}, u32[]{:S(2)}, u32[]{:S(2)}) collective-permute-start(bf16[128,1536]{1,0:T(8,128)(2,1)S(1)} %add_convert_fusion.3), channel_id=1, source_target_pairs={{12,0},{0,4},{4,8},{8,12},{13,1},{1,5},{5,9},{9,13},{14,2},{2,6},{... | collective-permute-start | bytes 1179656 | tf_op jit(solution)/shard_map/ppermute | solution.py:53
  389.7 19.9 %all-to-all-start.2 = ((bf16[8,192,384]{2,1,0:T(8,128)(2,1)}), bf16[8,192,384]{2,1,0:T(8,128)(2,1)S(1)}, u32[]{:S(2)}, u32[]{:S(2)}) async-start(bf16[8,192,384]{2,1,0:T(8,128)(2,1)} %bitcast.37), calls=%async_computation.3 | async-start | bytes 2359296 | tf_op jit(solution)/shard_map/all_to_all | solution.py:71
  412.0 17.0 %all-to-all-start.4 = ((bf16[8,24,1872]{2,1,0:T(8,128)(2,1)}), bf16[8,24,1872]{2,1,0:T(8,128)(2,1)}, u32[]{:S(2)}, u32[]{:S(2)}) async-start(bf16[8,24,1872]{2,1,0:T(8,128)(2,1)} %concatenate.66), calls=%async_computation.5 | async-start | bytes 1474560 | tf_op jit(solution)/shard_map/all_to_all | solution.py:71
  430.3 9.7 %collective-permute-start.63 = (bf16[8,12,384]{2,1,0:T(8,128)(2,1)S(1)}, bf16[8,12,384]{2,1,0:T(8,128)(2,1)S(1)}, u32[]{:S(2)}, u32[]{:S(2)}) collective-permute-start(bf16[8,12,384]{2,1,0:T(8,128)(2,1)S(1)} %fusion.9), channel_id=1, source_target_pairs={{0,1},{1,0},{2,3},{3,2},{4,5},{5,4},{6,7},{7,6},{8,9},{9,8},{10,11... | collective-permute-start | bytes 221192 | tf_op jit(solution)/shard_map/ppermute | solution.py:57
  430.9 8.4 %collective-permute-start.64 = (bf16[4,24,192]{2,1,0:T(8,128)(2,1)S(1)}, bf16[4,24,192]{2,1,0:T(8,128)(2,1)S(1)}, u32[]{:S(2)}, u32[]{:S(2)}) collective-permute-start(bf16[4,24,192]{2,1,0:T(8,128)(2,1)S(1)} %dynamic-slice_convert_fusion), channel_id=1, source_target_pairs={{0,1},{1,0},{2,3},{3,2},{4,5},{5,4},{6,7},{7,6},{8,9},{9,8},{10,11... | collective-permute-start | bytes 110600 | tf_op jit(solution)/shard_map/ppermute | solution.py:57
  (95 other events, 759.8 us)
Sparse Core Ops, SparseCore 0:
  30.7 109.0 all-gather.1
  255.8 106.4 reduce-scatter.1

commit v7 on v6

--- a/solution.py
+++ b/solution.py
@@ -773,21 +773,26 @@
         all_tokens, qkv, gain_attn[None], cos, sin, head_gain
     )
 
+    cot_sent = after(cotangent, token_shifts)
+    cot_shifts = [shift_x(cot_sent, d) for d in (1, 2, 3)]
+    kv, cot_shifts = lax.optimization_barrier((kv, cot_shifts))
+
     kv_own = [kv, swap(kv, "yhi")]
-    kv_sent = after(kv, kv_own[1])
+    kv_sent = kv
     kv_earlier = [shift_super(kv_sent, a, b) for a, b in ((2, 0), (2, 1), (1, 0), (1, 1))]
     state = attend_own(plan, rot_q, start_lanes, kv_own)
-    state, kv_earlier, cot_sent = lax.optimization_barrier((state, kv_earlier, cotangent))
-    cot_shifts = [shift_x(cot_sent, d) for d in (1, 2, 3)]
+    state, kv_earlier = lax.optimization_barrier((state, kv_earlier))
     mix, out_tiles, lse = attend_earlier(plan, rot_q, start_lanes, kv_earlier, state)
-    mix, cot_shifts = lax.optimization_barrier((mix, cot_shifts))
-    out_half = lax.dynamic_index_in_dim(ffn_full, x // 2, 0, keepdims=False)
     w_out_t = jnp.concatenate(
-        [out_half[:, i * PADDED + PART : (i + 1) * PADDED] for i in range(3)], axis=1
+        [
+            lax.dynamic_slice(ffn_full, (x // 2, 0, i * PADDED + PART), (1, WIDTH, FREE))[0]
+            for i in range(3)
+        ],
+        axis=1,
     )[:, :QUERY]
     w_out_t, mix = lax.optimization_barrier((w_out_t, mix))
-    cot_blocks = [[b, swap(b, "core")] for b in [cotangent] + cot_shifts]
-    all_cot = [b for p in cot_blocks for b in p]
+    cot_blocks = [[b, swap(b, "core")] for b in after([cotangent] + cot_shifts, state)]
+    mix, cot_blocks = lax.optimization_barrier((mix, cot_blocks))
 
     inputs = tokens.astype(F32)
     parts = [None] * 4
@@ -798,35 +803,43 @@
     scaled_ffn = hidden * scale_ffn
     normed_ffn = (scaled_ffn * gain_ffn).astype(BF16)
 
-    ffn_blocks = [[b] for b in [normed_ffn] + [shift_x(normed_ffn, d) for d in (1, 2, 3)]]
-    ffn_blocks[0].append(swap(normed_ffn, "core"))
-    ffn_outs = [None] * 4
-    before = {1: 0, 3: 0, 2: 1}
-    for d in (0, 1, 3, 2):
-        if d > 0:
-            block = after(ffn_blocks[d][0], ffn_outs[before[d]][0])
-            ffn_blocks[d] = [block, swap(block, "core")]
-        blocks = ffn_blocks[d]
-        if d == 3:
-            blocks = after(blocks, ffn_outs[1][0])
-        if d == 2:
-            blocks = after(blocks, ffn_outs[3][0])
-        ffn_outs[d] = ffn(*blocks, *cot_blocks[d], ffn_full)
+    ffn_other = swap(normed_ffn, "core")
+    near = [shift_x(normed_ffn, d) for d in (1, 3)]
+    far = shift_x(after(normed_ffn, ffn_other), 2)
+    ffn_blocks = [[b, swap(b, "core")] for b in (near[0], far, near[1])]
+    ffn_blocks = [[normed_ffn, ffn_other]] + ffn_blocks
+    ffn_calls = [((0, 0), (0, 1)), ((1, 0), (3, 0)), ((2, 0), (1, 1)), ((3, 1), (2, 1))]
+    ffn_order = [at for call in ffn_calls for at in call]
+    ffn_outs, part_of, out_of = [], {}, {}
+    for call in ffn_calls:
+        blocks = [ffn_blocks[d][c] for d, c in call]
+        if ffn_outs:
+            blocks = after(blocks, ffn_outs[-1][0])
+        ffn_outs.append(ffn(*blocks, *[cot_blocks[d][c] for d, c in call], ffn_full))
+        for i, at in enumerate(call):
+            part_of[at], out_of[at] = ffn_outs[-1][i], ffn_outs[-1][2 + i]
     acts, gus = [o[4] for o in ffn_outs], [o[5] for o in ffn_outs]
-    kept, gus, out_own, out_other = lax.optimization_barrier(
-        (near_keep([o[:2] for o in ffn_outs]), gus, [o[2] for o in ffn_outs], [o[3] for o in ffn_outs])
-    )
-    out_kept = jnp.stack(out_own).astype(F32) + swap(jnp.stack(out_other), "core").astype(F32)
-    out_kept = out_kept.astype(BF16)
+    kept = near_keep([(part_of[d, 0], part_of[d, 1]) for d in range(4)])
+    out_other = [out_of[d, 1] for d in range(4)]
+    kept, gus, out_other = lax.optimization_barrier((kept, gus, out_other))
+    out_other = swap(jnp.stack(out_other), "core")
     pair_total = near_sum(kept)
-    weight_grads = ffn_weights([b for p in ffn_blocks for b in p], all_cot, gus, acts)
-    pair_total, weight_grads, out_kept = lax.optimization_barrier((pair_total, weight_grads, out_kept))
-    ffn_sum = lax.psum_scatter(
-        weight_grads.reshape(2 * WIDTH, 3 * PART), WIDE, scatter_dimension=0, tiled=True
-    )
+    weight_grads = ffn_weights(
+        [ffn_blocks[d][c] for d, c in ffn_order],
+        [cot_blocks[d][c] for d, c in ffn_order],
+        gus,
+        acts,
+    )
+    pair_total, weight_grads, out_other = lax.optimization_barrier((pair_total, weight_grads, out_other))
     ffn_gain_part = jnp.sum(pair_total * scaled_ffn, axis=0)
     grad_hidden = cotangent.astype(F32) + rms_back(pair_total * gain_ffn, hidden, scale_ffn)
     grad_branch = grad_hidden.astype(BF16)
+    weight_grads, out_other = lax.optimization_barrier((weight_grads, out_other, grad_branch))[:2]
+    ffn_sum = lax.psum_scatter(
+        weight_grads.reshape(2 * WIDTH, 3 * PART), WIDE, scatter_dimension=0, tiled=True
+    )
+    out_kept = jnp.stack([out_of[d, 0] for d in range(4)]).astype(F32) + out_other.astype(F32)
+    out_kept = out_kept.astype(BF16)
     branches = [b for p in near_gather(grad_branch) for b in p]
     grad_mix = out_back(branches, w_out_t)
     out_total = near_sum(after([out_kept[d] for d in range(4)], branches))

time: 459 us -> 442 us (0.963)
  waiting for transfers between devices: 134 us -> 111 us
  local copies, waits for them, and re-layouts: 46.3 us -> 53.5 us
    ppermute x24, waiting for transfers between devices: 65 us -> 51.9 us  [shift_x(): return lax.ppermute(v, 'x', [((i + distance) % 4, i) for i in range(4)])]
    unnamed x177, local copies, waits for them, and re-layouts: 18.3 us -> 26.3 us
    ppermute x33, waiting for transfers between devices: 16.7 us -> 9.05 us  [swap(): return lax.ppermute(v, axis, [(0, 1), (1, 0)])]
    ppermute x8, starting transfers between devices: 26.8 us -> 22.2 us  [shift_super(): return lax.ppermute(v, ('ylo', 'z', 'yhi'), pairs)]
  transfers between devices with their start and end apart: 71 -> 71, of which waited for: 26 -> 25; matrix products, arithmetic and copies ran while one was open for 8% -> 9% of each run, Pallas kernels for 26% -> 27%
where the time goes in v7:
time: 442 us; the launch traced here: 434 us
  Pallas kernels  118 us (27%)
  waiting for transfers between devices  111 us (25%)
  starting transfers between devices  90.1 us (20%)
  local copies, waits for them, and re-layouts  53.5 us (12%)
  other arithmetic  28.1 us (6%)
  blocking collectives  17 us (4%)
  between operations  16.1 us (4%)
    ppermute x24, waiting for transfers between devices, shift_x(): return lax.ppermute(v, 'x', [((i + distance) % 4, i) for i in range(4)])  51.9 us
    pallas_call x1, Pallas kernels, back(): return call(plan, q, start, *kvs, grad, out, lse)  33.3 us
    pallas_call x4, Pallas kernels, ffn(): pl.pallas_call(ffn_kernel, out_shape=(jax.ShapeDtypeStruct((ROWS, WIDTH),...  29.9 us
    ppermute x24, starting transfers between devices, shift_x(): return lax.ppermute(v, 'x', [((i + distance) % 4, i) for i in range(4)])  28.2 us
    all_to_all x4, waiting for transfers between devices, exchange(): return lax.all_to_all(v, axes, split_axis=0, concat_axis=0, tiled=True)  27.6 us
    unnamed x177, local copies, waits for them, and re-layouts  26.3 us
    all_to_all x4, starting transfers between devices, exchange(): return lax.all_to_all(v, axes, split_axis=0, concat_axis=0, tiled=True)  24.4 us
    ppermute x8, waiting for transfers between devices, shift_super(): return lax.ppermute(v, ('ylo', 'z', 'yhi'), pairs)  22.4 us
  transfers between devices with their start and end apart: 71, of which 25 were waited for; matrix products, arithmetic and copies ran while one was open for 9% of the time, Pallas kernels for 27%

profile of v7, /device:TPU:8, one launch (start us, length us, event | category | flops | bytes accessed | tf_op | source)
XLA Modules:
  0.0 433.8 jit_solution(18345384243034030701)
XLA Ops:
  12.7 17.0 %all_to_all.25 = bf16[8,24,1920]{2,1,0:T(8,128)(2,1)S(1)} all-to-all(bf16[8,24,1920]{2,1,0:T(8,128)(2,1)S(1)} %concatenate.54), channel_id=1, replica_groups=mesh['ylo'=2,'z'=4,'x'=4,'core'=2,'yhi'=2] {'x','core'}, dimensions={0} | all-to-all | bytes 1474560 | tf_op jit(solution)/shard_map/all_to_all | solution.py:71
  36.1 8.5 %all-to-all-start.1 = ((bf16[16,96,384]{2,1,0:T(8,128)(2,1)}), bf16[16,96,384]{2,1,0:T(8,128)(2,1)S(1)}, u32[]{:S(2)}, u32[]{:S(2)}) async-start(bf16[16,96,384]{2,1,0:T(8,128)(2,1)} %broadcast_in_dim.27), calls=%async_computation.1 | async-start | bytes 2359296 | tf_op jit(solution)/shard_map/all_to_all | solution.py:71
  45.0 1.9 fusion.12
  47.5 5.6 %collective-permute-done.5.refs_6_.refs_10_ = bf16[128,1536]{1,0:T(8,128)(2,1)} collective-permute-done((bf16[128,1536]{1,0:T(8,128)(2,1)S(1)}, bf16[128,1536]{1,0:T(8,128)(2,1)}, u32[]{:S(2)}, u32[]{:S(2)}) %collective-permute-start.5) | collective-permute-done | bytes 393248 | tf_op jit(solution)/shard_map/ppermute | solution.py:53
  53.9 2.1 collective-permute-start.8
  57.9 10.6 %all-to-all-done.1 = bf16[16,96,384]{2,1,0:T(8,128)(2,1)S(1)} async-done(((bf16[16,96,384]{2,1,0:T(8,128)(2,1)}), bf16[16,96,384]{2,1,0:T(8,128)(2,1)S(1)}, u32[]{:S(2)}, u32[]{:S(2)}) %all-to-all-start.1) | async-done | bytes 1179680 | tf_op jit(solution)/shard_map/all_to_all | solution.py:71
  70.5 2.3 reshape.569.refs_8_.refs_12_
  75.9 4.9 %shard_map.237 = (bf16[1024,1536]{1,0:T(8,128)(2,1)S(1)}, bf16[8,128,192]{2,1,0:T(8,128)(2,1)S(1)}, bf16[8,128,128]{2,1,0:T(8,128)(2,1)}, f32[4,256,256]{2,1,0:T(8,128)S(1)}) custom-call(bf16[128,1536]{1,0:T(8,128)(2,1)S(1)} %copy-done.4, bf16[128,1536]{1,0:T(8,128)(2,1)S(1)} %collective-permute-done.refs_1_.refs_9_, bf16[128,1536]{1,0:T(8,128)(2,1)S(1)} %copy-done.16, ...), custom_call_target="tpu_custom_call" | custom-call | flops 1207959552 | bytes 10000000 | tf_op jit(solution)/shard_map/pallas_call | solution.py:168
  80.8 1.7 copy-done.1
  84.3 1.8 collective-permute-start.10
  86.3 2.1 collective-permute-start.11
  88.4 3.5 collective-permute-start.12
  91.8 2.1 collective-permute-start.13
  94.0 2.5 collective-permute-start.14
  96.5 4.3 collective-permute-done.10.refs_1_.refs_5_
  102.0 8.5 %shard_map.238 = (f32[4,64,768]{2,1,0:T(8,128)S(1)}, f32[4,1,768]{2,1,0:T(1,128)S(1)}) custom-call(s32[8,17]{1,0:T(8,128)S(1)} %stack.22.plan, bf16[8,128,192]{2,1,0:T(8,128)(2,1)S(1)} %copy-done.36, s32[4,1,768]{2,1,0:T(1,128)S(1)} %copy.103.start_ref, bf16[8,128,128]{2,1,0:T(8,128)(2,1)} %get-tuple-element.159.refs_0_.refs_4_, ...), custom_call_target="tpu_custom_call" | custom-call | flops 4000000000 | bytes 8000000 | tf_op jit(solution)/shard_map/pallas_call | solution.py:651
  110.5 6.7 %collective-permute-done.11.refs_0_ = bf16[8,128,128]{2,1,0:T(8,128)(2,1)S(1)} collective-permute-done((bf16[8,128,128]{2,1,0:T(8,128)(2,1)}, bf16[8,128,128]{2,1,0:T(8,128)(2,1)S(1)}, u32[]{:S(2)}, u32[]{:S(2)}) %collective-permute-start.11) | collective-permute-done | bytes 262176 | tf_op jit(solution)/shard_map/ppermute | solution.py:67
  118.7 6.5 %collective-permute-done.13.refs_2_ = bf16[8,128,128]{2,1,0:T(8,128)(2,1)S(1)} collective-permute-done((bf16[8,128,128]{2,1,0:T(8,128)(2,1)}, bf16[8,128,128]{2,1,0:T(8,128)(2,1)S(1)}, u32[]{:S(2)}, u32[]{:S(2)}) %collective-permute-start.13) | collective-permute-done | bytes 262176 | tf_op jit(solution)/shard_map/ppermute | solution.py:67
  126.4 9.2 %shard_map.239 = (bf16[8,128,192]{2,1,0:T(8,128)(2,1)S(1)}, f32[4,64,768]{2,1,0:T(8,128)S(1)}, f32[4,1,768]{2,1,0:T(1,128)S(1)}) custom-call(s32[8,17]{1,0:T(8,128)S(1)} %stack.22.plan, bf16[8,128,192]{2,1,0:T(8,128)(2,1)S(1)} %copy-done.37, s32[4,1,768]{2,1,0:T(1,128)S(1)} %copy.103.start_ref, bf16[8,128,128]{2,1,0:T(8,128)(2,1)S(1)} %collective-permute-done.11.refs_0_, ...), custom_call_target="tpu_custom_call" | custom-call | flops 8000000000 | bytes 8000000 | tf_op jit(solution)/shard_map/pallas_call | solution.py:658
  139.9 1.6 dynamic-slice_bitcast_fusion.2
  145.2 2.8 collective-permute-start.25
  150.0 15.0 %collective-permute-done.25 = bf16[128,1536]{1,0:T(8,128)(2,1)S(1)} collective-permute-done((bf16[128,1536]{1,0:T(8,128)(2,1)S(1)}, bf16[128,1536]{1,0:T(8,128)(2,1)S(1)}, u32[]{:S(2)}, u32[]{:S(2)}) %collective-permute-start.25) | collective-permute-done | bytes 393248 | tf_op jit(solution)/shard_map/ppermute | solution.py:53
  165.0 3.8 collective-permute-done.21
  170.3 1.8 collective-permute-start.29
  172.1 7.5 %shard_map.244 = (bf16[128,1536]{1,0:T(8,128)(2,1)S(1)}, bf16[128,1536]{1,0:T(8,128)(2,1)S(1)}, bf16[128,1536]{1,0:T(8,128)(2,1)S(1)}, bf16[128,1536]{1,0:T(8,12...) custom-call(bf16[128,1536]{1,0:T(8,128)(2,1)S(1)} %multiply_convert_fusion.x0_ref.refs_0_, ...), custom_call_target="tpu_custom_call" | custom-call | flops 4831838208 | bytes 14000000 | tf_op jit(solution)/shard_map/pallas_call | solution.py:324
  181.1 1.9 collective-permute-done.29.x1_ref.refs_3_
  183.5 7.5 %shard_map.245 = (bf16[128,1536]{1,0:T(8,128)(2,1)S(1)}, bf16[128,1536]{1,0:T(8,128)(2,1)S(1)}, bf16[128,1536]{1,0:T(8,128)(2,1)S(1)}, bf16[128,1536]{1,0:T(8,12...) custom-call(bf16[128,1536]{1,0:T(8,128)(2,1)S(1)} %collective-permute-done.28.x0_ref.refs_2_, ...), custom_call_target="tpu_custom_call" | custom-call | flops 4831838208 | bytes 14000000 | tf_op jit(solution)/shard_map/pallas_call | solution.py:324
  193.3 7.5 %shard_map.246 = (bf16[128,1536]{1,0:T(8,128)(2,1)S(1)}, bf16[128,1536]{1,0:T(8,128)(2,1)S(1)}, bf16[128,1536]{1,0:T(8,128)(2,1)S(1)}, bf16[128,1536]{1,0:T(8,12...) custom-call(bf16[128,1536]{1,0:T(8,128)(2,1)S(1)} %collective-permute-done.30.x0_ref.refs_4_, ...), custom_call_target="tpu_custom_call" | custom-call | flops 4831838208 | bytes 14000000 | tf_op jit(solution)/shard_map/pallas_call | solution.py:324
  203.8 7.5 %shard_map.247 = (bf16[128,1536]{1,0:T(8,128)(2,1)S(1)}, bf16[128,1536]{1,0:T(8,128)(2,1)S(1)}, bf16[128,1536]{1,0:T(8,128)(2,1)S(1)}, bf16[128,1536]{1,0:T(8,12...) custom-call(bf16[128,1536]{1,0:T(8,128)(2,1)S(1)} %collective-permute-done.33.x0_ref.refs_6_, ...), custom_call_target="tpu_custom_call" | custom-call | flops 4831838208 | bytes 14000000 | tf_op jit(solution)/shard_map/pallas_call | solution.py:324
  214.2 1.8 collective-permute-start.39
  216.9 15.3 %shard_map.248 = bf16[2,1536,1296]{2,1,0:T(8,128)(2,1)S(1)} custom-call(bf16[128,1536]{1,0:T(8,128)(2,1)S(1)} %multiply_convert_fusion.x0_ref.refs_0_, bf16[128,1536]{1,0:T(8,128)(2,1)S(1)} %collective-permute-done.26.x1_ref.refs_1_, bf16[128,1536]{1,0:T(8,128)(2,1)S(1)} %collective-permute-done.28.x0_ref.refs_2_, ...), custom_call_target="tpu_custom_call" | custom-call | flops 9663676416 | bytes 24000000 | tf_op jit(solution)/shard_map/pallas_call | solution.py:360
  232.2 3.5 copy-done.9
  237.9 2.0 fusion.45.refs_0_
  242.2 2.0 collective-permute-start.44
  245.8 2.2 add_convert_fusion
  248.0 4.8 %collective-permute-done.42.refs_2_ = bf16[128,1536]{1,0:T(8,128)(2,1)S(1)} collective-permute-done((bf16[128,1536]{1,0:T(8,128)(2,1)}, bf16[128,1536]{1,0:T(8,128)(2,1)S(1)}, u32[]{:S(2)}, u32[]{:S(2)}) %collective-permute-start.42) | collective-permute-done | bytes 393248 | tf_op jit(solution)/shard_map/ppermute | solution.py:53
  252.7 3.2 collective-permute-done.44.refs_4_
  255.9 7.7 %collective-permute-done.46.refs_6_ = bf16[128,1536]{1,0:T(8,128)(2,1)S(1)} collective-permute-done((bf16[128,1536]{1,0:T(8,128)(2,1)}, bf16[128,1536]{1,0:T(8,128)(2,1)S(1)}, u32[]{:S(2)}, u32[]{:S(2)}) %collective-permute-start.46) | collective-permute-done | bytes 393248 | tf_op jit(solution)/shard_map/ppermute | solution.py:53
  269.9 33.3 %shard_map.250 = (bf16[8,128,256]{2,1,0:T(8,128)(2,1)S(1)}, bf16[8,128,128]{2,1,0:T(8,128)(2,1)S(1)}, bf16[8,128,128]{2,1,0:T(8,128)(2,1)S(1)}, bf16[8,128,128]{...) custom-call(s32[8,17]{1,0:T(8,128)S(1)} %copy-done.34, ...), custom_call_target="tpu_custom_call" | custom-call | flops 30000001024 | bytes 8000000 | tf_op jit(solution)/shard_map/pallas_call | solution.py:672
  304.3 3.0 collective-permute-start.51
  307.3 1.9 collective-permute-start.52
  309.2 1.9 collective-permute-start.53
  311.1 6.0 %collective-permute-start.54 = (bf16[8,128,128]{2,1,0:T(8,128)(2,1)S(1)}, bf16[8,128,128]{2,1,0:T(8,128)(2,1)S(1)}, u32[]{:S(2)}, u32[]{:S(2)}) collective-permute-start(bf16[8,128,128]{2,1,0:T(8,128)(2,1)S(1)} %get-tuple-element.263), channel_id=1, source_target_pairs={{32,0},{33,1},{48,16},{49,17},{64,32},{65,33},{80,48},{81,49},{96,... | collective-permute-start | bytes 786440 | tf_op jit(solution)/shard_map/ppermute | solution.py:67
  317.2 2.2 collective-permute-start.55
  322.5 3.6 shard_map.253
  326.2 5.4 %collective-permute-done.54.refs_5_ = bf16[8,128,128]{2,1,0:T(8,128)(2,1)S(1)} collective-permute-done((bf16[8,128,128]{2,1,0:T(8,128)(2,1)S(1)}, bf16[8,128,128]{2,1,0:T(8,128)(2,1)S(1)}, u32[]{:S(2)}, u32[]{:S(2)}) %collective-permute-start.54) | collective-permute-done | bytes 262176 | tf_op jit(solution)/shard_map/ppermute | solution.py:67
  331.5 2.4 collective-permute-done.55.refs_6_
  337.0 3.5 shard_map.255
  345.0 2.0 copy-done.3
  347.0 3.5 shard_map.256
  351.5 6.8 %all-to-all-start.3 = ((bf16[8,192,192]{2,1,0:T(8,128)(2,1)}), bf16[8,192,192]{2,1,0:T(8,128)(2,1)}, u32[]{:S(2)}, u32[]{:S(2)}) async-start(bf16[8,192,192]{2,1,0:T(8,128)(2,1)} %bitcast.41), calls=%async_computation.4 | async-start | bytes 1572864 | tf_op jit(solution)/shard_map/all_to_all | solution.py:71
  358.3 1.8 add_convert_fusion.1
  360.1 2.7 collective-permute-start.62
  364.8 1.8 add_convert_fusion.3
  367.6 2.6 all-to-all-done.3
  370.2 4.8 %all-to-all-start.2 = ((bf16[8,192,384]{2,1,0:T(8,128)(2,1)}), bf16[8,192,384]{2,1,0:T(8,128)(2,1)}, u32[]{:S(2)}, u32[]{:S(2)}) async-start(bf16[8,192,384]{2,1,0:T(8,128)(2,1)} %bitcast.39), calls=%async_computation.3 | async-start | bytes 2359296 | tf_op jit(solution)/shard_map/all_to_all | solution.py:71
  376.3 3.5 collective-permute-done.62
  379.8 4.5 %collective-permute-done.58 = bf16[128,1536]{1,0:T(8,128)(2,1)S(1)} collective-permute-done((bf16[128,1536]{1,0:T(8,128)(2,1)}, bf16[128,1536]{1,0:T(8,128)(2,1)S(1)}, u32[]{:S(2)}, u32[]{:S(2)}) %collective-permute-start.58) | collective-permute-done | bytes 393248 | tf_op jit(solution)/shard_map/ppermute | solution.py:53
  386.0 4.6 %all-to-all-done.2 = bf16[8,192,384]{2,1,0:T(8,128)(2,1)} async-done(((bf16[8,192,384]{2,1,0:T(8,128)(2,1)}), bf16[8,192,384]{2,1,0:T(8,128)(2,1)}, u32[]{:S(2)}, u32[]{:S(2)}) %all-to-all-start.2) | async-done | bytes 1179680 | tf_op jit(solution)/shard_map/all_to_all | solution.py:71
  392.2 2.1 concatenate.66
  394.3 4.3 all-to-all-start.4
  398.7 3.0 fusion.6
  401.6 9.7 %all-to-all-done.4 = bf16[8,24,1872]{2,1,0:T(8,128)(2,1)} async-done(((bf16[8,24,1872]{2,1,0:T(8,128)(2,1)}), bf16[8,24,1872]{2,1,0:T(8,128)(2,1)}, u32[]{:S(2)}, u32[]{:S(2)}) %all-to-all-start.4) | async-done | bytes 718880 | tf_op jit(solution)/shard_map/all_to_all | solution.py:71
  413.9 2.7 collective-permute-start.64
  (417 shorter events, 92.9 us)
Async XLA Ops:
  7.2 132.7 %all-gather.2.cloned.1.call-start = ((), (), s32[]{:S(2)}) async-start(), calls=%async_computation.6 | async-start | bytes 10027008 | tf_op jit(solution)/shard_map/all_gather | solution.py:732
  30.6 23.3 %collective-permute-start = (bf16[128,1536]{1,0:T(8,128)(2,1)S(1)}, bf16[128,1536]{1,0:T(8,128)(2,1)S(1)}, u32[]{:S(2)}, u32[]{:S(2)}) collective-permute-start(bf16[128,1536]{1,0:T(8,128)(2,1)S(1)} %copy-done.4), channel_id=1, source_target_pairs={{0,2},{2,0},{1,3},{3,1},{4,6},{6,4},{5,7},{7,5},{8,10},{10,8},{9,1... | collective-permute-start | bytes 1179656 | tf_op jit(solution)/shard_map/ppermute | solution.py:57
  30.7 14.2 %collective-permute-start.1 = (bf16[128,1536]{1,0:T(8,128)(2,1)S(1)}, bf16[128,1536]{1,0:T(8,128)(2,1)S(1)}, u32[]{:S(2)}, u32[]{:S(2)}) collective-permute-start(bf16[128,1536]{1,0:T(8,128)(2,1)S(1)} %copy-done.4), channel_id=1, source_target_pairs={{4,0},{8,4},{12,8},{0,12},{5,1},{9,5},{13,9},{1,13},{6,2},{10,6},{... | collective-permute-start | bytes 1179656 | tf_op jit(solution)/shard_map/ppermute | solution.py:53
  31.9 15.0 %collective-permute-start.3 = (bf16[128,1536]{1,0:T(8,128)(2,1)S(1)}, bf16[128,1536]{1,0:T(8,128)(2,1)S(1)}, u32[]{:S(2)}, u32[]{:S(2)}) collective-permute-start(bf16[128,1536]{1,0:T(8,128)(2,1)S(1)} %copy-done.4), channel_id=1, source_target_pairs={{8,0},{12,4},{0,8},{4,12},{9,1},{13,5},{1,9},{5,13},{10,2},{14,6},... | collective-permute-start | bytes 1179656 | tf_op jit(solution)/shard_map/ppermute | solution.py:53
  33.4 19.7 %collective-permute-start.5 = (bf16[128,1536]{1,0:T(8,128)(2,1)S(1)}, bf16[128,1536]{1,0:T(8,128)(2,1)}, u32[]{:S(2)}, u32[]{:S(2)}) collective-permute-start(bf16[128,1536]{1,0:T(8,128)(2,1)S(1)} %copy-done.4), channel_id=1, source_target_pairs={{12,0},{0,4},{4,8},{8,12},{13,1},{1,5},{5,9},{9,13},{14,2},{2,6},{... | collective-permute-start | bytes 1179656 | tf_op jit(solution)/shard_map/ppermute | solution.py:53
  36.1 32.5 %all-to-all-start.1 = ((bf16[16,96,384]{2,1,0:T(8,128)(2,1)}), bf16[16,96,384]{2,1,0:T(8,128)(2,1)S(1)}, u32[]{:S(2)}, u32[]{:S(2)}) async-start(bf16[16,96,384]{2,1,0:T(8,128)(2,1)} %broadcast_in_dim.27), calls=%async_computation.1 | async-start | bytes 2359296 | tf_op jit(solution)/shard_map/all_to_all | solution.py:71
  44.6 347.5 %reduce-scatter.2.cloned.1.call-start = ((), (), s32[]{:S(2)}) async-start(), calls=%async_computation.7 | async-start | bytes 9191424 | tf_op jit(solution)/shard_map/reduce_scatter | solution.py:838
  44.9 11.1 %collective-permute-start.2 = (bf16[128,1536]{1,0:T(8,128)(2,1)S(1)}, bf16[128,1536]{1,0:T(8,128)(2,1)S(1)}, u32[]{:S(2)}, u32[]{:S(2)}) collective-permute-start(bf16[128,1536]{1,0:T(8,128)(2,1)S(1)} %collective-permute-done.1.refs_2_.refs_10_), channel_id=1, source_target_pairs={{0,2},{2,0},{1,3},{3,1},{4,6},{6,4},{5,7},{7,5},{8,10},{10,8},{9,1... | collective-permute-start | bytes 1179656 | tf_op jit(solution)/shard_map/ppermute | solution.py:57
  46.9 26.9 %collective-permute-start.4 = (bf16[128,1536]{1,0:T(8,128)(2,1)S(1)}, bf16[128,1536]{1,0:T(8,128)(2,1)}, u32[]{:S(2)}, u32[]{:S(2)}) collective-permute-start(bf16[128,1536]{1,0:T(8,128)(2,1)S(1)} %collective-permute-done.3.refs_4_.refs_8_), channel_id=1, source_target_pairs={{0,2},{2,0},{1,3},{3,1},{4,6},{6,4},{5,7},{7,5},{8,10},{10,8},{9,1... | collective-permute-start | bytes 1179656 | tf_op jit(solution)/shard_map/ppermute | solution.py:57
  53.1 20.7 %collective-permute-start.6 = (bf16[128,1536]{1,0:T(8,128)(2,1)}, bf16[128,1536]{1,0:T(8,128)(2,1)}, u32[]{:S(2)}, u32[]{:S(2)}) collective-permute-start(bf16[128,1536]{1,0:T(8,128)(2,1)} %collective-permute-done.5.refs_6_.refs_10_), channel_id=1, source_target_pairs={{0,2},{2,0},{1,3},{3,1},{4,6},{6,4},{5,7},{7,5},{8,10},{10,8},{9,1... | collective-permute-start | bytes 1179656 | tf_op jit(solution)/shard_map/ppermute | solution.py:57
  53.2 31.1 %collective-permute-start.7 = (bf16[128,1536]{1,0:T(8,128)(2,1)}, bf16[128,1536]{1,0:T(8,128)(2,1)}, u32[]{:S(2)}, u32[]{:S(2)}) collective-permute-start(bf16[128,1536]{1,0:T(8,128)(2,1)} %refs_8_.1), channel_id=1, source_target_pairs={{4,0},{8,4},{12,8},{0,12},{5,1},{9,5},{13,9},{1,13},{6,2},{10,6},{... | collective-permute-start | bytes 1179656 | tf_op jit(solution)/shard_map/ppermute | solution.py:53
  53.9 30.3 %collective-permute-start.8 = (bf16[128,1536]{1,0:T(8,128)(2,1)}, bf16[128,1536]{1,0:T(8,128)(2,1)}, u32[]{:S(2)}, u32[]{:S(2)}) collective-permute-start(bf16[128,1536]{1,0:T(8,128)(2,1)} %refs_8_.1), channel_id=1, source_target_pairs={{8,0},{12,4},{0,8},{4,12},{9,1},{13,5},{1,9},{5,13},{10,2},{14,6},... | collective-permute-start | bytes 1179656 | tf_op jit(solution)/shard_map/ppermute | solution.py:53
  56.7 27.5 %collective-permute-start.9 = (bf16[128,1536]{1,0:T(8,128)(2,1)}, bf16[128,1536]{1,0:T(8,128)(2,1)}, u32[]{:S(2)}, u32[]{:S(2)}) collective-permute-start(bf16[128,1536]{1,0:T(8,128)(2,1)} %refs_8_.1), channel_id=1, source_target_pairs={{12,0},{0,4},{4,8},{8,12},{13,1},{1,5},{5,9},{9,13},{14,2},{2,6},{... | collective-permute-start | bytes 1179656 | tf_op jit(solution)/shard_map/ppermute | solution.py:53
  84.3 16.6 %collective-permute-start.10 = (bf16[8,128,128]{2,1,0:T(8,128)(2,1)}, bf16[8,128,128]{2,1,0:T(8,128)(2,1)S(1)}, u32[]{:S(2)}, u32[]{:S(2)}) collective-permute-start(bf16[8,128,128]{2,1,0:T(8,128)(2,1)} %get-tuple-element.159.refs_0_.refs_4_), channel_id=1, source_target_pairs={{0,1},{1,0},{2,3},{3,2},{4,5},{5,4},{6,7},{7,6},{8,9},{9,8},{10,11... | collective-permute-start | bytes 786440 | tf_op jit(solution)/shard_map/ppermute | solution.py:57
  86.3 31.0 %collective-permute-start.11 = (bf16[8,128,128]{2,1,0:T(8,128)(2,1)}, bf16[8,128,128]{2,1,0:T(8,128)(2,1)S(1)}, u32[]{:S(2)}, u32[]{:S(2)}) collective-permute-start(bf16[8,128,128]{2,1,0:T(8,128)(2,1)} %get-tuple-element.159.refs_0_.refs_4_), channel_id=1, source_target_pairs={{0,32},{1,33},{16,48},{17,49},{32,64},{33,65},{48,80},{49,81},{64,... | collective-permute-start | bytes 786440 | tf_op jit(solution)/shard_map/ppermute | solution.py:67
  88.4 30.3 %collective-permute-start.12 = (bf16[8,128,128]{2,1,0:T(8,128)(2,1)}, bf16[8,128,128]{2,1,0:T(8,128)(2,1)S(1)}, u32[]{:S(2)}, u32[]{:S(2)}) collective-permute-start(bf16[8,128,128]{2,1,0:T(8,128)(2,1)} %get-tuple-element.159.refs_0_.refs_4_), channel_id=1, source_target_pairs={{0,33},{1,32},{16,49},{17,48},{32,65},{33,64},{48,81},{49,80},{64,... | collective-permute-start | bytes 786440 | tf_op jit(solution)/shard_map/ppermute | solution.py:67
  91.8 33.3 %collective-permute-start.13 = (bf16[8,128,128]{2,1,0:T(8,128)(2,1)}, bf16[8,128,128]{2,1,0:T(8,128)(2,1)S(1)}, u32[]{:S(2)}, u32[]{:S(2)}) collective-permute-start(bf16[8,128,128]{2,1,0:T(8,128)(2,1)} %get-tuple-element.159.refs_0_.refs_4_), channel_id=1, source_target_pairs={{0,16},{1,17},{16,32},{17,33},{32,48},{33,49},{48,64},{49,65},{64,... | collective-permute-start | bytes 786440 | tf_op jit(solution)/shard_map/ppermute | solution.py:67
  94.0 31.2 %collective-permute-start.14 = (bf16[8,128,128]{2,1,0:T(8,128)(2,1)}, bf16[8,128,128]{2,1,0:T(8,128)(2,1)S(1)}, u32[]{:S(2)}, u32[]{:S(2)}) collective-permute-start(bf16[8,128,128]{2,1,0:T(8,128)(2,1)} %get-tuple-element.159.refs_0_.refs_4_), channel_id=1, source_target_pairs={{0,17},{1,16},{16,33},{17,32},{32,49},{33,48},{48,65},{49,64},{64,... | collective-permute-start | bytes 786440 | tf_op jit(solution)/shard_map/ppermute | solution.py:67
  125.2 16.9 %collective-permute-start.15 = (bf16[128,1536]{1,0:T(8,128)(2,1)}, bf16[128,1536]{1,0:T(8,128)(2,1)}, u32[]{:S(2)}, u32[]{:S(2)}) collective-permute-start(bf16[128,1536]{1,0:T(8,128)(2,1)} %refs_8_.1), channel_id=1, source_target_pairs={{0,2},{2,0},{1,3},{3,1},{4,6},{6,4},{5,7},{7,5},{8,10},{10,8},{9,1... | collective-permute-start | bytes 1179656 | tf_op jit(solution)/shard_map/ppermute | solution.py:57
  125.2 16.9 %collective-permute-start.16 = (bf16[128,1536]{1,0:T(8,128)(2,1)}, bf16[128,1536]{1,0:T(8,128)(2,1)}, u32[]{:S(2)}, u32[]{:S(2)}) collective-permute-start(bf16[128,1536]{1,0:T(8,128)(2,1)} %collective-permute-done.7.c0_ref.refs_10_), channel_id=1, source_target_pairs={{0,2},{2,0},{1,3},{3,1},{4,6},{6,4},{5,7},{7,5},{8,10},{10,8},{9,1... | collective-permute-start | bytes 1179656 | tf_op jit(solution)/shard_map/ppermute | solution.py:57
  125.7 16.4 %collective-permute-start.17 = (bf16[128,1536]{1,0:T(8,128)(2,1)}, bf16[128,1536]{1,0:T(8,128)(2,1)}, u32[]{:S(2)}, u32[]{:S(2)}) collective-permute-start(bf16[128,1536]{1,0:T(8,128)(2,1)} %collective-permute-done.8.c0_ref.refs_12_), channel_id=1, source_target_pairs={{0,2},{2,0},{1,3},{3,1},{4,6},{6,4},{5,7},{7,5},{8,10},{10,8},{9,1... | collective-permute-start | bytes 1179656 | tf_op jit(solution)/shard_map/ppermute | solution.py:57
  125.7 16.4 %collective-permute-start.18 = (bf16[128,1536]{1,0:T(8,128)(2,1)}, bf16[128,1536]{1,0:T(8,128)(2,1)}, u32[]{:S(2)}, u32[]{:S(2)}) collective-permute-start(bf16[128,1536]{1,0:T(8,128)(2,1)} %collective-permute-done.9.c1_ref.refs_11_), channel_id=1, source_target_pairs={{0,2},{2,0},{1,3},{3,1},{4,6},{6,4},{5,7},{7,5},{8,10},{10,8},{9,1... | collective-permute-start | bytes 1179656 | tf_op jit(solution)/shard_map/ppermute | solution.py:57
  144.0 5.0 %collective-permute-start.20 = (bf16[128,1536]{1,0:T(8,128)(2,1)S(1)}, bf16[128,1536]{1,0:T(8,128)(2,1)S(1)}, u32[]{:S(2)}, u32[]{:S(2)}) collective-permute-start(bf16[128,1536]{1,0:T(8,128)(2,1)S(1)} %get-tuple-element.182), channel_id=1, source_target_pairs={{0,2},{2,0},{1,3},{3,1},{4,6},{6,4},{5,7},{7,5},{8,10},{10,8},{9,1... | collective-permute-start | bytes 1179656 | tf_op jit(solution)/shard_map/ppermute | solution.py:57
  144.5 5.5 %collective-permute-start.19 = (bf16[128,1536]{1,0:T(8,128)(2,1)S(1)}, bf16[128,1536]{1,0:T(8,128)(2,1)S(1)}, u32[]{:S(2)}, u32[]{:S(2)}) collective-permute-start(bf16[128,1536]{1,0:T(8,128)(2,1)S(1)} %get-tuple-element.180), channel_id=1, source_target_pairs={{0,2},{2,0},{1,3},{3,1},{4,6},{6,4},{5,7},{7,5},{8,10},{10,8},{9,1... | collective-permute-start | bytes 1179656 | tf_op jit(solution)/shard_map/ppermute | solution.py:57
  145.2 19.9 %collective-permute-start.25 = (bf16[128,1536]{1,0:T(8,128)(2,1)S(1)}, bf16[128,1536]{1,0:T(8,128)(2,1)S(1)}, u32[]{:S(2)}, u32[]{:S(2)}) collective-permute-start(bf16[128,1536]{1,0:T(8,128)(2,1)S(1)} %add_convert_fusion.10), channel_id=1, source_target_pairs={{4,0},{8,4},{12,8},{0,12},{5,1},{9,5},{13,9},{1,13},{6,2},{10,6},{... | collective-permute-start | bytes 1179656 | tf_op jit(solution)/shard_map/ppermute | solution.py:53
  148.1 16.9 %collective-permute-start.23 = (bf16[128,1536]{1,0:T(8,128)(2,1)S(1)}, bf16[128,1536]{1,0:T(8,128)(2,1)S(1)}, u32[]{:S(2)}, u32[]{:S(2)}) collective-permute-start(bf16[128,1536]{1,0:T(8,128)(2,1)S(1)} %add_convert_fusion.11), channel_id=1, source_target_pairs={{8,0},{12,4},{0,8},{4,12},{9,1},{13,5},{1,9},{5,13},{10,2},{14,6},... | collective-permute-start | bytes 1179656 | tf_op jit(solution)/shard_map/ppermute | solution.py:53
  149.1 19.8 %collective-permute-start.21 = (bf16[128,1536]{1,0:T(8,128)(2,1)S(1)}, bf16[128,1536]{1,0:T(8,128)(2,1)S(1)}, u32[]{:S(2)}, u32[]{:S(2)}) collective-permute-start(bf16[128,1536]{1,0:T(8,128)(2,1)S(1)} %add_convert_fusion.12), channel_id=1, source_target_pairs={{12,0},{0,4},{4,8},{8,12},{13,1},{1,5},{5,9},{9,13},{14,2},{2,6},{... | collective-permute-start | bytes 1179656 | tf_op jit(solution)/shard_map/ppermute | solution.py:53
  169.6 11.5 %collective-permute-start.28 = (bf16[128,1536]{1,0:T(8,128)(2,1)S(1)}, bf16[128,1536]{1,0:T(8,128)(2,1)S(1)}, u32[]{:S(2)}, u32[]{:S(2)}) collective-permute-start(bf16[128,1536]{1,0:T(8,128)(2,1)S(1)} %multiply_convert_fusion.x0_ref.refs_0_), channel_id=1, source_target_pairs={{4,0},{8,4},{12,8},{0,12},{5,1},{9,5},{13,9},{1,13},{6,2},{10,6},{... | collective-permute-start | bytes 1179656 | tf_op jit(solution)/shard_map/ppermute | solution.py:53
  170.3 12.8 %collective-permute-start.29 = (bf16[128,1536]{1,0:T(8,128)(2,1)S(1)}, bf16[128,1536]{1,0:T(8,128)(2,1)S(1)}, u32[]{:S(2)}, u32[]{:S(2)}) collective-permute-start(bf16[128,1536]{1,0:T(8,128)(2,1)S(1)} %multiply_convert_fusion.x0_ref.refs_0_), channel_id=1, source_target_pairs={{12,0},{0,4},{4,8},{8,12},{13,1},{1,5},{5,9},{9,13},{14,2},{2,6},{... | collective-permute-start | bytes 1179656 | tf_op jit(solution)/shard_map/ppermute | solution.py:53
  180.3 21.9 %collective-permute-start.27 = (bf16[128,1536]{1,0:T(8,128)(2,1)S(1)}, bf16[128,1536]{1,0:T(8,128)(2,1)S(1)}, u32[]{:S(2)}, u32[]{:S(2)}) collective-permute-start(bf16[128,1536]{1,0:T(8,128)(2,1)S(1)} %get-tuple-element.190), channel_id=1, source_target_pairs={{0,2},{2,0},{1,3},{3,1},{4,6},{6,4},{5,7},{7,5},{8,10},{10,8},{9,1... | collective-permute-start | bytes 1179656 | tf_op jit(solution)/shard_map/ppermute | solution.py:57
  180.3 13.0 %collective-permute-start.30 = (bf16[128,1536]{1,0:T(8,128)(2,1)S(1)}, bf16[128,1536]{1,0:T(8,128)(2,1)S(1)}, u32[]{:S(2)}, u32[]{:S(2)}) collective-permute-start(bf16[128,1536]{1,0:T(8,128)(2,1)S(1)} %multiply_convert_fusion.x0_ref.refs_0_), channel_id=1, source_target_pairs={{8,0},{12,4},{0,8},{4,12},{9,1},{13,5},{1,9},{5,13},{10,2},{14,6},... | collective-permute-start | bytes 1179656 | tf_op jit(solution)/shard_map/ppermute | solution.py:53
  183.0 10.3 %collective-permute-start.31 = (bf16[128,1536]{1,0:T(8,128)(2,1)S(1)}, bf16[128,1536]{1,0:T(8,128)(2,1)S(1)}, u32[]{:S(2)}, u32[]{:S(2)}) collective-permute-start(bf16[128,1536]{1,0:T(8,128)(2,1)S(1)} %collective-permute-done.28.x0_ref.refs_2_), channel_id=1, source_target_pairs={{0,2},{2,0},{1,3},{3,1},{4,6},{6,4},{5,7},{7,5},{8,10},{10,8},{9,1... | collective-permute-start | bytes 1179656 | tf_op jit(solution)/shard_map/ppermute | solution.py:57
  183.0 19.3 %collective-permute-start.33 = (bf16[128,1536]{1,0:T(8,128)(2,1)S(1)}, bf16[128,1536]{1,0:T(8,128)(2,1)S(1)}, u32[]{:S(2)}, u32[]{:S(2)}) collective-permute-start(bf16[128,1536]{1,0:T(8,128)(2,1)S(1)} %collective-permute-done.29.x1_ref.refs_3_), channel_id=1, source_target_pairs={{0,2},{2,0},{1,3},{3,1},{4,6},{6,4},{5,7},{7,5},{8,10},{10,8},{9,1... | collective-permute-start | bytes 1179656 | tf_op jit(solution)/shard_map/ppermute | solution.py:57
  201.6 10.3 %collective-permute-start.32 = (bf16[128,1536]{1,0:T(8,128)(2,1)S(1)}, bf16[128,1536]{1,0:T(8,128)(2,1)S(1)}, u32[]{:S(2)}, u32[]{:S(2)}) collective-permute-start(bf16[128,1536]{1,0:T(8,128)(2,1)S(1)} %get-tuple-element.201), channel_id=1, source_target_pairs={{0,2},{2,0},{1,3},{3,1},{4,6},{6,4},{5,7},{7,5},{8,10},{10,8},{9,1... | collective-permute-start | bytes 1179656 | tf_op jit(solution)/shard_map/ppermute | solution.py:57
  214.0 23.0 %collective-permute-start.40 = (bf16[4,128,1536]{2,1,0:T(8,128)(2,1)S(1)}, bf16[4,128,1536]{2,1,0:T(8,128)(2,1)S(1)}, u32[]{:S(2)}, u32[]{:S(2)}) collective-permute-start(bf16[4,128,1536]{2,1,0:T(8,128)(2,1)S(1)} %pad_maximum_fusion), channel_id=1, source_target_pairs={{0,2},{2,0},{1,3},{3,1},{4,6},{6,4},{5,7},{7,5},{8,10},{10,8},{9,1... | collective-permute-start | bytes 4718600 | tf_op jit(solution)/shard_map/ppermute | solution.py:57
  214.2 21.5 %collective-permute-start.39 = (bf16[128,1536]{1,0:T(8,128)(2,1)S(1)}, bf16[128,1536]{1,0:T(8,128)(2,1)S(1)}, u32[]{:S(2)}, u32[]{:S(2)}) collective-permute-start(bf16[128,1536]{1,0:T(8,128)(2,1)S(1)} %add_convert_fusion.6), channel_id=1, source_target_pairs={{4,0},{8,4},{12,8},{0,12},{5,1},{9,5},{13,9},{1,13},{6,2},{10,6},{... | collective-permute-start | bytes 1179656 | tf_op jit(solution)/shard_map/ppermute | solution.py:53
  216.0 19.7 %collective-permute-start.38 = (bf16[128,1536]{1,0:T(8,128)(2,1)S(1)}, bf16[128,1536]{1,0:T(8,128)(2,1)S(1)}, u32[]{:S(2)}, u32[]{:S(2)}) collective-permute-start(bf16[128,1536]{1,0:T(8,128)(2,1)S(1)} %add_convert_fusion.7), channel_id=1, source_target_pairs={{8,0},{12,4},{0,8},{4,12},{9,1},{13,5},{1,9},{5,13},{10,2},{14,6},... | collective-permute-start | bytes 1179656 | tf_op jit(solution)/shard_map/ppermute | solution.py:53
  216.3 20.4 %collective-permute-start.37 = (bf16[128,1536]{1,0:T(8,128)(2,1)S(1)}, bf16[128,1536]{1,0:T(8,128)(2,1)S(1)}, u32[]{:S(2)}, u32[]{:S(2)}) collective-permute-start(bf16[128,1536]{1,0:T(8,128)(2,1)S(1)} %add_convert_fusion.8), channel_id=1, source_target_pairs={{12,0},{0,4},{4,8},{8,12},{13,1},{1,5},{5,9},{9,13},{14,2},{2,6},{... | collective-permute-start | bytes 1179656 | tf_op jit(solution)/shard_map/ppermute | solution.py:53
  240.6 23.1 %collective-permute-start.41 = (bf16[128,1536]{1,0:T(8,128)(2,1)}, bf16[128,1536]{1,0:T(8,128)(2,1)S(1)}, u32[]{:S(2)}, u32[]{:S(2)}) collective-permute-start(bf16[128,1536]{1,0:T(8,128)(2,1)} %fusion.45.refs_0_), channel_id=1, source_target_pairs={{0,2},{2,0},{1,3},{3,1},{4,6},{6,4},{5,7},{7,5},{8,10},{10,8},{9,1... | collective-permute-start | bytes 1179656 | tf_op jit(solution)/shard_map/ppermute | solution.py:57
  240.6 12.1 %collective-permute-start.42 = (bf16[128,1536]{1,0:T(8,128)(2,1)}, bf16[128,1536]{1,0:T(8,128)(2,1)S(1)}, u32[]{:S(2)}, u32[]{:S(2)}) collective-permute-start(bf16[128,1536]{1,0:T(8,128)(2,1)} %fusion.45.refs_0_), channel_id=1, source_target_pairs={{4,0},{8,4},{12,8},{0,12},{5,1},{9,5},{13,9},{1,13},{6,2},{10,6},{... | collective-permute-start | bytes 1179656 | tf_op jit(solution)/shard_map/ppermute | solution.py:53
  242.2 13.7 %collective-permute-start.44 = (bf16[128,1536]{1,0:T(8,128)(2,1)}, bf16[128,1536]{1,0:T(8,128)(2,1)S(1)}, u32[]{:S(2)}, u32[]{:S(2)}) collective-permute-start(bf16[128,1536]{1,0:T(8,128)(2,1)} %fusion.45.refs_0_), channel_id=1, source_target_pairs={{8,0},{12,4},{0,8},{4,12},{9,1},{13,5},{1,9},{5,13},{10,2},{14,6},... | collective-permute-start | bytes 1179656 | tf_op jit(solution)/shard_map/ppermute | solution.py:53
  244.2 19.4 %collective-permute-start.46 = (bf16[128,1536]{1,0:T(8,128)(2,1)}, bf16[128,1536]{1,0:T(8,128)(2,1)S(1)}, u32[]{:S(2)}, u32[]{:S(2)}) collective-permute-start(bf16[128,1536]{1,0:T(8,128)(2,1)} %fusion.45.refs_0_), channel_id=1, source_target_pairs={{12,0},{0,4},{4,8},{8,12},{13,1},{1,5},{5,9},{9,13},{14,2},{2,6},{... | collective-permute-start | bytes 1179656 | tf_op jit(solution)/shard_map/ppermute | solution.py:53
  252.7 11.0 %collective-permute-start.43 = (bf16[128,1536]{1,0:T(8,128)(2,1)S(1)}, bf16[128,1536]{1,0:T(8,128)(2,1)S(1)}, u32[]{:S(2)}, u32[]{:S(2)}) collective-permute-start(bf16[128,1536]{1,0:T(8,128)(2,1)S(1)} %collective-permute-done.42.refs_2_), channel_id=1, source_target_pairs={{0,2},{2,0},{1,3},{3,1},{4,6},{6,4},{5,7},{7,5},{8,10},{10,8},{9,1... | collective-permute-start | bytes 1179656 | tf_op jit(solution)/shard_map/ppermute | solution.py:57
  255.9 7.8 %collective-permute-start.45 = (bf16[128,1536]{1,0:T(8,128)(2,1)S(1)}, bf16[128,1536]{1,0:T(8,128)(2,1)S(1)}, u32[]{:S(2)}, u32[]{:S(2)}) collective-permute-start(bf16[128,1536]{1,0:T(8,128)(2,1)S(1)} %collective-permute-done.44.refs_4_), channel_id=1, source_target_pairs={{0,2},{2,0},{1,3},{3,1},{4,6},{6,4},{5,7},{7,5},{8,10},{10,8},{9,1... | collective-permute-start | bytes 1179656 | tf_op jit(solution)/shard_map/ppermute | solution.py:57
  265.4 37.8 %collective-permute-start.50 = (bf16[128,1536]{1,0:T(8,128)(2,1)S(1)}, bf16[128,1536]{1,0:T(8,128)(2,1)S(1)}, u32[]{:S(2)}, u32[]{:S(2)}) collective-permute-start(bf16[128,1536]{1,0:T(8,128)(2,1)S(1)} %get-tuple-element.254), channel_id=1, source_target_pairs={{4,0},{8,4},{12,8},{0,12},{5,1},{9,5},{13,9},{1,13},{6,2},{10,6},{... | collective-permute-start | bytes 1179656 | tf_op jit(solution)/shard_map/ppermute | solution.py:53
  266.6 36.6 %collective-permute-start.49 = (bf16[128,1536]{1,0:T(8,128)(2,1)S(1)}, bf16[128,1536]{1,0:T(8,128)(2,1)S(1)}, u32[]{:S(2)}, u32[]{:S(2)}) collective-permute-start(bf16[128,1536]{1,0:T(8,128)(2,1)S(1)} %get-tuple-element.253), channel_id=1, source_target_pairs={{8,0},{12,4},{0,8},{4,12},{9,1},{13,5},{1,9},{5,13},{10,2},{14,6},... | collective-permute-start | bytes 1179656 | tf_op jit(solution)/shard_map/ppermute | solution.py:53
  268.1 35.1 %collective-permute-start.48 = (bf16[128,1536]{1,0:T(8,128)(2,1)S(1)}, bf16[128,1536]{1,0:T(8,128)(2,1)S(1)}, u32[]{:S(2)}, u32[]{:S(2)}) collective-permute-start(bf16[128,1536]{1,0:T(8,128)(2,1)S(1)} %get-tuple-element.252), channel_id=1, source_target_pairs={{12,0},{0,4},{4,8},{8,12},{13,1},{1,5},{5,9},{9,13},{14,2},{2,6},{... | collective-permute-start | bytes 1179656 | tf_op jit(solution)/shard_map/ppermute | solution.py:53
  304.3 21.9 %collective-permute-start.51 = (bf16[8,128,128]{2,1,0:T(8,128)(2,1)S(1)}, bf16[8,128,128]{2,1,0:T(8,128)(2,1)S(1)}, u32[]{:S(2)}, u32[]{:S(2)}) collective-permute-start(bf16[8,128,128]{2,1,0:T(8,128)(2,1)S(1)} %get-tuple-element.260), channel_id=1, source_target_pairs={{0,1},{1,0},{2,3},{3,2},{4,5},{5,4},{6,7},{7,6},{8,9},{9,8},{10,11... | collective-permute-start | bytes 786440 | tf_op jit(solution)/shard_map/ppermute | solution.py:57
  307.3 18.9 %collective-permute-start.52 = (bf16[8,128,128]{2,1,0:T(8,128)(2,1)S(1)}, bf16[8,128,128]{2,1,0:T(8,128)(2,1)S(1)}, u32[]{:S(2)}, u32[]{:S(2)}) collective-permute-start(bf16[8,128,128]{2,1,0:T(8,128)(2,1)S(1)} %get-tuple-element.261), channel_id=1, source_target_pairs={{16,0},{17,1},{32,16},{33,17},{48,32},{49,33},{64,48},{65,49},{80,... | collective-permute-start | bytes 786440 | tf_op jit(solution)/shard_map/ppermute | solution.py:67
  309.2 17.0 %collective-permute-start.53 = (bf16[8,128,128]{2,1,0:T(8,128)(2,1)S(1)}, bf16[8,128,128]{2,1,0:T(8,128)(2,1)S(1)}, u32[]{:S(2)}, u32[]{:S(2)}) collective-permute-start(bf16[8,128,128]{2,1,0:T(8,128)(2,1)S(1)} %get-tuple-element.262), channel_id=1, source_target_pairs={{16,1},{17,0},{32,17},{33,16},{48,33},{49,32},{64,49},{65,48},{80,... | collective-permute-start | bytes 786440 | tf_op jit(solution)/shard_map/ppermute | solution.py:67
  311.1 20.4 %collective-permute-start.54 = (bf16[8,128,128]{2,1,0:T(8,128)(2,1)S(1)}, bf16[8,128,128]{2,1,0:T(8,128)(2,1)S(1)}, u32[]{:S(2)}, u32[]{:S(2)}) collective-permute-start(bf16[8,128,128]{2,1,0:T(8,128)(2,1)S(1)} %get-tuple-element.263), channel_id=1, source_target_pairs={{32,0},{33,1},{48,16},{49,17},{64,32},{65,33},{80,48},{81,49},{96,... | collective-permute-start | bytes 786440 | tf_op jit(solution)/shard_map/ppermute | solution.py:67
  317.2 16.8 %collective-permute-start.55 = (bf16[8,128,128]{2,1,0:T(8,128)(2,1)S(1)}, bf16[8,128,128]{2,1,0:T(8,128)(2,1)S(1)}, u32[]{:S(2)}, u32[]{:S(2)}) collective-permute-start(bf16[8,128,128]{2,1,0:T(8,128)(2,1)S(1)} %get-tuple-element.264), channel_id=1, source_target_pairs={{32,1},{33,0},{48,17},{49,16},{64,33},{65,32},{80,49},{81,48},{96,... | collective-permute-start | bytes 786440 | tf_op jit(solution)/shard_map/ppermute | solution.py:67
  350.5 7.8 %collective-permute-start.61 = (bf16[128,1536]{1,0:T(8,128)(2,1)}, bf16[128,1536]{1,0:T(8,128)(2,1)}, u32[]{:S(2)}, u32[]{:S(2)}) collective-permute-start(bf16[128,1536]{1,0:T(8,128)(2,1)} %get-tuple-element.295), channel_id=1, source_target_pairs={{0,2},{2,0},{1,3},{3,1},{4,6},{6,4},{5,7},{7,5},{8,10},{10,8},{9,1... | collective-permute-start | bytes 1179656 | tf_op jit(solution)/shard_map/ppermute | solution.py:57
  350.5 12.3 %collective-permute-start.59 = (bf16[128,1536]{1,0:T(8,128)(2,1)S(1)}, bf16[128,1536]{1,0:T(8,128)(2,1)}, u32[]{:S(2)}, u32[]{:S(2)}) collective-permute-start(bf16[128,1536]{1,0:T(8,128)(2,1)S(1)} %copy-done.44), channel_id=1, source_target_pairs={{0,2},{2,0},{1,3},{3,1},{4,6},{6,4},{5,7},{7,5},{8,10},{10,8},{9,1... | collective-permute-start | bytes 1179656 | tf_op jit(solution)/shard_map/ppermute | solution.py:57
  351.0 13.8 %collective-permute-start.57 = (bf16[128,1536]{1,0:T(8,128)(2,1)S(1)}, bf16[128,1536]{1,0:T(8,128)(2,1)}, u32[]{:S(2)}, u32[]{:S(2)}) collective-permute-start(bf16[128,1536]{1,0:T(8,128)(2,1)S(1)} %copy-done.42), channel_id=1, source_target_pairs={{0,2},{2,0},{1,3},{3,1},{4,6},{6,4},{5,7},{7,5},{8,10},{10,8},{9,1... | collective-permute-start | bytes 1179656 | tf_op jit(solution)/shard_map/ppermute | solution.py:57
  351.1 25.2 %collective-permute-start.56 = (bf16[128,1536]{1,0:T(8,128)(2,1)S(1)}, bf16[128,1536]{1,0:T(8,128)(2,1)}, u32[]{:S(2)}, u32[]{:S(2)}) collective-permute-start(bf16[128,1536]{1,0:T(8,128)(2,1)S(1)} %copy-done.40), channel_id=1, source_target_pairs={{0,2},{2,0},{1,3},{3,1},{4,6},{6,4},{5,7},{7,5},{8,10},{10,8},{9,1... | collective-permute-start | bytes 1179656 | tf_op jit(solution)/shard_map/ppermute | solution.py:57
  351.5 18.7 %all-to-all-start.3 = ((bf16[8,192,192]{2,1,0:T(8,128)(2,1)}), bf16[8,192,192]{2,1,0:T(8,128)(2,1)}, u32[]{:S(2)}, u32[]{:S(2)}) async-start(bf16[8,192,192]{2,1,0:T(8,128)(2,1)} %bitcast.41), calls=%async_computation.4 | async-start | bytes 1572864 | tf_op jit(solution)/shard_map/all_to_all | solution.py:71
  360.1 19.7 %collective-permute-start.62 = (bf16[128,1536]{1,0:T(8,128)(2,1)}, bf16[128,1536]{1,0:T(8,128)(2,1)S(1)}, u32[]{:S(2)}, u32[]{:S(2)}) collective-permute-start(bf16[128,1536]{1,0:T(8,128)(2,1)} %add_convert_fusion.1), channel_id=1, source_target_pairs={{4,0},{8,4},{12,8},{0,12},{5,1},{9,5},{13,9},{1,13},{6,2},{10,6},{... | collective-permute-start | bytes 1179656 | tf_op jit(solution)/shard_map/ppermute | solution.py:53
  363.9 15.9 %collective-permute-start.60 = (bf16[128,1536]{1,0:T(8,128)(2,1)S(1)}, bf16[128,1536]{1,0:T(8,128)(2,1)S(1)}, u32[]{:S(2)}, u32[]{:S(2)}) collective-permute-start(bf16[128,1536]{1,0:T(8,128)(2,1)S(1)} %add_convert_fusion.2), channel_id=1, source_target_pairs={{8,0},{12,4},{0,8},{4,12},{9,1},{13,5},{1,9},{5,13},{10,2},{14,6},... | collective-permute-start | bytes 1179656 | tf_op jit(solution)/shard_map/ppermute | solution.py:53
  366.6 17.7 %collective-permute-start.58 = (bf16[128,1536]{1,0:T(8,128)(2,1)}, bf16[128,1536]{1,0:T(8,128)(2,1)S(1)}, u32[]{:S(2)}, u32[]{:S(2)}) collective-permute-start(bf16[128,1536]{1,0:T(8,128)(2,1)} %add_convert_fusion.3), channel_id=1, source_target_pairs={{12,0},{0,4},{4,8},{8,12},{13,1},{1,5},{5,9},{9,13},{14,2},{2,6},{... | collective-permute-start | bytes 1179656 | tf_op jit(solution)/shard_map/ppermute | solution.py:53
  370.2 20.4 %all-to-all-start.2 = ((bf16[8,192,384]{2,1,0:T(8,128)(2,1)}), bf16[8,192,384]{2,1,0:T(8,128)(2,1)}, u32[]{:S(2)}, u32[]{:S(2)}) async-start(bf16[8,192,384]{2,1,0:T(8,128)(2,1)} %bitcast.39), calls=%async_computation.3 | async-start | bytes 2359296 | tf_op jit(solution)/shard_map/all_to_all | solution.py:71
  394.3 17.0 %all-to-all-start.4 = ((bf16[8,24,1872]{2,1,0:T(8,128)(2,1)}), bf16[8,24,1872]{2,1,0:T(8,128)(2,1)}, u32[]{:S(2)}, u32[]{:S(2)}) async-start(bf16[8,24,1872]{2,1,0:T(8,128)(2,1)} %concatenate.66), calls=%async_computation.5 | async-start | bytes 1474560 | tf_op jit(solution)/shard_map/all_to_all | solution.py:71
  412.7 9.7 %collective-permute-start.63 = (bf16[8,12,384]{2,1,0:T(8,128)(2,1)S(1)}, bf16[8,12,384]{2,1,0:T(8,128)(2,1)S(1)}, u32[]{:S(2)}, u32[]{:S(2)}) collective-permute-start(bf16[8,12,384]{2,1,0:T(8,128)(2,1)S(1)} %fusion.9), channel_id=1, source_target_pairs={{0,1},{1,0},{2,3},{3,2},{4,5},{5,4},{6,7},{7,6},{8,9},{9,8},{10,11... | collective-permute-start | bytes 221192 | tf_op jit(solution)/shard_map/ppermute | solution.py:57
  413.9 7.6 %collective-permute-start.64 = (bf16[4,24,192]{2,1,0:T(8,128)(2,1)S(1)}, bf16[4,24,192]{2,1,0:T(8,128)(2,1)S(1)}, u32[]{:S(2)}, u32[]{:S(2)}) collective-permute-start(bf16[4,24,192]{2,1,0:T(8,128)(2,1)S(1)} %dynamic-slice_convert_fusion), channel_id=1, source_target_pairs={{0,1},{1,0},{2,3},{3,2},{4,5},{5,4},{6,7},{7,6},{8,9},{9,8},{10,11... | collective-permute-start | bytes 110600 | tf_op jit(solution)/shard_map/ppermute | solution.py:57
  (95 other events, 768.8 us)
Sparse Core Ops, SparseCore 0:
  30.7 108.9 all-gather.1
  240.1 106.5 reduce-scatter.1

commit v8 on v7

--- a/solution.py
+++ b/solution.py
@@ -113,7 +113,7 @@
     return pl.BlockSpec(shape, lambda *i: (0,) * len(shape))
 
 
-ROWS_OF = pl.BlockSpec((ROWS, WIDTH), lambda *i: (0, 0))
+IN_VMEM = pl.BlockSpec(memory_space=pltpu.VMEM)
 
 
 def stacked(a_ref, b_ref):
@@ -173,18 +173,9 @@
             jax.ShapeDtypeStruct((8, ROWS, 2 * HEAD), BF16),
             jax.ShapeDtypeStruct((4, PAIR, 4 * HEAD), F32),
         ),
-        grid=(1,),
-        in_specs=[ROWS_OF] * 8
-        + [all_of(WIDTH, 384), all_of(1, WIDTH)]
-        + [all_of(4, PAIR, 2 * HEAD)] * 2
-        + [all_of(1, 4 * HEAD)],
-        out_specs=(
-            all_of(4 * PAIR, WIDTH),
-            all_of(8, ROWS, QUERY),
-            all_of(8, ROWS, 2 * HEAD),
-            all_of(4, PAIR, 4 * HEAD),
-        ),
-        compiler_params=params(1, 40),
+        in_specs=[IN_VMEM] * 13,
+        out_specs=(IN_VMEM,) * 4,
+        compiler_params=params(0, 20),
         cost_estimate=cost(8 * PAIR * WIDTH * 384, 1e7),
     )(*xs, w, gain, cos, sin, head_gain)
 
@@ -223,7 +214,7 @@
     )(gq, raw, cos, sin, head_gain)
 
 
-def unproject_kernel(*refs):
+def unproject_kernel(half, *refs):
     graw_q_ref, g_refs, raw_ref, xs, (w_ref, cos_ref, sin_ref, head_gain_ref) = (
         refs[0], refs[1:7], refs[7], refs[8:12], refs[12:16],
     )
@@ -232,16 +223,18 @@
     lane = lax.broadcasted_iota(jnp.int32, (PAIR, 2 * HEAD), 1)
     for i in range(2):
         tiles = slice(2 * i, 2 * i + 2)
-        gkv = g_refs[0][tiles].astype(F32)
+        at = 2 * half + i
+        there = slice(2 * at, 2 * at + 2)
+        gkv = g_refs[0][there].astype(F32)
         for ref in g_refs[1:]:
-            gkv = gkv + ref[tiles].astype(F32)
+            gkv = gkv + ref[there].astype(F32)
         gkv = gkv.reshape(PAIR, 2 * HEAD)
         gk = jnp.where(lane < HEAD, 0.0, (gkv * HEAD**-0.5).astype(BF16).astype(F32))
         graw_k, gain = turned_back(
-            gk, raw_ref[i][:, 2 * HEAD :], cos_ref[i], sin_ref[i], head_gain_ref[...]
+            gk, raw_ref[at][:, 2 * HEAD :], cos_ref[at], sin_ref[at], head_gain_ref[...]
         )
         gains = gains + gain
-        graw_q = graw_q_ref[i].astype(F32)
+        graw_q = graw_q_ref[at].astype(F32)
         graw = [
             graw_q[:, : 2 * HEAD],
             jnp.where(lane < HEAD, graw_q[:, 2 * HEAD :], graw_k),
@@ -259,68 +252,49 @@
 
 
 def unproject(half, graw_q, gkvs, raw, xs, w, cos, sin, head_gain):
-    def at_half(*shape):
-        return pl.BlockSpec(shape, lambda i: (half,) + (0,) * (len(shape) - 1))
-
-    table = at_half(2, PAIR, 2 * HEAD)
     outs = (jax.ShapeDtypeStruct((ROWS, WIDTH), BF16),) * 4 + (
         jax.ShapeDtypeStruct((2 * PAIR, 2 * HEAD), BF16),
         jax.ShapeDtypeStruct((1, WIDTH), F32),
         jax.ShapeDtypeStruct((1, 2 * HEAD), F32),
     )
     return pl.pallas_call(
-        unproject_kernel,
+        functools.partial(unproject_kernel, half),
         out_shape=outs,
-        grid=(1,),
-        in_specs=[at_half(2, PAIR, 4 * HEAD)]
-        + [at_half(4, ROWS, 2 * HEAD)] * 6
-        + [at_half(2, PAIR, 4 * HEAD)]
-        + [ROWS_OF] * 4
-        + [all_of(WIDTH, 6 * HEAD), table, table, all_of(1, 4 * HEAD)],
-        out_specs=tuple(all_of(*o.shape) for o in outs),
-        compiler_params=params(1, 20),
+        in_specs=[IN_VMEM] * 16,
+        out_specs=(IN_VMEM,) * 7,
+        compiler_params=params(0, 16),
         cost_estimate=cost(4 * PAIR * WIDTH * 384, 8e6),
     )(graw_q, *gkvs, raw, *xs, w, cos, sin, head_gain)
 
 
 def ffn_kernel(
-    x0_ref, x1_ref, c0_ref, c1_ref, gu_w_ref, d_w_ref,
-    part0_ref, part1_ref, out0_ref, out1_ref, act_ref, gu_ref, total, out_total,
+    x0_ref, x1_ref, c0_ref, c1_ref, w_ref, part0_ref, part1_ref, out0_ref, out1_ref, act_ref, gu_ref
 ):
-    y = pl.program_id(0)
-    x = stacked(x0_ref, x1_ref)
-    gate_up = dot(x, gu_w_ref[0])
-    gate, up = gate_up[:, :PADDED], gate_up[:, PADDED:]
-    grad_act = dot(stacked(c0_ref, c1_ref), d_w_ref[0])
+    x, cot = stacked(x0_ref, x1_ref), stacked(c0_ref, c1_ref)
     own = lax.broadcasted_iota(jnp.int32, (PAIR, PADDED), 1) < PART
-    sig = 1.0 / (1.0 + jnp.exp(-gate))
-    silu = gate * sig
-    act = jnp.where(own, silu * up, 0.0).astype(BF16)
-    act_ref[0] = act
-    out_part = dot(act, d_w_ref[0], NT)
-    grad_act = jnp.where(own, grad_act, 0.0)
-    grad_gate = jnp.where(own, grad_act * up * sig * (1.0 + gate * (1.0 - sig)), 0.0)
-    grads = jnp.concatenate([grad_gate, jnp.where(own, grad_act * silu, 0.0)], axis=1).astype(BF16)
-    gu_ref[0] = grads
-    part = dot(grads, gu_w_ref[0], NT)
-
-    @pl.when(y == 0)
-    def _():
-        total[...] = part
-        out_total[...] = out_part
-
-    @pl.when(y == 1)
-    def _():
-        whole_part = (total[...] + part).astype(BF16)
-        part0_ref[...] = whole_part[:ROWS]
-        part1_ref[...] = whole_part[ROWS:]
-        whole_part = (out_total[...] + out_part).astype(BF16)
-        out0_ref[...] = whole_part[:ROWS]
-        out1_ref[...] = whole_part[ROWS:]
+    part, out_part = 0.0, 0.0
+    for y in range(2):
+        gate_up = dot(x, w_ref[y, :, : 2 * PADDED])
+        gate, up = gate_up[:, :PADDED], gate_up[:, PADDED:]
+        grad_act = jnp.where(own, dot(cot, w_ref[y, :, 2 * PADDED :]), 0.0)
+        sig = 1.0 / (1.0 + jnp.exp(-gate))
+        silu = gate * sig
+        act = jnp.where(own, silu * up, 0.0).astype(BF16)
+        act_ref[y] = act
+        out_part = out_part + dot(act, w_ref[y, :, 2 * PADDED :], NT)
+        grad_gate = jnp.where(own, grad_act * up * sig * (1.0 + gate * (1.0 - sig)), 0.0)
+        grad_up = jnp.where(own, grad_act * silu, 0.0)
+        grads = jnp.concatenate([grad_gate, grad_up], axis=1).astype(BF16)
+        gu_ref[y] = grads
+        part = part + dot(grads, w_ref[y, :, : 2 * PADDED], NT)
+    part, out_part = part.astype(BF16), out_part.astype(BF16)
+    part0_ref[...] = part[:ROWS]
+    part1_ref[...] = part[ROWS:]
+    out0_ref[...] = out_part[:ROWS]
+    out1_ref[...] = out_part[ROWS:]
 
 
 def ffn(x0, x1, c0, c1, w):
-    rows = ROWS_OF
     return pl.pallas_call(
         ffn_kernel,
         out_shape=(jax.ShapeDtypeStruct((ROWS, WIDTH), BF16),) * 4
@@ -328,18 +302,11 @@
             jax.ShapeDtypeStruct((2, PAIR, PADDED), BF16),
             jax.ShapeDtypeStruct((2, PAIR, 2 * PADDED), BF16),
         ),
-        grid=(2,),
-        in_specs=[rows] * 4
-        + [pl.BlockSpec((1, WIDTH, n * PADDED), lambda y, c=c: (y, 0, c)) for n, c in ((2, 0), (1, 2))],
-        out_specs=(rows,) * 4
-        + (
-            pl.BlockSpec((1, PAIR, PADDED), lambda y: (y, 0, 0)),
-            pl.BlockSpec((1, PAIR, 2 * PADDED), lambda y: (y, 0, 0)),
-        ),
-        scratch_shapes=[pltpu.VMEM((PAIR, WIDTH), F32)] * 2,
-        compiler_params=params(1, 32),
+        in_specs=[IN_VMEM] * 5,
+        out_specs=(IN_VMEM,) * 6,
+        compiler_params=params(0, 36),
         cost_estimate=cost(2 * 2 * PAIR * WIDTH * 6 * PADDED, 14e6),
-    )(x0, x1, c0, c1, w, w)
+    )(x0, x1, c0, c1, w)
 
 
 def ffn_weights_kernel(*refs):
@@ -636,7 +603,7 @@
             out_specs=out_specs,
             scratch_shapes=scratch,
         ),
-        compiler_params=params(1, 36 if back else 28),
+        compiler_params=params(1, 30 if back else 20),
         cost_estimate=cost(flops, 8e6, 1e7),
     )
 

time: 442 us -> 439 us (level)
    unnamed x177 -> x179, local copies, waits for them, and re-layouts: 26.3 us -> 26.5 us
  transfers between devices with their start and end apart: 71 -> 71, of which waited for: 25 -> 26; matrix products, arithmetic and copies ran while one was open for 9% -> 9% of each run, Pallas kernels for 27% -> 26%
where the time goes in v8:
time: 439 us; the launch traced here: 431 us
  Pallas kernels  114 us (26%)
  waiting for transfers between devices  112 us (26%)
  starting transfers between devices  89.9 us (20%)
  local copies, waits for them, and re-layouts  53.8 us (12%)
  other arithmetic  28.9 us (7%)
  blocking collectives  17 us (4%)
  between operations  15.8 us (4%)
    ppermute x24, waiting for transfers between devices, shift_x(): return lax.ppermute(v, 'x', [((i + distance) % 4, i) for i in range(4)])  53 us
    pallas_call x1, Pallas kernels, back(): return call(plan, q, start, *kvs, grad, out, lse)  33.2 us
    ppermute x24, starting transfers between devices, shift_x(): return lax.ppermute(v, 'x', [((i + distance) % 4, i) for i in range(4)])  28.2 us
    all_to_all x4, waiting for transfers between devices, exchange(): return lax.all_to_all(v, axes, split_axis=0, concat_axis=0, tiled=True)  28 us
    unnamed x179, local copies, waits for them, and re-layouts  26.5 us
    pallas_call x4, Pallas kernels, ffn(): pl.pallas_call(ffn_kernel, out_shape=(jax.ShapeDtypeStruct((ROWS, WIDTH),...  25.6 us
    all_to_all x4, starting transfers between devices, exchange(): return lax.all_to_all(v, axes, split_axis=0, concat_axis=0, tiled=True)  24.2 us
    ppermute x8, waiting for transfers between devices, shift_super(): return lax.ppermute(v, ('ylo', 'z', 'yhi'), pairs)  22.5 us
  transfers between devices with their start and end apart: 71, of which 26 were waited for; matrix products, arithmetic and copies ran while one was open for 9% of the time, Pallas kernels for 26%

profile of v8, /device:TPU:8, one launch (start us, length us, event | category | flops | bytes accessed | tf_op | source)
XLA Modules:
  0.0 430.9 jit_solution(9936399045285781274)
XLA Ops:
  12.7 17.0 %all_to_all.25 = bf16[8,24,1920]{2,1,0:T(8,128)(2,1)S(1)} all-to-all(bf16[8,24,1920]{2,1,0:T(8,128)(2,1)S(1)} %concatenate.54), channel_id=1, replica_groups=mesh['ylo'=2,'z'=4,'x'=4,'core'=2,'yhi'=2] {'x','core'}, dimensions={0} | all-to-all | bytes 1474560 | tf_op jit(solution)/shard_map/all_to_all | solution.py:71
  36.1 8.5 %all-to-all-start.1 = ((bf16[16,96,384]{2,1,0:T(8,128)(2,1)}), bf16[16,96,384]{2,1,0:T(8,128)(2,1)S(1)}, u32[]{:S(2)}, u32[]{:S(2)}) async-start(bf16[16,96,384]{2,1,0:T(8,128)(2,1)} %broadcast_in_dim.27), calls=%async_computation.1 | async-start | bytes 2359296 | tf_op jit(solution)/shard_map/all_to_all | solution.py:71
  45.0 1.9 fusion.12
  47.5 5.6 %collective-permute-done.5.refs_6_.refs_10_ = bf16[128,1536]{1,0:T(8,128)(2,1)} collective-permute-done((bf16[128,1536]{1,0:T(8,128)(2,1)S(1)}, bf16[128,1536]{1,0:T(8,128)(2,1)}, u32[]{:S(2)}, u32[]{:S(2)}) %collective-permute-start.5) | collective-permute-done | bytes 393248 | tf_op jit(solution)/shard_map/ppermute | solution.py:53
  53.9 2.1 collective-permute-start.8
  58.0 10.6 %all-to-all-done.1 = bf16[16,96,384]{2,1,0:T(8,128)(2,1)S(1)} async-done(((bf16[16,96,384]{2,1,0:T(8,128)(2,1)}), bf16[16,96,384]{2,1,0:T(8,128)(2,1)S(1)}, u32[]{:S(2)}, u32[]{:S(2)}) %all-to-all-start.1) | async-done | bytes 1179680 | tf_op jit(solution)/shard_map/all_to_all | solution.py:71
  70.5 2.3 reshape.569.refs_8_.refs_12_
  75.9 4.9 %shard_map.237 = (bf16[1024,1536]{1,0:T(8,128)(2,1)S(1)}, bf16[8,128,192]{2,1,0:T(8,128)(2,1)S(1)}, bf16[8,128,128]{2,1,0:T(8,128)(2,1)}, f32[4,256,256]{2,1,0:T(8,128)S(1)}) custom-call(bf16[128,1536]{1,0:T(8,128)(2,1)S(1)} %copy-done.3, bf16[128,1536]{1,0:T(8,128)(2,1)S(1)} %collective-permute-done.refs_1_.refs_9_, bf16[128,1536]{1,0:T(8,128)(2,1)S(1)} %copy-done.15, ...), custom_call_target="tpu_custom_call" | custom-call | flops 1207959552 | bytes 10000000 | tf_op jit(solution)/shard_map/pallas_call | solution.py:168
  80.8 1.7 copy-done
  84.3 1.8 collective-permute-start.10
  86.3 2.1 collective-permute-start.11
  88.4 3.5 collective-permute-start.12
  91.9 2.1 collective-permute-start.13
  94.0 2.5 collective-permute-start.14
  96.5 4.3 %collective-permute-done.10.refs_1_.refs_5_ = bf16[8,128,128]{2,1,0:T(8,128)(2,1)S(1)} collective-permute-done((bf16[8,128,128]{2,1,0:T(8,128)(2,1)}, bf16[8,128,128]{2,1,0:T(8,128)(2,1)S(1)}, u32[]{:S(2)}, u32[]{:S(2)}) %collective-permute-start.10) | collective-permute-done | bytes 262176 | tf_op jit(solution)/shard_map/ppermute | solution.py:57
  102.0 8.5 %shard_map.238 = (f32[4,64,768]{2,1,0:T(8,128)S(1)}, f32[4,1,768]{2,1,0:T(1,128)S(1)}) custom-call(s32[8,17]{1,0:T(8,128)S(1)} %stack.22.plan, bf16[8,128,192]{2,1,0:T(8,128)(2,1)S(1)} %copy-done.36, s32[4,1,768]{2,1,0:T(1,128)S(1)} %copy.103.start_ref, bf16[8,128,128]{2,1,0:T(8,128)(2,1)} %get-tuple-element.159.refs_0_.refs_4_, ...), custom_call_target="tpu_custom_call" | custom-call | flops 4000000000 | bytes 8000000 | tf_op jit(solution)/shard_map/pallas_call | solution.py:618
  110.6 6.7 %collective-permute-done.11.refs_0_ = bf16[8,128,128]{2,1,0:T(8,128)(2,1)S(1)} collective-permute-done((bf16[8,128,128]{2,1,0:T(8,128)(2,1)}, bf16[8,128,128]{2,1,0:T(8,128)(2,1)S(1)}, u32[]{:S(2)}, u32[]{:S(2)}) %collective-permute-start.11) | collective-permute-done | bytes 262176 | tf_op jit(solution)/shard_map/ppermute | solution.py:67
  118.7 6.5 %collective-permute-done.13.refs_2_ = bf16[8,128,128]{2,1,0:T(8,128)(2,1)S(1)} collective-permute-done((bf16[8,128,128]{2,1,0:T(8,128)(2,1)}, bf16[8,128,128]{2,1,0:T(8,128)(2,1)S(1)}, u32[]{:S(2)}, u32[]{:S(2)}) %collective-permute-start.13) | collective-permute-done | bytes 262176 | tf_op jit(solution)/shard_map/ppermute | solution.py:67
  126.6 9.2 %shard_map.239 = (bf16[8,128,192]{2,1,0:T(8,128)(2,1)S(1)}, f32[4,64,768]{2,1,0:T(8,128)S(1)}, f32[4,1,768]{2,1,0:T(1,128)S(1)}) custom-call(s32[8,17]{1,0:T(8,128)S(1)} %stack.22.plan, bf16[8,128,192]{2,1,0:T(8,128)(2,1)S(1)} %copy-done.37, s32[4,1,768]{2,1,0:T(1,128)S(1)} %copy.103.start_ref, bf16[8,128,128]{2,1,0:T(8,128)(2,1)S(1)} %collective-permute-done.11.refs_0_, ...), custom_call_target="tpu_custom_call" | custom-call | flops 8000000000 | bytes 8000000 | tf_op jit(solution)/shard_map/pallas_call | solution.py:625
  140.2 1.6 dynamic-slice_bitcast_fusion.2
  145.4 2.8 collective-permute-start.25
  150.3 15.0 %collective-permute-done.25 = bf16[128,1536]{1,0:T(8,128)(2,1)S(1)} collective-permute-done((bf16[128,1536]{1,0:T(8,128)(2,1)S(1)}, bf16[128,1536]{1,0:T(8,128)(2,1)S(1)}, u32[]{:S(2)}, u32[]{:S(2)}) %collective-permute-start.25) | collective-permute-done | bytes 393248 | tf_op jit(solution)/shard_map/ppermute | solution.py:53
  165.3 3.8 collective-permute-done.21
  172.3 6.4 %shard_map.244 = (bf16[128,1536]{1,0:T(8,128)(2,1)S(1)}, bf16[128,1536]{1,0:T(8,128)(2,1)S(1)}, bf16[128,1536]{1,0:T(8,128)(2,1)S(1)}, bf16[128,1536]{1,0:T(8,12...) custom-call(bf16[128,1536]{1,0:T(8,128)(2,1)S(1)} %multiply_convert_fusion.x0_ref.refs_0_, ...), custom_call_target="tpu_custom_call" | custom-call | flops 4831838208 | bytes 14000000 | tf_op jit(solution)/shard_map/pallas_call | solution.py:298
  181.6 1.7 collective-permute-done.29.x1_ref.refs_3_
  183.8 6.4 %shard_map.245 = (bf16[128,1536]{1,0:T(8,128)(2,1)S(1)}, bf16[128,1536]{1,0:T(8,128)(2,1)S(1)}, bf16[128,1536]{1,0:T(8,128)(2,1)S(1)}, bf16[128,1536]{1,0:T(8,12...) custom-call(bf16[128,1536]{1,0:T(8,128)(2,1)S(1)} %collective-permute-done.28.x0_ref.refs_2_, ...), custom_call_target="tpu_custom_call" | custom-call | flops 4831838208 | bytes 14000000 | tf_op jit(solution)/shard_map/pallas_call | solution.py:298
  192.5 6.4 %shard_map.246 = (bf16[128,1536]{1,0:T(8,128)(2,1)S(1)}, bf16[128,1536]{1,0:T(8,128)(2,1)S(1)}, bf16[128,1536]{1,0:T(8,128)(2,1)S(1)}, bf16[128,1536]{1,0:T(8,12...) custom-call(bf16[128,1536]{1,0:T(8,128)(2,1)S(1)} %collective-permute-done.30.x0_ref.refs_4_, ...), custom_call_target="tpu_custom_call" | custom-call | flops 4831838208 | bytes 14000000 | tf_op jit(solution)/shard_map/pallas_call | solution.py:298
  201.9 6.4 %shard_map.247 = (bf16[128,1536]{1,0:T(8,128)(2,1)S(1)}, bf16[128,1536]{1,0:T(8,128)(2,1)S(1)}, bf16[128,1536]{1,0:T(8,128)(2,1)S(1)}, bf16[128,1536]{1,0:T(8,12...) custom-call(bf16[128,1536]{1,0:T(8,128)(2,1)S(1)} %collective-permute-done.33.x0_ref.refs_6_, ...), custom_call_target="tpu_custom_call" | custom-call | flops 4831838208 | bytes 14000000 | tf_op jit(solution)/shard_map/pallas_call | solution.py:298
  211.2 1.8 collective-permute-start.39
  213.9 15.3 %shard_map.248 = bf16[2,1536,1296]{2,1,0:T(8,128)(2,1)S(1)} custom-call(bf16[128,1536]{1,0:T(8,128)(2,1)S(1)} %multiply_convert_fusion.x0_ref.refs_0_, bf16[128,1536]{1,0:T(8,128)(2,1)S(1)} %collective-permute-done.26.x1_ref.refs_1_, bf16[128,1536]{1,0:T(8,128)(2,1)S(1)} %collective-permute-done.28.x0_ref.refs_2_, ...), custom_call_target="tpu_custom_call" | custom-call | flops 9663676416 | bytes 24000000 | tf_op jit(solution)/shard_map/pallas_call | solution.py:327
  229.3 3.5 copy-done.8
  235.0 2.0 fusion.45.refs_0_
  237.6 1.6 collective-permute-start.42
  239.3 2.0 collective-permute-start.44
  242.8 2.2 add_convert_fusion
  245.0 4.7 %collective-permute-done.42.refs_2_ = bf16[128,1536]{1,0:T(8,128)(2,1)S(1)} collective-permute-done((bf16[128,1536]{1,0:T(8,128)(2,1)}, bf16[128,1536]{1,0:T(8,128)(2,1)S(1)}, u32[]{:S(2)}, u32[]{:S(2)}) %collective-permute-start.42) | collective-permute-done | bytes 393248 | tf_op jit(solution)/shard_map/ppermute | solution.py:53
  249.7 3.2 collective-permute-done.44.refs_4_
  253.0 7.7 %collective-permute-done.46.refs_6_ = bf16[128,1536]{1,0:T(8,128)(2,1)S(1)} collective-permute-done((bf16[128,1536]{1,0:T(8,128)(2,1)}, bf16[128,1536]{1,0:T(8,128)(2,1)S(1)}, u32[]{:S(2)}, u32[]{:S(2)}) %collective-permute-start.46) | collective-permute-done | bytes 393248 | tf_op jit(solution)/shard_map/ppermute | solution.py:53
  267.1 33.2 %shard_map.250 = (bf16[8,128,256]{2,1,0:T(8,128)(2,1)S(1)}, bf16[8,128,128]{2,1,0:T(8,128)(2,1)S(1)}, bf16[8,128,128]{2,1,0:T(8,128)(2,1)S(1)}, bf16[8,128,128]{...) custom-call(s32[8,17]{1,0:T(8,128)S(1)} %copy-done.34, ...), custom_call_target="tpu_custom_call" | custom-call | flops 30000001024 | bytes 8000000 | tf_op jit(solution)/shard_map/pallas_call | solution.py:639
  301.5 3.1 collective-permute-start.51
  304.6 1.9 collective-permute-start.52
  306.5 1.9 collective-permute-start.53
  308.4 6.0 %collective-permute-start.54 = (bf16[8,128,128]{2,1,0:T(8,128)(2,1)S(1)}, bf16[8,128,128]{2,1,0:T(8,128)(2,1)S(1)}, u32[]{:S(2)}, u32[]{:S(2)}) collective-permute-start(bf16[8,128,128]{2,1,0:T(8,128)(2,1)S(1)} %get-tuple-element.263), channel_id=1, source_target_pairs={{32,0},{33,1},{48,16},{49,17},{64,32},{65,33},{80,48},{81,49},{96,... | collective-permute-start | bytes 786440 | tf_op jit(solution)/shard_map/ppermute | solution.py:67
  314.4 2.1 collective-permute-start.55
  319.6 3.6 shard_map.253
  323.4 5.4 %collective-permute-done.54.refs_5_ = bf16[8,128,128]{2,1,0:T(8,128)(2,1)S(1)} collective-permute-done((bf16[8,128,128]{2,1,0:T(8,128)(2,1)S(1)}, bf16[8,128,128]{2,1,0:T(8,128)(2,1)S(1)}, u32[]{:S(2)}, u32[]{:S(2)}) %collective-permute-start.54) | collective-permute-done | bytes 262176 | tf_op jit(solution)/shard_map/ppermute | solution.py:67
  328.8 2.4 collective-permute-done.55.refs_6_
  334.3 3.5 shard_map.255
  342.3 2.0 copy-done.2
  344.2 3.5 shard_map.256
  348.8 6.6 %all-to-all-start.3 = ((bf16[8,192,192]{2,1,0:T(8,128)(2,1)}), bf16[8,192,192]{2,1,0:T(8,128)(2,1)}, u32[]{:S(2)}, u32[]{:S(2)}) async-start(bf16[8,192,192]{2,1,0:T(8,128)(2,1)} %bitcast.41), calls=%async_computation.4 | async-start | bytes 1572864 | tf_op jit(solution)/shard_map/all_to_all | solution.py:71
  355.4 1.8 add_convert_fusion.1
  357.2 2.7 collective-permute-start.62
  361.9 1.8 add_convert_fusion.3
  364.6 2.8 all-to-all-done.3
  367.5 4.8 %all-to-all-start.2 = ((bf16[8,192,384]{2,1,0:T(8,128)(2,1)}), bf16[8,192,384]{2,1,0:T(8,128)(2,1)}, u32[]{:S(2)}, u32[]{:S(2)}) async-start(bf16[8,192,384]{2,1,0:T(8,128)(2,1)} %bitcast.39), calls=%async_computation.3 | async-start | bytes 2359296 | tf_op jit(solution)/shard_map/all_to_all | solution.py:71
  373.6 3.5 collective-permute-done.62
  377.1 4.5 %collective-permute-done.58 = bf16[128,1536]{1,0:T(8,128)(2,1)S(1)} collective-permute-done((bf16[128,1536]{1,0:T(8,128)(2,1)}, bf16[128,1536]{1,0:T(8,128)(2,1)S(1)}, u32[]{:S(2)}, u32[]{:S(2)}) %collective-permute-start.58) | collective-permute-done | bytes 393248 | tf_op jit(solution)/shard_map/ppermute | solution.py:53
  383.2 4.9 %all-to-all-done.2 = bf16[8,192,384]{2,1,0:T(8,128)(2,1)} async-done(((bf16[8,192,384]{2,1,0:T(8,128)(2,1)}), bf16[8,192,384]{2,1,0:T(8,128)(2,1)}, u32[]{:S(2)}, u32[]{:S(2)}) %all-to-all-start.2) | async-done | bytes 1179680 | tf_op jit(solution)/shard_map/all_to_all | solution.py:71
  389.7 2.1 concatenate.66
  391.8 4.3 all-to-all-start.4
  396.2 3.0 fusion.6
  399.1 9.7 %all-to-all-done.4 = bf16[8,24,1872]{2,1,0:T(8,128)(2,1)} async-done(((bf16[8,24,1872]{2,1,0:T(8,128)(2,1)}), bf16[8,24,1872]{2,1,0:T(8,128)(2,1)}, u32[]{:S(2)}, u32[]{:S(2)}) %all-to-all-start.4) | async-done | bytes 718880 | tf_op jit(solution)/shard_map/all_to_all | solution.py:71
  411.0 3.0 collective-permute-start.64
  (419 shorter events, 94.4 us)
Async XLA Ops:
  7.2 132.9 %all-gather.2.cloned.1.call-start = ((), (), s32[]{:S(2)}) async-start(), calls=%async_computation.6 | async-start | bytes 10027008 | tf_op jit(solution)/shard_map/all_gather | solution.py:699
  30.6 23.3 %collective-permute-start = (bf16[128,1536]{1,0:T(8,128)(2,1)S(1)}, bf16[128,1536]{1,0:T(8,128)(2,1)S(1)}, u32[]{:S(2)}, u32[]{:S(2)}) collective-permute-start(bf16[128,1536]{1,0:T(8,128)(2,1)S(1)} %copy-done.3), channel_id=1, source_target_pairs={{0,2},{2,0},{1,3},{3,1},{4,6},{6,4},{5,7},{7,5},{8,10},{10,8},{9,1... | collective-permute-start | bytes 1179656 | tf_op jit(solution)/shard_map/ppermute | solution.py:57
  30.7 14.2 %collective-permute-start.1 = (bf16[128,1536]{1,0:T(8,128)(2,1)S(1)}, bf16[128,1536]{1,0:T(8,128)(2,1)S(1)}, u32[]{:S(2)}, u32[]{:S(2)}) collective-permute-start(bf16[128,1536]{1,0:T(8,128)(2,1)S(1)} %copy-done.3), channel_id=1, source_target_pairs={{4,0},{8,4},{12,8},{0,12},{5,1},{9,5},{13,9},{1,13},{6,2},{10,6},{... | collective-permute-start | bytes 1179656 | tf_op jit(solution)/shard_map/ppermute | solution.py:53
  31.9 15.0 %collective-permute-start.3 = (bf16[128,1536]{1,0:T(8,128)(2,1)S(1)}, bf16[128,1536]{1,0:T(8,128)(2,1)S(1)}, u32[]{:S(2)}, u32[]{:S(2)}) collective-permute-start(bf16[128,1536]{1,0:T(8,128)(2,1)S(1)} %copy-done.3), channel_id=1, source_target_pairs={{8,0},{12,4},{0,8},{4,12},{9,1},{13,5},{1,9},{5,13},{10,2},{14,6},... | collective-permute-start | bytes 1179656 | tf_op jit(solution)/shard_map/ppermute | solution.py:53
  33.4 19.7 %collective-permute-start.5 = (bf16[128,1536]{1,0:T(8,128)(2,1)S(1)}, bf16[128,1536]{1,0:T(8,128)(2,1)}, u32[]{:S(2)}, u32[]{:S(2)}) collective-permute-start(bf16[128,1536]{1,0:T(8,128)(2,1)S(1)} %copy-done.3), channel_id=1, source_target_pairs={{12,0},{0,4},{4,8},{8,12},{13,1},{1,5},{5,9},{9,13},{14,2},{2,6},{... | collective-permute-start | bytes 1179656 | tf_op jit(solution)/shard_map/ppermute | solution.py:53
  36.1 32.5 %all-to-all-start.1 = ((bf16[16,96,384]{2,1,0:T(8,128)(2,1)}), bf16[16,96,384]{2,1,0:T(8,128)(2,1)S(1)}, u32[]{:S(2)}, u32[]{:S(2)}) async-start(bf16[16,96,384]{2,1,0:T(8,128)(2,1)} %broadcast_in_dim.27), calls=%async_computation.1 | async-start | bytes 2359296 | tf_op jit(solution)/shard_map/all_to_all | solution.py:71
  44.7 345.0 %reduce-scatter.2.cloned.1.call-start = ((), (), s32[]{:S(2)}) async-start(), calls=%async_computation.7 | async-start | bytes 9191424 | tf_op jit(solution)/shard_map/reduce_scatter | solution.py:805
  44.9 11.1 %collective-permute-start.2 = (bf16[128,1536]{1,0:T(8,128)(2,1)S(1)}, bf16[128,1536]{1,0:T(8,128)(2,1)S(1)}, u32[]{:S(2)}, u32[]{:S(2)}) collective-permute-start(bf16[128,1536]{1,0:T(8,128)(2,1)S(1)} %collective-permute-done.1.refs_2_.refs_10_), channel_id=1, source_target_pairs={{0,2},{2,0},{1,3},{3,1},{4,6},{6,4},{5,7},{7,5},{8,10},{10,8},{9,1... | collective-permute-start | bytes 1179656 | tf_op jit(solution)/shard_map/ppermute | solution.py:57
  46.9 26.9 %collective-permute-start.4 = (bf16[128,1536]{1,0:T(8,128)(2,1)S(1)}, bf16[128,1536]{1,0:T(8,128)(2,1)}, u32[]{:S(2)}, u32[]{:S(2)}) collective-permute-start(bf16[128,1536]{1,0:T(8,128)(2,1)S(1)} %collective-permute-done.3.refs_4_.refs_8_), channel_id=1, source_target_pairs={{0,2},{2,0},{1,3},{3,1},{4,6},{6,4},{5,7},{7,5},{8,10},{10,8},{9,1... | collective-permute-start | bytes 1179656 | tf_op jit(solution)/shard_map/ppermute | solution.py:57
  53.1 20.7 %collective-permute-start.6 = (bf16[128,1536]{1,0:T(8,128)(2,1)}, bf16[128,1536]{1,0:T(8,128)(2,1)}, u32[]{:S(2)}, u32[]{:S(2)}) collective-permute-start(bf16[128,1536]{1,0:T(8,128)(2,1)} %collective-permute-done.5.refs_6_.refs_10_), channel_id=1, source_target_pairs={{0,2},{2,0},{1,3},{3,1},{4,6},{6,4},{5,7},{7,5},{8,10},{10,8},{9,1... | collective-permute-start | bytes 1179656 | tf_op jit(solution)/shard_map/ppermute | solution.py:57
  53.2 31.1 %collective-permute-start.7 = (bf16[128,1536]{1,0:T(8,128)(2,1)}, bf16[128,1536]{1,0:T(8,128)(2,1)}, u32[]{:S(2)}, u32[]{:S(2)}) collective-permute-start(bf16[128,1536]{1,0:T(8,128)(2,1)} %refs_8_.1), channel_id=1, source_target_pairs={{4,0},{8,4},{12,8},{0,12},{5,1},{9,5},{13,9},{1,13},{6,2},{10,6},{... | collective-permute-start | bytes 1179656 | tf_op jit(solution)/shard_map/ppermute | solution.py:53
  53.9 30.3 %collective-permute-start.8 = (bf16[128,1536]{1,0:T(8,128)(2,1)}, bf16[128,1536]{1,0:T(8,128)(2,1)}, u32[]{:S(2)}, u32[]{:S(2)}) collective-permute-start(bf16[128,1536]{1,0:T(8,128)(2,1)} %refs_8_.1), channel_id=1, source_target_pairs={{8,0},{12,4},{0,8},{4,12},{9,1},{13,5},{1,9},{5,13},{10,2},{14,6},... | collective-permute-start | bytes 1179656 | tf_op jit(solution)/shard_map/ppermute | solution.py:53
  56.8 27.5 %collective-permute-start.9 = (bf16[128,1536]{1,0:T(8,128)(2,1)}, bf16[128,1536]{1,0:T(8,128)(2,1)}, u32[]{:S(2)}, u32[]{:S(2)}) collective-permute-start(bf16[128,1536]{1,0:T(8,128)(2,1)} %refs_8_.1), channel_id=1, source_target_pairs={{12,0},{0,4},{4,8},{8,12},{13,1},{1,5},{5,9},{9,13},{14,2},{2,6},{... | collective-permute-start | bytes 1179656 | tf_op jit(solution)/shard_map/ppermute | solution.py:53
  84.3 16.5 %collective-permute-start.10 = (bf16[8,128,128]{2,1,0:T(8,128)(2,1)}, bf16[8,128,128]{2,1,0:T(8,128)(2,1)S(1)}, u32[]{:S(2)}, u32[]{:S(2)}) collective-permute-start(bf16[8,128,128]{2,1,0:T(8,128)(2,1)} %get-tuple-element.159.refs_0_.refs_4_), channel_id=1, source_target_pairs={{0,1},{1,0},{2,3},{3,2},{4,5},{5,4},{6,7},{7,6},{8,9},{9,8},{10,11... | collective-permute-start | bytes 786440 | tf_op jit(solution)/shard_map/ppermute | solution.py:57
  86.3 31.0 %collective-permute-start.11 = (bf16[8,128,128]{2,1,0:T(8,128)(2,1)}, bf16[8,128,128]{2,1,0:T(8,128)(2,1)S(1)}, u32[]{:S(2)}, u32[]{:S(2)}) collective-permute-start(bf16[8,128,128]{2,1,0:T(8,128)(2,1)} %get-tuple-element.159.refs_0_.refs_4_), channel_id=1, source_target_pairs={{0,32},{1,33},{16,48},{17,49},{32,64},{33,65},{48,80},{49,81},{64,... | collective-permute-start | bytes 786440 | tf_op jit(solution)/shard_map/ppermute | solution.py:67
  88.4 30.3 %collective-permute-start.12 = (bf16[8,128,128]{2,1,0:T(8,128)(2,1)}, bf16[8,128,128]{2,1,0:T(8,128)(2,1)S(1)}, u32[]{:S(2)}, u32[]{:S(2)}) collective-permute-start(bf16[8,128,128]{2,1,0:T(8,128)(2,1)} %get-tuple-element.159.refs_0_.refs_4_), channel_id=1, source_target_pairs={{0,33},{1,32},{16,49},{17,48},{32,65},{33,64},{48,81},{49,80},{64,... | collective-permute-start | bytes 786440 | tf_op jit(solution)/shard_map/ppermute | solution.py:67
  91.9 33.3 %collective-permute-start.13 = (bf16[8,128,128]{2,1,0:T(8,128)(2,1)}, bf16[8,128,128]{2,1,0:T(8,128)(2,1)S(1)}, u32[]{:S(2)}, u32[]{:S(2)}) collective-permute-start(bf16[8,128,128]{2,1,0:T(8,128)(2,1)} %get-tuple-element.159.refs_0_.refs_4_), channel_id=1, source_target_pairs={{0,16},{1,17},{16,32},{17,33},{32,48},{33,49},{48,64},{49,65},{64,... | collective-permute-start | bytes 786440 | tf_op jit(solution)/shard_map/ppermute | solution.py:67
  94.0 31.2 %collective-permute-start.14 = (bf16[8,128,128]{2,1,0:T(8,128)(2,1)}, bf16[8,128,128]{2,1,0:T(8,128)(2,1)S(1)}, u32[]{:S(2)}, u32[]{:S(2)}) collective-permute-start(bf16[8,128,128]{2,1,0:T(8,128)(2,1)} %get-tuple-element.159.refs_0_.refs_4_), channel_id=1, source_target_pairs={{0,17},{1,16},{16,33},{17,32},{32,49},{33,48},{48,65},{49,64},{64,... | collective-permute-start | bytes 786440 | tf_op jit(solution)/shard_map/ppermute | solution.py:67
  125.2 17.1 %collective-permute-start.15 = (bf16[128,1536]{1,0:T(8,128)(2,1)}, bf16[128,1536]{1,0:T(8,128)(2,1)}, u32[]{:S(2)}, u32[]{:S(2)}) collective-permute-start(bf16[128,1536]{1,0:T(8,128)(2,1)} %refs_8_.1), channel_id=1, source_target_pairs={{0,2},{2,0},{1,3},{3,1},{4,6},{6,4},{5,7},{7,5},{8,10},{10,8},{9,1... | collective-permute-start | bytes 1179656 | tf_op jit(solution)/shard_map/ppermute | solution.py:57
  125.2 17.1 %collective-permute-start.16 = (bf16[128,1536]{1,0:T(8,128)(2,1)}, bf16[128,1536]{1,0:T(8,128)(2,1)}, u32[]{:S(2)}, u32[]{:S(2)}) collective-permute-start(bf16[128,1536]{1,0:T(8,128)(2,1)} %collective-permute-done.7.c0_ref.refs_10_), channel_id=1, source_target_pairs={{0,2},{2,0},{1,3},{3,1},{4,6},{6,4},{5,7},{7,5},{8,10},{10,8},{9,1... | collective-permute-start | bytes 1179656 | tf_op jit(solution)/shard_map/ppermute | solution.py:57
  125.7 16.6 %collective-permute-start.17 = (bf16[128,1536]{1,0:T(8,128)(2,1)}, bf16[128,1536]{1,0:T(8,128)(2,1)}, u32[]{:S(2)}, u32[]{:S(2)}) collective-permute-start(bf16[128,1536]{1,0:T(8,128)(2,1)} %collective-permute-done.8.c0_ref.refs_12_), channel_id=1, source_target_pairs={{0,2},{2,0},{1,3},{3,1},{4,6},{6,4},{5,7},{7,5},{8,10},{10,8},{9,1... | collective-permute-start | bytes 1179656 | tf_op jit(solution)/shard_map/ppermute | solution.py:57
  125.7 16.6 %collective-permute-start.18 = (bf16[128,1536]{1,0:T(8,128)(2,1)}, bf16[128,1536]{1,0:T(8,128)(2,1)}, u32[]{:S(2)}, u32[]{:S(2)}) collective-permute-start(bf16[128,1536]{1,0:T(8,128)(2,1)} %collective-permute-done.9.c1_ref.refs_11_), channel_id=1, source_target_pairs={{0,2},{2,0},{1,3},{3,1},{4,6},{6,4},{5,7},{7,5},{8,10},{10,8},{9,1... | collective-permute-start | bytes 1179656 | tf_op jit(solution)/shard_map/ppermute | solution.py:57
  144.2 5.0 %collective-permute-start.20 = (bf16[128,1536]{1,0:T(8,128)(2,1)S(1)}, bf16[128,1536]{1,0:T(8,128)(2,1)S(1)}, u32[]{:S(2)}, u32[]{:S(2)}) collective-permute-start(bf16[128,1536]{1,0:T(8,128)(2,1)S(1)} %get-tuple-element.182), channel_id=1, source_target_pairs={{0,2},{2,0},{1,3},{3,1},{4,6},{6,4},{5,7},{7,5},{8,10},{10,8},{9,1... | collective-permute-start | bytes 1179656 | tf_op jit(solution)/shard_map/ppermute | solution.py:57
  144.7 5.5 %collective-permute-start.19 = (bf16[128,1536]{1,0:T(8,128)(2,1)S(1)}, bf16[128,1536]{1,0:T(8,128)(2,1)S(1)}, u32[]{:S(2)}, u32[]{:S(2)}) collective-permute-start(bf16[128,1536]{1,0:T(8,128)(2,1)S(1)} %get-tuple-element.180), channel_id=1, source_target_pairs={{0,2},{2,0},{1,3},{3,1},{4,6},{6,4},{5,7},{7,5},{8,10},{10,8},{9,1... | collective-permute-start | bytes 1179656 | tf_op jit(solution)/shard_map/ppermute | solution.py:57
  145.4 19.9 %collective-permute-start.25 = (bf16[128,1536]{1,0:T(8,128)(2,1)S(1)}, bf16[128,1536]{1,0:T(8,128)(2,1)S(1)}, u32[]{:S(2)}, u32[]{:S(2)}) collective-permute-start(bf16[128,1536]{1,0:T(8,128)(2,1)S(1)} %add_convert_fusion.10), channel_id=1, source_target_pairs={{4,0},{8,4},{12,8},{0,12},{5,1},{9,5},{13,9},{1,13},{6,2},{10,6},{... | collective-permute-start | bytes 1179656 | tf_op jit(solution)/shard_map/ppermute | solution.py:53
  148.3 16.9 %collective-permute-start.23 = (bf16[128,1536]{1,0:T(8,128)(2,1)S(1)}, bf16[128,1536]{1,0:T(8,128)(2,1)S(1)}, u32[]{:S(2)}, u32[]{:S(2)}) collective-permute-start(bf16[128,1536]{1,0:T(8,128)(2,1)S(1)} %add_convert_fusion.11), channel_id=1, source_target_pairs={{8,0},{12,4},{0,8},{4,12},{9,1},{13,5},{1,9},{5,13},{10,2},{14,6},... | collective-permute-start | bytes 1179656 | tf_op jit(solution)/shard_map/ppermute | solution.py:53
  149.3 19.8 %collective-permute-start.21 = (bf16[128,1536]{1,0:T(8,128)(2,1)S(1)}, bf16[128,1536]{1,0:T(8,128)(2,1)S(1)}, u32[]{:S(2)}, u32[]{:S(2)}) collective-permute-start(bf16[128,1536]{1,0:T(8,128)(2,1)S(1)} %add_convert_fusion.12), channel_id=1, source_target_pairs={{12,0},{0,4},{4,8},{8,12},{13,1},{1,5},{5,9},{9,13},{14,2},{2,6},{... | collective-permute-start | bytes 1179656 | tf_op jit(solution)/shard_map/ppermute | solution.py:53
  170.0 11.5 %collective-permute-start.28 = (bf16[128,1536]{1,0:T(8,128)(2,1)S(1)}, bf16[128,1536]{1,0:T(8,128)(2,1)S(1)}, u32[]{:S(2)}, u32[]{:S(2)}) collective-permute-start(bf16[128,1536]{1,0:T(8,128)(2,1)S(1)} %multiply_convert_fusion.x0_ref.refs_0_), channel_id=1, source_target_pairs={{4,0},{8,4},{12,8},{0,12},{5,1},{9,5},{13,9},{1,13},{6,2},{10,6},{... | collective-permute-start | bytes 1179656 | tf_op jit(solution)/shard_map/ppermute | solution.py:53
  170.7 12.5 %collective-permute-start.29 = (bf16[128,1536]{1,0:T(8,128)(2,1)S(1)}, bf16[128,1536]{1,0:T(8,128)(2,1)S(1)}, u32[]{:S(2)}, u32[]{:S(2)}) collective-permute-start(bf16[128,1536]{1,0:T(8,128)(2,1)S(1)} %multiply_convert_fusion.x0_ref.refs_0_), channel_id=1, source_target_pairs={{12,0},{0,4},{4,8},{8,12},{13,1},{1,5},{5,9},{9,13},{14,2},{2,6},{... | collective-permute-start | bytes 1179656 | tf_op jit(solution)/shard_map/ppermute | solution.py:53
  179.4 20.9 %collective-permute-start.27 = (bf16[128,1536]{1,0:T(8,128)(2,1)S(1)}, bf16[128,1536]{1,0:T(8,128)(2,1)S(1)}, u32[]{:S(2)}, u32[]{:S(2)}) collective-permute-start(bf16[128,1536]{1,0:T(8,128)(2,1)S(1)} %get-tuple-element.190), channel_id=1, source_target_pairs={{0,2},{2,0},{1,3},{3,1},{4,6},{6,4},{5,7},{7,5},{8,10},{10,8},{9,1... | collective-permute-start | bytes 1179656 | tf_op jit(solution)/shard_map/ppermute | solution.py:57
  179.4 13.0 %collective-permute-start.30 = (bf16[128,1536]{1,0:T(8,128)(2,1)S(1)}, bf16[128,1536]{1,0:T(8,128)(2,1)S(1)}, u32[]{:S(2)}, u32[]{:S(2)}) collective-permute-start(bf16[128,1536]{1,0:T(8,128)(2,1)S(1)} %multiply_convert_fusion.x0_ref.refs_0_), channel_id=1, source_target_pairs={{8,0},{12,4},{0,8},{4,12},{9,1},{13,5},{1,9},{5,13},{10,2},{14,6},... | collective-permute-start | bytes 1179656 | tf_op jit(solution)/shard_map/ppermute | solution.py:53
  183.3 9.2 %collective-permute-start.31 = (bf16[128,1536]{1,0:T(8,128)(2,1)S(1)}, bf16[128,1536]{1,0:T(8,128)(2,1)S(1)}, u32[]{:S(2)}, u32[]{:S(2)}) collective-permute-start(bf16[128,1536]{1,0:T(8,128)(2,1)S(1)} %collective-permute-done.28.x0_ref.refs_2_), channel_id=1, source_target_pairs={{0,2},{2,0},{1,3},{3,1},{4,6},{6,4},{5,7},{7,5},{8,10},{10,8},{9,1... | collective-permute-start | bytes 1179656 | tf_op jit(solution)/shard_map/ppermute | solution.py:57
  183.3 17.9 %collective-permute-start.33 = (bf16[128,1536]{1,0:T(8,128)(2,1)S(1)}, bf16[128,1536]{1,0:T(8,128)(2,1)S(1)}, u32[]{:S(2)}, u32[]{:S(2)}) collective-permute-start(bf16[128,1536]{1,0:T(8,128)(2,1)S(1)} %collective-permute-done.29.x1_ref.refs_3_), channel_id=1, source_target_pairs={{0,2},{2,0},{1,3},{3,1},{4,6},{6,4},{5,7},{7,5},{8,10},{10,8},{9,1... | collective-permute-start | bytes 1179656 | tf_op jit(solution)/shard_map/ppermute | solution.py:57
  199.6 9.3 %collective-permute-start.32 = (bf16[128,1536]{1,0:T(8,128)(2,1)S(1)}, bf16[128,1536]{1,0:T(8,128)(2,1)S(1)}, u32[]{:S(2)}, u32[]{:S(2)}) collective-permute-start(bf16[128,1536]{1,0:T(8,128)(2,1)S(1)} %get-tuple-element.201), channel_id=1, source_target_pairs={{0,2},{2,0},{1,3},{3,1},{4,6},{6,4},{5,7},{7,5},{8,10},{10,8},{9,1... | collective-permute-start | bytes 1179656 | tf_op jit(solution)/shard_map/ppermute | solution.py:57
  211.0 23.0 %collective-permute-start.40 = (bf16[4,128,1536]{2,1,0:T(8,128)(2,1)S(1)}, bf16[4,128,1536]{2,1,0:T(8,128)(2,1)S(1)}, u32[]{:S(2)}, u32[]{:S(2)}) collective-permute-start(bf16[4,128,1536]{2,1,0:T(8,128)(2,1)S(1)} %pad_maximum_fusion), channel_id=1, source_target_pairs={{0,2},{2,0},{1,3},{3,1},{4,6},{6,4},{5,7},{7,5},{8,10},{10,8},{9,1... | collective-permute-start | bytes 4718600 | tf_op jit(solution)/shard_map/ppermute | solution.py:57
  211.2 21.5 %collective-permute-start.39 = (bf16[128,1536]{1,0:T(8,128)(2,1)S(1)}, bf16[128,1536]{1,0:T(8,128)(2,1)S(1)}, u32[]{:S(2)}, u32[]{:S(2)}) collective-permute-start(bf16[128,1536]{1,0:T(8,128)(2,1)S(1)} %add_convert_fusion.6), channel_id=1, source_target_pairs={{4,0},{8,4},{12,8},{0,12},{5,1},{9,5},{13,9},{1,13},{6,2},{10,6},{... | collective-permute-start | bytes 1179656 | tf_op jit(solution)/shard_map/ppermute | solution.py:53
  213.0 19.7 %collective-permute-start.38 = (bf16[128,1536]{1,0:T(8,128)(2,1)S(1)}, bf16[128,1536]{1,0:T(8,128)(2,1)S(1)}, u32[]{:S(2)}, u32[]{:S(2)}) collective-permute-start(bf16[128,1536]{1,0:T(8,128)(2,1)S(1)} %add_convert_fusion.7), channel_id=1, source_target_pairs={{8,0},{12,4},{0,8},{4,12},{9,1},{13,5},{1,9},{5,13},{10,2},{14,6},... | collective-permute-start | bytes 1179656 | tf_op jit(solution)/shard_map/ppermute | solution.py:53
  213.3 20.5 %collective-permute-start.37 = (bf16[128,1536]{1,0:T(8,128)(2,1)S(1)}, bf16[128,1536]{1,0:T(8,128)(2,1)S(1)}, u32[]{:S(2)}, u32[]{:S(2)}) collective-permute-start(bf16[128,1536]{1,0:T(8,128)(2,1)S(1)} %add_convert_fusion.8), channel_id=1, source_target_pairs={{12,0},{0,4},{4,8},{8,12},{13,1},{1,5},{5,9},{9,13},{14,2},{2,6},{... | collective-permute-start | bytes 1179656 | tf_op jit(solution)/shard_map/ppermute | solution.py:53
  237.6 23.1 %collective-permute-start.41 = (bf16[128,1536]{1,0:T(8,128)(2,1)}, bf16[128,1536]{1,0:T(8,128)(2,1)S(1)}, u32[]{:S(2)}, u32[]{:S(2)}) collective-permute-start(bf16[128,1536]{1,0:T(8,128)(2,1)} %fusion.45.refs_0_), channel_id=1, source_target_pairs={{0,2},{2,0},{1,3},{3,1},{4,6},{6,4},{5,7},{7,5},{8,10},{10,8},{9,1... | collective-permute-start | bytes 1179656 | tf_op jit(solution)/shard_map/ppermute | solution.py:57
  237.6 12.1 %collective-permute-start.42 = (bf16[128,1536]{1,0:T(8,128)(2,1)}, bf16[128,1536]{1,0:T(8,128)(2,1)S(1)}, u32[]{:S(2)}, u32[]{:S(2)}) collective-permute-start(bf16[128,1536]{1,0:T(8,128)(2,1)} %fusion.45.refs_0_), channel_id=1, source_target_pairs={{4,0},{8,4},{12,8},{0,12},{5,1},{9,5},{13,9},{1,13},{6,2},{10,6},{... | collective-permute-start | bytes 1179656 | tf_op jit(solution)/shard_map/ppermute | solution.py:53
  239.3 13.7 %collective-permute-start.44 = (bf16[128,1536]{1,0:T(8,128)(2,1)}, bf16[128,1536]{1,0:T(8,128)(2,1)S(1)}, u32[]{:S(2)}, u32[]{:S(2)}) collective-permute-start(bf16[128,1536]{1,0:T(8,128)(2,1)} %fusion.45.refs_0_), channel_id=1, source_target_pairs={{8,0},{12,4},{0,8},{4,12},{9,1},{13,5},{1,9},{5,13},{10,2},{14,6},... | collective-permute-start | bytes 1179656 | tf_op jit(solution)/shard_map/ppermute | solution.py:53
  241.3 19.4 %collective-permute-start.46 = (bf16[128,1536]{1,0:T(8,128)(2,1)}, bf16[128,1536]{1,0:T(8,128)(2,1)S(1)}, u32[]{:S(2)}, u32[]{:S(2)}) collective-permute-start(bf16[128,1536]{1,0:T(8,128)(2,1)} %fusion.45.refs_0_), channel_id=1, source_target_pairs={{12,0},{0,4},{4,8},{8,12},{13,1},{1,5},{5,9},{9,13},{14,2},{2,6},{... | collective-permute-start | bytes 1179656 | tf_op jit(solution)/shard_map/ppermute | solution.py:53
  249.7 11.0 %collective-permute-start.43 = (bf16[128,1536]{1,0:T(8,128)(2,1)S(1)}, bf16[128,1536]{1,0:T(8,128)(2,1)S(1)}, u32[]{:S(2)}, u32[]{:S(2)}) collective-permute-start(bf16[128,1536]{1,0:T(8,128)(2,1)S(1)} %collective-permute-done.42.refs_2_), channel_id=1, source_target_pairs={{0,2},{2,0},{1,3},{3,1},{4,6},{6,4},{5,7},{7,5},{8,10},{10,8},{9,1... | collective-permute-start | bytes 1179656 | tf_op jit(solution)/shard_map/ppermute | solution.py:57
  253.0 7.8 %collective-permute-start.45 = (bf16[128,1536]{1,0:T(8,128)(2,1)S(1)}, bf16[128,1536]{1,0:T(8,128)(2,1)S(1)}, u32[]{:S(2)}, u32[]{:S(2)}) collective-permute-start(bf16[128,1536]{1,0:T(8,128)(2,1)S(1)} %collective-permute-done.44.refs_4_), channel_id=1, source_target_pairs={{0,2},{2,0},{1,3},{3,1},{4,6},{6,4},{5,7},{7,5},{8,10},{10,8},{9,1... | collective-permute-start | bytes 1179656 | tf_op jit(solution)/shard_map/ppermute | solution.py:57
  262.4 38.0 %collective-permute-start.50 = (bf16[128,1536]{1,0:T(8,128)(2,1)S(1)}, bf16[128,1536]{1,0:T(8,128)(2,1)S(1)}, u32[]{:S(2)}, u32[]{:S(2)}) collective-permute-start(bf16[128,1536]{1,0:T(8,128)(2,1)S(1)} %get-tuple-element.254), channel_id=1, source_target_pairs={{4,0},{8,4},{12,8},{0,12},{5,1},{9,5},{13,9},{1,13},{6,2},{10,6},{... | collective-permute-start | bytes 1179656 | tf_op jit(solution)/shard_map/ppermute | solution.py:53
  263.6 36.8 %collective-permute-start.49 = (bf16[128,1536]{1,0:T(8,128)(2,1)S(1)}, bf16[128,1536]{1,0:T(8,128)(2,1)S(1)}, u32[]{:S(2)}, u32[]{:S(2)}) collective-permute-start(bf16[128,1536]{1,0:T(8,128)(2,1)S(1)} %get-tuple-element.253), channel_id=1, source_target_pairs={{8,0},{12,4},{0,8},{4,12},{9,1},{13,5},{1,9},{5,13},{10,2},{14,6},... | collective-permute-start | bytes 1179656 | tf_op jit(solution)/shard_map/ppermute | solution.py:53
  265.1 35.3 %collective-permute-start.48 = (bf16[128,1536]{1,0:T(8,128)(2,1)S(1)}, bf16[128,1536]{1,0:T(8,128)(2,1)S(1)}, u32[]{:S(2)}, u32[]{:S(2)}) collective-permute-start(bf16[128,1536]{1,0:T(8,128)(2,1)S(1)} %get-tuple-element.252), channel_id=1, source_target_pairs={{12,0},{0,4},{4,8},{8,12},{13,1},{1,5},{5,9},{9,13},{14,2},{2,6},{... | collective-permute-start | bytes 1179656 | tf_op jit(solution)/shard_map/ppermute | solution.py:53
  301.5 21.8 %collective-permute-start.51 = (bf16[8,128,128]{2,1,0:T(8,128)(2,1)S(1)}, bf16[8,128,128]{2,1,0:T(8,128)(2,1)S(1)}, u32[]{:S(2)}, u32[]{:S(2)}) collective-permute-start(bf16[8,128,128]{2,1,0:T(8,128)(2,1)S(1)} %get-tuple-element.260), channel_id=1, source_target_pairs={{0,1},{1,0},{2,3},{3,2},{4,5},{5,4},{6,7},{7,6},{8,9},{9,8},{10,11... | collective-permute-start | bytes 786440 | tf_op jit(solution)/shard_map/ppermute | solution.py:57
  304.6 18.8 %collective-permute-start.52 = (bf16[8,128,128]{2,1,0:T(8,128)(2,1)S(1)}, bf16[8,128,128]{2,1,0:T(8,128)(2,1)S(1)}, u32[]{:S(2)}, u32[]{:S(2)}) collective-permute-start(bf16[8,128,128]{2,1,0:T(8,128)(2,1)S(1)} %get-tuple-element.261), channel_id=1, source_target_pairs={{16,0},{17,1},{32,16},{33,17},{48,32},{49,33},{64,48},{65,49},{80,... | collective-permute-start | bytes 786440 | tf_op jit(solution)/shard_map/ppermute | solution.py:67
  306.5 16.9 %collective-permute-start.53 = (bf16[8,128,128]{2,1,0:T(8,128)(2,1)S(1)}, bf16[8,128,128]{2,1,0:T(8,128)(2,1)S(1)}, u32[]{:S(2)}, u32[]{:S(2)}) collective-permute-start(bf16[8,128,128]{2,1,0:T(8,128)(2,1)S(1)} %get-tuple-element.262), channel_id=1, source_target_pairs={{16,1},{17,0},{32,17},{33,16},{48,33},{49,32},{64,49},{65,48},{80,... | collective-permute-start | bytes 786440 | tf_op jit(solution)/shard_map/ppermute | solution.py:67
  308.4 20.4 %collective-permute-start.54 = (bf16[8,128,128]{2,1,0:T(8,128)(2,1)S(1)}, bf16[8,128,128]{2,1,0:T(8,128)(2,1)S(1)}, u32[]{:S(2)}, u32[]{:S(2)}) collective-permute-start(bf16[8,128,128]{2,1,0:T(8,128)(2,1)S(1)} %get-tuple-element.263), channel_id=1, source_target_pairs={{32,0},{33,1},{48,16},{49,17},{64,32},{65,33},{80,48},{81,49},{96,... | collective-permute-start | bytes 786440 | tf_op jit(solution)/shard_map/ppermute | solution.py:67
  314.4 16.8 %collective-permute-start.55 = (bf16[8,128,128]{2,1,0:T(8,128)(2,1)S(1)}, bf16[8,128,128]{2,1,0:T(8,128)(2,1)S(1)}, u32[]{:S(2)}, u32[]{:S(2)}) collective-permute-start(bf16[8,128,128]{2,1,0:T(8,128)(2,1)S(1)} %get-tuple-element.264), channel_id=1, source_target_pairs={{32,1},{33,0},{48,17},{49,16},{64,33},{65,32},{80,49},{81,48},{96,... | collective-permute-start | bytes 786440 | tf_op jit(solution)/shard_map/ppermute | solution.py:67
  347.8 7.6 %collective-permute-start.61 = (bf16[128,1536]{1,0:T(8,128)(2,1)}, bf16[128,1536]{1,0:T(8,128)(2,1)}, u32[]{:S(2)}, u32[]{:S(2)}) collective-permute-start(bf16[128,1536]{1,0:T(8,128)(2,1)} %get-tuple-element.295), channel_id=1, source_target_pairs={{0,2},{2,0},{1,3},{3,1},{4,6},{6,4},{5,7},{7,5},{8,10},{10,8},{9,1... | collective-permute-start | bytes 1179656 | tf_op jit(solution)/shard_map/ppermute | solution.py:57
  347.8 12.2 %collective-permute-start.59 = (bf16[128,1536]{1,0:T(8,128)(2,1)S(1)}, bf16[128,1536]{1,0:T(8,128)(2,1)}, u32[]{:S(2)}, u32[]{:S(2)}) collective-permute-start(bf16[128,1536]{1,0:T(8,128)(2,1)S(1)} %copy-done.44), channel_id=1, source_target_pairs={{0,2},{2,0},{1,3},{3,1},{4,6},{6,4},{5,7},{7,5},{8,10},{10,8},{9,1... | collective-permute-start | bytes 1179656 | tf_op jit(solution)/shard_map/ppermute | solution.py:57
  348.3 13.6 %collective-permute-start.57 = (bf16[128,1536]{1,0:T(8,128)(2,1)S(1)}, bf16[128,1536]{1,0:T(8,128)(2,1)}, u32[]{:S(2)}, u32[]{:S(2)}) collective-permute-start(bf16[128,1536]{1,0:T(8,128)(2,1)S(1)} %copy-done.42), channel_id=1, source_target_pairs={{0,2},{2,0},{1,3},{3,1},{4,6},{6,4},{5,7},{7,5},{8,10},{10,8},{9,1... | collective-permute-start | bytes 1179656 | tf_op jit(solution)/shard_map/ppermute | solution.py:57
  348.4 25.2 %collective-permute-start.56 = (bf16[128,1536]{1,0:T(8,128)(2,1)S(1)}, bf16[128,1536]{1,0:T(8,128)(2,1)}, u32[]{:S(2)}, u32[]{:S(2)}) collective-permute-start(bf16[128,1536]{1,0:T(8,128)(2,1)S(1)} %copy-done.40), channel_id=1, source_target_pairs={{0,2},{2,0},{1,3},{3,1},{4,6},{6,4},{5,7},{7,5},{8,10},{10,8},{9,1... | collective-permute-start | bytes 1179656 | tf_op jit(solution)/shard_map/ppermute | solution.py:57
  348.8 18.7 %all-to-all-start.3 = ((bf16[8,192,192]{2,1,0:T(8,128)(2,1)}), bf16[8,192,192]{2,1,0:T(8,128)(2,1)}, u32[]{:S(2)}, u32[]{:S(2)}) async-start(bf16[8,192,192]{2,1,0:T(8,128)(2,1)} %bitcast.41), calls=%async_computation.4 | async-start | bytes 1572864 | tf_op jit(solution)/shard_map/all_to_all | solution.py:71
  357.2 19.8 %collective-permute-start.62 = (bf16[128,1536]{1,0:T(8,128)(2,1)}, bf16[128,1536]{1,0:T(8,128)(2,1)S(1)}, u32[]{:S(2)}, u32[]{:S(2)}) collective-permute-start(bf16[128,1536]{1,0:T(8,128)(2,1)} %add_convert_fusion.1), channel_id=1, source_target_pairs={{4,0},{8,4},{12,8},{0,12},{5,1},{9,5},{13,9},{1,13},{6,2},{10,6},{... | collective-permute-start | bytes 1179656 | tf_op jit(solution)/shard_map/ppermute | solution.py:53
  361.1 16.0 %collective-permute-start.60 = (bf16[128,1536]{1,0:T(8,128)(2,1)S(1)}, bf16[128,1536]{1,0:T(8,128)(2,1)S(1)}, u32[]{:S(2)}, u32[]{:S(2)}) collective-permute-start(bf16[128,1536]{1,0:T(8,128)(2,1)S(1)} %add_convert_fusion.2), channel_id=1, source_target_pairs={{8,0},{12,4},{0,8},{4,12},{9,1},{13,5},{1,9},{5,13},{10,2},{14,6},... | collective-permute-start | bytes 1179656 | tf_op jit(solution)/shard_map/ppermute | solution.py:53
  363.8 17.9 %collective-permute-start.58 = (bf16[128,1536]{1,0:T(8,128)(2,1)}, bf16[128,1536]{1,0:T(8,128)(2,1)S(1)}, u32[]{:S(2)}, u32[]{:S(2)}) collective-permute-start(bf16[128,1536]{1,0:T(8,128)(2,1)} %add_convert_fusion.3), channel_id=1, source_target_pairs={{12,0},{0,4},{4,8},{8,12},{13,1},{1,5},{5,9},{9,13},{14,2},{2,6},{... | collective-permute-start | bytes 1179656 | tf_op jit(solution)/shard_map/ppermute | solution.py:53
  367.5 20.7 %all-to-all-start.2 = ((bf16[8,192,384]{2,1,0:T(8,128)(2,1)}), bf16[8,192,384]{2,1,0:T(8,128)(2,1)}, u32[]{:S(2)}, u32[]{:S(2)}) async-start(bf16[8,192,384]{2,1,0:T(8,128)(2,1)} %bitcast.39), calls=%async_computation.3 | async-start | bytes 2359296 | tf_op jit(solution)/shard_map/all_to_all | solution.py:71
  391.8 17.0 %all-to-all-start.4 = ((bf16[8,24,1872]{2,1,0:T(8,128)(2,1)}), bf16[8,24,1872]{2,1,0:T(8,128)(2,1)}, u32[]{:S(2)}, u32[]{:S(2)}) async-start(bf16[8,24,1872]{2,1,0:T(8,128)(2,1)} %concatenate.66), calls=%async_computation.5 | async-start | bytes 1474560 | tf_op jit(solution)/shard_map/all_to_all | solution.py:71
  410.1 9.6 %collective-permute-start.63 = (bf16[8,12,384]{2,1,0:T(8,128)(2,1)S(1)}, bf16[8,12,384]{2,1,0:T(8,128)(2,1)S(1)}, u32[]{:S(2)}, u32[]{:S(2)}) collective-permute-start(bf16[8,12,384]{2,1,0:T(8,128)(2,1)S(1)} %fusion.9), channel_id=1, source_target_pairs={{0,1},{1,0},{2,3},{3,2},{4,5},{5,4},{6,7},{7,6},{8,9},{9,8},{10,11... | collective-permute-start | bytes 221192 | tf_op jit(solution)/shard_map/ppermute | solution.py:57
  411.0 8.0 %collective-permute-start.64 = (bf16[4,24,192]{2,1,0:T(8,128)(2,1)S(1)}, bf16[4,24,192]{2,1,0:T(8,128)(2,1)S(1)}, u32[]{:S(2)}, u32[]{:S(2)}) collective-permute-start(bf16[4,24,192]{2,1,0:T(8,128)(2,1)S(1)} %dynamic-slice_convert_fusion), channel_id=1, source_target_pairs={{0,1},{1,0},{2,3},{3,2},{4,5},{5,4},{6,7},{7,6},{8,9},{9,8},{10,11... | collective-permute-start | bytes 110600 | tf_op jit(solution)/shard_map/ppermute | solution.py:57
  (96 other events, 758.8 us)
Sparse Core Ops, SparseCore 0:
  30.7 108.9 all-gather.1
  237.1 106.8 reduce-scatter.1

commit v9 on v8

--- a/solution.py
+++ b/solution.py
@@ -564,7 +564,7 @@
         dkv[rows_of(j), :] += dot(sides, both)
         return dqt + dot(kvt[HEAD:, rows_of(j)], grads)
 
-    dqt = key_loops(plan, 11, 0, (2, 1), start_ref[0], visit, jnp.zeros((HEAD, LANES), F32))
+    dqt = key_loops(plan, 11, 0, (4, 2, 1), start_ref[0], visit, jnp.zeros((HEAD, LANES), F32))
     for c in (0, 1):
         dq = from_lanes(dqt * HEAD**-0.5, c)
         dq_ref[c] = jnp.concatenate([dq, jnp.zeros((ROWS, HEAD), F32)], axis=1).astype(BF16)

time: 439 us -> 437 us (level)
  no operation moved by 1% of the time
where the time goes in v9:
time: 437 us; the launch traced here: 429 us
  Pallas kernels  113 us (26%)
  waiting for transfers between devices  110 us (25%)
  starting transfers between devices  90.2 us (21%)
  local copies, waits for them, and re-layouts  53.8 us (12%)
  other arithmetic  28.9 us (7%)
  blocking collectives  17 us (4%)
  between operations  16 us (4%)
    ppermute x24, waiting for transfers between devices, shift_x(): return lax.ppermute(v, 'x', [((i + distance) % 4, i) for i in range(4)])  52.4 us
    pallas_call x1, Pallas kernels, back(): return call(plan, q, start, *kvs, grad, out, lse)  32.3 us
    ppermute x24, starting transfers between devices, shift_x(): return lax.ppermute(v, 'x', [((i + distance) % 4, i) for i in range(4)])  28.2 us
    all_to_all x4, waiting for transfers between devices, exchange(): return lax.all_to_all(v, axes, split_axis=0, concat_axis=0, tiled=True)  27.4 us
    unnamed x179, local copies, waits for them, and re-layouts  26.6 us
    pallas_call x4, Pallas kernels, ffn(): pl.pallas_call(ffn_kernel, out_shape=(jax.ShapeDtypeStruct((ROWS, WIDTH),...  25.6 us
    all_to_all x4, starting transfers between devices, exchange(): return lax.all_to_all(v, axes, split_axis=0, concat_axis=0, tiled=True)  23.7 us
    ppermute x8, waiting for transfers between devices, shift_super(): return lax.ppermute(v, ('ylo', 'z', 'yhi'), pairs)  22.6 us
  transfers between devices with their start and end apart: 71, of which 26 were waited for; matrix products, arithmetic and copies ran while one was open for 9% of the time, Pallas kernels for 26%

profile of v9, /device:TPU:8, one launch (start us, length us, event | category | flops | bytes accessed | tf_op | source)
XLA Modules:
  0.0 429.2 jit_solution(18028851138353741635)
XLA Ops:
  12.7 17.0 %all_to_all.25 = bf16[8,24,1920]{2,1,0:T(8,128)(2,1)S(1)} all-to-all(bf16[8,24,1920]{2,1,0:T(8,128)(2,1)S(1)} %concatenate.54), channel_id=1, replica_groups=mesh['ylo'=2,'z'=4,'x'=4,'core'=2,'yhi'=2] {'x','core'}, dimensions={0} | all-to-all | bytes 1474560 | tf_op jit(solution)/shard_map/all_to_all | solution.py:71
  36.1 8.5 %all-to-all-start.1 = ((bf16[16,96,384]{2,1,0:T(8,128)(2,1)}), bf16[16,96,384]{2,1,0:T(8,128)(2,1)S(1)}, u32[]{:S(2)}, u32[]{:S(2)}) async-start(bf16[16,96,384]{2,1,0:T(8,128)(2,1)} %broadcast_in_dim.27), calls=%async_computation.1 | async-start | bytes 2359296 | tf_op jit(solution)/shard_map/all_to_all | solution.py:71
  45.0 1.9 fusion.12
  47.5 5.6 %collective-permute-done.5.refs_6_.refs_10_ = bf16[128,1536]{1,0:T(8,128)(2,1)} collective-permute-done((bf16[128,1536]{1,0:T(8,128)(2,1)S(1)}, bf16[128,1536]{1,0:T(8,128)(2,1)}, u32[]{:S(2)}, u32[]{:S(2)}) %collective-permute-start.5) | collective-permute-done | bytes 393248 | tf_op jit(solution)/shard_map/ppermute | solution.py:53
  53.9 2.1 collective-permute-start.8
  58.0 10.6 %all-to-all-done.1 = bf16[16,96,384]{2,1,0:T(8,128)(2,1)S(1)} async-done(((bf16[16,96,384]{2,1,0:T(8,128)(2,1)}), bf16[16,96,384]{2,1,0:T(8,128)(2,1)S(1)}, u32[]{:S(2)}, u32[]{:S(2)}) %all-to-all-start.1) | async-done | bytes 1179680 | tf_op jit(solution)/shard_map/all_to_all | solution.py:71
  70.5 2.3 reshape.569.refs_8_.refs_12_
  75.9 4.9 %shard_map.237 = (bf16[1024,1536]{1,0:T(8,128)(2,1)S(1)}, bf16[8,128,192]{2,1,0:T(8,128)(2,1)S(1)}, bf16[8,128,128]{2,1,0:T(8,128)(2,1)}, f32[4,256,256]{2,1,0:T(8,128)S(1)}) custom-call(bf16[128,1536]{1,0:T(8,128)(2,1)S(1)} %copy-done.3, bf16[128,1536]{1,0:T(8,128)(2,1)S(1)} %collective-permute-done.refs_1_.refs_9_, bf16[128,1536]{1,0:T(8,128)(2,1)S(1)} %copy-done.15, ...), custom_call_target="tpu_custom_call" | custom-call | flops 1207959552 | bytes 10000000 | tf_op jit(solution)/shard_map/pallas_call | solution.py:168
  80.8 1.7 copy-done
  84.3 1.8 collective-permute-start.10
  86.3 2.1 collective-permute-start.11
  88.4 3.5 collective-permute-start.12
  91.9 2.1 collective-permute-start.13
  94.0 2.5 collective-permute-start.14
  96.5 4.3 %collective-permute-done.10.refs_1_.refs_5_ = bf16[8,128,128]{2,1,0:T(8,128)(2,1)S(1)} collective-permute-done((bf16[8,128,128]{2,1,0:T(8,128)(2,1)}, bf16[8,128,128]{2,1,0:T(8,128)(2,1)S(1)}, u32[]{:S(2)}, u32[]{:S(2)}) %collective-permute-start.10) | collective-permute-done | bytes 262176 | tf_op jit(solution)/shard_map/ppermute | solution.py:57
  102.0 8.5 %shard_map.238 = (f32[4,64,768]{2,1,0:T(8,128)S(1)}, f32[4,1,768]{2,1,0:T(1,128)S(1)}) custom-call(s32[8,17]{1,0:T(8,128)S(1)} %stack.22.plan, bf16[8,128,192]{2,1,0:T(8,128)(2,1)S(1)} %copy-done.36, s32[4,1,768]{2,1,0:T(1,128)S(1)} %copy.103.start_ref, bf16[8,128,128]{2,1,0:T(8,128)(2,1)} %get-tuple-element.159.refs_0_.refs_4_, ...), custom_call_target="tpu_custom_call" | custom-call | flops 4000000000 | bytes 8000000 | tf_op jit(solution)/shard_map/pallas_call | solution.py:618
  110.6 6.7 %collective-permute-done.11.refs_0_ = bf16[8,128,128]{2,1,0:T(8,128)(2,1)S(1)} collective-permute-done((bf16[8,128,128]{2,1,0:T(8,128)(2,1)}, bf16[8,128,128]{2,1,0:T(8,128)(2,1)S(1)}, u32[]{:S(2)}, u32[]{:S(2)}) %collective-permute-start.11) | collective-permute-done | bytes 262176 | tf_op jit(solution)/shard_map/ppermute | solution.py:67
  118.7 6.5 %collective-permute-done.13.refs_2_ = bf16[8,128,128]{2,1,0:T(8,128)(2,1)S(1)} collective-permute-done((bf16[8,128,128]{2,1,0:T(8,128)(2,1)}, bf16[8,128,128]{2,1,0:T(8,128)(2,1)S(1)}, u32[]{:S(2)}, u32[]{:S(2)}) %collective-permute-start.13) | collective-permute-done | bytes 262176 | tf_op jit(solution)/shard_map/ppermute | solution.py:67
  126.6 9.2 %shard_map.239 = (bf16[8,128,192]{2,1,0:T(8,128)(2,1)S(1)}, f32[4,64,768]{2,1,0:T(8,128)S(1)}, f32[4,1,768]{2,1,0:T(1,128)S(1)}) custom-call(s32[8,17]{1,0:T(8,128)S(1)} %stack.22.plan, bf16[8,128,192]{2,1,0:T(8,128)(2,1)S(1)} %copy-done.37, s32[4,1,768]{2,1,0:T(1,128)S(1)} %copy.103.start_ref, bf16[8,128,128]{2,1,0:T(8,128)(2,1)S(1)} %collective-permute-done.11.refs_0_, ...), custom_call_target="tpu_custom_call" | custom-call | flops 8000000000 | bytes 8000000 | tf_op jit(solution)/shard_map/pallas_call | solution.py:625
  140.2 1.6 dynamic-slice_bitcast_fusion.2
  145.4 2.8 collective-permute-start.25
  150.3 15.0 %collective-permute-done.25 = bf16[128,1536]{1,0:T(8,128)(2,1)S(1)} collective-permute-done((bf16[128,1536]{1,0:T(8,128)(2,1)S(1)}, bf16[128,1536]{1,0:T(8,128)(2,1)S(1)}, u32[]{:S(2)}, u32[]{:S(2)}) %collective-permute-start.25) | collective-permute-done | bytes 393248 | tf_op jit(solution)/shard_map/ppermute | solution.py:53
  165.3 3.8 collective-permute-done.21
  172.3 6.4 %shard_map.244 = (bf16[128,1536]{1,0:T(8,128)(2,1)S(1)}, bf16[128,1536]{1,0:T(8,128)(2,1)S(1)}, bf16[128,1536]{1,0:T(8,128)(2,1)S(1)}, bf16[128,1536]{1,0:T(8,12...) custom-call(bf16[128,1536]{1,0:T(8,128)(2,1)S(1)} %multiply_convert_fusion.x0_ref.refs_0_, ...), custom_call_target="tpu_custom_call" | custom-call | flops 4831838208 | bytes 14000000 | tf_op jit(solution)/shard_map/pallas_call | solution.py:298
  181.6 1.7 collective-permute-done.29.x1_ref.refs_3_
  183.8 6.4 %shard_map.245 = (bf16[128,1536]{1,0:T(8,128)(2,1)S(1)}, bf16[128,1536]{1,0:T(8,128)(2,1)S(1)}, bf16[128,1536]{1,0:T(8,128)(2,1)S(1)}, bf16[128,1536]{1,0:T(8,12...) custom-call(bf16[128,1536]{1,0:T(8,128)(2,1)S(1)} %collective-permute-done.28.x0_ref.refs_2_, ...), custom_call_target="tpu_custom_call" | custom-call | flops 4831838208 | bytes 14000000 | tf_op jit(solution)/shard_map/pallas_call | solution.py:298
  192.5 6.4 %shard_map.246 = (bf16[128,1536]{1,0:T(8,128)(2,1)S(1)}, bf16[128,1536]{1,0:T(8,128)(2,1)S(1)}, bf16[128,1536]{1,0:T(8,128)(2,1)S(1)}, bf16[128,1536]{1,0:T(8,12...) custom-call(bf16[128,1536]{1,0:T(8,128)(2,1)S(1)} %collective-permute-done.30.x0_ref.refs_4_, ...), custom_call_target="tpu_custom_call" | custom-call | flops 4831838208 | bytes 14000000 | tf_op jit(solution)/shard_map/pallas_call | solution.py:298
  201.9 6.4 %shard_map.247 = (bf16[128,1536]{1,0:T(8,128)(2,1)S(1)}, bf16[128,1536]{1,0:T(8,128)(2,1)S(1)}, bf16[128,1536]{1,0:T(8,128)(2,1)S(1)}, bf16[128,1536]{1,0:T(8,12...) custom-call(bf16[128,1536]{1,0:T(8,128)(2,1)S(1)} %collective-permute-done.33.x0_ref.refs_6_, ...), custom_call_target="tpu_custom_call" | custom-call | flops 4831838208 | bytes 14000000 | tf_op jit(solution)/shard_map/pallas_call | solution.py:298
  211.4 1.8 collective-permute-start.39
  214.1 15.4 %shard_map.248 = bf16[2,1536,1296]{2,1,0:T(8,128)(2,1)S(1)} custom-call(bf16[128,1536]{1,0:T(8,128)(2,1)S(1)} %multiply_convert_fusion.x0_ref.refs_0_, bf16[128,1536]{1,0:T(8,128)(2,1)S(1)} %collective-permute-done.26.x1_ref.refs_1_, bf16[128,1536]{1,0:T(8,128)(2,1)S(1)} %collective-permute-done.28.x0_ref.refs_2_, ...), custom_call_target="tpu_custom_call" | custom-call | flops 9663676416 | bytes 24000000 | tf_op jit(solution)/shard_map/pallas_call | solution.py:327
  229.5 3.5 copy-done.8
  235.0 2.0 fusion.45.refs_0_
  237.6 1.8 collective-permute-start.42
  239.5 2.0 collective-permute-start.44
  243.0 2.2 add_convert_fusion
  245.2 12.1 %collective-permute-done.42.refs_2_ = bf16[128,1536]{1,0:T(8,128)(2,1)S(1)} collective-permute-done((bf16[128,1536]{1,0:T(8,128)(2,1)}, bf16[128,1536]{1,0:T(8,128)(2,1)S(1)}, u32[]{:S(2)}, u32[]{:S(2)}) %collective-permute-start.42) | collective-permute-done | bytes 393248 | tf_op jit(solution)/shard_map/ppermute | solution.py:53
  257.8 3.1 collective-permute-done.46.refs_6_
  267.1 32.3 %shard_map.250 = (bf16[8,128,256]{2,1,0:T(8,128)(2,1)S(1)}, bf16[8,128,128]{2,1,0:T(8,128)(2,1)S(1)}, bf16[8,128,128]{2,1,0:T(8,128)(2,1)S(1)}, bf16[8,128,128]{...) custom-call(s32[8,17]{1,0:T(8,128)S(1)} %copy-done.34, ...), custom_call_target="tpu_custom_call" | custom-call | flops 30000001024 | bytes 8000000 | tf_op jit(solution)/shard_map/pallas_call | solution.py:639
  300.5 3.0 collective-permute-start.51
  303.6 2.1 collective-permute-start.52
  305.7 1.9 collective-permute-start.53
  307.6 6.0 %collective-permute-start.54 = (bf16[8,128,128]{2,1,0:T(8,128)(2,1)S(1)}, bf16[8,128,128]{2,1,0:T(8,128)(2,1)S(1)}, u32[]{:S(2)}, u32[]{:S(2)}) collective-permute-start(bf16[8,128,128]{2,1,0:T(8,128)(2,1)S(1)} %get-tuple-element.263), channel_id=1, source_target_pairs={{32,0},{33,1},{48,16},{49,17},{64,32},{65,33},{80,48},{81,49},{96,... | collective-permute-start | bytes 786440 | tf_op jit(solution)/shard_map/ppermute | solution.py:67
  313.6 1.9 collective-permute-start.55
  318.7 3.6 shard_map.253
  323.4 3.9 collective-permute-done.54.refs_5_
  327.4 3.0 collective-permute-done.55.refs_6_
  333.5 3.5 shard_map.255
  341.4 2.0 copy-done.2
  343.4 3.5 shard_map.256
  348.0 5.7 %all-to-all-start.3 = ((bf16[8,192,192]{2,1,0:T(8,128)(2,1)}), bf16[8,192,192]{2,1,0:T(8,128)(2,1)}, u32[]{:S(2)}, u32[]{:S(2)}) async-start(bf16[8,192,192]{2,1,0:T(8,128)(2,1)} %bitcast.41), calls=%async_computation.4 | async-start | bytes 1572864 | tf_op jit(solution)/shard_map/all_to_all | solution.py:71
  353.7 1.8 add_convert_fusion.1
  355.5 2.8 collective-permute-start.62
  360.2 1.8 add_convert_fusion.3
  363.0 2.5 all-to-all-done.3
  365.4 4.8 %all-to-all-start.2 = ((bf16[8,192,384]{2,1,0:T(8,128)(2,1)}), bf16[8,192,384]{2,1,0:T(8,128)(2,1)}, u32[]{:S(2)}, u32[]{:S(2)}) async-start(bf16[8,192,384]{2,1,0:T(8,128)(2,1)} %bitcast.39), calls=%async_computation.3 | async-start | bytes 2359296 | tf_op jit(solution)/shard_map/all_to_all | solution.py:71
  371.6 3.6 collective-permute-done.62
  375.1 4.6 %collective-permute-done.58 = bf16[128,1536]{1,0:T(8,128)(2,1)S(1)} collective-permute-done((bf16[128,1536]{1,0:T(8,128)(2,1)}, bf16[128,1536]{1,0:T(8,128)(2,1)S(1)}, u32[]{:S(2)}, u32[]{:S(2)}) %collective-permute-start.58) | collective-permute-done | bytes 393248 | tf_op jit(solution)/shard_map/ppermute | solution.py:53
  379.7 1.6 fusion
  381.3 4.7 %all-to-all-done.2 = bf16[8,192,384]{2,1,0:T(8,128)(2,1)} async-done(((bf16[8,192,384]{2,1,0:T(8,128)(2,1)}), bf16[8,192,384]{2,1,0:T(8,128)(2,1)}, u32[]{:S(2)}, u32[]{:S(2)}) %all-to-all-start.2) | async-done | bytes 1179680 | tf_op jit(solution)/shard_map/all_to_all | solution.py:71
  387.6 2.1 concatenate.66
  389.8 4.7 %all-to-all-start.4 = ((bf16[8,24,1872]{2,1,0:T(8,128)(2,1)}), bf16[8,24,1872]{2,1,0:T(8,128)(2,1)}, u32[]{:S(2)}, u32[]{:S(2)}) async-start(bf16[8,24,1872]{2,1,0:T(8,128)(2,1)} %concatenate.66), calls=%async_computation.5 | async-start | bytes 1474560 | tf_op jit(solution)/shard_map/all_to_all | solution.py:71
  394.5 3.0 fusion.6
  397.5 9.6 %all-to-all-done.4 = bf16[8,24,1872]{2,1,0:T(8,128)(2,1)} async-done(((bf16[8,24,1872]{2,1,0:T(8,128)(2,1)}), bf16[8,24,1872]{2,1,0:T(8,128)(2,1)}, u32[]{:S(2)}, u32[]{:S(2)}) %all-to-all-start.4) | async-done | bytes 718880 | tf_op jit(solution)/shard_map/all_to_all | solution.py:71
  409.8 2.3 collective-permute-start.64
  (419 shorter events, 94.5 us)
Async XLA Ops:
  7.2 132.9 %all-gather.2.cloned.1.call-start = ((), (), s32[]{:S(2)}) async-start(), calls=%async_computation.6 | async-start | bytes 10027008 | tf_op jit(solution)/shard_map/all_gather | solution.py:699
  30.6 23.3 %collective-permute-start = (bf16[128,1536]{1,0:T(8,128)(2,1)S(1)}, bf16[128,1536]{1,0:T(8,128)(2,1)S(1)}, u32[]{:S(2)}, u32[]{:S(2)}) collective-permute-start(bf16[128,1536]{1,0:T(8,128)(2,1)S(1)} %copy-done.3), channel_id=1, source_target_pairs={{0,2},{2,0},{1,3},{3,1},{4,6},{6,4},{5,7},{7,5},{8,10},{10,8},{9,1... | collective-permute-start | bytes 1179656 | tf_op jit(solution)/shard_map/ppermute | solution.py:57
  30.7 14.2 %collective-permute-start.1 = (bf16[128,1536]{1,0:T(8,128)(2,1)S(1)}, bf16[128,1536]{1,0:T(8,128)(2,1)S(1)}, u32[]{:S(2)}, u32[]{:S(2)}) collective-permute-start(bf16[128,1536]{1,0:T(8,128)(2,1)S(1)} %copy-done.3), channel_id=1, source_target_pairs={{4,0},{8,4},{12,8},{0,12},{5,1},{9,5},{13,9},{1,13},{6,2},{10,6},{... | collective-permute-start | bytes 1179656 | tf_op jit(solution)/shard_map/ppermute | solution.py:53
  31.9 15.0 %collective-permute-start.3 = (bf16[128,1536]{1,0:T(8,128)(2,1)S(1)}, bf16[128,1536]{1,0:T(8,128)(2,1)S(1)}, u32[]{:S(2)}, u32[]{:S(2)}) collective-permute-start(bf16[128,1536]{1,0:T(8,128)(2,1)S(1)} %copy-done.3), channel_id=1, source_target_pairs={{8,0},{12,4},{0,8},{4,12},{9,1},{13,5},{1,9},{5,13},{10,2},{14,6},... | collective-permute-start | bytes 1179656 | tf_op jit(solution)/shard_map/ppermute | solution.py:53
  33.4 19.7 %collective-permute-start.5 = (bf16[128,1536]{1,0:T(8,128)(2,1)S(1)}, bf16[128,1536]{1,0:T(8,128)(2,1)}, u32[]{:S(2)}, u32[]{:S(2)}) collective-permute-start(bf16[128,1536]{1,0:T(8,128)(2,1)S(1)} %copy-done.3), channel_id=1, source_target_pairs={{12,0},{0,4},{4,8},{8,12},{13,1},{1,5},{5,9},{9,13},{14,2},{2,6},{... | collective-permute-start | bytes 1179656 | tf_op jit(solution)/shard_map/ppermute | solution.py:53
  36.1 32.5 %all-to-all-start.1 = ((bf16[16,96,384]{2,1,0:T(8,128)(2,1)}), bf16[16,96,384]{2,1,0:T(8,128)(2,1)S(1)}, u32[]{:S(2)}, u32[]{:S(2)}) async-start(bf16[16,96,384]{2,1,0:T(8,128)(2,1)} %broadcast_in_dim.27), calls=%async_computation.1 | async-start | bytes 2359296 | tf_op jit(solution)/shard_map/all_to_all | solution.py:71
  44.7 342.9 %reduce-scatter.2.cloned.1.call-start = ((), (), s32[]{:S(2)}) async-start(), calls=%async_computation.7 | async-start | bytes 9191424 | tf_op jit(solution)/shard_map/reduce_scatter | solution.py:805
  44.9 11.1 %collective-permute-start.2 = (bf16[128,1536]{1,0:T(8,128)(2,1)S(1)}, bf16[128,1536]{1,0:T(8,128)(2,1)S(1)}, u32[]{:S(2)}, u32[]{:S(2)}) collective-permute-start(bf16[128,1536]{1,0:T(8,128)(2,1)S(1)} %collective-permute-done.1.refs_2_.refs_10_), channel_id=1, source_target_pairs={{0,2},{2,0},{1,3},{3,1},{4,6},{6,4},{5,7},{7,5},{8,10},{10,8},{9,1... | collective-permute-start | bytes 1179656 | tf_op jit(solution)/shard_map/ppermute | solution.py:57
  46.9 26.9 %collective-permute-start.4 = (bf16[128,1536]{1,0:T(8,128)(2,1)S(1)}, bf16[128,1536]{1,0:T(8,128)(2,1)}, u32[]{:S(2)}, u32[]{:S(2)}) collective-permute-start(bf16[128,1536]{1,0:T(8,128)(2,1)S(1)} %collective-permute-done.3.refs_4_.refs_8_), channel_id=1, source_target_pairs={{0,2},{2,0},{1,3},{3,1},{4,6},{6,4},{5,7},{7,5},{8,10},{10,8},{9,1... | collective-permute-start | bytes 1179656 | tf_op jit(solution)/shard_map/ppermute | solution.py:57
  53.1 20.7 %collective-permute-start.6 = (bf16[128,1536]{1,0:T(8,128)(2,1)}, bf16[128,1536]{1,0:T(8,128)(2,1)}, u32[]{:S(2)}, u32[]{:S(2)}) collective-permute-start(bf16[128,1536]{1,0:T(8,128)(2,1)} %collective-permute-done.5.refs_6_.refs_10_), channel_id=1, source_target_pairs={{0,2},{2,0},{1,3},{3,1},{4,6},{6,4},{5,7},{7,5},{8,10},{10,8},{9,1... | collective-permute-start | bytes 1179656 | tf_op jit(solution)/shard_map/ppermute | solution.py:57
  53.2 31.1 %collective-permute-start.7 = (bf16[128,1536]{1,0:T(8,128)(2,1)}, bf16[128,1536]{1,0:T(8,128)(2,1)}, u32[]{:S(2)}, u32[]{:S(2)}) collective-permute-start(bf16[128,1536]{1,0:T(8,128)(2,1)} %refs_8_.1), channel_id=1, source_target_pairs={{4,0},{8,4},{12,8},{0,12},{5,1},{9,5},{13,9},{1,13},{6,2},{10,6},{... | collective-permute-start | bytes 1179656 | tf_op jit(solution)/shard_map/ppermute | solution.py:53
  53.9 30.3 %collective-permute-start.8 = (bf16[128,1536]{1,0:T(8,128)(2,1)}, bf16[128,1536]{1,0:T(8,128)(2,1)}, u32[]{:S(2)}, u32[]{:S(2)}) collective-permute-start(bf16[128,1536]{1,0:T(8,128)(2,1)} %refs_8_.1), channel_id=1, source_target_pairs={{8,0},{12,4},{0,8},{4,12},{9,1},{13,5},{1,9},{5,13},{10,2},{14,6},... | collective-permute-start | bytes 1179656 | tf_op jit(solution)/shard_map/ppermute | solution.py:53
  56.8 27.5 %collective-permute-start.9 = (bf16[128,1536]{1,0:T(8,128)(2,1)}, bf16[128,1536]{1,0:T(8,128)(2,1)}, u32[]{:S(2)}, u32[]{:S(2)}) collective-permute-start(bf16[128,1536]{1,0:T(8,128)(2,1)} %refs_8_.1), channel_id=1, source_target_pairs={{12,0},{0,4},{4,8},{8,12},{13,1},{1,5},{5,9},{9,13},{14,2},{2,6},{... | collective-permute-start | bytes 1179656 | tf_op jit(solution)/shard_map/ppermute | solution.py:53
  84.3 16.5 %collective-permute-start.10 = (bf16[8,128,128]{2,1,0:T(8,128)(2,1)}, bf16[8,128,128]{2,1,0:T(8,128)(2,1)S(1)}, u32[]{:S(2)}, u32[]{:S(2)}) collective-permute-start(bf16[8,128,128]{2,1,0:T(8,128)(2,1)} %get-tuple-element.159.refs_0_.refs_4_), channel_id=1, source_target_pairs={{0,1},{1,0},{2,3},{3,2},{4,5},{5,4},{6,7},{7,6},{8,9},{9,8},{10,11... | collective-permute-start | bytes 786440 | tf_op jit(solution)/shard_map/ppermute | solution.py:57
  86.3 31.0 %collective-permute-start.11 = (bf16[8,128,128]{2,1,0:T(8,128)(2,1)}, bf16[8,128,128]{2,1,0:T(8,128)(2,1)S(1)}, u32[]{:S(2)}, u32[]{:S(2)}) collective-permute-start(bf16[8,128,128]{2,1,0:T(8,128)(2,1)} %get-tuple-element.159.refs_0_.refs_4_), channel_id=1, source_target_pairs={{0,32},{1,33},{16,48},{17,49},{32,64},{33,65},{48,80},{49,81},{64,... | collective-permute-start | bytes 786440 | tf_op jit(solution)/shard_map/ppermute | solution.py:67
  88.4 30.3 %collective-permute-start.12 = (bf16[8,128,128]{2,1,0:T(8,128)(2,1)}, bf16[8,128,128]{2,1,0:T(8,128)(2,1)S(1)}, u32[]{:S(2)}, u32[]{:S(2)}) collective-permute-start(bf16[8,128,128]{2,1,0:T(8,128)(2,1)} %get-tuple-element.159.refs_0_.refs_4_), channel_id=1, source_target_pairs={{0,33},{1,32},{16,49},{17,48},{32,65},{33,64},{48,81},{49,80},{64,... | collective-permute-start | bytes 786440 | tf_op jit(solution)/shard_map/ppermute | solution.py:67
  91.9 33.3 %collective-permute-start.13 = (bf16[8,128,128]{2,1,0:T(8,128)(2,1)}, bf16[8,128,128]{2,1,0:T(8,128)(2,1)S(1)}, u32[]{:S(2)}, u32[]{:S(2)}) collective-permute-start(bf16[8,128,128]{2,1,0:T(8,128)(2,1)} %get-tuple-element.159.refs_0_.refs_4_), channel_id=1, source_target_pairs={{0,16},{1,17},{16,32},{17,33},{32,48},{33,49},{48,64},{49,65},{64,... | collective-permute-start | bytes 786440 | tf_op jit(solution)/shard_map/ppermute | solution.py:67
  94.0 31.2 %collective-permute-start.14 = (bf16[8,128,128]{2,1,0:T(8,128)(2,1)}, bf16[8,128,128]{2,1,0:T(8,128)(2,1)S(1)}, u32[]{:S(2)}, u32[]{:S(2)}) collective-permute-start(bf16[8,128,128]{2,1,0:T(8,128)(2,1)} %get-tuple-element.159.refs_0_.refs_4_), channel_id=1, source_target_pairs={{0,17},{1,16},{16,33},{17,32},{32,49},{33,48},{48,65},{49,64},{64,... | collective-permute-start | bytes 786440 | tf_op jit(solution)/shard_map/ppermute | solution.py:67
  125.2 17.1 %collective-permute-start.15 = (bf16[128,1536]{1,0:T(8,128)(2,1)}, bf16[128,1536]{1,0:T(8,128)(2,1)}, u32[]{:S(2)}, u32[]{:S(2)}) collective-permute-start(bf16[128,1536]{1,0:T(8,128)(2,1)} %refs_8_.1), channel_id=1, source_target_pairs={{0,2},{2,0},{1,3},{3,1},{4,6},{6,4},{5,7},{7,5},{8,10},{10,8},{9,1... | collective-permute-start | bytes 1179656 | tf_op jit(solution)/shard_map/ppermute | solution.py:57
  125.2 17.1 %collective-permute-start.16 = (bf16[128,1536]{1,0:T(8,128)(2,1)}, bf16[128,1536]{1,0:T(8,128)(2,1)}, u32[]{:S(2)}, u32[]{:S(2)}) collective-permute-start(bf16[128,1536]{1,0:T(8,128)(2,1)} %collective-permute-done.7.c0_ref.refs_10_), channel_id=1, source_target_pairs={{0,2},{2,0},{1,3},{3,1},{4,6},{6,4},{5,7},{7,5},{8,10},{10,8},{9,1... | collective-permute-start | bytes 1179656 | tf_op jit(solution)/shard_map/ppermute | solution.py:57
  125.7 16.6 %collective-permute-start.17 = (bf16[128,1536]{1,0:T(8,128)(2,1)}, bf16[128,1536]{1,0:T(8,128)(2,1)}, u32[]{:S(2)}, u32[]{:S(2)}) collective-permute-start(bf16[128,1536]{1,0:T(8,128)(2,1)} %collective-permute-done.8.c0_ref.refs_12_), channel_id=1, source_target_pairs={{0,2},{2,0},{1,3},{3,1},{4,6},{6,4},{5,7},{7,5},{8,10},{10,8},{9,1... | collective-permute-start | bytes 1179656 | tf_op jit(solution)/shard_map/ppermute | solution.py:57
  125.7 16.6 %collective-permute-start.18 = (bf16[128,1536]{1,0:T(8,128)(2,1)}, bf16[128,1536]{1,0:T(8,128)(2,1)}, u32[]{:S(2)}, u32[]{:S(2)}) collective-permute-start(bf16[128,1536]{1,0:T(8,128)(2,1)} %collective-permute-done.9.c1_ref.refs_11_), channel_id=1, source_target_pairs={{0,2},{2,0},{1,3},{3,1},{4,6},{6,4},{5,7},{7,5},{8,10},{10,8},{9,1... | collective-permute-start | bytes 1179656 | tf_op jit(solution)/shard_map/ppermute | solution.py:57
  143.3 5.0 %collective-permute-start.22 = (bf16[128,1536]{1,0:T(8,128)(2,1)S(1)}, bf16[128,1536]{1,0:T(8,128)(2,1)S(1)}, u32[]{:S(2)}, u32[]{:S(2)}) collective-permute-start(bf16[128,1536]{1,0:T(8,128)(2,1)S(1)} %get-tuple-element.184), channel_id=1, source_target_pairs={{0,2},{2,0},{1,3},{3,1},{4,6},{6,4},{5,7},{7,5},{8,10},{10,8},{9,1... | collective-permute-start | bytes 1179656 | tf_op jit(solution)/shard_map/ppermute | solution.py:57
  144.2 5.0 %collective-permute-start.20 = (bf16[128,1536]{1,0:T(8,128)(2,1)S(1)}, bf16[128,1536]{1,0:T(8,128)(2,1)S(1)}, u32[]{:S(2)}, u32[]{:S(2)}) collective-permute-start(bf16[128,1536]{1,0:T(8,128)(2,1)S(1)} %get-tuple-element.182), channel_id=1, source_target_pairs={{0,2},{2,0},{1,3},{3,1},{4,6},{6,4},{5,7},{7,5},{8,10},{10,8},{9,1... | collective-permute-start | bytes 1179656 | tf_op jit(solution)/shard_map/ppermute | solution.py:57
  144.7 5.5 %collective-permute-start.19 = (bf16[128,1536]{1,0:T(8,128)(2,1)S(1)}, bf16[128,1536]{1,0:T(8,128)(2,1)S(1)}, u32[]{:S(2)}, u32[]{:S(2)}) collective-permute-start(bf16[128,1536]{1,0:T(8,128)(2,1)S(1)} %get-tuple-element.180), channel_id=1, source_target_pairs={{0,2},{2,0},{1,3},{3,1},{4,6},{6,4},{5,7},{7,5},{8,10},{10,8},{9,1... | collective-permute-start | bytes 1179656 | tf_op jit(solution)/shard_map/ppermute | solution.py:57
  145.4 19.9 %collective-permute-start.25 = (bf16[128,1536]{1,0:T(8,128)(2,1)S(1)}, bf16[128,1536]{1,0:T(8,128)(2,1)S(1)}, u32[]{:S(2)}, u32[]{:S(2)}) collective-permute-start(bf16[128,1536]{1,0:T(8,128)(2,1)S(1)} %add_convert_fusion.10), channel_id=1, source_target_pairs={{4,0},{8,4},{12,8},{0,12},{5,1},{9,5},{13,9},{1,13},{6,2},{10,6},{... | collective-permute-start | bytes 1179656 | tf_op jit(solution)/shard_map/ppermute | solution.py:53
  148.3 16.9 %collective-permute-start.23 = (bf16[128,1536]{1,0:T(8,128)(2,1)S(1)}, bf16[128,1536]{1,0:T(8,128)(2,1)S(1)}, u32[]{:S(2)}, u32[]{:S(2)}) collective-permute-start(bf16[128,1536]{1,0:T(8,128)(2,1)S(1)} %add_convert_fusion.11), channel_id=1, source_target_pairs={{8,0},{12,4},{0,8},{4,12},{9,1},{13,5},{1,9},{5,13},{10,2},{14,6},... | collective-permute-start | bytes 1179656 | tf_op jit(solution)/shard_map/ppermute | solution.py:53
  149.3 19.8 %collective-permute-start.21 = (bf16[128,1536]{1,0:T(8,128)(2,1)S(1)}, bf16[128,1536]{1,0:T(8,128)(2,1)S(1)}, u32[]{:S(2)}, u32[]{:S(2)}) collective-permute-start(bf16[128,1536]{1,0:T(8,128)(2,1)S(1)} %add_convert_fusion.12), channel_id=1, source_target_pairs={{12,0},{0,4},{4,8},{8,12},{13,1},{1,5},{5,9},{9,13},{14,2},{2,6},{... | collective-permute-start | bytes 1179656 | tf_op jit(solution)/shard_map/ppermute | solution.py:53
  170.0 11.5 %collective-permute-start.28 = (bf16[128,1536]{1,0:T(8,128)(2,1)S(1)}, bf16[128,1536]{1,0:T(8,128)(2,1)S(1)}, u32[]{:S(2)}, u32[]{:S(2)}) collective-permute-start(bf16[128,1536]{1,0:T(8,128)(2,1)S(1)} %multiply_convert_fusion.x0_ref.refs_0_), channel_id=1, source_target_pairs={{4,0},{8,4},{12,8},{0,12},{5,1},{9,5},{13,9},{1,13},{6,2},{10,6},{... | collective-permute-start | bytes 1179656 | tf_op jit(solution)/shard_map/ppermute | solution.py:53
  170.7 12.5 %collective-permute-start.29 = (bf16[128,1536]{1,0:T(8,128)(2,1)S(1)}, bf16[128,1536]{1,0:T(8,128)(2,1)S(1)}, u32[]{:S(2)}, u32[]{:S(2)}) collective-permute-start(bf16[128,1536]{1,0:T(8,128)(2,1)S(1)} %multiply_convert_fusion.x0_ref.refs_0_), channel_id=1, source_target_pairs={{12,0},{0,4},{4,8},{8,12},{13,1},{1,5},{5,9},{9,13},{14,2},{2,6},{... | collective-permute-start | bytes 1179656 | tf_op jit(solution)/shard_map/ppermute | solution.py:53
  179.4 21.1 %collective-permute-start.27 = (bf16[128,1536]{1,0:T(8,128)(2,1)S(1)}, bf16[128,1536]{1,0:T(8,128)(2,1)S(1)}, u32[]{:S(2)}, u32[]{:S(2)}) collective-permute-start(bf16[128,1536]{1,0:T(8,128)(2,1)S(1)} %get-tuple-element.190), channel_id=1, source_target_pairs={{0,2},{2,0},{1,3},{3,1},{4,6},{6,4},{5,7},{7,5},{8,10},{10,8},{9,1... | collective-permute-start | bytes 1179656 | tf_op jit(solution)/shard_map/ppermute | solution.py:57
  179.5 13.0 %collective-permute-start.30 = (bf16[128,1536]{1,0:T(8,128)(2,1)S(1)}, bf16[128,1536]{1,0:T(8,128)(2,1)S(1)}, u32[]{:S(2)}, u32[]{:S(2)}) collective-permute-start(bf16[128,1536]{1,0:T(8,128)(2,1)S(1)} %multiply_convert_fusion.x0_ref.refs_0_), channel_id=1, source_target_pairs={{8,0},{12,4},{0,8},{4,12},{9,1},{13,5},{1,9},{5,13},{10,2},{14,6},... | collective-permute-start | bytes 1179656 | tf_op jit(solution)/shard_map/ppermute | solution.py:53
  183.3 9.2 %collective-permute-start.31 = (bf16[128,1536]{1,0:T(8,128)(2,1)S(1)}, bf16[128,1536]{1,0:T(8,128)(2,1)S(1)}, u32[]{:S(2)}, u32[]{:S(2)}) collective-permute-start(bf16[128,1536]{1,0:T(8,128)(2,1)S(1)} %collective-permute-done.28.x0_ref.refs_2_), channel_id=1, source_target_pairs={{0,2},{2,0},{1,3},{3,1},{4,6},{6,4},{5,7},{7,5},{8,10},{10,8},{9,1... | collective-permute-start | bytes 1179656 | tf_op jit(solution)/shard_map/ppermute | solution.py:57
  183.3 18.1 %collective-permute-start.33 = (bf16[128,1536]{1,0:T(8,128)(2,1)S(1)}, bf16[128,1536]{1,0:T(8,128)(2,1)S(1)}, u32[]{:S(2)}, u32[]{:S(2)}) collective-permute-start(bf16[128,1536]{1,0:T(8,128)(2,1)S(1)} %collective-permute-done.29.x1_ref.refs_3_), channel_id=1, source_target_pairs={{0,2},{2,0},{1,3},{3,1},{4,6},{6,4},{5,7},{7,5},{8,10},{10,8},{9,1... | collective-permute-start | bytes 1179656 | tf_op jit(solution)/shard_map/ppermute | solution.py:57
  199.6 9.3 %collective-permute-start.32 = (bf16[128,1536]{1,0:T(8,128)(2,1)S(1)}, bf16[128,1536]{1,0:T(8,128)(2,1)S(1)}, u32[]{:S(2)}, u32[]{:S(2)}) collective-permute-start(bf16[128,1536]{1,0:T(8,128)(2,1)S(1)} %get-tuple-element.201), channel_id=1, source_target_pairs={{0,2},{2,0},{1,3},{3,1},{4,6},{6,4},{5,7},{7,5},{8,10},{10,8},{9,1... | collective-permute-start | bytes 1179656 | tf_op jit(solution)/shard_map/ppermute | solution.py:57
  211.0 23.0 %collective-permute-start.40 = (bf16[4,128,1536]{2,1,0:T(8,128)(2,1)S(1)}, bf16[4,128,1536]{2,1,0:T(8,128)(2,1)S(1)}, u32[]{:S(2)}, u32[]{:S(2)}) collective-permute-start(bf16[4,128,1536]{2,1,0:T(8,128)(2,1)S(1)} %pad_maximum_fusion), channel_id=1, source_target_pairs={{0,2},{2,0},{1,3},{3,1},{4,6},{6,4},{5,7},{7,5},{8,10},{10,8},{9,1... | collective-permute-start | bytes 4718600 | tf_op jit(solution)/shard_map/ppermute | solution.py:57
  211.4 21.5 %collective-permute-start.39 = (bf16[128,1536]{1,0:T(8,128)(2,1)S(1)}, bf16[128,1536]{1,0:T(8,128)(2,1)S(1)}, u32[]{:S(2)}, u32[]{:S(2)}) collective-permute-start(bf16[128,1536]{1,0:T(8,128)(2,1)S(1)} %add_convert_fusion.6), channel_id=1, source_target_pairs={{4,0},{8,4},{12,8},{0,12},{5,1},{9,5},{13,9},{1,13},{6,2},{10,6},{... | collective-permute-start | bytes 1179656 | tf_op jit(solution)/shard_map/ppermute | solution.py:53
  213.2 19.7 %collective-permute-start.38 = (bf16[128,1536]{1,0:T(8,128)(2,1)S(1)}, bf16[128,1536]{1,0:T(8,128)(2,1)S(1)}, u32[]{:S(2)}, u32[]{:S(2)}) collective-permute-start(bf16[128,1536]{1,0:T(8,128)(2,1)S(1)} %add_convert_fusion.7), channel_id=1, source_target_pairs={{8,0},{12,4},{0,8},{4,12},{9,1},{13,5},{1,9},{5,13},{10,2},{14,6},... | collective-permute-start | bytes 1179656 | tf_op jit(solution)/shard_map/ppermute | solution.py:53
  213.5 20.3 %collective-permute-start.37 = (bf16[128,1536]{1,0:T(8,128)(2,1)S(1)}, bf16[128,1536]{1,0:T(8,128)(2,1)S(1)}, u32[]{:S(2)}, u32[]{:S(2)}) collective-permute-start(bf16[128,1536]{1,0:T(8,128)(2,1)S(1)} %add_convert_fusion.8), channel_id=1, source_target_pairs={{12,0},{0,4},{4,8},{8,12},{13,1},{1,5},{5,9},{9,13},{14,2},{2,6},{... | collective-permute-start | bytes 1179656 | tf_op jit(solution)/shard_map/ppermute | solution.py:53
  237.6 23.3 %collective-permute-start.41 = (bf16[128,1536]{1,0:T(8,128)(2,1)}, bf16[128,1536]{1,0:T(8,128)(2,1)S(1)}, u32[]{:S(2)}, u32[]{:S(2)}) collective-permute-start(bf16[128,1536]{1,0:T(8,128)(2,1)} %fusion.45.refs_0_), channel_id=1, source_target_pairs={{0,2},{2,0},{1,3},{3,1},{4,6},{6,4},{5,7},{7,5},{8,10},{10,8},{9,1... | collective-permute-start | bytes 1179656 | tf_op jit(solution)/shard_map/ppermute | solution.py:57
  237.6 19.6 %collective-permute-start.42 = (bf16[128,1536]{1,0:T(8,128)(2,1)}, bf16[128,1536]{1,0:T(8,128)(2,1)S(1)}, u32[]{:S(2)}, u32[]{:S(2)}) collective-permute-start(bf16[128,1536]{1,0:T(8,128)(2,1)} %fusion.45.refs_0_), channel_id=1, source_target_pairs={{4,0},{8,4},{12,8},{0,12},{5,1},{9,5},{13,9},{1,13},{6,2},{10,6},{... | collective-permute-start | bytes 1179656 | tf_op jit(solution)/shard_map/ppermute | solution.py:53
  239.5 17.8 %collective-permute-start.44 = (bf16[128,1536]{1,0:T(8,128)(2,1)}, bf16[128,1536]{1,0:T(8,128)(2,1)S(1)}, u32[]{:S(2)}, u32[]{:S(2)}) collective-permute-start(bf16[128,1536]{1,0:T(8,128)(2,1)} %fusion.45.refs_0_), channel_id=1, source_target_pairs={{8,0},{12,4},{0,8},{4,12},{9,1},{13,5},{1,9},{5,13},{10,2},{14,6},... | collective-permute-start | bytes 1179656 | tf_op jit(solution)/shard_map/ppermute | solution.py:53
  241.5 19.4 %collective-permute-start.46 = (bf16[128,1536]{1,0:T(8,128)(2,1)}, bf16[128,1536]{1,0:T(8,128)(2,1)S(1)}, u32[]{:S(2)}, u32[]{:S(2)}) collective-permute-start(bf16[128,1536]{1,0:T(8,128)(2,1)} %fusion.45.refs_0_), channel_id=1, source_target_pairs={{12,0},{0,4},{4,8},{8,12},{13,1},{1,5},{5,9},{9,13},{14,2},{2,6},{... | collective-permute-start | bytes 1179656 | tf_op jit(solution)/shard_map/ppermute | solution.py:53
  257.3 3.7 collective-permute-start.45
  262.6 36.8 %collective-permute-start.50 = (bf16[128,1536]{1,0:T(8,128)(2,1)S(1)}, bf16[128,1536]{1,0:T(8,128)(2,1)S(1)}, u32[]{:S(2)}, u32[]{:S(2)}) collective-permute-start(bf16[128,1536]{1,0:T(8,128)(2,1)S(1)} %get-tuple-element.254), channel_id=1, source_target_pairs={{4,0},{8,4},{12,8},{0,12},{5,1},{9,5},{13,9},{1,13},{6,2},{10,6},{... | collective-permute-start | bytes 1179656 | tf_op jit(solution)/shard_map/ppermute | solution.py:53
  263.8 35.6 %collective-permute-start.49 = (bf16[128,1536]{1,0:T(8,128)(2,1)S(1)}, bf16[128,1536]{1,0:T(8,128)(2,1)S(1)}, u32[]{:S(2)}, u32[]{:S(2)}) collective-permute-start(bf16[128,1536]{1,0:T(8,128)(2,1)S(1)} %get-tuple-element.253), channel_id=1, source_target_pairs={{8,0},{12,4},{0,8},{4,12},{9,1},{13,5},{1,9},{5,13},{10,2},{14,6},... | collective-permute-start | bytes 1179656 | tf_op jit(solution)/shard_map/ppermute | solution.py:53
  265.3 34.1 %collective-permute-start.48 = (bf16[128,1536]{1,0:T(8,128)(2,1)S(1)}, bf16[128,1536]{1,0:T(8,128)(2,1)S(1)}, u32[]{:S(2)}, u32[]{:S(2)}) collective-permute-start(bf16[128,1536]{1,0:T(8,128)(2,1)S(1)} %get-tuple-element.252), channel_id=1, source_target_pairs={{12,0},{0,4},{4,8},{8,12},{13,1},{1,5},{5,9},{9,13},{14,2},{2,6},{... | collective-permute-start | bytes 1179656 | tf_op jit(solution)/shard_map/ppermute | solution.py:53
  300.5 21.9 %collective-permute-start.51 = (bf16[8,128,128]{2,1,0:T(8,128)(2,1)S(1)}, bf16[8,128,128]{2,1,0:T(8,128)(2,1)S(1)}, u32[]{:S(2)}, u32[]{:S(2)}) collective-permute-start(bf16[8,128,128]{2,1,0:T(8,128)(2,1)S(1)} %get-tuple-element.260), channel_id=1, source_target_pairs={{0,1},{1,0},{2,3},{3,2},{4,5},{5,4},{6,7},{7,6},{8,9},{9,8},{10,11... | collective-permute-start | bytes 786440 | tf_op jit(solution)/shard_map/ppermute | solution.py:57
  303.6 18.9 %collective-permute-start.52 = (bf16[8,128,128]{2,1,0:T(8,128)(2,1)S(1)}, bf16[8,128,128]{2,1,0:T(8,128)(2,1)S(1)}, u32[]{:S(2)}, u32[]{:S(2)}) collective-permute-start(bf16[8,128,128]{2,1,0:T(8,128)(2,1)S(1)} %get-tuple-element.261), channel_id=1, source_target_pairs={{16,0},{17,1},{32,16},{33,17},{48,32},{49,33},{64,48},{65,49},{80,... | collective-permute-start | bytes 786440 | tf_op jit(solution)/shard_map/ppermute | solution.py:67
  305.7 17.7 %collective-permute-start.53 = (bf16[8,128,128]{2,1,0:T(8,128)(2,1)S(1)}, bf16[8,128,128]{2,1,0:T(8,128)(2,1)S(1)}, u32[]{:S(2)}, u32[]{:S(2)}) collective-permute-start(bf16[8,128,128]{2,1,0:T(8,128)(2,1)S(1)} %get-tuple-element.262), channel_id=1, source_target_pairs={{16,1},{17,0},{32,17},{33,16},{48,33},{49,32},{64,49},{65,48},{80,... | collective-permute-start | bytes 786440 | tf_op jit(solution)/shard_map/ppermute | solution.py:67
  307.6 19.7 %collective-permute-start.54 = (bf16[8,128,128]{2,1,0:T(8,128)(2,1)S(1)}, bf16[8,128,128]{2,1,0:T(8,128)(2,1)S(1)}, u32[]{:S(2)}, u32[]{:S(2)}) collective-permute-start(bf16[8,128,128]{2,1,0:T(8,128)(2,1)S(1)} %get-tuple-element.263), channel_id=1, source_target_pairs={{32,0},{33,1},{48,16},{49,17},{64,32},{65,33},{80,48},{81,49},{96,... | collective-permute-start | bytes 786440 | tf_op jit(solution)/shard_map/ppermute | solution.py:67
  313.6 16.8 %collective-permute-start.55 = (bf16[8,128,128]{2,1,0:T(8,128)(2,1)S(1)}, bf16[8,128,128]{2,1,0:T(8,128)(2,1)S(1)}, u32[]{:S(2)}, u32[]{:S(2)}) collective-permute-start(bf16[8,128,128]{2,1,0:T(8,128)(2,1)S(1)} %get-tuple-element.264), channel_id=1, source_target_pairs={{32,1},{33,0},{48,17},{49,16},{64,33},{65,32},{80,49},{81,48},{96,... | collective-permute-start | bytes 786440 | tf_op jit(solution)/shard_map/ppermute | solution.py:67
  347.0 6.7 %collective-permute-start.61 = (bf16[128,1536]{1,0:T(8,128)(2,1)}, bf16[128,1536]{1,0:T(8,128)(2,1)}, u32[]{:S(2)}, u32[]{:S(2)}) collective-permute-start(bf16[128,1536]{1,0:T(8,128)(2,1)} %get-tuple-element.295), channel_id=1, source_target_pairs={{0,2},{2,0},{1,3},{3,1},{4,6},{6,4},{5,7},{7,5},{8,10},{10,8},{9,1... | collective-permute-start | bytes 1179656 | tf_op jit(solution)/shard_map/ppermute | solution.py:57
  347.0 11.3 %collective-permute-start.59 = (bf16[128,1536]{1,0:T(8,128)(2,1)S(1)}, bf16[128,1536]{1,0:T(8,128)(2,1)}, u32[]{:S(2)}, u32[]{:S(2)}) collective-permute-start(bf16[128,1536]{1,0:T(8,128)(2,1)S(1)} %copy-done.44), channel_id=1, source_target_pairs={{0,2},{2,0},{1,3},{3,1},{4,6},{6,4},{5,7},{7,5},{8,10},{10,8},{9,1... | collective-permute-start | bytes 1179656 | tf_op jit(solution)/shard_map/ppermute | solution.py:57
  347.5 12.7 %collective-permute-start.57 = (bf16[128,1536]{1,0:T(8,128)(2,1)S(1)}, bf16[128,1536]{1,0:T(8,128)(2,1)}, u32[]{:S(2)}, u32[]{:S(2)}) collective-permute-start(bf16[128,1536]{1,0:T(8,128)(2,1)S(1)} %copy-done.42), channel_id=1, source_target_pairs={{0,2},{2,0},{1,3},{3,1},{4,6},{6,4},{5,7},{7,5},{8,10},{10,8},{9,1... | collective-permute-start | bytes 1179656 | tf_op jit(solution)/shard_map/ppermute | solution.py:57
  347.6 24.0 %collective-permute-start.56 = (bf16[128,1536]{1,0:T(8,128)(2,1)S(1)}, bf16[128,1536]{1,0:T(8,128)(2,1)}, u32[]{:S(2)}, u32[]{:S(2)}) collective-permute-start(bf16[128,1536]{1,0:T(8,128)(2,1)S(1)} %copy-done.40), channel_id=1, source_target_pairs={{0,2},{2,0},{1,3},{3,1},{4,6},{6,4},{5,7},{7,5},{8,10},{10,8},{9,1... | collective-permute-start | bytes 1179656 | tf_op jit(solution)/shard_map/ppermute | solution.py:57
  348.0 17.4 %all-to-all-start.3 = ((bf16[8,192,192]{2,1,0:T(8,128)(2,1)}), bf16[8,192,192]{2,1,0:T(8,128)(2,1)}, u32[]{:S(2)}, u32[]{:S(2)}) async-start(bf16[8,192,192]{2,1,0:T(8,128)(2,1)} %bitcast.41), calls=%async_computation.4 | async-start | bytes 1572864 | tf_op jit(solution)/shard_map/all_to_all | solution.py:71
  355.5 19.6 %collective-permute-start.62 = (bf16[128,1536]{1,0:T(8,128)(2,1)}, bf16[128,1536]{1,0:T(8,128)(2,1)S(1)}, u32[]{:S(2)}, u32[]{:S(2)}) collective-permute-start(bf16[128,1536]{1,0:T(8,128)(2,1)} %add_convert_fusion.1), channel_id=1, source_target_pairs={{4,0},{8,4},{12,8},{0,12},{5,1},{9,5},{13,9},{1,13},{6,2},{10,6},{... | collective-permute-start | bytes 1179656 | tf_op jit(solution)/shard_map/ppermute | solution.py:53
  359.4 15.7 %collective-permute-start.60 = (bf16[128,1536]{1,0:T(8,128)(2,1)S(1)}, bf16[128,1536]{1,0:T(8,128)(2,1)S(1)}, u32[]{:S(2)}, u32[]{:S(2)}) collective-permute-start(bf16[128,1536]{1,0:T(8,128)(2,1)S(1)} %add_convert_fusion.2), channel_id=1, source_target_pairs={{8,0},{12,4},{0,8},{4,12},{9,1},{13,5},{1,9},{5,13},{10,2},{14,6},... | collective-permute-start | bytes 1179656 | tf_op jit(solution)/shard_map/ppermute | solution.py:53
  362.0 17.6 %collective-permute-start.58 = (bf16[128,1536]{1,0:T(8,128)(2,1)}, bf16[128,1536]{1,0:T(8,128)(2,1)S(1)}, u32[]{:S(2)}, u32[]{:S(2)}) collective-permute-start(bf16[128,1536]{1,0:T(8,128)(2,1)} %add_convert_fusion.3), channel_id=1, source_target_pairs={{12,0},{0,4},{4,8},{8,12},{13,1},{1,5},{5,9},{9,13},{14,2},{2,6},{... | collective-permute-start | bytes 1179656 | tf_op jit(solution)/shard_map/ppermute | solution.py:53
  365.4 20.6 %all-to-all-start.2 = ((bf16[8,192,384]{2,1,0:T(8,128)(2,1)}), bf16[8,192,384]{2,1,0:T(8,128)(2,1)}, u32[]{:S(2)}, u32[]{:S(2)}) async-start(bf16[8,192,384]{2,1,0:T(8,128)(2,1)} %bitcast.39), calls=%async_computation.3 | async-start | bytes 2359296 | tf_op jit(solution)/shard_map/all_to_all | solution.py:71
  389.8 17.4 %all-to-all-start.4 = ((bf16[8,24,1872]{2,1,0:T(8,128)(2,1)}), bf16[8,24,1872]{2,1,0:T(8,128)(2,1)}, u32[]{:S(2)}, u32[]{:S(2)}) async-start(bf16[8,24,1872]{2,1,0:T(8,128)(2,1)} %concatenate.66), calls=%async_computation.5 | async-start | bytes 1474560 | tf_op jit(solution)/shard_map/all_to_all | solution.py:71
  408.4 9.4 %collective-permute-start.63 = (bf16[8,12,384]{2,1,0:T(8,128)(2,1)S(1)}, bf16[8,12,384]{2,1,0:T(8,128)(2,1)S(1)}, u32[]{:S(2)}, u32[]{:S(2)}) collective-permute-start(bf16[8,12,384]{2,1,0:T(8,128)(2,1)S(1)} %fusion.9), channel_id=1, source_target_pairs={{0,1},{1,0},{2,3},{3,2},{4,5},{5,4},{6,7},{7,6},{8,9},{9,8},{10,11... | collective-permute-start | bytes 221192 | tf_op jit(solution)/shard_map/ppermute | solution.py:57
  409.8 7.3 %collective-permute-start.64 = (bf16[4,24,192]{2,1,0:T(8,128)(2,1)S(1)}, bf16[4,24,192]{2,1,0:T(8,128)(2,1)S(1)}, u32[]{:S(2)}, u32[]{:S(2)}) collective-permute-start(bf16[4,24,192]{2,1,0:T(8,128)(2,1)S(1)} %dynamic-slice_convert_fusion), channel_id=1, source_target_pairs={{0,1},{1,0},{2,3},{3,2},{4,5},{5,4},{6,7},{7,6},{8,9},{9,8},{10,11... | collective-permute-start | bytes 110600 | tf_op jit(solution)/shard_map/ppermute | solution.py:57
  (96 other events, 756.4 us)
Sparse Core Ops, SparseCore 0:
  30.7 108.9 all-gather.1
  237.2 105.9 reduce-scatter.1

commit v10 on v9

--- a/solution.py
+++ b/solution.py
@@ -394,7 +394,7 @@
 
 
 def pack_q(normed, graw, out_grad):
-    tall = 256
+    tall = 512
     return pl.pallas_call(
         pack_q_kernel,
         out_shape=jax.ShapeDtypeStruct((WIDTH, 2 * QUERY), BF16),
@@ -420,7 +420,7 @@
 
 
 def pack_kv(normed, gkvs, gains):
-    tall = 256
+    tall = 512
     return pl.pallas_call(
         pack_kv_kernel,
         out_shape=jax.ShapeDtypeStruct((WIDTH, QUERY), BF16),
@@ -510,7 +510,7 @@
         total = total + jnp.sum(weights, axis=0, keepdims=True)
         return total, accum + dot(kvt[:HEAD, rows_of(j)], weights.astype(BF16))
 
-    return key_loops(plan, at, base, (4, 2, 1), start_ref[0], visit, state)
+    return key_loops(plan, at, base, (8, 4, 2, 1), start_ref[0], visit, state)
 
 
 def attend_own_kernel(plan, q_ref, start_ref, *refs):

time: 437 us -> 436 us (level)
  no operation moved by 1% of the time
where the time goes in v10:
time: 436 us; the launch traced here: 428 us
  waiting for transfers between devices  111 us (25%)
  Pallas kernels  111 us (25%)
  starting transfers between devices  90.5 us (21%)
  local copies, waits for them, and re-layouts  53.8 us (12%)
  other arithmetic  28.9 us (7%)
  blocking collectives  17 us (4%)
  between operations  16 us (4%)
    ppermute x24, waiting for transfers between devices, shift_x(): return lax.ppermute(v, 'x', [((i + distance) % 4, i) for i in range(4)])  52 us
    pallas_call x1, Pallas kernels, back(): return call(plan, q, start, *kvs, grad, out, lse)  32.3 us
    ppermute x24, starting transfers between devices, shift_x(): return lax.ppermute(v, 'x', [((i + distance) % 4, i) for i in range(4)])  28.2 us
    all_to_all x4, waiting for transfers between devices, exchange(): return lax.all_to_all(v, axes, split_axis=0, concat_axis=0, tiled=True)  27.5 us
    unnamed x179, local copies, waits for them, and re-layouts  26.5 us
    pallas_call x4, Pallas kernels, ffn(): pl.pallas_call(ffn_kernel, out_shape=(jax.ShapeDtypeStruct((ROWS, WIDTH),...  25.6 us
    all_to_all x4, starting transfers between devices, exchange(): return lax.all_to_all(v, axes, split_axis=0, concat_axis=0, tiled=True)  23.6 us
    ppermute x8, waiting for transfers between devices, shift_super(): return lax.ppermute(v, ('ylo', 'z', 'yhi'), pairs)  23.6 us
  transfers between devices with their start and end apart: 71, of which 26 were waited for; matrix products, arithmetic and copies ran while one was open for 9% of the time, Pallas kernels for 26%

profile of v10, /device:TPU:8, one launch (start us, length us, event | category | flops | bytes accessed | tf_op | source)
XLA Modules:
  0.0 428.1 jit_solution(1161356332859644540)
XLA Ops:
  12.7 17.0 %all_to_all.25 = bf16[8,24,1920]{2,1,0:T(8,128)(2,1)S(1)} all-to-all(bf16[8,24,1920]{2,1,0:T(8,128)(2,1)S(1)} %concatenate.54), channel_id=1, replica_groups=mesh['ylo'=2,'z'=4,'x'=4,'core'=2,'yhi'=2] {'x','core'}, dimensions={0} | all-to-all | bytes 1474560 | tf_op jit(solution)/shard_map/all_to_all | solution.py:71
  36.1 8.5 %all-to-all-start.1 = ((bf16[16,96,384]{2,1,0:T(8,128)(2,1)}), bf16[16,96,384]{2,1,0:T(8,128)(2,1)S(1)}, u32[]{:S(2)}, u32[]{:S(2)}) async-start(bf16[16,96,384]{2,1,0:T(8,128)(2,1)} %broadcast_in_dim.27), calls=%async_computation.1 | async-start | bytes 2359296 | tf_op jit(solution)/shard_map/all_to_all | solution.py:71
  45.0 1.9 fusion.12
  47.5 5.6 %collective-permute-done.5.refs_6_.refs_10_ = bf16[128,1536]{1,0:T(8,128)(2,1)} collective-permute-done((bf16[128,1536]{1,0:T(8,128)(2,1)S(1)}, bf16[128,1536]{1,0:T(8,128)(2,1)}, u32[]{:S(2)}, u32[]{:S(2)}) %collective-permute-start.5) | collective-permute-done | bytes 393248 | tf_op jit(solution)/shard_map/ppermute | solution.py:53
  53.9 2.1 collective-permute-start.8
  58.0 10.6 %all-to-all-done.1 = bf16[16,96,384]{2,1,0:T(8,128)(2,1)S(1)} async-done(((bf16[16,96,384]{2,1,0:T(8,128)(2,1)}), bf16[16,96,384]{2,1,0:T(8,128)(2,1)S(1)}, u32[]{:S(2)}, u32[]{:S(2)}) %all-to-all-start.1) | async-done | bytes 1179680 | tf_op jit(solution)/shard_map/all_to_all | solution.py:71
  70.5 2.3 reshape.569.refs_8_.refs_12_
  75.9 4.9 %shard_map.237 = (bf16[1024,1536]{1,0:T(8,128)(2,1)S(1)}, bf16[8,128,192]{2,1,0:T(8,128)(2,1)S(1)}, bf16[8,128,128]{2,1,0:T(8,128)(2,1)}, f32[4,256,256]{2,1,0:T(8,128)S(1)}) custom-call(bf16[128,1536]{1,0:T(8,128)(2,1)S(1)} %copy-done.3, bf16[128,1536]{1,0:T(8,128)(2,1)S(1)} %collective-permute-done.refs_1_.refs_9_, bf16[128,1536]{1,0:T(8,128)(2,1)S(1)} %copy-done.15, ...), custom_call_target="tpu_custom_call" | custom-call | flops 1207959552 | bytes 10000000 | tf_op jit(solution)/shard_map/pallas_call | solution.py:168
  80.8 1.7 copy-done
  84.3 1.8 collective-permute-start.10
  86.3 2.1 collective-permute-start.11
  88.4 3.5 collective-permute-start.12
  91.9 2.1 collective-permute-start.13
  94.0 2.8 collective-permute-start.14
  96.8 4.1 collective-permute-done.10.refs_1_.refs_5_
  102.0 8.6 %shard_map.238 = (f32[4,64,768]{2,1,0:T(8,128)S(1)}, f32[4,1,768]{2,1,0:T(1,128)S(1)}) custom-call(s32[8,17]{1,0:T(8,128)S(1)} %stack.22.plan, bf16[8,128,192]{2,1,0:T(8,128)(2,1)S(1)} %copy-done.36, s32[4,1,768]{2,1,0:T(1,128)S(1)} %copy.103.start_ref, bf16[8,128,128]{2,1,0:T(8,128)(2,1)} %get-tuple-element.159.refs_0_.refs_4_, ...), custom_call_target="tpu_custom_call" | custom-call | flops 4000000000 | bytes 8000000 | tf_op jit(solution)/shard_map/pallas_call | solution.py:618
  110.6 6.7 %collective-permute-done.11.refs_0_ = bf16[8,128,128]{2,1,0:T(8,128)(2,1)S(1)} collective-permute-done((bf16[8,128,128]{2,1,0:T(8,128)(2,1)}, bf16[8,128,128]{2,1,0:T(8,128)(2,1)S(1)}, u32[]{:S(2)}, u32[]{:S(2)}) %collective-permute-start.11) | collective-permute-done | bytes 262176 | tf_op jit(solution)/shard_map/ppermute | solution.py:67
  118.7 6.5 %collective-permute-done.13.refs_2_ = bf16[8,128,128]{2,1,0:T(8,128)(2,1)S(1)} collective-permute-done((bf16[8,128,128]{2,1,0:T(8,128)(2,1)}, bf16[8,128,128]{2,1,0:T(8,128)(2,1)S(1)}, u32[]{:S(2)}, u32[]{:S(2)}) %collective-permute-start.13) | collective-permute-done | bytes 262176 | tf_op jit(solution)/shard_map/ppermute | solution.py:67
  126.7 9.2 %shard_map.239 = (bf16[8,128,192]{2,1,0:T(8,128)(2,1)S(1)}, f32[4,64,768]{2,1,0:T(8,128)S(1)}, f32[4,1,768]{2,1,0:T(1,128)S(1)}) custom-call(s32[8,17]{1,0:T(8,128)S(1)} %stack.22.plan, bf16[8,128,192]{2,1,0:T(8,128)(2,1)S(1)} %copy-done.37, s32[4,1,768]{2,1,0:T(1,128)S(1)} %copy.103.start_ref, bf16[8,128,128]{2,1,0:T(8,128)(2,1)S(1)} %collective-permute-done.11.refs_0_, ...), custom_call_target="tpu_custom_call" | custom-call | flops 8000000000 | bytes 8000000 | tf_op jit(solution)/shard_map/pallas_call | solution.py:625
  140.3 1.6 dynamic-slice_bitcast_fusion.2
  145.5 2.8 collective-permute-start.25
  150.6 14.8 %collective-permute-done.25 = bf16[128,1536]{1,0:T(8,128)(2,1)S(1)} collective-permute-done((bf16[128,1536]{1,0:T(8,128)(2,1)S(1)}, bf16[128,1536]{1,0:T(8,128)(2,1)S(1)}, u32[]{:S(2)}, u32[]{:S(2)}) %collective-permute-start.25) | collective-permute-done | bytes 393248 | tf_op jit(solution)/shard_map/ppermute | solution.py:53
  165.4 3.8 collective-permute-done.21
  172.3 6.4 %shard_map.244 = (bf16[128,1536]{1,0:T(8,128)(2,1)S(1)}, bf16[128,1536]{1,0:T(8,128)(2,1)S(1)}, bf16[128,1536]{1,0:T(8,128)(2,1)S(1)}, bf16[128,1536]{1,0:T(8,12...) custom-call(bf16[128,1536]{1,0:T(8,128)(2,1)S(1)} %multiply_convert_fusion.x0_ref.refs_0_, ...), custom_call_target="tpu_custom_call" | custom-call | flops 4831838208 | bytes 14000000 | tf_op jit(solution)/shard_map/pallas_call | solution.py:298
  183.9 6.4 %shard_map.245 = (bf16[128,1536]{1,0:T(8,128)(2,1)S(1)}, bf16[128,1536]{1,0:T(8,128)(2,1)S(1)}, bf16[128,1536]{1,0:T(8,128)(2,1)S(1)}, bf16[128,1536]{1,0:T(8,12...) custom-call(bf16[128,1536]{1,0:T(8,128)(2,1)S(1)} %collective-permute-done.28.x0_ref.refs_2_, ...), custom_call_target="tpu_custom_call" | custom-call | flops 4831838208 | bytes 14000000 | tf_op jit(solution)/shard_map/pallas_call | solution.py:298
  192.5 6.4 %shard_map.246 = (bf16[128,1536]{1,0:T(8,128)(2,1)S(1)}, bf16[128,1536]{1,0:T(8,128)(2,1)S(1)}, bf16[128,1536]{1,0:T(8,128)(2,1)S(1)}, bf16[128,1536]{1,0:T(8,12...) custom-call(bf16[128,1536]{1,0:T(8,128)(2,1)S(1)} %collective-permute-done.30.x0_ref.refs_4_, ...), custom_call_target="tpu_custom_call" | custom-call | flops 4831838208 | bytes 14000000 | tf_op jit(solution)/shard_map/pallas_call | solution.py:298
  201.9 6.4 %shard_map.247 = (bf16[128,1536]{1,0:T(8,128)(2,1)S(1)}, bf16[128,1536]{1,0:T(8,128)(2,1)S(1)}, bf16[128,1536]{1,0:T(8,128)(2,1)S(1)}, bf16[128,1536]{1,0:T(8,12...) custom-call(bf16[128,1536]{1,0:T(8,128)(2,1)S(1)} %collective-permute-done.33.x0_ref.refs_6_, ...), custom_call_target="tpu_custom_call" | custom-call | flops 4831838208 | bytes 14000000 | tf_op jit(solution)/shard_map/pallas_call | solution.py:298
  211.4 1.8 collective-permute-start.39
  214.1 15.3 %shard_map.248 = bf16[2,1536,1296]{2,1,0:T(8,128)(2,1)S(1)} custom-call(bf16[128,1536]{1,0:T(8,128)(2,1)S(1)} %multiply_convert_fusion.x0_ref.refs_0_, bf16[128,1536]{1,0:T(8,128)(2,1)S(1)} %collective-permute-done.26.x1_ref.refs_1_, bf16[128,1536]{1,0:T(8,128)(2,1)S(1)} %collective-permute-done.28.x0_ref.refs_2_, ...), custom_call_target="tpu_custom_call" | custom-call | flops 9663676416 | bytes 24000000 | tf_op jit(solution)/shard_map/pallas_call | solution.py:327
  229.4 3.5 copy-done.8
  234.9 2.0 fusion.45.refs_0_
  237.6 1.8 collective-permute-start.42
  239.4 2.1 collective-permute-start.44
  242.9 2.2 add_convert_fusion
  245.2 12.0 %collective-permute-done.42.refs_2_ = bf16[128,1536]{1,0:T(8,128)(2,1)S(1)} collective-permute-done((bf16[128,1536]{1,0:T(8,128)(2,1)}, bf16[128,1536]{1,0:T(8,128)(2,1)S(1)}, u32[]{:S(2)}, u32[]{:S(2)}) %collective-permute-start.42) | collective-permute-done | bytes 393248 | tf_op jit(solution)/shard_map/ppermute | solution.py:53
  257.7 3.1 collective-permute-done.46.refs_6_
  267.0 32.3 %shard_map.250 = (bf16[8,128,256]{2,1,0:T(8,128)(2,1)S(1)}, bf16[8,128,128]{2,1,0:T(8,128)(2,1)S(1)}, bf16[8,128,128]{2,1,0:T(8,128)(2,1)S(1)}, bf16[8,128,128]{...) custom-call(s32[8,17]{1,0:T(8,128)S(1)} %copy-done.34, ...), custom_call_target="tpu_custom_call" | custom-call | flops 30000001024 | bytes 8000000 | tf_op jit(solution)/shard_map/pallas_call | solution.py:639
  300.5 3.0 collective-permute-start.51
  303.5 2.1 collective-permute-start.52
  305.6 1.9 collective-permute-start.53
  307.6 6.0 %collective-permute-start.54 = (bf16[8,128,128]{2,1,0:T(8,128)(2,1)S(1)}, bf16[8,128,128]{2,1,0:T(8,128)(2,1)S(1)}, u32[]{:S(2)}, u32[]{:S(2)}) collective-permute-start(bf16[8,128,128]{2,1,0:T(8,128)(2,1)S(1)} %get-tuple-element.263), channel_id=1, source_target_pairs={{32,0},{33,1},{48,16},{49,17},{64,32},{65,33},{80,48},{81,49},{96,... | collective-permute-start | bytes 786440 | tf_op jit(solution)/shard_map/ppermute | solution.py:67
  313.6 1.9 collective-permute-start.55
  318.7 2.6 shard_map.253
  321.4 1.8 collective-permute-done.53.refs_4_
  323.2 4.0 collective-permute-done.54.refs_5_
  327.2 3.1 collective-permute-done.55.refs_6_
  333.4 3.5 shard_map.255
  341.4 2.0 copy-done.2
  343.4 2.5 shard_map.256
  347.0 5.7 %all-to-all-start.3 = ((bf16[8,192,192]{2,1,0:T(8,128)(2,1)}), bf16[8,192,192]{2,1,0:T(8,128)(2,1)}, u32[]{:S(2)}, u32[]{:S(2)}) async-start(bf16[8,192,192]{2,1,0:T(8,128)(2,1)} %bitcast.41), calls=%async_computation.4 | async-start | bytes 1572864 | tf_op jit(solution)/shard_map/all_to_all | solution.py:71
  352.6 1.8 add_convert_fusion.1
  354.4 2.7 collective-permute-start.62
  359.1 1.8 add_convert_fusion.3
  361.9 2.5 all-to-all-done.3
  364.4 4.8 %all-to-all-start.2 = ((bf16[8,192,384]{2,1,0:T(8,128)(2,1)}), bf16[8,192,384]{2,1,0:T(8,128)(2,1)}, u32[]{:S(2)}, u32[]{:S(2)}) async-start(bf16[8,192,384]{2,1,0:T(8,128)(2,1)} %bitcast.39), calls=%async_computation.3 | async-start | bytes 2359296 | tf_op jit(solution)/shard_map/all_to_all | solution.py:71
  370.5 3.6 collective-permute-done.62
  374.1 4.5 %collective-permute-done.58 = bf16[128,1536]{1,0:T(8,128)(2,1)S(1)} collective-permute-done((bf16[128,1536]{1,0:T(8,128)(2,1)}, bf16[128,1536]{1,0:T(8,128)(2,1)S(1)}, u32[]{:S(2)}, u32[]{:S(2)}) %collective-permute-start.58) | collective-permute-done | bytes 393248 | tf_op jit(solution)/shard_map/ppermute | solution.py:53
  378.6 1.6 fusion
  380.2 4.8 %all-to-all-done.2 = bf16[8,192,384]{2,1,0:T(8,128)(2,1)} async-done(((bf16[8,192,384]{2,1,0:T(8,128)(2,1)}), bf16[8,192,384]{2,1,0:T(8,128)(2,1)}, u32[]{:S(2)}, u32[]{:S(2)}) %all-to-all-start.2) | async-done | bytes 1179680 | tf_op jit(solution)/shard_map/all_to_all | solution.py:71
  386.6 2.1 concatenate.66
  388.7 4.6 %all-to-all-start.4 = ((bf16[8,24,1872]{2,1,0:T(8,128)(2,1)}), bf16[8,24,1872]{2,1,0:T(8,128)(2,1)}, u32[]{:S(2)}, u32[]{:S(2)}) async-start(bf16[8,24,1872]{2,1,0:T(8,128)(2,1)} %concatenate.66), calls=%async_computation.5 | async-start | bytes 1474560 | tf_op jit(solution)/shard_map/all_to_all | solution.py:71
  393.4 3.0 fusion.6
  396.4 9.6 %all-to-all-done.4 = bf16[8,24,1872]{2,1,0:T(8,128)(2,1)} async-done(((bf16[8,24,1872]{2,1,0:T(8,128)(2,1)}), bf16[8,24,1872]{2,1,0:T(8,128)(2,1)}, u32[]{:S(2)}, u32[]{:S(2)}) %all-to-all-start.4) | async-done | bytes 718880 | tf_op jit(solution)/shard_map/all_to_all | solution.py:71
  408.7 2.2 collective-permute-start.64
  (419 shorter events, 95.3 us)
Async XLA Ops:
  7.2 133.0 %all-gather.2.cloned.1.call-start = ((), (), s32[]{:S(2)}) async-start(), calls=%async_computation.6 | async-start | bytes 10027008 | tf_op jit(solution)/shard_map/all_gather | solution.py:699
  30.6 23.3 %collective-permute-start = (bf16[128,1536]{1,0:T(8,128)(2,1)S(1)}, bf16[128,1536]{1,0:T(8,128)(2,1)S(1)}, u32[]{:S(2)}, u32[]{:S(2)}) collective-permute-start(bf16[128,1536]{1,0:T(8,128)(2,1)S(1)} %copy-done.3), channel_id=1, source_target_pairs={{0,2},{2,0},{1,3},{3,1},{4,6},{6,4},{5,7},{7,5},{8,10},{10,8},{9,1... | collective-permute-start | bytes 1179656 | tf_op jit(solution)/shard_map/ppermute | solution.py:57
  30.7 14.2 %collective-permute-start.1 = (bf16[128,1536]{1,0:T(8,128)(2,1)S(1)}, bf16[128,1536]{1,0:T(8,128)(2,1)S(1)}, u32[]{:S(2)}, u32[]{:S(2)}) collective-permute-start(bf16[128,1536]{1,0:T(8,128)(2,1)S(1)} %copy-done.3), channel_id=1, source_target_pairs={{4,0},{8,4},{12,8},{0,12},{5,1},{9,5},{13,9},{1,13},{6,2},{10,6},{... | collective-permute-start | bytes 1179656 | tf_op jit(solution)/shard_map/ppermute | solution.py:53
  31.9 15.0 %collective-permute-start.3 = (bf16[128,1536]{1,0:T(8,128)(2,1)S(1)}, bf16[128,1536]{1,0:T(8,128)(2,1)S(1)}, u32[]{:S(2)}, u32[]{:S(2)}) collective-permute-start(bf16[128,1536]{1,0:T(8,128)(2,1)S(1)} %copy-done.3), channel_id=1, source_target_pairs={{8,0},{12,4},{0,8},{4,12},{9,1},{13,5},{1,9},{5,13},{10,2},{14,6},... | collective-permute-start | bytes 1179656 | tf_op jit(solution)/shard_map/ppermute | solution.py:53
  33.4 19.7 %collective-permute-start.5 = (bf16[128,1536]{1,0:T(8,128)(2,1)S(1)}, bf16[128,1536]{1,0:T(8,128)(2,1)}, u32[]{:S(2)}, u32[]{:S(2)}) collective-permute-start(bf16[128,1536]{1,0:T(8,128)(2,1)S(1)} %copy-done.3), channel_id=1, source_target_pairs={{12,0},{0,4},{4,8},{8,12},{13,1},{1,5},{5,9},{9,13},{14,2},{2,6},{... | collective-permute-start | bytes 1179656 | tf_op jit(solution)/shard_map/ppermute | solution.py:53
  36.1 32.5 %all-to-all-start.1 = ((bf16[16,96,384]{2,1,0:T(8,128)(2,1)}), bf16[16,96,384]{2,1,0:T(8,128)(2,1)S(1)}, u32[]{:S(2)}, u32[]{:S(2)}) async-start(bf16[16,96,384]{2,1,0:T(8,128)(2,1)} %broadcast_in_dim.27), calls=%async_computation.1 | async-start | bytes 2359296 | tf_op jit(solution)/shard_map/all_to_all | solution.py:71
  44.7 341.9 %reduce-scatter.2.cloned.1.call-start = ((), (), s32[]{:S(2)}) async-start(), calls=%async_computation.7 | async-start | bytes 9191424 | tf_op jit(solution)/shard_map/reduce_scatter | solution.py:805
  44.9 11.1 %collective-permute-start.2 = (bf16[128,1536]{1,0:T(8,128)(2,1)S(1)}, bf16[128,1536]{1,0:T(8,128)(2,1)S(1)}, u32[]{:S(2)}, u32[]{:S(2)}) collective-permute-start(bf16[128,1536]{1,0:T(8,128)(2,1)S(1)} %collective-permute-done.1.refs_2_.refs_10_), channel_id=1, source_target_pairs={{0,2},{2,0},{1,3},{3,1},{4,6},{6,4},{5,7},{7,5},{8,10},{10,8},{9,1... | collective-permute-start | bytes 1179656 | tf_op jit(solution)/shard_map/ppermute | solution.py:57
  46.9 26.9 %collective-permute-start.4 = (bf16[128,1536]{1,0:T(8,128)(2,1)S(1)}, bf16[128,1536]{1,0:T(8,128)(2,1)}, u32[]{:S(2)}, u32[]{:S(2)}) collective-permute-start(bf16[128,1536]{1,0:T(8,128)(2,1)S(1)} %collective-permute-done.3.refs_4_.refs_8_), channel_id=1, source_target_pairs={{0,2},{2,0},{1,3},{3,1},{4,6},{6,4},{5,7},{7,5},{8,10},{10,8},{9,1... | collective-permute-start | bytes 1179656 | tf_op jit(solution)/shard_map/ppermute | solution.py:57
  53.1 20.7 %collective-permute-start.6 = (bf16[128,1536]{1,0:T(8,128)(2,1)}, bf16[128,1536]{1,0:T(8,128)(2,1)}, u32[]{:S(2)}, u32[]{:S(2)}) collective-permute-start(bf16[128,1536]{1,0:T(8,128)(2,1)} %collective-permute-done.5.refs_6_.refs_10_), channel_id=1, source_target_pairs={{0,2},{2,0},{1,3},{3,1},{4,6},{6,4},{5,7},{7,5},{8,10},{10,8},{9,1... | collective-permute-start | bytes 1179656 | tf_op jit(solution)/shard_map/ppermute | solution.py:57
  53.2 31.1 %collective-permute-start.7 = (bf16[128,1536]{1,0:T(8,128)(2,1)}, bf16[128,1536]{1,0:T(8,128)(2,1)}, u32[]{:S(2)}, u32[]{:S(2)}) collective-permute-start(bf16[128,1536]{1,0:T(8,128)(2,1)} %refs_8_.1), channel_id=1, source_target_pairs={{4,0},{8,4},{12,8},{0,12},{5,1},{9,5},{13,9},{1,13},{6,2},{10,6},{... | collective-permute-start | bytes 1179656 | tf_op jit(solution)/shard_map/ppermute | solution.py:53
  53.9 30.3 %collective-permute-start.8 = (bf16[128,1536]{1,0:T(8,128)(2,1)}, bf16[128,1536]{1,0:T(8,128)(2,1)}, u32[]{:S(2)}, u32[]{:S(2)}) collective-permute-start(bf16[128,1536]{1,0:T(8,128)(2,1)} %refs_8_.1), channel_id=1, source_target_pairs={{8,0},{12,4},{0,8},{4,12},{9,1},{13,5},{1,9},{5,13},{10,2},{14,6},... | collective-permute-start | bytes 1179656 | tf_op jit(solution)/shard_map/ppermute | solution.py:53
  56.8 27.5 %collective-permute-start.9 = (bf16[128,1536]{1,0:T(8,128)(2,1)}, bf16[128,1536]{1,0:T(8,128)(2,1)}, u32[]{:S(2)}, u32[]{:S(2)}) collective-permute-start(bf16[128,1536]{1,0:T(8,128)(2,1)} %refs_8_.1), channel_id=1, source_target_pairs={{12,0},{0,4},{4,8},{8,12},{13,1},{1,5},{5,9},{9,13},{14,2},{2,6},{... | collective-permute-start | bytes 1179656 | tf_op jit(solution)/shard_map/ppermute | solution.py:53
  84.3 16.5 %collective-permute-start.10 = (bf16[8,128,128]{2,1,0:T(8,128)(2,1)}, bf16[8,128,128]{2,1,0:T(8,128)(2,1)S(1)}, u32[]{:S(2)}, u32[]{:S(2)}) collective-permute-start(bf16[8,128,128]{2,1,0:T(8,128)(2,1)} %get-tuple-element.159.refs_0_.refs_4_), channel_id=1, source_target_pairs={{0,1},{1,0},{2,3},{3,2},{4,5},{5,4},{6,7},{7,6},{8,9},{9,8},{10,11... | collective-permute-start | bytes 786440 | tf_op jit(solution)/shard_map/ppermute | solution.py:57
  86.3 31.0 %collective-permute-start.11 = (bf16[8,128,128]{2,1,0:T(8,128)(2,1)}, bf16[8,128,128]{2,1,0:T(8,128)(2,1)S(1)}, u32[]{:S(2)}, u32[]{:S(2)}) collective-permute-start(bf16[8,128,128]{2,1,0:T(8,128)(2,1)} %get-tuple-element.159.refs_0_.refs_4_), channel_id=1, source_target_pairs={{0,32},{1,33},{16,48},{17,49},{32,64},{33,65},{48,80},{49,81},{64,... | collective-permute-start | bytes 786440 | tf_op jit(solution)/shard_map/ppermute | solution.py:67
  88.4 30.3 %collective-permute-start.12 = (bf16[8,128,128]{2,1,0:T(8,128)(2,1)}, bf16[8,128,128]{2,1,0:T(8,128)(2,1)S(1)}, u32[]{:S(2)}, u32[]{:S(2)}) collective-permute-start(bf16[8,128,128]{2,1,0:T(8,128)(2,1)} %get-tuple-element.159.refs_0_.refs_4_), channel_id=1, source_target_pairs={{0,33},{1,32},{16,49},{17,48},{32,65},{33,64},{48,81},{49,80},{64,... | collective-permute-start | bytes 786440 | tf_op jit(solution)/shard_map/ppermute | solution.py:67
  91.9 33.3 %collective-permute-start.13 = (bf16[8,128,128]{2,1,0:T(8,128)(2,1)}, bf16[8,128,128]{2,1,0:T(8,128)(2,1)S(1)}, u32[]{:S(2)}, u32[]{:S(2)}) collective-permute-start(bf16[8,128,128]{2,1,0:T(8,128)(2,1)} %get-tuple-element.159.refs_0_.refs_4_), channel_id=1, source_target_pairs={{0,16},{1,17},{16,32},{17,33},{32,48},{33,49},{48,64},{49,65},{64,... | collective-permute-start | bytes 786440 | tf_op jit(solution)/shard_map/ppermute | solution.py:67
  94.0 31.2 %collective-permute-start.14 = (bf16[8,128,128]{2,1,0:T(8,128)(2,1)}, bf16[8,128,128]{2,1,0:T(8,128)(2,1)S(1)}, u32[]{:S(2)}, u32[]{:S(2)}) collective-permute-start(bf16[8,128,128]{2,1,0:T(8,128)(2,1)} %get-tuple-element.159.refs_0_.refs_4_), channel_id=1, source_target_pairs={{0,17},{1,16},{16,33},{17,32},{32,49},{33,48},{48,65},{49,64},{64,... | collective-permute-start | bytes 786440 | tf_op jit(solution)/shard_map/ppermute | solution.py:67
  125.2 17.2 %collective-permute-start.15 = (bf16[128,1536]{1,0:T(8,128)(2,1)}, bf16[128,1536]{1,0:T(8,128)(2,1)}, u32[]{:S(2)}, u32[]{:S(2)}) collective-permute-start(bf16[128,1536]{1,0:T(8,128)(2,1)} %refs_8_.1), channel_id=1, source_target_pairs={{0,2},{2,0},{1,3},{3,1},{4,6},{6,4},{5,7},{7,5},{8,10},{10,8},{9,1... | collective-permute-start | bytes 1179656 | tf_op jit(solution)/shard_map/ppermute | solution.py:57
  125.2 17.2 %collective-permute-start.16 = (bf16[128,1536]{1,0:T(8,128)(2,1)}, bf16[128,1536]{1,0:T(8,128)(2,1)}, u32[]{:S(2)}, u32[]{:S(2)}) collective-permute-start(bf16[128,1536]{1,0:T(8,128)(2,1)} %collective-permute-done.7.c0_ref.refs_10_), channel_id=1, source_target_pairs={{0,2},{2,0},{1,3},{3,1},{4,6},{6,4},{5,7},{7,5},{8,10},{10,8},{9,1... | collective-permute-start | bytes 1179656 | tf_op jit(solution)/shard_map/ppermute | solution.py:57
  125.7 16.7 %collective-permute-start.17 = (bf16[128,1536]{1,0:T(8,128)(2,1)}, bf16[128,1536]{1,0:T(8,128)(2,1)}, u32[]{:S(2)}, u32[]{:S(2)}) collective-permute-start(bf16[128,1536]{1,0:T(8,128)(2,1)} %collective-permute-done.8.c0_ref.refs_12_), channel_id=1, source_target_pairs={{0,2},{2,0},{1,3},{3,1},{4,6},{6,4},{5,7},{7,5},{8,10},{10,8},{9,1... | collective-permute-start | bytes 1179656 | tf_op jit(solution)/shard_map/ppermute | solution.py:57
  125.7 16.7 %collective-permute-start.18 = (bf16[128,1536]{1,0:T(8,128)(2,1)}, bf16[128,1536]{1,0:T(8,128)(2,1)}, u32[]{:S(2)}, u32[]{:S(2)}) collective-permute-start(bf16[128,1536]{1,0:T(8,128)(2,1)} %collective-permute-done.9.c1_ref.refs_11_), channel_id=1, source_target_pairs={{0,2},{2,0},{1,3},{3,1},{4,6},{6,4},{5,7},{7,5},{8,10},{10,8},{9,1... | collective-permute-start | bytes 1179656 | tf_op jit(solution)/shard_map/ppermute | solution.py:57
  143.4 5.0 %collective-permute-start.22 = (bf16[128,1536]{1,0:T(8,128)(2,1)S(1)}, bf16[128,1536]{1,0:T(8,128)(2,1)S(1)}, u32[]{:S(2)}, u32[]{:S(2)}) collective-permute-start(bf16[128,1536]{1,0:T(8,128)(2,1)S(1)} %get-tuple-element.184), channel_id=1, source_target_pairs={{0,2},{2,0},{1,3},{3,1},{4,6},{6,4},{5,7},{7,5},{8,10},{10,8},{9,1... | collective-permute-start | bytes 1179656 | tf_op jit(solution)/shard_map/ppermute | solution.py:57
  144.3 5.0 %collective-permute-start.20 = (bf16[128,1536]{1,0:T(8,128)(2,1)S(1)}, bf16[128,1536]{1,0:T(8,128)(2,1)S(1)}, u32[]{:S(2)}, u32[]{:S(2)}) collective-permute-start(bf16[128,1536]{1,0:T(8,128)(2,1)S(1)} %get-tuple-element.182), channel_id=1, source_target_pairs={{0,2},{2,0},{1,3},{3,1},{4,6},{6,4},{5,7},{7,5},{8,10},{10,8},{9,1... | collective-permute-start | bytes 1179656 | tf_op jit(solution)/shard_map/ppermute | solution.py:57
  144.9 5.7 %collective-permute-start.19 = (bf16[128,1536]{1,0:T(8,128)(2,1)S(1)}, bf16[128,1536]{1,0:T(8,128)(2,1)S(1)}, u32[]{:S(2)}, u32[]{:S(2)}) collective-permute-start(bf16[128,1536]{1,0:T(8,128)(2,1)S(1)} %get-tuple-element.180), channel_id=1, source_target_pairs={{0,2},{2,0},{1,3},{3,1},{4,6},{6,4},{5,7},{7,5},{8,10},{10,8},{9,1... | collective-permute-start | bytes 1179656 | tf_op jit(solution)/shard_map/ppermute | solution.py:57
  145.5 19.9 %collective-permute-start.25 = (bf16[128,1536]{1,0:T(8,128)(2,1)S(1)}, bf16[128,1536]{1,0:T(8,128)(2,1)S(1)}, u32[]{:S(2)}, u32[]{:S(2)}) collective-permute-start(bf16[128,1536]{1,0:T(8,128)(2,1)S(1)} %add_convert_fusion.10), channel_id=1, source_target_pairs={{4,0},{8,4},{12,8},{0,12},{5,1},{9,5},{13,9},{1,13},{6,2},{10,6},{... | collective-permute-start | bytes 1179656 | tf_op jit(solution)/shard_map/ppermute | solution.py:53
  148.4 16.9 %collective-permute-start.23 = (bf16[128,1536]{1,0:T(8,128)(2,1)S(1)}, bf16[128,1536]{1,0:T(8,128)(2,1)S(1)}, u32[]{:S(2)}, u32[]{:S(2)}) collective-permute-start(bf16[128,1536]{1,0:T(8,128)(2,1)S(1)} %add_convert_fusion.11), channel_id=1, source_target_pairs={{8,0},{12,4},{0,8},{4,12},{9,1},{13,5},{1,9},{5,13},{10,2},{14,6},... | collective-permute-start | bytes 1179656 | tf_op jit(solution)/shard_map/ppermute | solution.py:53
  149.5 19.8 %collective-permute-start.21 = (bf16[128,1536]{1,0:T(8,128)(2,1)S(1)}, bf16[128,1536]{1,0:T(8,128)(2,1)S(1)}, u32[]{:S(2)}, u32[]{:S(2)}) collective-permute-start(bf16[128,1536]{1,0:T(8,128)(2,1)S(1)} %add_convert_fusion.12), channel_id=1, source_target_pairs={{12,0},{0,4},{4,8},{8,12},{13,1},{1,5},{5,9},{9,13},{14,2},{2,6},{... | collective-permute-start | bytes 1179656 | tf_op jit(solution)/shard_map/ppermute | solution.py:53
  170.2 11.5 %collective-permute-start.28 = (bf16[128,1536]{1,0:T(8,128)(2,1)S(1)}, bf16[128,1536]{1,0:T(8,128)(2,1)S(1)}, u32[]{:S(2)}, u32[]{:S(2)}) collective-permute-start(bf16[128,1536]{1,0:T(8,128)(2,1)S(1)} %multiply_convert_fusion.x0_ref.refs_0_), channel_id=1, source_target_pairs={{4,0},{8,4},{12,8},{0,12},{5,1},{9,5},{13,9},{1,13},{6,2},{10,6},{... | collective-permute-start | bytes 1179656 | tf_op jit(solution)/shard_map/ppermute | solution.py:53
  170.8 12.4 %collective-permute-start.29 = (bf16[128,1536]{1,0:T(8,128)(2,1)S(1)}, bf16[128,1536]{1,0:T(8,128)(2,1)S(1)}, u32[]{:S(2)}, u32[]{:S(2)}) collective-permute-start(bf16[128,1536]{1,0:T(8,128)(2,1)S(1)} %multiply_convert_fusion.x0_ref.refs_0_), channel_id=1, source_target_pairs={{12,0},{0,4},{4,8},{8,12},{13,1},{1,5},{5,9},{9,13},{14,2},{2,6},{... | collective-permute-start | bytes 1179656 | tf_op jit(solution)/shard_map/ppermute | solution.py:53
  179.4 21.1 %collective-permute-start.27 = (bf16[128,1536]{1,0:T(8,128)(2,1)S(1)}, bf16[128,1536]{1,0:T(8,128)(2,1)S(1)}, u32[]{:S(2)}, u32[]{:S(2)}) collective-permute-start(bf16[128,1536]{1,0:T(8,128)(2,1)S(1)} %get-tuple-element.190), channel_id=1, source_target_pairs={{0,2},{2,0},{1,3},{3,1},{4,6},{6,4},{5,7},{7,5},{8,10},{10,8},{9,1... | collective-permute-start | bytes 1179656 | tf_op jit(solution)/shard_map/ppermute | solution.py:57
  179.4 13.0 %collective-permute-start.30 = (bf16[128,1536]{1,0:T(8,128)(2,1)S(1)}, bf16[128,1536]{1,0:T(8,128)(2,1)S(1)}, u32[]{:S(2)}, u32[]{:S(2)}) collective-permute-start(bf16[128,1536]{1,0:T(8,128)(2,1)S(1)} %multiply_convert_fusion.x0_ref.refs_0_), channel_id=1, source_target_pairs={{8,0},{12,4},{0,8},{4,12},{9,1},{13,5},{1,9},{5,13},{10,2},{14,6},... | collective-permute-start | bytes 1179656 | tf_op jit(solution)/shard_map/ppermute | solution.py:53
  183.2 9.2 %collective-permute-start.31 = (bf16[128,1536]{1,0:T(8,128)(2,1)S(1)}, bf16[128,1536]{1,0:T(8,128)(2,1)S(1)}, u32[]{:S(2)}, u32[]{:S(2)}) collective-permute-start(bf16[128,1536]{1,0:T(8,128)(2,1)S(1)} %collective-permute-done.28.x0_ref.refs_2_), channel_id=1, source_target_pairs={{0,2},{2,0},{1,3},{3,1},{4,6},{6,4},{5,7},{7,5},{8,10},{10,8},{9,1... | collective-permute-start | bytes 1179656 | tf_op jit(solution)/shard_map/ppermute | solution.py:57
  183.2 18.1 %collective-permute-start.33 = (bf16[128,1536]{1,0:T(8,128)(2,1)S(1)}, bf16[128,1536]{1,0:T(8,128)(2,1)S(1)}, u32[]{:S(2)}, u32[]{:S(2)}) collective-permute-start(bf16[128,1536]{1,0:T(8,128)(2,1)S(1)} %collective-permute-done.29.x1_ref.refs_3_), channel_id=1, source_target_pairs={{0,2},{2,0},{1,3},{3,1},{4,6},{6,4},{5,7},{7,5},{8,10},{10,8},{9,1... | collective-permute-start | bytes 1179656 | tf_op jit(solution)/shard_map/ppermute | solution.py:57
  199.6 9.3 %collective-permute-start.32 = (bf16[128,1536]{1,0:T(8,128)(2,1)S(1)}, bf16[128,1536]{1,0:T(8,128)(2,1)S(1)}, u32[]{:S(2)}, u32[]{:S(2)}) collective-permute-start(bf16[128,1536]{1,0:T(8,128)(2,1)S(1)} %get-tuple-element.201), channel_id=1, source_target_pairs={{0,2},{2,0},{1,3},{3,1},{4,6},{6,4},{5,7},{7,5},{8,10},{10,8},{9,1... | collective-permute-start | bytes 1179656 | tf_op jit(solution)/shard_map/ppermute | solution.py:57
  211.0 23.0 %collective-permute-start.40 = (bf16[4,128,1536]{2,1,0:T(8,128)(2,1)S(1)}, bf16[4,128,1536]{2,1,0:T(8,128)(2,1)S(1)}, u32[]{:S(2)}, u32[]{:S(2)}) collective-permute-start(bf16[4,128,1536]{2,1,0:T(8,128)(2,1)S(1)} %pad_maximum_fusion), channel_id=1, source_target_pairs={{0,2},{2,0},{1,3},{3,1},{4,6},{6,4},{5,7},{7,5},{8,10},{10,8},{9,1... | collective-permute-start | bytes 4718600 | tf_op jit(solution)/shard_map/ppermute | solution.py:57
  211.4 21.5 %collective-permute-start.39 = (bf16[128,1536]{1,0:T(8,128)(2,1)S(1)}, bf16[128,1536]{1,0:T(8,128)(2,1)S(1)}, u32[]{:S(2)}, u32[]{:S(2)}) collective-permute-start(bf16[128,1536]{1,0:T(8,128)(2,1)S(1)} %add_convert_fusion.6), channel_id=1, source_target_pairs={{4,0},{8,4},{12,8},{0,12},{5,1},{9,5},{13,9},{1,13},{6,2},{10,6},{... | collective-permute-start | bytes 1179656 | tf_op jit(solution)/shard_map/ppermute | solution.py:53
  213.2 19.7 %collective-permute-start.38 = (bf16[128,1536]{1,0:T(8,128)(2,1)S(1)}, bf16[128,1536]{1,0:T(8,128)(2,1)S(1)}, u32[]{:S(2)}, u32[]{:S(2)}) collective-permute-start(bf16[128,1536]{1,0:T(8,128)(2,1)S(1)} %add_convert_fusion.7), channel_id=1, source_target_pairs={{8,0},{12,4},{0,8},{4,12},{9,1},{13,5},{1,9},{5,13},{10,2},{14,6},... | collective-permute-start | bytes 1179656 | tf_op jit(solution)/shard_map/ppermute | solution.py:53
  213.5 20.3 %collective-permute-start.37 = (bf16[128,1536]{1,0:T(8,128)(2,1)S(1)}, bf16[128,1536]{1,0:T(8,128)(2,1)S(1)}, u32[]{:S(2)}, u32[]{:S(2)}) collective-permute-start(bf16[128,1536]{1,0:T(8,128)(2,1)S(1)} %add_convert_fusion.8), channel_id=1, source_target_pairs={{12,0},{0,4},{4,8},{8,12},{13,1},{1,5},{5,9},{9,13},{14,2},{2,6},{... | collective-permute-start | bytes 1179656 | tf_op jit(solution)/shard_map/ppermute | solution.py:53
  237.6 23.3 %collective-permute-start.41 = (bf16[128,1536]{1,0:T(8,128)(2,1)}, bf16[128,1536]{1,0:T(8,128)(2,1)S(1)}, u32[]{:S(2)}, u32[]{:S(2)}) collective-permute-start(bf16[128,1536]{1,0:T(8,128)(2,1)} %fusion.45.refs_0_), channel_id=1, source_target_pairs={{0,2},{2,0},{1,3},{3,1},{4,6},{6,4},{5,7},{7,5},{8,10},{10,8},{9,1... | collective-permute-start | bytes 1179656 | tf_op jit(solution)/shard_map/ppermute | solution.py:57
  237.6 19.6 %collective-permute-start.42 = (bf16[128,1536]{1,0:T(8,128)(2,1)}, bf16[128,1536]{1,0:T(8,128)(2,1)S(1)}, u32[]{:S(2)}, u32[]{:S(2)}) collective-permute-start(bf16[128,1536]{1,0:T(8,128)(2,1)} %fusion.45.refs_0_), channel_id=1, source_target_pairs={{4,0},{8,4},{12,8},{0,12},{5,1},{9,5},{13,9},{1,13},{6,2},{10,6},{... | collective-permute-start | bytes 1179656 | tf_op jit(solution)/shard_map/ppermute | solution.py:53
  239.4 17.8 %collective-permute-start.44 = (bf16[128,1536]{1,0:T(8,128)(2,1)}, bf16[128,1536]{1,0:T(8,128)(2,1)S(1)}, u32[]{:S(2)}, u32[]{:S(2)}) collective-permute-start(bf16[128,1536]{1,0:T(8,128)(2,1)} %fusion.45.refs_0_), channel_id=1, source_target_pairs={{8,0},{12,4},{0,8},{4,12},{9,1},{13,5},{1,9},{5,13},{10,2},{14,6},... | collective-permute-start | bytes 1179656 | tf_op jit(solution)/shard_map/ppermute | solution.py:53
  241.5 19.3 %collective-permute-start.46 = (bf16[128,1536]{1,0:T(8,128)(2,1)}, bf16[128,1536]{1,0:T(8,128)(2,1)S(1)}, u32[]{:S(2)}, u32[]{:S(2)}) collective-permute-start(bf16[128,1536]{1,0:T(8,128)(2,1)} %fusion.45.refs_0_), channel_id=1, source_target_pairs={{12,0},{0,4},{4,8},{8,12},{13,1},{1,5},{5,9},{9,13},{14,2},{2,6},{... | collective-permute-start | bytes 1179656 | tf_op jit(solution)/shard_map/ppermute | solution.py:53
  257.2 3.7 collective-permute-start.45
  262.6 36.8 %collective-permute-start.50 = (bf16[128,1536]{1,0:T(8,128)(2,1)S(1)}, bf16[128,1536]{1,0:T(8,128)(2,1)S(1)}, u32[]{:S(2)}, u32[]{:S(2)}) collective-permute-start(bf16[128,1536]{1,0:T(8,128)(2,1)S(1)} %get-tuple-element.254), channel_id=1, source_target_pairs={{4,0},{8,4},{12,8},{0,12},{5,1},{9,5},{13,9},{1,13},{6,2},{10,6},{... | collective-permute-start | bytes 1179656 | tf_op jit(solution)/shard_map/ppermute | solution.py:53
  263.7 35.6 %collective-permute-start.49 = (bf16[128,1536]{1,0:T(8,128)(2,1)S(1)}, bf16[128,1536]{1,0:T(8,128)(2,1)S(1)}, u32[]{:S(2)}, u32[]{:S(2)}) collective-permute-start(bf16[128,1536]{1,0:T(8,128)(2,1)S(1)} %get-tuple-element.253), channel_id=1, source_target_pairs={{8,0},{12,4},{0,8},{4,12},{9,1},{13,5},{1,9},{5,13},{10,2},{14,6},... | collective-permute-start | bytes 1179656 | tf_op jit(solution)/shard_map/ppermute | solution.py:53
  265.3 34.1 %collective-permute-start.48 = (bf16[128,1536]{1,0:T(8,128)(2,1)S(1)}, bf16[128,1536]{1,0:T(8,128)(2,1)S(1)}, u32[]{:S(2)}, u32[]{:S(2)}) collective-permute-start(bf16[128,1536]{1,0:T(8,128)(2,1)S(1)} %get-tuple-element.252), channel_id=1, source_target_pairs={{12,0},{0,4},{4,8},{8,12},{13,1},{1,5},{5,9},{9,13},{14,2},{2,6},{... | collective-permute-start | bytes 1179656 | tf_op jit(solution)/shard_map/ppermute | solution.py:53
  300.5 20.9 %collective-permute-start.51 = (bf16[8,128,128]{2,1,0:T(8,128)(2,1)S(1)}, bf16[8,128,128]{2,1,0:T(8,128)(2,1)S(1)}, u32[]{:S(2)}, u32[]{:S(2)}) collective-permute-start(bf16[8,128,128]{2,1,0:T(8,128)(2,1)S(1)} %get-tuple-element.260), channel_id=1, source_target_pairs={{0,1},{1,0},{2,3},{3,2},{4,5},{5,4},{6,7},{7,6},{8,9},{9,8},{10,11... | collective-permute-start | bytes 786440 | tf_op jit(solution)/shard_map/ppermute | solution.py:57
  303.5 17.9 %collective-permute-start.52 = (bf16[8,128,128]{2,1,0:T(8,128)(2,1)S(1)}, bf16[8,128,128]{2,1,0:T(8,128)(2,1)S(1)}, u32[]{:S(2)}, u32[]{:S(2)}) collective-permute-start(bf16[8,128,128]{2,1,0:T(8,128)(2,1)S(1)} %get-tuple-element.261), channel_id=1, source_target_pairs={{16,0},{17,1},{32,16},{33,17},{48,32},{49,33},{64,48},{65,49},{80,... | collective-permute-start | bytes 786440 | tf_op jit(solution)/shard_map/ppermute | solution.py:67
  305.6 17.5 %collective-permute-start.53 = (bf16[8,128,128]{2,1,0:T(8,128)(2,1)S(1)}, bf16[8,128,128]{2,1,0:T(8,128)(2,1)S(1)}, u32[]{:S(2)}, u32[]{:S(2)}) collective-permute-start(bf16[8,128,128]{2,1,0:T(8,128)(2,1)S(1)} %get-tuple-element.262), channel_id=1, source_target_pairs={{16,1},{17,0},{32,17},{33,16},{48,33},{49,32},{64,49},{65,48},{80,... | collective-permute-start | bytes 786440 | tf_op jit(solution)/shard_map/ppermute | solution.py:67
  307.6 19.6 %collective-permute-start.54 = (bf16[8,128,128]{2,1,0:T(8,128)(2,1)S(1)}, bf16[8,128,128]{2,1,0:T(8,128)(2,1)S(1)}, u32[]{:S(2)}, u32[]{:S(2)}) collective-permute-start(bf16[8,128,128]{2,1,0:T(8,128)(2,1)S(1)} %get-tuple-element.263), channel_id=1, source_target_pairs={{32,0},{33,1},{48,16},{49,17},{64,32},{65,33},{80,48},{81,49},{96,... | collective-permute-start | bytes 786440 | tf_op jit(solution)/shard_map/ppermute | solution.py:67
  313.6 16.8 %collective-permute-start.55 = (bf16[8,128,128]{2,1,0:T(8,128)(2,1)S(1)}, bf16[8,128,128]{2,1,0:T(8,128)(2,1)S(1)}, u32[]{:S(2)}, u32[]{:S(2)}) collective-permute-start(bf16[8,128,128]{2,1,0:T(8,128)(2,1)S(1)} %get-tuple-element.264), channel_id=1, source_target_pairs={{32,1},{33,0},{48,17},{49,16},{64,33},{65,32},{80,49},{81,48},{96,... | collective-permute-start | bytes 786440 | tf_op jit(solution)/shard_map/ppermute | solution.py:67
  345.9 6.7 %collective-permute-start.61 = (bf16[128,1536]{1,0:T(8,128)(2,1)}, bf16[128,1536]{1,0:T(8,128)(2,1)}, u32[]{:S(2)}, u32[]{:S(2)}) collective-permute-start(bf16[128,1536]{1,0:T(8,128)(2,1)} %get-tuple-element.295), channel_id=1, source_target_pairs={{0,2},{2,0},{1,3},{3,1},{4,6},{6,4},{5,7},{7,5},{8,10},{10,8},{9,1... | collective-permute-start | bytes 1179656 | tf_op jit(solution)/shard_map/ppermute | solution.py:57
  345.9 11.3 %collective-permute-start.59 = (bf16[128,1536]{1,0:T(8,128)(2,1)S(1)}, bf16[128,1536]{1,0:T(8,128)(2,1)}, u32[]{:S(2)}, u32[]{:S(2)}) collective-permute-start(bf16[128,1536]{1,0:T(8,128)(2,1)S(1)} %copy-done.44), channel_id=1, source_target_pairs={{0,2},{2,0},{1,3},{3,1},{4,6},{6,4},{5,7},{7,5},{8,10},{10,8},{9,1... | collective-permute-start | bytes 1179656 | tf_op jit(solution)/shard_map/ppermute | solution.py:57
  346.4 12.7 %collective-permute-start.57 = (bf16[128,1536]{1,0:T(8,128)(2,1)S(1)}, bf16[128,1536]{1,0:T(8,128)(2,1)}, u32[]{:S(2)}, u32[]{:S(2)}) collective-permute-start(bf16[128,1536]{1,0:T(8,128)(2,1)S(1)} %copy-done.42), channel_id=1, source_target_pairs={{0,2},{2,0},{1,3},{3,1},{4,6},{6,4},{5,7},{7,5},{8,10},{10,8},{9,1... | collective-permute-start | bytes 1179656 | tf_op jit(solution)/shard_map/ppermute | solution.py:57
  346.5 24.0 %collective-permute-start.56 = (bf16[128,1536]{1,0:T(8,128)(2,1)S(1)}, bf16[128,1536]{1,0:T(8,128)(2,1)}, u32[]{:S(2)}, u32[]{:S(2)}) collective-permute-start(bf16[128,1536]{1,0:T(8,128)(2,1)S(1)} %copy-done.40), channel_id=1, source_target_pairs={{0,2},{2,0},{1,3},{3,1},{4,6},{6,4},{5,7},{7,5},{8,10},{10,8},{9,1... | collective-permute-start | bytes 1179656 | tf_op jit(solution)/shard_map/ppermute | solution.py:57
  347.0 17.4 %all-to-all-start.3 = ((bf16[8,192,192]{2,1,0:T(8,128)(2,1)}), bf16[8,192,192]{2,1,0:T(8,128)(2,1)}, u32[]{:S(2)}, u32[]{:S(2)}) async-start(bf16[8,192,192]{2,1,0:T(8,128)(2,1)} %bitcast.41), calls=%async_computation.4 | async-start | bytes 1572864 | tf_op jit(solution)/shard_map/all_to_all | solution.py:71
  354.4 19.6 %collective-permute-start.62 = (bf16[128,1536]{1,0:T(8,128)(2,1)}, bf16[128,1536]{1,0:T(8,128)(2,1)S(1)}, u32[]{:S(2)}, u32[]{:S(2)}) collective-permute-start(bf16[128,1536]{1,0:T(8,128)(2,1)} %add_convert_fusion.1), channel_id=1, source_target_pairs={{4,0},{8,4},{12,8},{0,12},{5,1},{9,5},{13,9},{1,13},{6,2},{10,6},{... | collective-permute-start | bytes 1179656 | tf_op jit(solution)/shard_map/ppermute | solution.py:53
  358.3 15.8 %collective-permute-start.60 = (bf16[128,1536]{1,0:T(8,128)(2,1)S(1)}, bf16[128,1536]{1,0:T(8,128)(2,1)S(1)}, u32[]{:S(2)}, u32[]{:S(2)}) collective-permute-start(bf16[128,1536]{1,0:T(8,128)(2,1)S(1)} %add_convert_fusion.2), channel_id=1, source_target_pairs={{8,0},{12,4},{0,8},{4,12},{9,1},{13,5},{1,9},{5,13},{10,2},{14,6},... | collective-permute-start | bytes 1179656 | tf_op jit(solution)/shard_map/ppermute | solution.py:53
  361.0 17.6 %collective-permute-start.58 = (bf16[128,1536]{1,0:T(8,128)(2,1)}, bf16[128,1536]{1,0:T(8,128)(2,1)S(1)}, u32[]{:S(2)}, u32[]{:S(2)}) collective-permute-start(bf16[128,1536]{1,0:T(8,128)(2,1)} %add_convert_fusion.3), channel_id=1, source_target_pairs={{12,0},{0,4},{4,8},{8,12},{13,1},{1,5},{5,9},{9,13},{14,2},{2,6},{... | collective-permute-start | bytes 1179656 | tf_op jit(solution)/shard_map/ppermute | solution.py:53
  364.4 20.6 %all-to-all-start.2 = ((bf16[8,192,384]{2,1,0:T(8,128)(2,1)}), bf16[8,192,384]{2,1,0:T(8,128)(2,1)}, u32[]{:S(2)}, u32[]{:S(2)}) async-start(bf16[8,192,384]{2,1,0:T(8,128)(2,1)} %bitcast.39), calls=%async_computation.3 | async-start | bytes 2359296 | tf_op jit(solution)/shard_map/all_to_all | solution.py:71
  388.7 17.3 %all-to-all-start.4 = ((bf16[8,24,1872]{2,1,0:T(8,128)(2,1)}), bf16[8,24,1872]{2,1,0:T(8,128)(2,1)}, u32[]{:S(2)}, u32[]{:S(2)}) async-start(bf16[8,24,1872]{2,1,0:T(8,128)(2,1)} %concatenate.66), calls=%async_computation.5 | async-start | bytes 1474560 | tf_op jit(solution)/shard_map/all_to_all | solution.py:71
  407.3 9.4 %collective-permute-start.63 = (bf16[8,12,384]{2,1,0:T(8,128)(2,1)S(1)}, bf16[8,12,384]{2,1,0:T(8,128)(2,1)S(1)}, u32[]{:S(2)}, u32[]{:S(2)}) collective-permute-start(bf16[8,12,384]{2,1,0:T(8,128)(2,1)S(1)} %fusion.9), channel_id=1, source_target_pairs={{0,1},{1,0},{2,3},{3,2},{4,5},{5,4},{6,7},{7,6},{8,9},{9,8},{10,11... | collective-permute-start | bytes 221192 | tf_op jit(solution)/shard_map/ppermute | solution.py:57
  408.7 7.2 %collective-permute-start.64 = (bf16[4,24,192]{2,1,0:T(8,128)(2,1)S(1)}, bf16[4,24,192]{2,1,0:T(8,128)(2,1)S(1)}, u32[]{:S(2)}, u32[]{:S(2)}) collective-permute-start(bf16[4,24,192]{2,1,0:T(8,128)(2,1)S(1)} %dynamic-slice_convert_fusion), channel_id=1, source_target_pairs={{0,1},{1,0},{2,3},{3,2},{4,5},{5,4},{6,7},{7,6},{8,9},{9,8},{10,11... | collective-permute-start | bytes 110600 | tf_op jit(solution)/shard_map/ppermute | solution.py:57
  (96 other events, 753.4 us)
Sparse Core Ops, SparseCore 0:
  30.7 108.9 all-gather.1
  237.1 105.9 reduce-scatter.1
